TPU v7x, 32 devices: a whole 2x2x4 slice. The times are simulated.
32 devices in a mesh: groups: 2 (over y), row: 8 (over z, x), col: 2 (over core).
Axes of the slice: x: 2, y: 2, z: 4, core: 2. Of those that a mesh axis runs over, the one named last changes fastest.
Arguments:
- pair_in: bfloat16 [32, 16, 128], P(('groups', 'row'), 'col'), parts along dimension 0, may hold values from -6 to 6
- token_mask: int32 [32], P('groups'), parts along dimension 0, may hold values 0 or 1
- positions: int32 [32], P('groups'), parts along dimension 0, may hold values from 0 to 127
- relpos_table: bfloat16 [128, 128], replicated, may hold values from -6 to 6
- tri_norm_in: float32 [128], replicated, may hold values from 0.5 to 1.5
- tri_in_weight: bfloat16 [128, 256], replicated, may hold values from -0.5 to 0.5
- tri_in_gate: bfloat16 [128, 256], replicated, may hold values from -0.5 to 0.5
- tri_out_gate: bfloat16 [128, 128], replicated, may hold values from -0.5 to 0.5
- tri_norm_out: float32 [128], replicated, may hold values from 0.5 to 1.5
- tri_out_weight: bfloat16 [128, 128], replicated, may hold values from -0.5 to 0.5
- att_norm: float32 [128], replicated, may hold values from 0.5 to 1.5
- att_qkv: bfloat16 [128, 384], replicated, may hold values from -0.5 to 0.5
- att_gate: bfloat16 [128, 128], replicated, may hold values from -0.5 to 0.5
- att_bias: bfloat16 [128, 4], replicated, may hold values from -12 to 12
- att_out: bfloat16 [128, 128], replicated, may hold values from -0.5 to 0.5
Outputs:
- pair_out: bfloat16 [32, 16, 128], P(('groups', 'row'), 'col'), parts along dimension 0
There are 2 independent parts, one for each index of `groups`. A program takes and returns all parts, laid end to end along the dimension named above; an argument that names none is the same for every part. Nothing has to cross between parts.
All inputs are finite; a program needn't handle non-finite values.
Results may differ from a plain program's by a relative error of at most 0.012.
The roundings to bfloat16 on the way count: a program that leaves them out, or rounds other values in their place, can miss the bound.
Values may be sent and summed in bfloat16 or wider, within the bound.
No kernel may reach another device: no remote copies, remote signals or barrier semaphores. Data moves between devices by JAX's collectives and lax.ppermute only.
A program may use at most 64 MiB of HBM per device.

v0:
```python
import math

import jax
import jax.numpy as jnp
from jax import lax
from jax.sharding import PartitionSpec as P

epsilon = 1e-05


def layer_norm(values, gain):
    mean_val = jnp.mean(values, axis=-1, keepdims=True)
    centred = values - mean_val
    var_val = jnp.mean(centred * centred, axis=-1, keepdims=True)
    return centred * lax.rsqrt(var_val + epsilon) * gain


def attend_column(query_col, key_col, value_col, bias_all, key_bias, block_rows):
    tok_total = query_col.shape[0]
    scale = 1.0 / math.sqrt(query_col.shape[2])

    def one_block(block_idx):
        scores = (
            jnp.einsum("ihe,khe->hik", query_col, key_col, preferred_element_type=jnp.float32)
            * scale
        )
        scores = scores + bias_all.astype(jnp.float32) + key_bias[None, None, :]
        row_max = jnp.max(scores, axis=-1, keepdims=True)
        expo_f = jnp.exp(scores - row_max)
        totals = jnp.sum(expo_f, axis=-1)
        weights = expo_f.astype(jnp.bfloat16)
        result = jnp.einsum("hik,khe->ihe", weights, value_col, preferred_element_type=jnp.float32)
        return result / jnp.transpose(totals)[:, :, None]

    blocks = lax.map(one_block, jnp.arange(tok_total // block_rows))
    return blocks.reshape(tok_total, query_col.shape[1], query_col.shape[2])


def column_attention(columns, att_qkv, att_gate, bias_all, key_bias, head_local, head_dim):
    tok_total, col_count, channels = columns.shape
    local_width = head_local * head_dim
    weight_three = att_qkv.reshape(channels, 3, channels)
    qkv_all = jnp.einsum(
        "kmc,ctd->tmkd", columns, weight_three, preferred_element_type=jnp.float32
    ).astype(jnp.bfloat16)
    qkv_all = qkv_all.reshape(3, col_count, tok_total, head_local, head_dim)
    gate_val = jax.nn.sigmoid(
        jnp.einsum("kmc,cd->kmd", columns, att_gate, preferred_element_type=jnp.float32)
    )
    block_rows = min(1024, tok_total)

    def one_column(triple):
        return attend_column(triple[0], triple[1], triple[2], bias_all, key_bias, block_rows)

    attended = lax.map(one_column, (qkv_all[0], qkv_all[1], qkv_all[2]))
    attended = jnp.transpose(attended, (1, 0, 2, 3)).reshape(tok_total, col_count, local_width)
    return (gate_val * attended).astype(jnp.bfloat16)


def on_device(
    pair_in,
    token_mask,
    positions,
    relpos_table,
    tri_norm_in,
    tri_in_weight,
    tri_in_gate,
    tri_out_gate,
    tri_norm_out,
    tri_out_weight,
    att_norm,
    att_qkv,
    att_gate,
    att_bias,
    att_out,
):
    row_count, col_count, channels = pair_in.shape
    row_first = lax.axis_index("row") * row_count
    col_first = lax.axis_index("col") * col_count
    mask_float = token_mask.astype(jnp.float32)
    row_mask = lax.dynamic_slice_in_dim(mask_float, row_first, row_count)
    col_mask = lax.dynamic_slice_in_dim(mask_float, col_first, col_count)
    row_pos = lax.dynamic_slice_in_dim(positions, row_first, row_count)
    col_pos = lax.dynamic_slice_in_dim(positions, col_first, col_count)
    bin_count = relpos_table.shape[0]
    bin_centre = bin_count // 2
    bucket = jnp.clip(row_pos[:, None] - col_pos[None, :], -bin_centre, bin_centre - 1) + bin_centre
    onehot = (bucket[:, :, None] == jnp.arange(bin_count, dtype=jnp.int32)[None, None, :]).astype(
        jnp.bfloat16
    )
    residual = pair_in.astype(jnp.float32) + jnp.einsum(
        "rjb,bc->rjc", onehot, relpos_table, preferred_element_type=jnp.float32
    )
    normed = layer_norm(residual, tri_norm_in).astype(jnp.bfloat16)
    pair_mask = row_mask[:, None] * col_mask[None, :]
    gate_in = jnp.einsum("rjc,cd->drj", normed, tri_in_gate, preferred_element_type=jnp.float32)
    proj_in = jnp.einsum("rjc,cd->drj", normed, tri_in_weight, preferred_element_type=jnp.float32)
    projected = (jax.nn.sigmoid(gate_in) * proj_in * pair_mask[None, :, :]).astype(jnp.bfloat16)
    left_ch, right_ch = (
        lax.all_to_all(projected[:channels], "row", split_axis=0, concat_axis=1, tiled=True),
        lax.all_to_all(projected[channels:], "row", split_axis=0, concat_axis=1, tiled=True),
    )
    right_rows = lax.all_to_all(right_ch, "col", split_axis=1, concat_axis=2, tiled=True)
    product_sum = jnp.einsum(
        "cik,cjk->cij",
        lax.all_gather(left_ch, "col", axis=2, tiled=True),
        right_rows,
        preferred_element_type=jnp.float32,
    )
    products = product_sum.astype(jnp.bfloat16)
    product_tile = lax.all_to_all(products, "row", split_axis=1, concat_axis=0, tiled=True)
    tri_x = jnp.transpose(product_tile, (1, 2, 0)).astype(jnp.float32)
    normed_out = layer_norm(tri_x, tri_norm_out).astype(jnp.bfloat16)
    out_gate = jax.nn.sigmoid(
        jnp.einsum("rjc,cd->rjd", normed, tri_out_gate, preferred_element_type=jnp.float32)
    )
    residual = residual + out_gate * jnp.einsum(
        "rjc,cd->rjd", normed_out, tri_out_weight, preferred_element_type=jnp.float32
    )
    normed_att = layer_norm(residual, att_norm).astype(jnp.bfloat16)
    bias_piece = jnp.einsum(
        "kic,ch->hik", normed_att, att_bias, preferred_element_type=jnp.float32
    ).astype(jnp.bfloat16)
    key_bias = (mask_float - 1.0) * 1000000000.0
    head_count = att_bias.shape[1]
    head_dim = channels // head_count
    columns = lax.all_to_all(normed_att, "row", split_axis=1, concat_axis=0, tiled=True)
    bias_half = lax.all_gather(bias_piece, "col", axis=1, tiled=True)
    bias_all = lax.all_gather(bias_half, "row", axis=2, tiled=True)
    gated = column_attention(columns, att_qkv, att_gate, bias_all, key_bias, head_count, head_dim)
    gated_tile = lax.all_to_all(gated, "row", split_axis=0, concat_axis=1, tiled=True)
    update = jnp.einsum("rjc,cd->rjd", gated_tile, att_out, preferred_element_type=jnp.float32)
    return (residual + update).astype(jnp.bfloat16)


def solution(mesh):
    return jax.shard_map(
        on_device,
        mesh=mesh,
        in_specs=(
            P(("groups", "row"), "col", None),
            P("groups"),
            P("groups"),
            P(),
            P(),
            P(),
            P(),
            P(),
            P(),
            P(),
            P(),
            P(),
            P(),
            P(),
            P(),
        ),
        out_specs=P(("groups", "row"), "col", None),
        check_vma=False,
    )
```

profile of v0, /device:TPU:0, one launch (start us, length us, event | category | flops | bytes accessed | tf_op | source)
XLA Modules:
  0.0 92.8 jit_solution(1812011191039637279)
XLA Ops:
  0.0 0.8 dynamic_slice.19
  0.8 0.7 dynamic_slice.20
  1.5 0.7 convert_element_type.76
  2.4 0.3 fusion.44
  2.7 0.2 multiply_reduce_fusion.2
  2.8 0.6 copy-done.4
  3.6 0.1 fusion.6
  3.9 0.2 copy.108
  4.1 0.7 reshape.147
  4.8 7.3 %all-to-all-start.1 = ((bf16[8,2,128]{2,1,0:T(2,128)(2,1)}), bf16[8,2,128]{2,1,0:T(2,128)(2,1)S(1)}, u32[]{:S(2)}, u32[]{:S(2)}) async-start(bf16[8,2,128]{2,1,0:T(2,128)(2,1)} %reshape.147), calls=%async_computation.1 | async-start | bytes 8192 | tf_op jit(solution)/shard_map/all_to_all | solution.py:101
  12.0 0.1 copy.104
  12.2 0.7 reshape.145
  12.9 5.6 %all-to-all-done.1 = bf16[8,2,128]{2,1,0:T(2,128)(2,1)S(1)} async-done(((bf16[8,2,128]{2,1,0:T(2,128)(2,1)}), bf16[8,2,128]{2,1,0:T(2,128)(2,1)S(1)}, u32[]{:S(2)}, u32[]{:S(2)}) %all-to-all-start.1) | async-done | bytes 4128 | tf_op jit(solution)/shard_map/all_to_all | solution.py:101
  18.5 0.1 reshape.148
  18.7 0.1 reshape.149
  18.8 3.7 %all_to_all.96 = bf16[2,2,512]{2,1,0:T(2,128)(2,1)S(1)} all-to-all(bf16[2,2,512]{2,1,0:T(2,128)(2,1)S(1)} %reshape.149), channel_id=1, replica_groups=mesh['groups'=2,'row'=8,'col'=2] {'col'}, dimensions={0} | all-to-all | bytes 8192 | tf_op jit(solution)/shard_map/all_to_all | solution.py:103
  22.5 3.3 %all-to-all-start = ((bf16[8,2,128]{2,1,0:T(2,128)(2,1)}), bf16[8,2,128]{2,1,0:T(2,128)(2,1)S(1)}, u32[]{:S(2)}, u32[]{:S(2)}) async-start(bf16[8,2,128]{2,1,0:T(2,128)(2,1)} %reshape.145), calls=%async_computation | async-start | bytes 8192 | tf_op jit(solution)/shard_map/all_to_all | solution.py:100
  25.9 0.1 fusion.17
  26.0 0.1 reshape.150
  26.2 6.0 %all-to-all-done = bf16[8,2,128]{2,1,0:T(2,128)(2,1)S(1)} async-done(((bf16[8,2,128]{2,1,0:T(2,128)(2,1)}), bf16[8,2,128]{2,1,0:T(2,128)(2,1)S(1)}, u32[]{:S(2)}, u32[]{:S(2)}) %all-to-all-start) | async-done | bytes 4128 | tf_op jit(solution)/shard_map/all_to_all | solution.py:100
  32.2 0.1 reshape.146
  32.4 0.1 copy.107
  32.5 1.9 %all_gather.9 = bf16[16,16,16]{1,2,0:T(8,128)(2,1)S(1)} all-gather(bf16[16,16,8]{1,2,0:T(8,128)(2,1)S(1)} %copy.107), channel_id=1, replica_groups=mesh['groups'=2,'row'=8,'col'=2] {'col'}, dimensions={2}, use_global_device_ids=true | all-gather | bytes 12288 | tf_op jit(solution)/shard_map/all_gather | solution.py:106
  34.4 0.1 convolution_convert_fusion
  34.5 0.1 copy.113
  34.6 0.7 reshape.151
  35.3 3.4 %all-to-all-start.3 = ((bf16[8,2,128]{2,1,0:T(2,128)(2,1)}), bf16[8,2,128]{2,1,0:T(2,128)(2,1)S(1)}, u32[]{:S(2)}, u32[]{:S(2)}) async-start(bf16[8,2,128]{2,1,0:T(2,128)(2,1)} %reshape.151), calls=%async_computation.3 | async-start | bytes 8192 | tf_op jit(solution)/shard_map/all_to_all | solution.py:111
  38.8 0.1 copy.116
  38.9 6.2 %all-to-all-done.3 = bf16[8,2,128]{2,1,0:T(2,128)(2,1)S(1)} async-done(((bf16[8,2,128]{2,1,0:T(2,128)(2,1)}), bf16[8,2,128]{2,1,0:T(2,128)(2,1)S(1)}, u32[]{:S(2)}, u32[]{:S(2)}) %all-to-all-start.3) | async-done | bytes 4128 | tf_op jit(solution)/shard_map/all_to_all | solution.py:111
  45.4 0.2 multiply_reduce_fusion.1
  45.6 0.4 copy-done.9
  46.0 0.2 copy-done.13
  46.2 0.3 fusion.45
  46.5 0.2 multiply_reduce_fusion
  46.7 0.7 copy-done.5
  47.4 0.6 copy.115
  48.0 3.4 %all-to-all-start.4 = ((bf16[2,8,128]{2,0,1:T(2,128)(2,1)}), bf16[2,8,128]{2,0,1:T(2,128)(2,1)S(1)}, u32[]{:S(2)}, u32[]{:S(2)}) async-start(bf16[2,8,128]{2,0,1:T(2,128)(2,1)} %copy.115), calls=%async_computation.4 | async-start | bytes 8192 | tf_op jit(solution)/shard_map/all_to_all | solution.py:127
  51.5 0.1 fusion.21
  51.6 0.1 copy.120
  51.7 1.8 %all_gather.10 = bf16[4,16,2]{0,2,1:T(2,128)(2,1)S(1)} all-gather(bf16[4,8,2]{0,2,1:T(2,128)(2,1)S(1)} %copy.120), channel_id=1, replica_groups=mesh['groups'=2,'row'=8,'col'=2] {'col'}, dimensions={1}, use_global_device_ids=true | all-gather | bytes 384 | tf_op jit(solution)/shard_map/all_gather | solution.py:128
  53.6 26.5 %all_gather.11 = bf16[4,16,16]{1,0,2:T(4,128)(2,1)S(1)} all-gather(bf16[4,16,2]{1,0,2:T(4,128)(2,1)S(1)} %copy.121), channel_id=1, replica_groups=mesh['groups'=2,'row'=8,'col'=2] {'row'}, dimensions={2}, use_global_device_ids=true | all-gather | bytes 2304 | tf_op jit(solution)/shard_map/all_gather | solution.py:129
  80.1 0.1 fusion.8
  80.5 0.2 fusion.46
  80.7 0.2 fusion
  81.0 0.7 copy-done.10
  81.7 0.1 fusion.20
  81.8 10.2 %all_to_all.97 = bf16[8,2,128]{2,1,0:T(2,128)(2,1)S(1)} all-to-all(bf16[8,2,128]{2,1,0:T(2,128)(2,1)S(1)} %bitcast.129), channel_id=1, replica_groups=mesh['groups'=2,'row'=8,'col'=2] {'row'}, dimensions={0} | all-to-all | bytes 8192 | tf_op jit(solution)/shard_map/all_to_all | solution.py:131
  92.1 0.7 fusion.19
  (60 shorter events, 1.7 us)
Async XLA Ops:
  0.0 3.6 %copy-start = (bf16[128,256]{1,0:T(8,128)(2,1)S(1)}, bf16[128,256]{1,0:T(8,128)(2,1)}, u32[]{:S(2)}) copy-start(bf16[128,256]{1,0:T(8,128)(2,1)} %param.21) | copy-start | bytes 196612
  0.0 2.4 %copy-start.7 = (bf16[128,128]{1,0:T(8,128)(2,1)S(1)}, bf16[128,128]{1,0:T(8,128)(2,1)}, u32[]{:S(2)}) copy-start(bf16[128,128]{1,0:T(8,128)(2,1)} %param.18) | copy-start | bytes 98308
  1.5 0.9 copy-start.11
  2.8 0.7 copy-start.4
  2.8 1.0 %copy-start.6 = (bf16[128,256]{1,0:T(8,128)(2,1)S(1)}, bf16[128,256]{1,0:T(8,128)(2,1)}, u32[]{:S(2)}) copy-start(bf16[128,256]{1,0:T(8,128)(2,1)} %param.20) | copy-start | bytes 196612
  4.8 13.7 %all-to-all-start.1 = ((bf16[8,2,128]{2,1,0:T(2,128)(2,1)}), bf16[8,2,128]{2,1,0:T(2,128)(2,1)S(1)}, u32[]{:S(2)}, u32[]{:S(2)}) async-start(bf16[8,2,128]{2,1,0:T(2,128)(2,1)} %reshape.147), calls=%async_computation.1 | async-start | bytes 8192 | tf_op jit(solution)/shard_map/all_to_all | solution.py:101
  18.7 7.1 %copy-start.8 = (bf16[128,128]{1,0:T(8,128)(2,1)S(1)}, bf16[128,128]{1,0:T(8,128)(2,1)}, u32[]{:S(2)}) copy-start(bf16[128,128]{1,0:T(8,128)(2,1)} %param.22) | copy-start | bytes 98308
  22.5 9.6 %all-to-all-start = ((bf16[8,2,128]{2,1,0:T(2,128)(2,1)}), bf16[8,2,128]{2,1,0:T(2,128)(2,1)S(1)}, u32[]{:S(2)}, u32[]{:S(2)}) async-start(bf16[8,2,128]{2,1,0:T(2,128)(2,1)} %reshape.145), calls=%async_computation | async-start | bytes 8192 | tf_op jit(solution)/shard_map/all_to_all | solution.py:100
  34.4 4.4 %copy-start.1 = (bf16[128,384]{1,0:T(8,128)(2,1)S(1)}, bf16[128,384]{1,0:T(8,128)(2,1)}, u32[]{:S(2)}) copy-start(bf16[128,384]{1,0:T(8,128)(2,1)} %param.26) | copy-start | bytes 294916
  35.3 3.5 %copy-start.12 = (s32[16]{0:T(128)S(1)}, s32[16]{0:T(128)}, u32[]{:S(2)}) copy-start(s32[16]{0:T(128)} %param.16) | copy-start | bytes 196
  35.3 9.8 %all-to-all-start.3 = ((bf16[8,2,128]{2,1,0:T(2,128)(2,1)}), bf16[8,2,128]{2,1,0:T(2,128)(2,1)S(1)}, u32[]{:S(2)}, u32[]{:S(2)}) async-start(bf16[8,2,128]{2,1,0:T(2,128)(2,1)} %reshape.151), calls=%async_computation.3 | async-start | bytes 8192 | tf_op jit(solution)/shard_map/all_to_all | solution.py:111
  45.2 0.8 copy-start.9
  45.6 0.7 copy-start.13
  46.7 0.7 copy-start.5
  48.0 3.5 %copy-start.3 = (bf16[128,4]{0,1:T(4,128)(2,1)S(1)}, bf16[128,4]{0,1:T(4,128)(2,1)}, u32[]{:S(2)}) copy-start(bf16[128,4]{0,1:T(4,128)(2,1)} %param.28) | copy-start | bytes 3076
  48.0 32.1 %all-to-all-start.4 = ((bf16[2,8,128]{2,0,1:T(2,128)(2,1)}), bf16[2,8,128]{2,0,1:T(2,128)(2,1)S(1)}, u32[]{:S(2)}, u32[]{:S(2)}) async-start(bf16[2,8,128]{2,0,1:T(2,128)(2,1)} %copy.115), calls=%async_computation.4 | async-start | bytes 8192 | tf_op jit(solution)/shard_map/all_to_all | solution.py:127
  80.9 0.8 copy-start.10
  81.8 10.3 %copy-start.2 = (bf16[128,128]{1,0:T(8,128)(2,1)S(1)}, bf16[128,128]{1,0:T(8,128)(2,1)}, u32[]{:S(2)}) copy-start(bf16[128,128]{1,0:T(8,128)(2,1)} %param.29) | copy-start | bytes 98308
where the time goes:
time: 93.6 us; the launch traced here: 92.8 us
  blocking collectives  44.1 us (47%)
  waiting for transfers between devices  17.7 us (19%)
  starting transfers between devices  17.4 us (19%)
  local copies, waits for them, and re-layouts  9.23 us (10%)
  matrix products  2.48 us (3%)
  other arithmetic  1.61 us (2%)
    all_gather x1, blocking collectives, on_device(): bias_all = lax.all_gather(bias_half, 'row', axis=2, tiled=True)  26.5 us
    all_to_all x1, blocking collectives, on_device(): lax.all_to_all(gated, 'row', split_axis=0, concat_axis=1, tiled=True)  10.2 us
    all_to_all x1, starting transfers between devices, on_device(): lax.all_to_all(projected[channels:], 'row', split_axis=0, concat_axis=1,...  7.25 us
    all_to_all x1, waiting for transfers between devices, on_device(): lax.all_to_all(products, 'row', split_axis=1, concat_axis=0, tiled=True)  6.17 us
    all_to_all x1, waiting for transfers between devices, on_device(): lax.all_to_all(projected[:channels], 'row', split_axis=0, concat_axis=1,...  5.96 us
    all_to_all x1, waiting for transfers between devices, on_device(): lax.all_to_all(projected[channels:], 'row', split_axis=0, concat_axis=1,...  5.62 us
    unnamed x40, local copies, waits for them, and re-layouts  5.45 us
    all_to_all x1, blocking collectives, on_device(): lax.all_to_all(right_ch, 'col', split_axis=1, concat_axis=2, tiled=True)  3.69 us
  transfers between devices with their start and end apart: 4, of which 3 were waited for; matrix products, arithmetic and copies ran while one was open for 2% of the time, Pallas kernels for 0%

commit v1 on v0

--- a/solution.py
+++ b/solution.py
@@ -1,11 +1,16 @@
+import functools
 import math
 
 import jax
 import jax.numpy as jnp
 from jax import lax
+from jax.experimental import pallas as pl
+from jax.experimental.pallas import tpu as pltpu
 from jax.sharding import PartitionSpec as P
 
 epsilon = 1e-05
+
+WHOLE_PAIR_BYTES = 256 * 1024
 
 
 def layer_norm(values, gain):
@@ -13,6 +18,220 @@
     centred = values - mean_val
     var_val = jnp.mean(centred * centred, axis=-1, keepdims=True)
     return centred * lax.rsqrt(var_val + epsilon) * gain
+
+
+def sigmoid(values):
+    return 0.5 * jnp.tanh(0.5 * values) + 0.5
+
+
+def dot(left, right):
+    return jnp.dot(left, right, preferred_element_type=jnp.float32)
+
+
+def dot_t(left, right):
+    return lax.dot_general(
+        left, right, (((1,), (1,)), ((), ())), preferred_element_type=jnp.float32
+    )
+
+
+def round_bf16(values):
+    return values.astype(jnp.bfloat16).astype(jnp.float32)
+
+
+def whole_pair_kernel(
+    row_dim,
+    heads,
+    mask_ref,
+    pos_ref,
+    pair_ref,
+    table_ref,
+    norm_in_ref,
+    in_weight_ref,
+    in_gate_ref,
+    out_gate_ref,
+    norm_out_ref,
+    out_weight_ref,
+    att_norm_ref,
+    qkv_ref,
+    att_gate_ref,
+    att_bias_ref,
+    att_out_ref,
+    out_ref,
+    base_ref,
+    normed_ref,
+    left_ref,
+    right_ref,
+    att_ref,
+    upd_ref,
+):
+    blocks, rows, cols, width = pair_ref.shape
+    col_dim = blocks // row_dim
+    tokens = row_dim * rows
+    bins = table_ref.shape[0]
+    head_dim = width // heads
+    row_first = lax.axis_index("row") * rows
+    col_first = pl.multiple_of(lax.axis_index("col") * cols, cols)
+    f32, bf16 = jnp.float32, jnp.bfloat16
+
+    sub = lax.broadcasted_iota(jnp.int32, (cols, bins), 0)
+    lane = lax.broadcasted_iota(jnp.int32, (cols, bins), 1)
+    col_pos, col_mask = [], []
+    for half in range(col_dim):
+        pos_vec = jnp.zeros((cols, bins), jnp.int32)
+        mask_vec = jnp.zeros((cols, bins), jnp.int32)
+        for c in range(cols):
+            pos_vec = jnp.where(sub == c, pos_ref[half * cols + c], pos_vec)
+            mask_vec = jnp.where(sub == c, mask_ref[half * cols + c], mask_vec)
+        col_pos.append(pos_vec)
+        col_mask.append(mask_vec)
+    hot, pair, masks = [], [], []
+    for i in range(tokens):
+        for half in range(col_dim):
+            bucket = jnp.clip(pos_ref[i] - col_pos[half], -(bins // 2), bins // 2 - 1) + bins // 2
+            hot.append((bucket == lane).astype(f32))
+            masks.append((col_mask[half] * mask_ref[i]).astype(f32)[:, :1])
+            pair.append(pair_ref[(i // rows) * col_dim + half].astype(f32)[i % rows])
+    hot = jnp.concatenate(hot, axis=0).astype(bf16)
+    masks = jnp.concatenate(masks, axis=0)
+    base = jnp.concatenate(pair, axis=0) + dot(hot, table_ref[...])
+    base_ref[...] = base
+
+    normed = layer_norm(base, norm_in_ref[...]).astype(bf16)
+    normed_ref[...] = normed.astype(f32)
+    projected = sigmoid(dot(normed, in_gate_ref[...])) * dot(normed, in_weight_ref[...]) * masks
+    projected = round_bf16(projected)
+    left_ref[...] = projected[:, :width]
+    right_ref[...] = projected[:, width:]
+
+    right_at = [right_ref[pl.ds(col_first * tokens + m, cols, stride=tokens), :] for m in range(tokens)]
+    products = []
+    for i in range(tokens):
+        total = left_ref[pl.ds(i * tokens, 1), :] * right_at[0]
+        for m in range(1, tokens):
+            total = total + left_ref[pl.ds(i * tokens + m, 1), :] * right_at[m]
+        products.append(total)
+    extra = [None] * rows
+    for m in range(tokens):
+        left_at = left_ref[pl.ds(m, tokens, stride=tokens), :]
+        for r in range(rows):
+            term = left_at * right_ref[pl.ds((row_first + r) * tokens + m, 1), :]
+            extra[r] = term if m == 0 else extra[r] + term
+    products = round_bf16(jnp.concatenate(products + extra, axis=0))
+
+    def chosen(ref):
+        own = [ref[pl.ds(i * tokens + col_first, cols), :] for i in range(tokens)]
+        own += [ref[pl.ds(row_first + r, tokens, stride=tokens), :] for r in range(rows)]
+        return jnp.concatenate(own, axis=0)
+
+    normed_out = layer_norm(products, norm_out_ref[...]).astype(bf16)
+    out_gate = sigmoid(dot(chosen(normed_ref).astype(bf16), out_gate_ref[...]))
+    updated = chosen(base_ref) + out_gate * dot(normed_out, out_weight_ref[...])
+    normed_att = layer_norm(updated, att_norm_ref[...]).astype(bf16)
+    own_pairs = rows * cols
+    column_pairs = tokens * cols
+    upd_ref[...] = updated[:column_pairs]
+    att_f = normed_att.astype(f32)
+    att_ref[...] = att_f[:column_pairs]
+
+    own_at = pl.ds(pl.multiple_of(row_first * cols, own_pairs), own_pairs)
+    own = att_ref[own_at, :].astype(bf16)
+    column = normed_att[:column_pairs]
+    queries = dot(own, qkv_ref[:, :width])
+    keys = dot(column, qkv_ref[:, width : 2 * width]).astype(bf16)
+    values = dot(column, qkv_ref[:, 2 * width :]).astype(bf16)
+    own_gate = sigmoid(dot(own, att_gate_ref[...]))
+
+    bias = []
+    for r in range(rows):
+        part = att_f[column_pairs + r * tokens : column_pairs + (r + 1) * tokens]
+        spread = jnp.concatenate(
+            [jnp.broadcast_to(part[k : k + 1], (cols, width)) for k in range(tokens)], axis=0
+        )
+        bias.append(round_bf16(dot_t(att_bias_ref[...], spread.astype(bf16))))
+
+    head_of = lax.broadcasted_iota(jnp.int32, (own_pairs, width), 1) // head_dim
+    queries = round_bf16(queries)
+    by_head = jnp.concatenate(
+        [jnp.where(head_of == h, queries, 0.0) for h in range(heads)], axis=0
+    ).astype(bf16)
+    scores = dot_t(by_head, keys) * (1.0 / math.sqrt(head_dim))
+    biases = jnp.concatenate(
+        [jnp.broadcast_to(bias[r][h : h + 1], (cols, column_pairs)) for h in range(heads) for r in range(rows)],
+        axis=0,
+    )
+    lane_row = lax.broadcasted_iota(jnp.int32, (1, column_pairs), 1)
+    key_mask = jnp.zeros((1, column_pairs), jnp.int32)
+    for k in range(tokens):
+        key_mask = jnp.where(lane_row // cols == k, mask_ref[k], key_mask)
+    key_bias = (key_mask.astype(f32) - 1.0) * 1000000000.0
+    scores = scores + biases + key_bias
+    same = (
+        lax.broadcasted_iota(jnp.int32, scores.shape, 1) % cols
+        == lax.broadcasted_iota(jnp.int32, scores.shape, 0) % cols
+    )
+    scores = jnp.where(same, scores, -jnp.inf)
+    expo = jnp.exp(scores - jnp.max(scores, axis=-1, keepdims=True))
+    totals = jnp.sum(expo, axis=-1, keepdims=True)
+    mixed = dot(expo.astype(bf16), values) / totals
+    attended = jnp.zeros((own_pairs, width), f32)
+    for h in range(heads):
+        attended = jnp.where(head_of == h, mixed[h * own_pairs : (h + 1) * own_pairs], attended)
+
+    gated = (own_gate * attended).astype(bf16)
+    result = upd_ref[own_at, :] + dot(gated, att_out_ref[...])
+    out_ref[...] = result.reshape(rows, cols, width).astype(bf16)
+
+
+def whole_pair_on_device(
+    row_dim,
+    pair_in,
+    token_mask,
+    positions,
+    relpos_table,
+    tri_norm_in,
+    tri_in_weight,
+    tri_in_gate,
+    tri_out_gate,
+    tri_norm_out,
+    tri_out_weight,
+    att_norm,
+    att_qkv,
+    att_gate,
+    att_bias,
+    att_out,
+):
+    rows, cols, width = pair_in.shape
+    tokens = row_dim * rows
+    heads = att_bias.shape[1]
+    pair = lax.all_gather(pair_in, ("row", "col"), axis=0, tiled=False)
+    in_vmem = pl.BlockSpec(memory_space=pltpu.VMEM)
+    in_smem = pl.BlockSpec(memory_space=pltpu.SMEM)
+    wide = pltpu.VMEM((tokens * tokens, width), jnp.float32)
+    column = pltpu.VMEM((tokens * cols, width), jnp.float32)
+    return pl.pallas_call(
+        functools.partial(whole_pair_kernel, row_dim, heads),
+        out_shape=jax.ShapeDtypeStruct(pair_in.shape, pair_in.dtype),
+        in_specs=[in_smem] * 2 + [in_vmem] * 13,
+        out_specs=in_vmem,
+        scratch_shapes=[wide] * 4 + [column] * 2,
+        compiler_params=pltpu.CompilerParams(vmem_limit_bytes=16 * 1024 * 1024),
+    )(
+        token_mask,
+        positions,
+        pair,
+        relpos_table,
+        tri_norm_in.reshape(1, width),
+        tri_in_weight,
+        tri_in_gate,
+        tri_out_gate,
+        tri_norm_out.reshape(1, width),
+        tri_out_weight,
+        att_norm.reshape(1, width),
+        att_qkv,
+        att_gate,
+        att_bias.T,
+        att_out,
+    )
 
 
 def attend_column(query_col, key_col, value_col, bias_all, key_bias, block_rows):
@@ -57,7 +276,7 @@
     return (gate_val * attended).astype(jnp.bfloat16)
 
 
-def on_device(
+def split_pair_on_device(
     pair_in,
     token_mask,
     positions,
@@ -133,27 +352,20 @@
     return (residual + update).astype(jnp.bfloat16)
 
 
+def on_device(row_dim, pair_in, *others):
+    rows, cols, width = pair_in.shape
+    tokens = row_dim * rows
+    whole_bytes = tokens * tokens * width * pair_in.dtype.itemsize
+    if whole_bytes <= WHOLE_PAIR_BYTES and cols % 8 == 0 and width % 128 == 0:
+        return whole_pair_on_device(row_dim, pair_in, *others)
+    return split_pair_on_device(pair_in, *others)
+
+
 def solution(mesh):
     return jax.shard_map(
-        on_device,
+        functools.partial(on_device, mesh.shape["row"]),
         mesh=mesh,
-        in_specs=(
-            P(("groups", "row"), "col", None),
-            P("groups"),
-            P("groups"),
-            P(),
-            P(),
-            P(),
-            P(),
-            P(),
-            P(),
-            P(),
-            P(),
-            P(),
-            P(),
-            P(),
-            P(),
-        ),
+        in_specs=(P(("groups", "row"), "col", None), P("groups"), P("groups")) + (P(),) * 12,
         out_specs=P(("groups", "row"), "col", None),
         check_vma=False,
     )

time: 93.6 us -> 33.3 us (0.36)
  blocking collectives: 44.1 us -> 23.6 us
  waiting for transfers between devices: 17.7 us -> 0 us
  starting transfers between devices: 17.4 us -> 0 us
  local copies, waits for them, and re-layouts: 9.23 us -> 6.18 us
  Pallas kernels: 0 us -> 2.89 us
  matrix products: 2.48 us -> 0 us
  other arithmetic: 1.61 us -> 0 us
    all_to_all x4 -> x0, waiting for transfers between devices: 17.7 us -> none  [the longest x1 6.17 us: on_device(): lax.all_to_all(products, 'row', split_axis=1, concat_axis=0, tiled=True)]
    all_to_all x4 -> x0, starting transfers between devices: 17.4 us -> none  [the longest x1 7.25 us: on_device(): lax.all_to_all(projected[channels:], 'row', split_axis=0, concat_axis=1,...]
    all_to_all x2 -> x0, blocking collectives: 13.9 us -> none  [the longest x1 10.2 us: on_device(): lax.all_to_all(gated, 'row', split_axis=0, concat_axis=1, tiled=True)]
    all_gather x3 -> x1, blocking collectives: 30.1 us -> 23.6 us  [whole_pair_on_device(): pair = lax.all_gather(pair_in, ('row', 'col'), axis=0, tiled=False)]
    pallas_call x0 -> x1, Pallas kernels: none -> 2.89 us  [whole_pair_on_device(): pl.pallas_call(functools.partial(whole_pair_kernel, row_dim, heads), out_...]
    dot_general x12 -> x0, matrix products: 2.48 us -> none  [the longest x1 0.73 us: on_device(): jnp.einsum('rjc,cd->rjd', gated_tile, att_out, preferred_element_type=jnp...]
    dynamic_slice x4 -> x0, local copies, waits for them, and re-layouts: 1.64 us -> none  [the longest x1 0.77 us: on_device(): row_pos = lax.dynamic_slice_in_dim(positions, row_first, row_count)]
    unnamed x40 -> x28, local copies, waits for them, and re-layouts: 5.45 us -> 6.18 us
  transfers between devices with their start and end apart: 4 -> 0, of which waited for: 3 -> 0; matrix products, arithmetic and copies ran while one was open for 2% -> 0% of each run, Pallas kernels for 0% -> 0%
where the time goes in v1:
time: 33.3 us; the launch traced here: 32.7 us
  blocking collectives  23.6 us (71%)
  local copies, waits for them, and re-layouts  6.18 us (19%)
  Pallas kernels  2.89 us (9%)
    all_gather x1, blocking collectives, whole_pair_on_device(): pair = lax.all_gather(pair_in, ('row', 'col'), axis=0, tiled=False)  23.6 us
    unnamed x28, local copies, waits for them, and re-layouts  6.18 us
    pallas_call x1, Pallas kernels, whole_pair_on_device(): pl.pallas_call(functools.partial(whole_pair_kernel, row_dim, heads), out_...  2.89 us

profile of v1, /device:TPU:0, one launch (start us, length us, event | category | flops | bytes accessed | tf_op | source)
XLA Modules:
  0.0 32.7 jit_solution(1326550093349185837)
XLA Ops:
  0.0 0.0 copy-start.1
  0.0 0.0 copy-start.10
  0.0 0.0 copy-start.11
  0.0 0.0 copy-start.12
  0.0 0.0 copy-start.13
  0.0 23.6 %all-gather = bf16[32,8,128]{2,1,0:T(8,128)(2,1)S(1)} all-gather(bf16[2,8,128]{2,1,0:T(8,128)(2,1)} %param.15), channel_id=2, replica_groups=mesh['groups'=2,'row'=8,'col'=2] {'row','col'}, dimensions={0}, use_global_device_ids=true | all-gather | bytes 69632 | tf_op jit(solution)/shard_map/all_gather | solution.py:206
  23.6 0.0 copy-start.8
  23.6 0.0 copy-start.9
  23.6 0.0 copy-done.1
  23.7 0.0 copy-done.10
  23.7 0.0 copy-done.11
  23.7 0.0 copy-done.12
  23.7 0.0 copy-done.13
  23.7 0.6 %copy-done.8 = bf16[128,4]{0,1:T(4,128)(2,1)S(1)} copy-done((bf16[128,4]{0,1:T(4,128)(2,1)S(1)}, bf16[128,4]{0,1:T(4,128)(2,1)}, u32[]{:S(2)}) %copy-start.8) | copy-done | bytes 1048
  24.3 0.0 copy-done.9
  24.3 0.0 copy-start
  24.3 0.9 %copy-done = bf16[128,384]{1,0:T(8,128)(2,1)S(1)} copy-done((bf16[128,384]{1,0:T(8,128)(2,1)S(1)}, bf16[128,384]{1,0:T(8,128)(2,1)}, u32[]{:S(2)}) %copy-start) | copy-done | bytes 98328
  25.2 0.0 copy-start.2
  25.2 0.8 %copy-done.2 = bf16[128,256]{1,0:T(8,128)(2,1)S(1)} copy-done((bf16[128,256]{1,0:T(8,128)(2,1)S(1)}, bf16[128,256]{1,0:T(8,128)(2,1)}, u32[]{:S(2)}) %copy-start.2) | copy-done | bytes 65560
  26.1 0.0 copy-start.3
  26.1 0.8 %copy-done.3 = bf16[128,128]{1,0:T(8,128)(2,1)S(1)} copy-done((bf16[128,128]{1,0:T(8,128)(2,1)S(1)}, bf16[128,128]{1,0:T(8,128)(2,1)}, u32[]{:S(2)}) %copy-start.3) | copy-done | bytes 32792
  26.8 0.0 copy-start.4
  26.8 0.8 %copy-done.4 = bf16[128,128]{1,0:T(8,128)(2,1)S(1)} copy-done((bf16[128,128]{1,0:T(8,128)(2,1)S(1)}, bf16[128,128]{1,0:T(8,128)(2,1)}, u32[]{:S(2)}) %copy-start.4) | copy-done | bytes 32792
  27.6 0.0 copy-start.5
  27.6 0.8 %copy-done.5 = bf16[128,128]{1,0:T(8,128)(2,1)S(1)} copy-done((bf16[128,128]{1,0:T(8,128)(2,1)S(1)}, bf16[128,128]{1,0:T(8,128)(2,1)}, u32[]{:S(2)}) %copy-start.5) | copy-done | bytes 32792
  28.3 0.0 copy-start.6
  28.3 0.8 %copy-done.6 = bf16[128,128]{1,0:T(8,128)(2,1)S(1)} copy-done((bf16[128,128]{1,0:T(8,128)(2,1)S(1)}, bf16[128,128]{1,0:T(8,128)(2,1)}, u32[]{:S(2)}) %copy-start.6) | copy-done | bytes 32792
  29.1 0.0 copy-start.7
  29.1 0.8 %copy-done.7 = bf16[128,128]{1,0:T(8,128)(2,1)S(1)} copy-done((bf16[128,128]{1,0:T(8,128)(2,1)S(1)}, bf16[128,128]{1,0:T(8,128)(2,1)}, u32[]{:S(2)}) %copy-start.7) | copy-done | bytes 32792
  29.9 2.9 %shard_map.145 = bf16[2,8,128]{2,1,0:T(8,128)(2,1)} custom-call(s32[16]{0:T(128)S(1)} %copy-done.9, s32[16]{0:T(128)S(1)} %copy-done.10, bf16[16,2,8,128]{3,2,1,0:T(8,128)(2,1)S(1)} %bitcast.5, bf16[128,128]{1,0:T(8,128)(2,1)S(1)} %copy-done.3, f32[1,128]{1,0:T(1,128)S(1)} %bitcast.7, bf16[128,256]{1,0:T(8,128)(2,1)S(1)} %copy-done.1, ...), custom_call_target="tpu_custom_call" | custom-call | tf_op jit(solution)/shard_map/pallas_call | solution.py:211
Async XLA Ops:
  0.0 23.6 %copy-start.1 = (bf16[128,256]{1,0:T(8,128)(2,1)S(1)}, bf16[128,256]{1,0:T(8,128)(2,1)}, u32[]{:S(2)}) copy-start(bf16[128,256]{1,0:T(8,128)(2,1)} %in_weight_ref.1) | copy-start | bytes 196612
  0.0 23.7 %copy-start.10 = (s32[16]{0:T(128)S(1)}, s32[16]{0:T(128)}, u32[]{:S(2)}) copy-start(s32[16]{0:T(128)} %pos_ref.1) | copy-start | bytes 196
  0.0 23.7 %copy-start.11 = (f32[128]{0:T(128)S(1)}, f32[128]{0:T(128)}, u32[]{:S(2)}) copy-start(f32[128]{0:T(128)} %param.19) | copy-start | bytes 1540
  0.0 23.7 %copy-start.12 = (f32[128]{0:T(128)S(1)}, f32[128]{0:T(128)}, u32[]{:S(2)}) copy-start(f32[128]{0:T(128)} %param.23) | copy-start | bytes 1540
  0.0 23.7 %copy-start.13 = (f32[128]{0:T(128)S(1)}, f32[128]{0:T(128)}, u32[]{:S(2)}) copy-start(f32[128]{0:T(128)} %param.25) | copy-start | bytes 1540
  23.6 0.7 %copy-start.8 = (bf16[128,4]{0,1:T(4,128)(2,1)S(1)}, bf16[128,4]{0,1:T(4,128)(2,1)}, u32[]{:S(2)}) copy-start(bf16[128,4]{0,1:T(4,128)(2,1)} %param.28) | copy-start | bytes 3076
  23.6 0.7 %copy-start.9 = (s32[16]{0:T(128)S(1)}, s32[16]{0:T(128)}, u32[]{:S(2)}) copy-start(s32[16]{0:T(128)} %mask_ref.1) | copy-start | bytes 196
  24.3 0.9 %copy-start = (bf16[128,384]{1,0:T(8,128)(2,1)S(1)}, bf16[128,384]{1,0:T(8,128)(2,1)}, u32[]{:S(2)}) copy-start(bf16[128,384]{1,0:T(8,128)(2,1)} %qkv_ref.1) | copy-start | bytes 294916
  25.2 0.8 %copy-start.2 = (bf16[128,256]{1,0:T(8,128)(2,1)S(1)}, bf16[128,256]{1,0:T(8,128)(2,1)}, u32[]{:S(2)}) copy-start(bf16[128,256]{1,0:T(8,128)(2,1)} %in_gate_ref.1) | copy-start | bytes 196612
  26.1 0.8 %copy-start.3 = (bf16[128,128]{1,0:T(8,128)(2,1)S(1)}, bf16[128,128]{1,0:T(8,128)(2,1)}, u32[]{:S(2)}) copy-start(bf16[128,128]{1,0:T(8,128)(2,1)} %table_ref.1) | copy-start | bytes 98308
  26.8 0.8 %copy-start.4 = (bf16[128,128]{1,0:T(8,128)(2,1)S(1)}, bf16[128,128]{1,0:T(8,128)(2,1)}, u32[]{:S(2)}) copy-start(bf16[128,128]{1,0:T(8,128)(2,1)} %out_gate_ref.1) | copy-start | bytes 98308
  27.6 0.8 %copy-start.5 = (bf16[128,128]{1,0:T(8,128)(2,1)S(1)}, bf16[128,128]{1,0:T(8,128)(2,1)}, u32[]{:S(2)}) copy-start(bf16[128,128]{1,0:T(8,128)(2,1)} %out_weight_ref.1) | copy-start | bytes 98308
  28.3 0.8 %copy-start.6 = (bf16[128,128]{1,0:T(8,128)(2,1)S(1)}, bf16[128,128]{1,0:T(8,128)(2,1)}, u32[]{:S(2)}) copy-start(bf16[128,128]{1,0:T(8,128)(2,1)} %att_gate_ref.1) | copy-start | bytes 98308
  29.1 0.8 %copy-start.7 = (bf16[128,128]{1,0:T(8,128)(2,1)S(1)}, bf16[128,128]{1,0:T(8,128)(2,1)}, u32[]{:S(2)}) copy-start(bf16[128,128]{1,0:T(8,128)(2,1)} %att_out_ref.1) | copy-start | bytes 98308

commit v2 on v1

--- a/solution.py
+++ b/solution.py
@@ -38,12 +38,16 @@
     return values.astype(jnp.bfloat16).astype(jnp.float32)
 
 
-def whole_pair_kernel(
+def whole_pair_kernel(row_dim, blocks, heads, mask_ref, pos_ref, *refs):
+    whole_pair_steps(row_dim, heads, mask_ref, pos_ref, refs[:blocks], *refs[blocks:])
+
+
+def whole_pair_steps(
     row_dim,
     heads,
     mask_ref,
     pos_ref,
-    pair_ref,
+    block_refs,
     table_ref,
     norm_in_ref,
     in_weight_ref,
@@ -64,14 +68,22 @@
     att_ref,
     upd_ref,
 ):
-    blocks, rows, cols, width = pair_ref.shape
-    col_dim = blocks // row_dim
+    rows, cols, width = block_refs[0].shape
+    col_dim = len(block_refs) // row_dim
     tokens = row_dim * rows
     bins = table_ref.shape[0]
     head_dim = width // heads
     row_first = lax.axis_index("row") * rows
     col_first = pl.multiple_of(lax.axis_index("col") * cols, cols)
     f32, bf16 = jnp.float32, jnp.bfloat16
+
+    me = lax.axis_index("row") * col_dim + lax.axis_index("col")
+    for m, block_ref in enumerate(block_refs):
+        owner = me ^ m
+        block = block_ref[...].astype(f32)
+        for r in range(rows):
+            first = (owner // col_dim * rows + r) * tokens + owner % col_dim * cols
+            base_ref[pl.ds(pl.multiple_of(first, cols), cols), :] = block[r]
 
     sub = lax.broadcasted_iota(jnp.int32, (cols, bins), 0)
     lane = lax.broadcasted_iota(jnp.int32, (cols, bins), 1)
@@ -84,16 +96,15 @@
             mask_vec = jnp.where(sub == c, mask_ref[half * cols + c], mask_vec)
         col_pos.append(pos_vec)
         col_mask.append(mask_vec)
-    hot, pair, masks = [], [], []
+    hot, masks = [], []
     for i in range(tokens):
         for half in range(col_dim):
             bucket = jnp.clip(pos_ref[i] - col_pos[half], -(bins // 2), bins // 2 - 1) + bins // 2
             hot.append((bucket == lane).astype(f32))
             masks.append((col_mask[half] * mask_ref[i]).astype(f32)[:, :1])
-            pair.append(pair_ref[(i // rows) * col_dim + half].astype(f32)[i % rows])
     hot = jnp.concatenate(hot, axis=0).astype(bf16)
     masks = jnp.concatenate(masks, axis=0)
-    base = jnp.concatenate(pair, axis=0) + dot(hot, table_ref[...])
+    base = base_ref[...] + dot(hot, table_ref[...])
     base_ref[...] = base
 
     normed = layer_norm(base, norm_in_ref[...]).astype(bf16)
@@ -184,6 +195,7 @@
 
 def whole_pair_on_device(
     row_dim,
+    col_dim,
     pair_in,
     token_mask,
     positions,
@@ -203,22 +215,26 @@
     rows, cols, width = pair_in.shape
     tokens = row_dim * rows
     heads = att_bias.shape[1]
-    pair = lax.all_gather(pair_in, ("row", "col"), axis=0, tiled=False)
+    blocks = row_dim * col_dim
+    pair = [pair_in]
+    for m in range(1, blocks):
+        partners = [(device, device ^ m) for device in range(blocks)]
+        pair.append(lax.ppermute(pair_in, ("row", "col"), partners))
     in_vmem = pl.BlockSpec(memory_space=pltpu.VMEM)
     in_smem = pl.BlockSpec(memory_space=pltpu.SMEM)
     wide = pltpu.VMEM((tokens * tokens, width), jnp.float32)
     column = pltpu.VMEM((tokens * cols, width), jnp.float32)
     return pl.pallas_call(
-        functools.partial(whole_pair_kernel, row_dim, heads),
+        functools.partial(whole_pair_kernel, row_dim, blocks, heads),
         out_shape=jax.ShapeDtypeStruct(pair_in.shape, pair_in.dtype),
-        in_specs=[in_smem] * 2 + [in_vmem] * 13,
+        in_specs=[in_smem] * 2 + [in_vmem] * (blocks + 12),
         out_specs=in_vmem,
         scratch_shapes=[wide] * 4 + [column] * 2,
         compiler_params=pltpu.CompilerParams(vmem_limit_bytes=16 * 1024 * 1024),
     )(
         token_mask,
         positions,
-        pair,
+        *pair,
         relpos_table,
         tri_norm_in.reshape(1, width),
         tri_in_weight,
@@ -352,18 +368,20 @@
     return (residual + update).astype(jnp.bfloat16)
 
 
-def on_device(row_dim, pair_in, *others):
+def on_device(row_dim, col_dim, pair_in, *others):
     rows, cols, width = pair_in.shape
     tokens = row_dim * rows
     whole_bytes = tokens * tokens * width * pair_in.dtype.itemsize
-    if whole_bytes <= WHOLE_PAIR_BYTES and cols % 8 == 0 and width % 128 == 0:
-        return whole_pair_on_device(row_dim, pair_in, *others)
+    blocks = row_dim * col_dim
+    tiled = cols % 8 == 0 and width % 128 == 0 and blocks & (blocks - 1) == 0
+    if whole_bytes <= WHOLE_PAIR_BYTES and tiled:
+        return whole_pair_on_device(row_dim, col_dim, pair_in, *others)
     return split_pair_on_device(pair_in, *others)
 
 
 def solution(mesh):
     return jax.shard_map(
-        functools.partial(on_device, mesh.shape["row"]),
+        functools.partial(on_device, mesh.shape["row"], mesh.shape["col"]),
         mesh=mesh,
         in_specs=(P(("groups", "row"), "col", None), P("groups"), P("groups")) + (P(),) * 12,
         out_specs=P(("groups", "row"), "col", None),

time: 33.3 us -> 38.5 us (1.16)
  blocking collectives: 23.6 us -> 0 us
  starting transfers between devices: 0 us -> 22.9 us
  waiting for transfers between devices: 0 us -> 4.93 us
  local copies, waits for them, and re-layouts: 6.18 us -> 7.07 us
    all_gather x1 -> x0, blocking collectives: 23.6 us -> none  [whole_pair_on_device(): pair = lax.all_gather(pair_in, ('row', 'col'), axis=0, tiled=False)]
    ppermute x0 -> x15, starting transfers between devices: none -> 22.9 us  [whole_pair_on_device(): pair.append(lax.ppermute(pair_in, ('row', 'col'), partners))]
    ppermute x0 -> x15, waiting for transfers between devices: none -> 4.93 us  [whole_pair_on_device(): pair.append(lax.ppermute(pair_in, ('row', 'col'), partners))]
    unnamed x28 -> x30, local copies, waits for them, and re-layouts: 6.18 us -> 7.07 us
  transfers between devices with their start and end apart: 0 -> 15, of which waited for: 0 -> 2; matrix products, arithmetic and copies ran while one was open for 0% -> 0% of each run, Pallas kernels for 0% -> 0%
where the time goes in v2:
time: 38.5 us; the launch traced here: 37.9 us
  starting transfers between devices  22.9 us (59%)
  local copies, waits for them, and re-layouts  7.07 us (18%)
  waiting for transfers between devices  4.93 us (13%)
  Pallas kernels  2.87 us (7%)
    ppermute x15, starting transfers between devices, whole_pair_on_device(): pair.append(lax.ppermute(pair_in, ('row', 'col'), partners))  22.9 us
    unnamed x30, local copies, waits for them, and re-layouts  7.07 us
    ppermute x15, waiting for transfers between devices, whole_pair_on_device(): pair.append(lax.ppermute(pair_in, ('row', 'col'), partners))  4.93 us
    pallas_call x1, Pallas kernels, whole_pair_on_device(): pl.pallas_call(functools.partial(whole_pair_kernel, row_dim, blocks, head...  2.87 us
  transfers between devices with their start and end apart: 15, of which 2 were waited for; matrix products, arithmetic and copies ran while one was open for 0% of the time, Pallas kernels for 0%

profile of v2, /device:TPU:0, one launch (start us, length us, event | category | flops | bytes accessed | tf_op | source)
XLA Modules:
  0.0 37.9 jit_solution(2653362647874354181)
XLA Ops:
  0.0 6.0 %collective-permute-start.13 = (bf16[2,8,128]{2,1,0:T(8,128)(2,1)}, bf16[2,8,128]{2,1,0:T(8,128)(2,1)S(1)}, u32[]{:S(2)}, u32[]{:S(2)}) collective-permute-start(bf16[2,8,128]{2,1,0:T(8,128)(2,1)} %refs_0_.1), channel_id=1, source_target_pairs={{0,14},{1,15},{2,12},{3,13},{4,10},{5,11},{6,8},{7,9},{8,6},{9,7},... | collective-permute-start | bytes 12296 | tf_op jit(solution)/shard_map/ppermute | solution.py:222
  6.0 0.0 collective-permute-start.12
  6.0 3.0 %collective-permute-start.11 = (bf16[2,8,128]{2,1,0:T(8,128)(2,1)}, bf16[2,8,128]{2,1,0:T(8,128)(2,1)S(1)}, u32[]{:S(2)}, u32[]{:S(2)}) collective-permute-start(bf16[2,8,128]{2,1,0:T(8,128)(2,1)} %refs_0_.1), channel_id=1, source_target_pairs={{0,12},{1,13},{2,14},{3,15},{4,8},{5,9},{6,10},{7,11},{8,4},{9,5},... | collective-permute-start | bytes 12296 | tf_op jit(solution)/shard_map/ppermute | solution.py:222
  9.0 0.0 collective-permute-start.10
  9.0 4.1 %collective-permute-start.9 = (bf16[2,8,128]{2,1,0:T(8,128)(2,1)}, bf16[2,8,128]{2,1,0:T(8,128)(2,1)S(1)}, u32[]{:S(2)}, u32[]{:S(2)}) collective-permute-start(bf16[2,8,128]{2,1,0:T(8,128)(2,1)} %refs_0_.1), channel_id=1, source_target_pairs={{0,10},{1,11},{2,8},{3,9},{4,14},{5,15},{6,12},{7,13},{8,2},{9,3},... | collective-permute-start | bytes 12296 | tf_op jit(solution)/shard_map/ppermute | solution.py:222
  13.1 0.0 collective-permute-done.13.refs_14_
  13.1 0.0 collective-permute-start.8
  13.1 0.0 collective-permute-done.12.refs_13_
  13.1 2.1 %collective-permute-start.7 = (bf16[2,8,128]{2,1,0:T(8,128)(2,1)}, bf16[2,8,128]{2,1,0:T(8,128)(2,1)S(1)}, u32[]{:S(2)}, u32[]{:S(2)}) collective-permute-start(bf16[2,8,128]{2,1,0:T(8,128)(2,1)} %refs_0_.1), channel_id=1, source_target_pairs={{0,8},{1,9},{2,10},{3,11},{4,12},{5,13},{6,14},{7,15},{8,0},{9,1},... | collective-permute-start | bytes 12296 | tf_op jit(solution)/shard_map/ppermute | solution.py:222
  15.2 0.0 collective-permute-done.11.refs_12_
  15.2 0.0 collective-permute-start.6
  15.2 0.0 collective-permute-done.10.refs_11_
  15.2 3.2 %collective-permute-start.5 = (bf16[2,8,128]{2,1,0:T(8,128)(2,1)}, bf16[2,8,128]{2,1,0:T(8,128)(2,1)S(1)}, u32[]{:S(2)}, u32[]{:S(2)}) collective-permute-start(bf16[2,8,128]{2,1,0:T(8,128)(2,1)} %refs_0_.1), channel_id=1, source_target_pairs={{0,6},{1,7},{2,4},{3,5},{4,2},{5,3},{6,0},{7,1},{8,14},{9,15},{10,... | collective-permute-start | bytes 12296 | tf_op jit(solution)/shard_map/ppermute | solution.py:222
  18.4 0.0 collective-permute-done.9.refs_10_
  18.4 0.0 collective-permute-start.4
  18.4 0.0 collective-permute-done.8.refs_9_
  18.4 1.2 %collective-permute-start.3 = (bf16[2,8,128]{2,1,0:T(8,128)(2,1)}, bf16[2,8,128]{2,1,0:T(8,128)(2,1)S(1)}, u32[]{:S(2)}, u32[]{:S(2)}) collective-permute-start(bf16[2,8,128]{2,1,0:T(8,128)(2,1)} %refs_0_.1), channel_id=1, source_target_pairs={{0,4},{1,5},{2,6},{3,7},{4,0},{5,1},{6,2},{7,3},{8,12},{9,13},{10,... | collective-permute-start | bytes 12296 | tf_op jit(solution)/shard_map/ppermute | solution.py:222
  19.6 0.0 collective-permute-done.7.refs_8_
  19.6 0.8 %collective-permute-start.2 = (bf16[2,8,128]{2,1,0:T(8,128)(2,1)}, bf16[2,8,128]{2,1,0:T(8,128)(2,1)S(1)}, u32[]{:S(2)}, u32[]{:S(2)}) collective-permute-start(bf16[2,8,128]{2,1,0:T(8,128)(2,1)} %refs_0_.1), channel_id=1, source_target_pairs={{0,3},{1,2},{2,1},{3,0},{4,7},{5,6},{6,5},{7,4},{8,11},{9,10},{10,... | collective-permute-start | bytes 12296 | tf_op jit(solution)/shard_map/ppermute | solution.py:222
  20.4 0.0 collective-permute-done.6.refs_7_
  20.4 1.5 %collective-permute-start.1 = (bf16[2,8,128]{2,1,0:T(8,128)(2,1)}, bf16[2,8,128]{2,1,0:T(8,128)(2,1)S(1)}, u32[]{:S(2)}, u32[]{:S(2)}) collective-permute-start(bf16[2,8,128]{2,1,0:T(8,128)(2,1)} %refs_0_.1), channel_id=1, source_target_pairs={{0,2},{1,3},{2,0},{3,1},{4,6},{5,7},{6,4},{7,5},{8,10},{9,11},{10,... | collective-permute-start | bytes 12296 | tf_op jit(solution)/shard_map/ppermute | solution.py:222
  21.9 0.0 collective-permute-done.5.refs_6_
  21.9 0.0 collective-permute-start
  21.9 0.0 collective-permute-done.4.refs_5_
  21.9 1.1 %collective-permute-start.14 = (bf16[2,8,128]{2,1,0:T(8,128)(2,1)}, bf16[2,8,128]{2,1,0:T(8,128)(2,1)S(1)}, u32[]{:S(2)}, u32[]{:S(2)}) collective-permute-start(bf16[2,8,128]{2,1,0:T(8,128)(2,1)} %refs_0_.1), channel_id=1, source_target_pairs={{0,15},{1,14},{2,13},{3,12},{4,11},{5,10},{6,9},{7,8},{8,7},{9,6},... | collective-permute-start | bytes 12296 | tf_op jit(solution)/shard_map/ppermute | solution.py:222
  23.0 0.0 collective-permute-done.3.refs_4_
  23.0 0.0 collective-permute-done.2.refs_3_
  23.0 1.2 %collective-permute-done.1.refs_2_ = bf16[2,8,128]{2,1,0:T(8,128)(2,1)S(1)} collective-permute-done((bf16[2,8,128]{2,1,0:T(8,128)(2,1)}, bf16[2,8,128]{2,1,0:T(8,128)(2,1)S(1)}, u32[]{:S(2)}, u32[]{:S(2)}) %collective-permute-start.1) | collective-permute-done | bytes 4128 | tf_op jit(solution)/shard_map/ppermute | solution.py:222
  24.2 0.0 collective-permute-done.refs_1_
  24.2 3.7 %collective-permute-done.14.refs_15_ = bf16[2,8,128]{2,1,0:T(8,128)(2,1)S(1)} collective-permute-done((bf16[2,8,128]{2,1,0:T(8,128)(2,1)}, bf16[2,8,128]{2,1,0:T(8,128)(2,1)S(1)}, u32[]{:S(2)}, u32[]{:S(2)}) %collective-permute-start.14) | collective-permute-done | bytes 4128 | tf_op jit(solution)/shard_map/ppermute | solution.py:222
  27.9 0.0 copy-start.9
  27.9 0.0 copy-start.10
  27.9 0.0 copy-done.8
  27.9 0.6 %copy-done.11 = s32[16]{0:T(128)S(1)} copy-done((s32[16]{0:T(128)S(1)}, s32[16]{0:T(128)}, u32[]{:S(2)}) %copy-start.11) | copy-done | bytes 88
  28.6 0.0 copy-done.12
  28.6 0.0 copy-done.13
  28.6 0.0 copy-done.14
  28.6 0.0 copy-done.9
  28.6 0.0 copy-done.10
  28.6 0.9 %copy-done = bf16[128,384]{1,0:T(8,128)(2,1)S(1)} copy-done((bf16[128,384]{1,0:T(8,128)(2,1)S(1)}, bf16[128,384]{1,0:T(8,128)(2,1)}, u32[]{:S(2)}) %copy-start) | copy-done | bytes 98328
  29.5 0.8 %copy-done.1 = bf16[128,256]{1,0:T(8,128)(2,1)S(1)} copy-done((bf16[128,256]{1,0:T(8,128)(2,1)S(1)}, bf16[128,256]{1,0:T(8,128)(2,1)}, u32[]{:S(2)}) %copy-start.1) | copy-done | bytes 65560
  30.4 0.8 %copy-done.2 = bf16[128,256]{1,0:T(8,128)(2,1)S(1)} copy-done((bf16[128,256]{1,0:T(8,128)(2,1)S(1)}, bf16[128,256]{1,0:T(8,128)(2,1)}, u32[]{:S(2)}) %copy-start.2) | copy-done | bytes 65560
  31.2 0.8 %copy-done.3 = bf16[128,128]{1,0:T(8,128)(2,1)S(1)} copy-done((bf16[128,128]{1,0:T(8,128)(2,1)S(1)}, bf16[128,128]{1,0:T(8,128)(2,1)}, u32[]{:S(2)}) %copy-start.3) | copy-done | bytes 32792
  32.0 0.8 %copy-done.4 = bf16[128,128]{1,0:T(8,128)(2,1)S(1)} copy-done((bf16[128,128]{1,0:T(8,128)(2,1)S(1)}, bf16[128,128]{1,0:T(8,128)(2,1)}, u32[]{:S(2)}) %copy-start.4) | copy-done | bytes 32792
  32.7 0.8 %copy-done.5 = bf16[128,128]{1,0:T(8,128)(2,1)S(1)} copy-done((bf16[128,128]{1,0:T(8,128)(2,1)S(1)}, bf16[128,128]{1,0:T(8,128)(2,1)}, u32[]{:S(2)}) %copy-start.5) | copy-done | bytes 32792
  33.5 0.8 %copy-done.6 = bf16[128,128]{1,0:T(8,128)(2,1)S(1)} copy-done((bf16[128,128]{1,0:T(8,128)(2,1)S(1)}, bf16[128,128]{1,0:T(8,128)(2,1)}, u32[]{:S(2)}) %copy-start.6) | copy-done | bytes 32792
  34.3 0.8 %copy-done.7 = bf16[128,128]{1,0:T(8,128)(2,1)S(1)} copy-done((bf16[128,128]{1,0:T(8,128)(2,1)S(1)}, bf16[128,128]{1,0:T(8,128)(2,1)}, u32[]{:S(2)}) %copy-start.7) | copy-done | bytes 32792
  35.0 2.9 %shard_map.145 = bf16[2,8,128]{2,1,0:T(8,128)(2,1)} custom-call(s32[16]{0:T(128)S(1)} %copy-done.10, s32[16]{0:T(128)S(1)} %copy-done.11, bf16[2,8,128]{2,1,0:T(8,128)(2,1)S(1)} %copy-done.8, bf16[2,8,128]{2,1,0:T(8,128)(2,1)S(1)} %collective-permute-done.refs_1_, bf16[2,8,128]{2,1,0:T(8,128)(2,1)S(1)} %collective-permute-done.1.refs_2_, ...), custom_call_target="tpu_custom_call" | custom-call | tf_op jit(solution)/shard_map/pallas_call | solution.py:227
  (13 shorter events, 0.0 us)
Async XLA Ops:
  0.0 27.9 %copy-start.8 = (bf16[2,8,128]{2,1,0:T(8,128)(2,1)S(1)}, bf16[2,8,128]{2,1,0:T(8,128)(2,1)}, u32[]{:S(2)}) copy-start(bf16[2,8,128]{2,1,0:T(8,128)(2,1)} %refs_0_.1) | copy-start | bytes 12292
  0.0 13.1 %collective-permute-start.13 = (bf16[2,8,128]{2,1,0:T(8,128)(2,1)}, bf16[2,8,128]{2,1,0:T(8,128)(2,1)S(1)}, u32[]{:S(2)}, u32[]{:S(2)}) collective-permute-start(bf16[2,8,128]{2,1,0:T(8,128)(2,1)} %refs_0_.1), channel_id=1, source_target_pairs={{0,14},{1,15},{2,12},{3,13},{4,10},{5,11},{6,8},{7,9},{8,6},{9,7},... | collective-permute-start | bytes 12296 | tf_op jit(solution)/shard_map/ppermute | solution.py:222
  6.0 7.1 %collective-permute-start.12 = (bf16[2,8,128]{2,1,0:T(8,128)(2,1)}, bf16[2,8,128]{2,1,0:T(8,128)(2,1)S(1)}, u32[]{:S(2)}, u32[]{:S(2)}) collective-permute-start(bf16[2,8,128]{2,1,0:T(8,128)(2,1)} %refs_0_.1), channel_id=1, source_target_pairs={{0,13},{1,12},{2,15},{3,14},{4,9},{5,8},{6,11},{7,10},{8,5},{9,4},... | collective-permute-start | bytes 12296 | tf_op jit(solution)/shard_map/ppermute | solution.py:222
  6.0 9.2 %collective-permute-start.11 = (bf16[2,8,128]{2,1,0:T(8,128)(2,1)}, bf16[2,8,128]{2,1,0:T(8,128)(2,1)S(1)}, u32[]{:S(2)}, u32[]{:S(2)}) collective-permute-start(bf16[2,8,128]{2,1,0:T(8,128)(2,1)} %refs_0_.1), channel_id=1, source_target_pairs={{0,12},{1,13},{2,14},{3,15},{4,8},{5,9},{6,10},{7,11},{8,4},{9,5},... | collective-permute-start | bytes 12296 | tf_op jit(solution)/shard_map/ppermute | solution.py:222
  9.0 6.2 %collective-permute-start.10 = (bf16[2,8,128]{2,1,0:T(8,128)(2,1)}, bf16[2,8,128]{2,1,0:T(8,128)(2,1)S(1)}, u32[]{:S(2)}, u32[]{:S(2)}) collective-permute-start(bf16[2,8,128]{2,1,0:T(8,128)(2,1)} %refs_0_.1), channel_id=1, source_target_pairs={{0,11},{1,10},{2,9},{3,8},{4,15},{5,14},{6,13},{7,12},{8,3},{9,2},... | collective-permute-start | bytes 12296 | tf_op jit(solution)/shard_map/ppermute | solution.py:222
  9.0 9.4 %collective-permute-start.9 = (bf16[2,8,128]{2,1,0:T(8,128)(2,1)}, bf16[2,8,128]{2,1,0:T(8,128)(2,1)S(1)}, u32[]{:S(2)}, u32[]{:S(2)}) collective-permute-start(bf16[2,8,128]{2,1,0:T(8,128)(2,1)} %refs_0_.1), channel_id=1, source_target_pairs={{0,10},{1,11},{2,8},{3,9},{4,14},{5,15},{6,12},{7,13},{8,2},{9,3},... | collective-permute-start | bytes 12296 | tf_op jit(solution)/shard_map/ppermute | solution.py:222
  13.1 5.3 %collective-permute-start.8 = (bf16[2,8,128]{2,1,0:T(8,128)(2,1)}, bf16[2,8,128]{2,1,0:T(8,128)(2,1)S(1)}, u32[]{:S(2)}, u32[]{:S(2)}) collective-permute-start(bf16[2,8,128]{2,1,0:T(8,128)(2,1)} %refs_0_.1), channel_id=1, source_target_pairs={{0,9},{1,8},{2,11},{3,10},{4,13},{5,12},{6,15},{7,14},{8,1},{9,0},... | collective-permute-start | bytes 12296 | tf_op jit(solution)/shard_map/ppermute | solution.py:222
  13.1 6.5 %collective-permute-start.7 = (bf16[2,8,128]{2,1,0:T(8,128)(2,1)}, bf16[2,8,128]{2,1,0:T(8,128)(2,1)S(1)}, u32[]{:S(2)}, u32[]{:S(2)}) collective-permute-start(bf16[2,8,128]{2,1,0:T(8,128)(2,1)} %refs_0_.1), channel_id=1, source_target_pairs={{0,8},{1,9},{2,10},{3,11},{4,12},{5,13},{6,14},{7,15},{8,0},{9,1},... | collective-permute-start | bytes 12296 | tf_op jit(solution)/shard_map/ppermute | solution.py:222
  15.2 5.2 %collective-permute-start.6 = (bf16[2,8,128]{2,1,0:T(8,128)(2,1)}, bf16[2,8,128]{2,1,0:T(8,128)(2,1)S(1)}, u32[]{:S(2)}, u32[]{:S(2)}) collective-permute-start(bf16[2,8,128]{2,1,0:T(8,128)(2,1)} %refs_0_.1), channel_id=1, source_target_pairs={{0,7},{1,6},{2,5},{3,4},{4,3},{5,2},{6,1},{7,0},{8,15},{9,14},{10,... | collective-permute-start | bytes 12296 | tf_op jit(solution)/shard_map/ppermute | solution.py:222
  15.2 6.7 %collective-permute-start.5 = (bf16[2,8,128]{2,1,0:T(8,128)(2,1)}, bf16[2,8,128]{2,1,0:T(8,128)(2,1)S(1)}, u32[]{:S(2)}, u32[]{:S(2)}) collective-permute-start(bf16[2,8,128]{2,1,0:T(8,128)(2,1)} %refs_0_.1), channel_id=1, source_target_pairs={{0,6},{1,7},{2,4},{3,5},{4,2},{5,3},{6,0},{7,1},{8,14},{9,15},{10,... | collective-permute-start | bytes 12296 | tf_op jit(solution)/shard_map/ppermute | solution.py:222
  18.4 3.5 %collective-permute-start.4 = (bf16[2,8,128]{2,1,0:T(8,128)(2,1)}, bf16[2,8,128]{2,1,0:T(8,128)(2,1)S(1)}, u32[]{:S(2)}, u32[]{:S(2)}) collective-permute-start(bf16[2,8,128]{2,1,0:T(8,128)(2,1)} %refs_0_.1), channel_id=1, source_target_pairs={{0,5},{1,4},{2,7},{3,6},{4,1},{5,0},{6,3},{7,2},{8,13},{9,12},{10,... | collective-permute-start | bytes 12296 | tf_op jit(solution)/shard_map/ppermute | solution.py:222
  18.4 4.6 %collective-permute-start.3 = (bf16[2,8,128]{2,1,0:T(8,128)(2,1)}, bf16[2,8,128]{2,1,0:T(8,128)(2,1)S(1)}, u32[]{:S(2)}, u32[]{:S(2)}) collective-permute-start(bf16[2,8,128]{2,1,0:T(8,128)(2,1)} %refs_0_.1), channel_id=1, source_target_pairs={{0,4},{1,5},{2,6},{3,7},{4,0},{5,1},{6,2},{7,3},{8,12},{9,13},{10,... | collective-permute-start | bytes 12296 | tf_op jit(solution)/shard_map/ppermute | solution.py:222
  19.6 3.4 %collective-permute-start.2 = (bf16[2,8,128]{2,1,0:T(8,128)(2,1)}, bf16[2,8,128]{2,1,0:T(8,128)(2,1)S(1)}, u32[]{:S(2)}, u32[]{:S(2)}) collective-permute-start(bf16[2,8,128]{2,1,0:T(8,128)(2,1)} %refs_0_.1), channel_id=1, source_target_pairs={{0,3},{1,2},{2,1},{3,0},{4,7},{5,6},{6,5},{7,4},{8,11},{9,10},{10,... | collective-permute-start | bytes 12296 | tf_op jit(solution)/shard_map/ppermute | solution.py:222
  20.4 3.8 %collective-permute-start.1 = (bf16[2,8,128]{2,1,0:T(8,128)(2,1)}, bf16[2,8,128]{2,1,0:T(8,128)(2,1)S(1)}, u32[]{:S(2)}, u32[]{:S(2)}) collective-permute-start(bf16[2,8,128]{2,1,0:T(8,128)(2,1)} %refs_0_.1), channel_id=1, source_target_pairs={{0,2},{1,3},{2,0},{3,1},{4,6},{5,7},{6,4},{7,5},{8,10},{9,11},{10,... | collective-permute-start | bytes 12296 | tf_op jit(solution)/shard_map/ppermute | solution.py:222
  21.9 2.3 %collective-permute-start = (bf16[2,8,128]{2,1,0:T(8,128)(2,1)}, bf16[2,8,128]{2,1,0:T(8,128)(2,1)S(1)}, u32[]{:S(2)}, u32[]{:S(2)}) collective-permute-start(bf16[2,8,128]{2,1,0:T(8,128)(2,1)} %refs_0_.1), channel_id=1, source_target_pairs={{0,1},{1,0},{2,3},{3,2},{4,5},{5,4},{6,7},{7,6},{8,9},{9,8},{10,11... | collective-permute-start | bytes 12296 | tf_op jit(solution)/shard_map/ppermute | solution.py:222
  21.9 6.0 %collective-permute-start.14 = (bf16[2,8,128]{2,1,0:T(8,128)(2,1)}, bf16[2,8,128]{2,1,0:T(8,128)(2,1)S(1)}, u32[]{:S(2)}, u32[]{:S(2)}) collective-permute-start(bf16[2,8,128]{2,1,0:T(8,128)(2,1)} %refs_0_.1), channel_id=1, source_target_pairs={{0,15},{1,14},{2,13},{3,12},{4,11},{5,10},{6,9},{7,8},{8,7},{9,6},... | collective-permute-start | bytes 12296 | tf_op jit(solution)/shard_map/ppermute | solution.py:222
  27.9 0.7 %copy-start.11 = (s32[16]{0:T(128)S(1)}, s32[16]{0:T(128)}, u32[]{:S(2)}) copy-start(s32[16]{0:T(128)} %pos_ref.1) | copy-start | bytes 196
  27.9 0.7 %copy-start.12 = (f32[128]{0:T(128)S(1)}, f32[128]{0:T(128)}, u32[]{:S(2)}) copy-start(f32[128]{0:T(128)} %param.19) | copy-start | bytes 1540
  27.9 0.7 %copy-start.13 = (f32[128]{0:T(128)S(1)}, f32[128]{0:T(128)}, u32[]{:S(2)}) copy-start(f32[128]{0:T(128)} %param.23) | copy-start | bytes 1540
  27.9 0.7 %copy-start.14 = (f32[128]{0:T(128)S(1)}, f32[128]{0:T(128)}, u32[]{:S(2)}) copy-start(f32[128]{0:T(128)} %param.25) | copy-start | bytes 1540
  27.9 0.7 %copy-start.9 = (bf16[128,4]{0,1:T(4,128)(2,1)S(1)}, bf16[128,4]{0,1:T(4,128)(2,1)}, u32[]{:S(2)}) copy-start(bf16[128,4]{0,1:T(4,128)(2,1)} %param.28) | copy-start | bytes 3076
  27.9 0.7 %copy-start.10 = (s32[16]{0:T(128)S(1)}, s32[16]{0:T(128)}, u32[]{:S(2)}) copy-start(s32[16]{0:T(128)} %mask_ref.1) | copy-start | bytes 196
  28.6 0.9 %copy-start = (bf16[128,384]{1,0:T(8,128)(2,1)S(1)}, bf16[128,384]{1,0:T(8,128)(2,1)}, u32[]{:S(2)}) copy-start(bf16[128,384]{1,0:T(8,128)(2,1)} %refs_24_.1) | copy-start | bytes 294916
  29.5 0.8 %copy-start.1 = (bf16[128,256]{1,0:T(8,128)(2,1)S(1)}, bf16[128,256]{1,0:T(8,128)(2,1)}, u32[]{:S(2)}) copy-start(bf16[128,256]{1,0:T(8,128)(2,1)} %refs_18_.1) | copy-start | bytes 196612
  30.4 0.8 %copy-start.2 = (bf16[128,256]{1,0:T(8,128)(2,1)S(1)}, bf16[128,256]{1,0:T(8,128)(2,1)}, u32[]{:S(2)}) copy-start(bf16[128,256]{1,0:T(8,128)(2,1)} %refs_19_.1) | copy-start | bytes 196612
  31.2 0.8 %copy-start.3 = (bf16[128,128]{1,0:T(8,128)(2,1)S(1)}, bf16[128,128]{1,0:T(8,128)(2,1)}, u32[]{:S(2)}) copy-start(bf16[128,128]{1,0:T(8,128)(2,1)} %refs_16_.1) | copy-start | bytes 98308
  32.0 0.8 %copy-start.4 = (bf16[128,128]{1,0:T(8,128)(2,1)S(1)}, bf16[128,128]{1,0:T(8,128)(2,1)}, u32[]{:S(2)}) copy-start(bf16[128,128]{1,0:T(8,128)(2,1)} %refs_20_.1) | copy-start | bytes 98308
  32.7 0.8 %copy-start.5 = (bf16[128,128]{1,0:T(8,128)(2,1)S(1)}, bf16[128,128]{1,0:T(8,128)(2,1)}, u32[]{:S(2)}) copy-start(bf16[128,128]{1,0:T(8,128)(2,1)} %refs_22_.1) | copy-start | bytes 98308
  33.5 0.8 %copy-start.6 = (bf16[128,128]{1,0:T(8,128)(2,1)S(1)}, bf16[128,128]{1,0:T(8,128)(2,1)}, u32[]{:S(2)}) copy-start(bf16[128,128]{1,0:T(8,128)(2,1)} %refs_25_.1) | copy-start | bytes 98308
  34.3 0.8 %copy-start.7 = (bf16[128,128]{1,0:T(8,128)(2,1)S(1)}, bf16[128,128]{1,0:T(8,128)(2,1)}, u32[]{:S(2)}) copy-start(bf16[128,128]{1,0:T(8,128)(2,1)} %refs_27_.1) | copy-start | bytes 98308

commit v3 on v2

--- a/solution.py
+++ b/solution.py
@@ -11,6 +11,7 @@
 epsilon = 1e-05
 
 WHOLE_PAIR_BYTES = 256 * 1024
+STAGE_FLOPS = 10**9
 
 
 def layer_norm(values, gain):
@@ -38,17 +39,39 @@
     return values.astype(jnp.bfloat16).astype(jnp.float32)
 
 
-def whole_pair_kernel(row_dim, blocks, heads, mask_ref, pos_ref, *refs):
-    whole_pair_steps(row_dim, heads, mask_ref, pos_ref, refs[:blocks], *refs[blocks:])
+def stage_kernel(cols, mask_ref, pos_ref, table_ref, rel_ref, pair_mask_ref):
+    tokens = pos_ref.shape[0]
+    bins = table_ref.shape[0]
+    sub = lax.broadcasted_iota(jnp.int32, (cols, bins), 0)
+    lane = lax.broadcasted_iota(jnp.int32, (cols, bins), 1)
+    hot = [None] * (tokens * tokens // cols)
+    for half in range(tokens // cols):
+        pos_vec = jnp.zeros((cols, bins), jnp.int32)
+        mask_vec = jnp.zeros((cols, bins), jnp.int32)
+        for c in range(cols):
+            pos_vec = jnp.where(sub == c, pos_ref[half * cols + c], pos_vec)
+            mask_vec = jnp.where(sub == c, mask_ref[half * cols + c], mask_vec)
+        for i in range(tokens):
+            at = i * (tokens // cols) + half
+            bucket = jnp.clip(pos_ref[i] - pos_vec, -(bins // 2), bins // 2 - 1) + bins // 2
+            hot[at] = (bucket == lane).astype(jnp.float32)
+            pair_mask_ref[at * cols : (at + 1) * cols, :] = (mask_vec * mask_ref[i]).astype(jnp.float32)
+    hot = jnp.concatenate(hot, axis=0).astype(jnp.bfloat16)
+    rel_ref[...] = dot(hot, table_ref[...])
+
+
+def whole_pair_kernel(row_dim, col_dim, heads, pieces, *refs):
+    whole_pair_steps(row_dim, col_dim, heads, refs[:pieces], *refs[pieces:])
 
 
 def whole_pair_steps(
     row_dim,
+    col_dim,
     heads,
+    piece_refs,
     mask_ref,
-    pos_ref,
-    block_refs,
-    table_ref,
+    rel_ref,
+    pair_mask_ref,
     norm_in_ref,
     in_weight_ref,
     in_gate_ref,
@@ -68,51 +91,30 @@
     att_ref,
     upd_ref,
 ):
-    rows, cols, width = block_refs[0].shape
-    col_dim = len(block_refs) // row_dim
+    rows, cols, width = piece_refs[0].shape[1:]
     tokens = row_dim * rows
-    bins = table_ref.shape[0]
     head_dim = width // heads
     row_first = lax.axis_index("row") * rows
     col_first = pl.multiple_of(lax.axis_index("col") * cols, cols)
     f32, bf16 = jnp.float32, jnp.bfloat16
 
     me = lax.axis_index("row") * col_dim + lax.axis_index("col")
-    for m, block_ref in enumerate(block_refs):
+    blocks = [piece_ref[at].astype(f32) for piece_ref in piece_refs for at in range(piece_ref.shape[0])]
+    for m, block in enumerate(blocks):
         owner = me ^ m
-        block = block_ref[...].astype(f32)
         for r in range(rows):
             first = (owner // col_dim * rows + r) * tokens + owner % col_dim * cols
             base_ref[pl.ds(pl.multiple_of(first, cols), cols), :] = block[r]
 
-    sub = lax.broadcasted_iota(jnp.int32, (cols, bins), 0)
-    lane = lax.broadcasted_iota(jnp.int32, (cols, bins), 1)
-    col_pos, col_mask = [], []
-    for half in range(col_dim):
-        pos_vec = jnp.zeros((cols, bins), jnp.int32)
-        mask_vec = jnp.zeros((cols, bins), jnp.int32)
-        for c in range(cols):
-            pos_vec = jnp.where(sub == c, pos_ref[half * cols + c], pos_vec)
-            mask_vec = jnp.where(sub == c, mask_ref[half * cols + c], mask_vec)
-        col_pos.append(pos_vec)
-        col_mask.append(mask_vec)
-    hot, masks = [], []
-    for i in range(tokens):
-        for half in range(col_dim):
-            bucket = jnp.clip(pos_ref[i] - col_pos[half], -(bins // 2), bins // 2 - 1) + bins // 2
-            hot.append((bucket == lane).astype(f32))
-            masks.append((col_mask[half] * mask_ref[i]).astype(f32)[:, :1])
-    hot = jnp.concatenate(hot, axis=0).astype(bf16)
-    masks = jnp.concatenate(masks, axis=0)
-    base = base_ref[...] + dot(hot, table_ref[...])
+    base = base_ref[...] + rel_ref[...]
     base_ref[...] = base
 
     normed = layer_norm(base, norm_in_ref[...]).astype(bf16)
     normed_ref[...] = normed.astype(f32)
-    projected = sigmoid(dot(normed, in_gate_ref[...])) * dot(normed, in_weight_ref[...]) * masks
-    projected = round_bf16(projected)
-    left_ref[...] = projected[:, :width]
-    right_ref[...] = projected[:, width:]
+    projected = sigmoid(dot(normed, in_gate_ref[...])) * dot(normed, in_weight_ref[...])
+    pair_mask = pair_mask_ref[...]
+    left_ref[...] = round_bf16(projected[:, :width] * pair_mask)
+    right_ref[...] = round_bf16(projected[:, width:] * pair_mask)
 
     right_at = [right_ref[pl.ds(col_first * tokens + m, cols, stride=tokens), :] for m in range(tokens)]
     products = []
@@ -216,26 +218,17 @@
     tokens = row_dim * rows
     heads = att_bias.shape[1]
     blocks = row_dim * col_dim
-    pair = [pair_in]
-    for m in range(1, blocks):
-        partners = [(device, device ^ m) for device in range(blocks)]
-        pair.append(lax.ppermute(pair_in, ("row", "col"), partners))
-    in_vmem = pl.BlockSpec(memory_space=pltpu.VMEM)
-    in_smem = pl.BlockSpec(memory_space=pltpu.SMEM)
-    wide = pltpu.VMEM((tokens * tokens, width), jnp.float32)
-    column = pltpu.VMEM((tokens * cols, width), jnp.float32)
-    return pl.pallas_call(
-        functools.partial(whole_pair_kernel, row_dim, blocks, heads),
-        out_shape=jax.ShapeDtypeStruct(pair_in.shape, pair_in.dtype),
-        in_specs=[in_smem] * 2 + [in_vmem] * (blocks + 12),
-        out_specs=in_vmem,
-        scratch_shapes=[wide] * 4 + [column] * 2,
-        compiler_params=pltpu.CompilerParams(vmem_limit_bytes=16 * 1024 * 1024),
-    )(
-        token_mask,
-        positions,
-        *pair,
-        relpos_table,
+    pair = [pair_in[None]]
+    step = 1
+    while step < blocks:
+        partners = [(device, device ^ step) for device in range(blocks)]
+        held = jnp.concatenate(pair, axis=0)
+        pair.append(lax.ppermute(held, ("row", "col"), partners))
+        step *= 2
+
+    vmem = pl.BlockSpec(memory_space=pltpu.VMEM)
+    smem = pl.BlockSpec(memory_space=pltpu.SMEM)
+    weights = (
         tri_norm_in.reshape(1, width),
         tri_in_weight,
         tri_in_gate,
@@ -248,6 +241,26 @@
         att_bias.T,
         att_out,
     )
+    wide = pltpu.VMEM((tokens * tokens, width), jnp.float32)
+    column = pltpu.VMEM((tokens * cols, width), jnp.float32)
+    params = pltpu.CompilerParams(vmem_limit_bytes=16 * 1024 * 1024)
+    wide_out = jax.ShapeDtypeStruct((tokens * tokens, width), jnp.float32)
+    rel, pair_mask = pl.pallas_call(
+        functools.partial(stage_kernel, cols),
+        out_shape=[wide_out] * 2,
+        in_specs=[smem] * 2 + [vmem],
+        out_specs=[vmem] * 2,
+        compiler_params=params,
+        cost_estimate=pl.CostEstimate(flops=STAGE_FLOPS, bytes_accessed=2**20, transcendentals=0),
+    )(token_mask, positions, relpos_table)
+    return pl.pallas_call(
+        functools.partial(whole_pair_kernel, row_dim, col_dim, heads, len(pair)),
+        out_shape=jax.ShapeDtypeStruct(pair_in.shape, pair_in.dtype),
+        in_specs=[vmem] * len(pair) + [smem] + [vmem] * (2 + len(weights)),
+        out_specs=vmem,
+        scratch_shapes=[wide] * 4 + [column] * 2,
+        compiler_params=params,
+    )(*pair, token_mask, rel, pair_mask, *weights)
 
 
 def attend_column(query_col, key_col, value_col, bias_all, key_bias, block_rows):

time: 38.5 us -> 19.3 us (0.50); the launches traced: 37.9 us -> 19.1 us
  starting transfers between devices: 22.9 us -> 8.55 us
  local copies, waits for them, and re-layouts: 7.07 us -> 0.68 us
  other arithmetic: 0 us -> 0.7 us
  Pallas kernels: 2.87 us -> 3.53 us
  waiting for transfers between devices: 4.93 us -> 5.48 us
    ppermute x15 -> x4, starting transfers between devices: 22.9 us -> 8.55 us  [whole_pair_on_device(): pair.append(lax.ppermute(held, ('row', 'col'), partners))]
    unnamed x30, local copies, waits for them, and re-layouts: 7.07 us -> 0.68 us
    concatenate x0 -> x3, other arithmetic: none -> 0.7 us  [whole_pair_on_device(): held = jnp.concatenate(pair, axis=0)]
    pallas_call x1 -> x2, Pallas kernels: 2.87 us -> 3.53 us  [the longest x1 2.82 us: whole_pair_on_device(): pl.pallas_call(functools.partial(whole_pair_kernel, row_dim, col_dim, hea...]
    ppermute x15 -> x4, waiting for transfers between devices: 4.93 us -> 5.48 us  [whole_pair_on_device(): pair.append(lax.ppermute(held, ('row', 'col'), partners))]
  transfers between devices with their start and end apart: 15 -> 4, of which waited for: 2 -> 4; matrix products, arithmetic and copies ran while one was open for 0% -> 0% of each run, Pallas kernels for 0% -> 4%
where the time goes in v3:
time: 19.3 us; the launch traced here: 19.1 us
  starting transfers between devices  8.55 us (44%)
  waiting for transfers between devices  5.48 us (28%)
  Pallas kernels  3.53 us (18%)
  other arithmetic  0.7 us (4%)
  local copies, waits for them, and re-layouts  0.68 us (4%)
    ppermute x4, starting transfers between devices, whole_pair_on_device(): pair.append(lax.ppermute(held, ('row', 'col'), partners))  8.55 us
    ppermute x4, waiting for transfers between devices, whole_pair_on_device(): pair.append(lax.ppermute(held, ('row', 'col'), partners))  5.48 us
    pallas_call x1, Pallas kernels, whole_pair_on_device(): pl.pallas_call(functools.partial(whole_pair_kernel, row_dim, col_dim, hea...  2.82 us
    pallas_call x1, Pallas kernels, whole_pair_on_device(): pl.pallas_call(functools.partial(stage_kernel, cols), out_shape=[wide_out...  0.71 us
    concatenate x3, other arithmetic, whole_pair_on_device(): held = jnp.concatenate(pair, axis=0)  0.7 us
    unnamed x30, local copies, waits for them, and re-layouts  0.68 us
  transfers between devices with their start and end apart: 4, of which 4 were waited for; matrix products, arithmetic and copies ran while one was open for 0% of the time, Pallas kernels for 4%

profile of v3, /device:TPU:0, one launch (start us, length us, event | category | flops | bytes accessed | tf_op | source)
XLA Modules:
  0.0 19.1 jit_solution(14976202008656603014)
XLA Ops:
  0.0 0.0 copy-start.1
  0.0 0.5 %collective-permute-start = (bf16[1,2,8,128]{3,2,1,0:T(8,128)(2,1)}, bf16[1,2,8,128]{3,2,1,0:T(8,128)(2,1)S(1)}, u32[]{:S(2)}, u32[]{:S(2)}) collective-permute-start(bf16[1,2,8,128]{3,2,1,0:T(8,128)(2,1)} %bitcast.5), channel_id=1, source_target_pairs={{0,1},{1,0},{2,3},{3,2},{4,5},{5,4},{6,7},{7,6},{8,9},{9,8},{10,11... | collective-permute-start | bytes 12296 | tf_op jit(solution)/shard_map/ppermute | solution.py:226
  0.5 1.0 %collective-permute-done.refs_1_ = bf16[1,2,8,128]{3,2,1,0:T(8,128)(2,1)S(1)} collective-permute-done((bf16[1,2,8,128]{3,2,1,0:T(8,128)(2,1)}, bf16[1,2,8,128]{3,2,1,0:T(8,128)(2,1)S(1)}, u32[]{:S(2)}, u32[]{:S(2)}) %collective-permute-start) | collective-permute-done | bytes 4128 | tf_op jit(solution)/shard_map/ppermute | solution.py:226
  1.5 0.7 %pad_maximum_fusion.2 = bf16[2,2,8,128]{3,2,1,0:T(8,128)(2,1)S(1)} fusion(bf16[1,2,8,128]{3,2,1,0:T(8,128)(2,1)S(1)} %collective-permute-done.refs_1_, bf16[1,2,8,128]{3,2,1,0:T(8,128)(2,1)} %bitcast.6), kind=kLoop, calls=%fused_computation.2 | loop fusion | flops 4096 | bytes 16384 | tf_op jit(solution)/shard_map/concatenate | solution.py:225
  2.2 2.8 %collective-permute-start.1 = (bf16[2,2,8,128]{3,2,1,0:T(8,128)(2,1)S(1)}, bf16[2,2,8,128]{3,2,1,0:T(8,128)(2,1)S(1)}, u32[]{:S(2)}, u32[]{:S(2)}) collective-permute-start(bf16[2,2,8,128]{3,2,1,0:T(8,128)(2,1)S(1)} %pad_maximum_fusion.2), channel_id=1, source_target_pairs={{0,2},{1,3},{2,0},{3,1},{4,6},{5,7},{6,4},{7,5},{8,10},{9,11},{10,... | collective-permute-start | bytes 24584 | tf_op jit(solution)/shard_map/ppermute | solution.py:226
  5.0 1.6 %collective-permute-done.1.refs_2_ = bf16[2,2,8,128]{3,2,1,0:T(8,128)(2,1)S(1)} collective-permute-done((bf16[2,2,8,128]{3,2,1,0:T(8,128)(2,1)S(1)}, bf16[2,2,8,128]{3,2,1,0:T(8,128)(2,1)S(1)}, u32[]{:S(2)}, u32[]{:S(2)}) %collective-permute-start.1) | collective-permute-done | bytes 8224 | tf_op jit(solution)/shard_map/ppermute | solution.py:226
  6.6 0.0 copy-done.1
  6.6 0.0 copy-start.9
  6.7 0.0 copy-start.13
  6.7 0.0 copy-start.14
  6.7 2.2 %collective-permute-start.2 = (bf16[4,2,8,128]{3,2,1,0:T(8,128)(2,1)S(1)}, bf16[4,2,8,128]{3,2,1,0:T(8,128)(2,1)S(1)}, u32[]{:S(2)}, u32[]{:S(2)}) collective-permute-start(bf16[4,2,8,128]{3,2,1,0:T(8,128)(2,1)S(1)} %pad_maximum_fusion.1), channel_id=1, source_target_pairs={{0,4},{1,5},{2,6},{3,7},{4,0},{5,1},{6,2},{7,3},{8,12},{9,13},{10,... | collective-permute-start | bytes 49160 | tf_op jit(solution)/shard_map/ppermute | solution.py:226
  8.9 1.7 %collective-permute-done.2.refs_3_ = bf16[4,2,8,128]{3,2,1,0:T(8,128)(2,1)S(1)} collective-permute-done((bf16[4,2,8,128]{3,2,1,0:T(8,128)(2,1)S(1)}, bf16[4,2,8,128]{3,2,1,0:T(8,128)(2,1)S(1)}, u32[]{:S(2)}, u32[]{:S(2)}) %collective-permute-start.2) | collective-permute-done | bytes 16416 | tf_op jit(solution)/shard_map/ppermute | solution.py:226
  10.6 0.0 copy-start
  10.6 0.0 copy-start.2
  10.6 0.0 copy-start.3
  10.6 3.1 %collective-permute-start.3 = (bf16[8,2,8,128]{3,2,1,0:T(8,128)(2,1)S(1)}, bf16[8,2,8,128]{3,2,1,0:T(8,128)(2,1)S(1)}, u32[]{:S(2)}, u32[]{:S(2)}) collective-permute-start(bf16[8,2,8,128]{3,2,1,0:T(8,128)(2,1)S(1)} %pad_maximum_fusion), channel_id=1, source_target_pairs={{0,8},{1,9},{2,10},{3,11},{4,12},{5,13},{6,14},{7,15},{8,0},{9,1},... | collective-permute-start | bytes 98312 | tf_op jit(solution)/shard_map/ppermute | solution.py:226
  13.7 0.0 copy-done.9
  13.7 0.0 copy-done.13
  13.7 0.0 copy-done.14
  13.7 0.0 copy-start.4
  13.7 0.0 copy-start.5
  13.7 0.0 copy-start.6
  13.8 0.0 copy-start.7
  13.8 0.0 copy-start.11
  13.8 0.0 copy-start.12
  13.8 0.7 %shard_map.145 = (f32[256,128]{1,0:T(8,128)S(1)}, f32[256,128]{1,0:T(8,128)S(1)}) custom-call(s32[16]{0:T(128)S(1)} %copy-done.9, s32[16]{0:T(128)S(1)} %copy-done.14, bf16[128,128]{1,0:T(8,128)(2,1)S(1)} %copy-done.13), custom_call_target="tpu_custom_call" | custom-call | flops 1000000000 | bytes 1048576 | tf_op jit(solution)/shard_map/pallas_call | solution.py:248
  14.5 1.1 %collective-permute-done.3.refs_4_ = bf16[8,2,8,128]{3,2,1,0:T(8,128)(2,1)S(1)} collective-permute-done((bf16[8,2,8,128]{3,2,1,0:T(8,128)(2,1)S(1)}, bf16[8,2,8,128]{3,2,1,0:T(8,128)(2,1)S(1)}, u32[]{:S(2)}, u32[]{:S(2)}) %collective-permute-start.3) | collective-permute-done | bytes 32800 | tf_op jit(solution)/shard_map/ppermute | solution.py:226
  15.6 0.0 copy-start.8
  15.6 0.0 copy-start.10
  15.6 0.0 copy-done
  15.6 0.0 copy-done.2
  15.6 0.0 copy-done.3
  15.6 0.0 copy-done.4
  15.6 0.0 copy-done.5
  15.7 0.0 copy-done.6
  15.7 0.0 copy-done.7
  15.7 0.0 copy-done.11
  15.7 0.0 copy-done.12
  15.7 0.6 %copy-done.8 = bf16[128,4]{0,1:T(4,128)(2,1)S(1)} copy-done((bf16[128,4]{0,1:T(4,128)(2,1)S(1)}, bf16[128,4]{0,1:T(4,128)(2,1)}, u32[]{:S(2)}) %copy-start.8) | copy-done | bytes 1048
  16.3 0.0 copy-done.10
  16.3 2.8 %shard_map.146 = bf16[2,8,128]{2,1,0:T(8,128)(2,1)} custom-call(bf16[1,2,8,128]{3,2,1,0:T(8,128)(2,1)S(1)} %bitcast.9, bf16[1,2,8,128]{3,2,1,0:T(8,128)(2,1)S(1)} %collective-permute-done.refs_1_, bf16[2,2,8,128]{3,2,1,0:T(8,128)(2,1)S(1)} %collective-permute-done.1.refs_2_, bf16[4,2,8,128]{3,2,1,0:T(8,128)(2,1)S(1)} %collective-permute-done.2.refs_3_, ...), custom_call_target="tpu_custom_call" | custom-call | tf_op jit(solution)/shard_map/pallas_call | solution.py:256
  (2 shorter events, 0.0 us)
Async XLA Ops:
  0.0 6.6 %copy-start.1 = (bf16[2,8,128]{2,1,0:T(8,128)(2,1)S(1)}, bf16[2,8,128]{2,1,0:T(8,128)(2,1)}, u32[]{:S(2)}) copy-start(bf16[2,8,128]{2,1,0:T(8,128)(2,1)} %param.15) | copy-start | bytes 12292
  0.0 1.5 %collective-permute-start = (bf16[1,2,8,128]{3,2,1,0:T(8,128)(2,1)}, bf16[1,2,8,128]{3,2,1,0:T(8,128)(2,1)S(1)}, u32[]{:S(2)}, u32[]{:S(2)}) collective-permute-start(bf16[1,2,8,128]{3,2,1,0:T(8,128)(2,1)} %bitcast.5), channel_id=1, source_target_pairs={{0,1},{1,0},{2,3},{3,2},{4,5},{5,4},{6,7},{7,6},{8,9},{9,8},{10,11... | collective-permute-start | bytes 12296 | tf_op jit(solution)/shard_map/ppermute | solution.py:226
  2.2 4.5 %collective-permute-start.1 = (bf16[2,2,8,128]{3,2,1,0:T(8,128)(2,1)S(1)}, bf16[2,2,8,128]{3,2,1,0:T(8,128)(2,1)S(1)}, u32[]{:S(2)}, u32[]{:S(2)}) collective-permute-start(bf16[2,2,8,128]{3,2,1,0:T(8,128)(2,1)S(1)} %pad_maximum_fusion.2), channel_id=1, source_target_pairs={{0,2},{1,3},{2,0},{3,1},{4,6},{5,7},{6,4},{7,5},{8,10},{9,11},{10,... | collective-permute-start | bytes 24584 | tf_op jit(solution)/shard_map/ppermute | solution.py:226
  6.6 7.1 %copy-start.9 = (s32[16]{0:T(128)S(1)}, s32[16]{0:T(128)}, u32[]{:S(2)}) copy-start(s32[16]{0:T(128)} %refs_5_.1) | copy-start | bytes 196
  6.7 7.1 %copy-start.13 = (bf16[128,128]{1,0:T(8,128)(2,1)S(1)}, bf16[128,128]{1,0:T(8,128)(2,1)}, u32[]{:S(2)}) copy-start(bf16[128,128]{1,0:T(8,128)(2,1)} %table_ref.1) | copy-start | bytes 98308
  6.7 7.0 %copy-start.14 = (s32[16]{0:T(128)S(1)}, s32[16]{0:T(128)}, u32[]{:S(2)}) copy-start(s32[16]{0:T(128)} %pos_ref.1) | copy-start | bytes 196
  6.7 3.9 %collective-permute-start.2 = (bf16[4,2,8,128]{3,2,1,0:T(8,128)(2,1)S(1)}, bf16[4,2,8,128]{3,2,1,0:T(8,128)(2,1)S(1)}, u32[]{:S(2)}, u32[]{:S(2)}) collective-permute-start(bf16[4,2,8,128]{3,2,1,0:T(8,128)(2,1)S(1)} %pad_maximum_fusion.1), channel_id=1, source_target_pairs={{0,4},{1,5},{2,6},{3,7},{4,0},{5,1},{6,2},{7,3},{8,12},{9,13},{10,... | collective-permute-start | bytes 49160 | tf_op jit(solution)/shard_map/ppermute | solution.py:226
  10.6 5.0 %copy-start = (bf16[128,384]{1,0:T(8,128)(2,1)S(1)}, bf16[128,384]{1,0:T(8,128)(2,1)}, u32[]{:S(2)}) copy-start(bf16[128,384]{1,0:T(8,128)(2,1)} %refs_15_.1) | copy-start | bytes 294916
  10.6 5.0 %copy-start.2 = (bf16[128,256]{1,0:T(8,128)(2,1)S(1)}, bf16[128,256]{1,0:T(8,128)(2,1)}, u32[]{:S(2)}) copy-start(bf16[128,256]{1,0:T(8,128)(2,1)} %refs_9_.1) | copy-start | bytes 196612
  10.6 5.0 %copy-start.3 = (bf16[128,256]{1,0:T(8,128)(2,1)S(1)}, bf16[128,256]{1,0:T(8,128)(2,1)}, u32[]{:S(2)}) copy-start(bf16[128,256]{1,0:T(8,128)(2,1)} %refs_10_.1) | copy-start | bytes 196612
  10.6 5.0 %collective-permute-start.3 = (bf16[8,2,8,128]{3,2,1,0:T(8,128)(2,1)S(1)}, bf16[8,2,8,128]{3,2,1,0:T(8,128)(2,1)S(1)}, u32[]{:S(2)}, u32[]{:S(2)}) collective-permute-start(bf16[8,2,8,128]{3,2,1,0:T(8,128)(2,1)S(1)} %pad_maximum_fusion), channel_id=1, source_target_pairs={{0,8},{1,9},{2,10},{3,11},{4,12},{5,13},{6,14},{7,15},{8,0},{9,1},... | collective-permute-start | bytes 98312 | tf_op jit(solution)/shard_map/ppermute | solution.py:226
  13.7 1.9 %copy-start.4 = (bf16[128,128]{1,0:T(8,128)(2,1)S(1)}, bf16[128,128]{1,0:T(8,128)(2,1)}, u32[]{:S(2)}) copy-start(bf16[128,128]{1,0:T(8,128)(2,1)} %refs_11_.1) | copy-start | bytes 98308
  13.7 1.9 %copy-start.5 = (bf16[128,128]{1,0:T(8,128)(2,1)S(1)}, bf16[128,128]{1,0:T(8,128)(2,1)}, u32[]{:S(2)}) copy-start(bf16[128,128]{1,0:T(8,128)(2,1)} %refs_13_.1) | copy-start | bytes 98308
  13.7 1.9 %copy-start.6 = (bf16[128,128]{1,0:T(8,128)(2,1)S(1)}, bf16[128,128]{1,0:T(8,128)(2,1)}, u32[]{:S(2)}) copy-start(bf16[128,128]{1,0:T(8,128)(2,1)} %refs_16_.1) | copy-start | bytes 98308
  13.8 1.9 %copy-start.7 = (bf16[128,128]{1,0:T(8,128)(2,1)S(1)}, bf16[128,128]{1,0:T(8,128)(2,1)}, u32[]{:S(2)}) copy-start(bf16[128,128]{1,0:T(8,128)(2,1)} %refs_18_.1) | copy-start | bytes 98308
  13.8 1.9 %copy-start.11 = (f32[128]{0:T(128)S(1)}, f32[128]{0:T(128)}, u32[]{:S(2)}) copy-start(f32[128]{0:T(128)} %param.23) | copy-start | bytes 1540
  13.8 1.9 %copy-start.12 = (f32[128]{0:T(128)S(1)}, f32[128]{0:T(128)}, u32[]{:S(2)}) copy-start(f32[128]{0:T(128)} %param.25) | copy-start | bytes 1540
  15.6 0.7 %copy-start.8 = (bf16[128,4]{0,1:T(4,128)(2,1)S(1)}, bf16[128,4]{0,1:T(4,128)(2,1)}, u32[]{:S(2)}) copy-start(bf16[128,4]{0,1:T(4,128)(2,1)} %param.28) | copy-start | bytes 3076
  15.6 0.7 %copy-start.10 = (f32[128]{0:T(128)S(1)}, f32[128]{0:T(128)}, u32[]{:S(2)}) copy-start(f32[128]{0:T(128)} %param.19) | copy-start | bytes 1540

commit v4 on v3

--- a/solution.py
+++ b/solution.py
@@ -39,7 +39,11 @@
     return values.astype(jnp.bfloat16).astype(jnp.float32)
 
 
-def stage_kernel(cols, mask_ref, pos_ref, table_ref, rel_ref, pair_mask_ref):
+def stage_kernel(hubs, mask_ref, pos_ref, chip_ref, table_ref, held_ref, rel_ref, pair_mask_ref):
+    cols = chip_ref.shape[2]
+    row, col = lax.axis_index("row"), lax.axis_index("col")
+    is_hub = (col == 1) & ((row == hubs[0]) | (row == hubs[1]))
+    held_ref[...] = jnp.where(is_hub, chip_ref[...].astype(jnp.float32), 0.0).astype(held_ref.dtype)
     tokens = pos_ref.shape[0]
     bins = table_ref.shape[0]
     sub = lax.broadcasted_iota(jnp.int32, (cols, bins), 0)
@@ -60,15 +64,13 @@
     rel_ref[...] = dot(hot, table_ref[...])
 
 
-def whole_pair_kernel(row_dim, col_dim, heads, pieces, *refs):
-    whole_pair_steps(row_dim, col_dim, heads, refs[:pieces], *refs[pieces:])
-
-
-def whole_pair_steps(
+def whole_pair_kernel(
     row_dim,
-    col_dim,
     heads,
-    piece_refs,
+    near_ref,
+    far_ref,
+    near_sent_ref,
+    far_sent_ref,
     mask_ref,
     rel_ref,
     pair_mask_ref,
@@ -91,20 +93,27 @@
     att_ref,
     upd_ref,
 ):
-    rows, cols, width = piece_refs[0].shape[1:]
+    rows, cols, width = near_ref.shape[1:]
     tokens = row_dim * rows
     head_dim = width // heads
     row_first = lax.axis_index("row") * rows
     col_first = pl.multiple_of(lax.axis_index("col") * cols, cols)
     f32, bf16 = jnp.float32, jnp.bfloat16
 
-    me = lax.axis_index("row") * col_dim + lax.axis_index("col")
-    blocks = [piece_ref[at].astype(f32) for piece_ref in piece_refs for at in range(piece_ref.shape[0])]
-    for m, block in enumerate(blocks):
-        owner = me ^ m
-        for r in range(rows):
-            first = (owner // col_dim * rows + r) * tokens + owner % col_dim * cols
-            base_ref[pl.ds(pl.multiple_of(first, cols), cols), :] = block[r]
+    odd = lax.axis_index("col") == 1
+    first_half = lax.axis_index("row") < row_dim // 2
+    col_dim = 2
+    for here, sent, counts_up in (
+        (near_ref, near_sent_ref, first_half),
+        (far_ref, far_sent_ref, jnp.logical_not(first_half)),
+    ):
+        for at in range(near_ref.shape[0]):
+            q, half = at // col_dim, at % col_dim
+            owner = jnp.where(counts_up, q, row_dim - 1 - q)
+            block = jnp.where(odd, here[at].astype(f32), sent[at].astype(f32))
+            for r in range(rows):
+                first = (owner * rows + r) * tokens + half * cols
+                base_ref[pl.ds(pl.multiple_of(first, cols), cols), :] = block[r]
 
     base = base_ref[...] + rel_ref[...]
     base_ref[...] = base
@@ -197,7 +206,6 @@
 
 def whole_pair_on_device(
     row_dim,
-    col_dim,
     pair_in,
     token_mask,
     positions,
@@ -217,14 +225,22 @@
     rows, cols, width = pair_in.shape
     tokens = row_dim * rows
     heads = att_bias.shape[1]
-    blocks = row_dim * col_dim
-    pair = [pair_in[None]]
-    step = 1
-    while step < blocks:
-        partners = [(device, device ^ step) for device in range(blocks)]
-        held = jnp.concatenate(pair, axis=0)
-        pair.append(lax.ppermute(held, ("row", "col"), partners))
-        step *= 2
+    def move(values, pairs):
+        ids = [(src[0] * 2 + src[1], dst[0] * 2 + dst[1]) for src, dst in pairs]
+        return lax.ppermute(values, ("row", "col"), ids)
+
+    last, count = row_dim - 1, row_dim // 2
+    hub = count // 2
+    hubs = (hub, last - hub)
+    hub_devices = [(row, 1) for row in hubs]
+    everywhere = range(row_dim)
+    even = move(pair_in[None], [((row, 0), (row, 1)) for row in everywhere])
+    chip = jnp.concatenate([even, pair_in[None]], axis=0)
+    at_hub = {
+        q: move(chip, [((q, 1), hub_devices[0]), ((last - q, 1), hub_devices[1])])
+        for q in range(count)
+        if q != hub
+    }
 
     vmem = pl.BlockSpec(memory_space=pltpu.VMEM)
     smem = pl.BlockSpec(memory_space=pltpu.SMEM)
@@ -245,16 +261,27 @@
     column = pltpu.VMEM((tokens * cols, width), jnp.float32)
     params = pltpu.CompilerParams(vmem_limit_bytes=16 * 1024 * 1024)
     wide_out = jax.ShapeDtypeStruct((tokens * tokens, width), jnp.float32)
-    rel, pair_mask = pl.pallas_call(
-        functools.partial(stage_kernel, cols),
-        out_shape=[wide_out] * 2,
-        in_specs=[smem] * 2 + [vmem],
-        out_specs=[vmem] * 2,
+    held, rel, pair_mask = pl.pallas_call(
+        functools.partial(stage_kernel, hubs),
+        out_shape=[jax.ShapeDtypeStruct(chip.shape, chip.dtype)] + [wide_out] * 2,
+        in_specs=[smem] * 2 + [vmem] * 2,
+        out_specs=[vmem] * 3,
         compiler_params=params,
         cost_estimate=pl.CostEstimate(flops=STAGE_FLOPS, bytes_accessed=2**20, transcendentals=0),
-    )(token_mask, positions, relpos_table)
+    )(token_mask, positions, chip, relpos_table)
+
+    side = jnp.concatenate([held if q == hub else at_hub[q] for q in range(count)], axis=0)
+    others = [q for q in range(count) if q != hub]
+    near, far = side, None
+    for q in others:
+        near = near + move(side, [(hub_devices[0], (q, 1)), (hub_devices[1], (last - q, 1))])
+    for q in others + [hub]:
+        part = move(side, [(hub_devices[0], (last - q, 1)), (hub_devices[1], (q, 1))])
+        far = part if far is None else far + part
+    to_even = [((row, 1), (row, 0)) for row in everywhere]
+    pair = (near, far, move(near, to_even), move(far, to_even))
     return pl.pallas_call(
-        functools.partial(whole_pair_kernel, row_dim, col_dim, heads, len(pair)),
+        functools.partial(whole_pair_kernel, row_dim, heads),
         out_shape=jax.ShapeDtypeStruct(pair_in.shape, pair_in.dtype),
         in_specs=[vmem] * len(pair) + [smem] + [vmem] * (2 + len(weights)),
         out_specs=vmem,
@@ -385,10 +412,9 @@
     rows, cols, width = pair_in.shape
     tokens = row_dim * rows
     whole_bytes = tokens * tokens * width * pair_in.dtype.itemsize
-    blocks = row_dim * col_dim
-    tiled = cols % 8 == 0 and width % 128 == 0 and blocks & (blocks - 1) == 0
+    tiled = cols % 8 == 0 and width % 128 == 0 and row_dim % 4 == 0 and col_dim == 2
     if whole_bytes <= WHOLE_PAIR_BYTES and tiled:
-        return whole_pair_on_device(row_dim, col_dim, pair_in, *others)
+        return whole_pair_on_device(row_dim, pair_in, *others)
     return split_pair_on_device(pair_in, *others)
 
 

time: 19.3 us -> 32.6 us (1.69)
  waiting for transfers between devices: 5.48 us -> 14.4 us
  starting transfers between devices: 8.55 us -> 11.8 us
  local copies, waits for them, and re-layouts: 0.68 us -> 1.45 us
    ppermute x4 -> x13, waiting for transfers between devices: 5.48 us -> 14.4 us  [move(): return lax.ppermute(values, ('row', 'col'), ids)]
    ppermute x4 -> x13, starting transfers between devices: 8.55 us -> 11.8 us  [move(): return lax.ppermute(values, ('row', 'col'), ids)]
    unnamed x30 -> x31, local copies, waits for them, and re-layouts: 0.68 us -> 1.44 us
    concatenate x3 -> x1, other arithmetic: 0.7 us -> 0.69 us  [whole_pair_on_device(): chip = jnp.concatenate([even, pair_in[None]], axis=0)]
  transfers between devices with their start and end apart: 4 -> 13, of which waited for: 4 -> 3; matrix products, arithmetic and copies ran while one was open for 0% -> 0% of each run, Pallas kernels for 4% -> 2%
where the time goes in v4:
time: 32.6 us; the launch traced here: 32.2 us
  waiting for transfers between devices  14.4 us (44%)
  starting transfers between devices  11.8 us (36%)
  Pallas kernels  3.44 us (11%)
  local copies, waits for them, and re-layouts  1.45 us (4%)
  other arithmetic  0.71 us (2%)
  between operations  0.38 us (1%)
    ppermute x13, waiting for transfers between devices, move(): return lax.ppermute(values, ('row', 'col'), ids)  14.4 us
    ppermute x13, starting transfers between devices, move(): return lax.ppermute(values, ('row', 'col'), ids)  11.8 us
    pallas_call x1, Pallas kernels, whole_pair_on_device(): pl.pallas_call(functools.partial(whole_pair_kernel, row_dim, heads), out_...  2.72 us
    unnamed x31, local copies, waits for them, and re-layouts  1.44 us
    pallas_call x1, Pallas kernels, whole_pair_on_device(): pl.pallas_call(functools.partial(stage_kernel, hubs), out_shape=[jax.Shap...  0.72 us
    concatenate x1, other arithmetic, whole_pair_on_device(): chip = jnp.concatenate([even, pair_in[None]], axis=0)  0.69 us
  transfers between devices with their start and end apart: 13, of which 3 were waited for; matrix products, arithmetic and copies ran while one was open for 0% of the time, Pallas kernels for 2%

profile of v4, /device:TPU:0, one launch (start us, length us, event | category | flops | bytes accessed | tf_op | source)
XLA Modules:
  0.0 32.2 jit_solution(1934668654051351745)
XLA Ops:
  0.0 2.5 %collective-permute-start = (bf16[1,2,8,128]{3,2,1,0:T(8,128)(2,1)}, bf16[1,2,8,128]{3,2,1,0:T(8,128)(2,1)S(1)}, u32[]{:S(2)}, u32[]{:S(2)}) collective-permute-start(bf16[1,2,8,128]{3,2,1,0:T(8,128)(2,1)} %bitcast.9), channel_id=1, source_target_pairs={{0,1},{2,3},{4,5},{6,7},{8,9},{10,11},{12,13},{14,15},{16,17},{18,... | collective-permute-start | bytes 12296 | tf_op jit(solution)/shard_map/ppermute | solution.py:230
  2.5 1.0 %collective-permute-done = bf16[1,2,8,128]{3,2,1,0:T(8,128)(2,1)S(1)} collective-permute-done((bf16[1,2,8,128]{3,2,1,0:T(8,128)(2,1)}, bf16[1,2,8,128]{3,2,1,0:T(8,128)(2,1)S(1)}, u32[]{:S(2)}, u32[]{:S(2)}) %collective-permute-start) | collective-permute-done | bytes 4128 | tf_op jit(solution)/shard_map/ppermute | solution.py:230
  3.5 0.7 %pad_maximum_fusion.chip_ref = bf16[2,2,8,128]{3,2,1,0:T(8,128)(2,1)S(1)} fusion(bf16[1,2,8,128]{3,2,1,0:T(8,128)(2,1)} %bitcast.10, bf16[1,2,8,128]{3,2,1,0:T(8,128)(2,1)S(1)} %collective-permute-done), kind=kLoop, calls=%fused_computation.6 | loop fusion | flops 4096 | bytes 16384 | tf_op jit(solution)/shard_map/concatenate | solution.py:238
  4.2 0.6 %collective-permute-start.1 = (bf16[2,2,8,128]{3,2,1,0:T(8,128)(2,1)S(1)}, bf16[2,2,8,128]{3,2,1,0:T(8,128)(2,1)S(1)}, u32[]{:S(2)}, u32[]{:S(2)}) collective-permute-start(bf16[2,2,8,128]{3,2,1,0:T(8,128)(2,1)S(1)} %pad_maximum_fusion.chip_ref), channel_id=1, source_target_pairs={{1,5},{15,11},{17,21},{31,27}} | collective-permute-start | bytes 24584 | tf_op jit(solution)/shard_map/ppermute | solution.py:230
  4.9 0.7 %collective-permute-start.2 = (bf16[2,2,8,128]{3,2,1,0:T(8,128)(2,1)S(1)}, bf16[2,2,8,128]{3,2,1,0:T(8,128)(2,1)S(1)}, u32[]{:S(2)}, u32[]{:S(2)}) collective-permute-start(bf16[2,2,8,128]{3,2,1,0:T(8,128)(2,1)S(1)} %pad_maximum_fusion.chip_ref), channel_id=1, source_target_pairs={{3,5},{13,11},{19,21},{29,27}} | collective-permute-start | bytes 24584 | tf_op jit(solution)/shard_map/ppermute | solution.py:230
  5.5 0.7 %collective-permute-start.3 = (bf16[2,2,8,128]{3,2,1,0:T(8,128)(2,1)S(1)}, bf16[2,2,8,128]{3,2,1,0:T(8,128)(2,1)S(1)}, u32[]{:S(2)}, u32[]{:S(2)}) collective-permute-start(bf16[2,2,8,128]{3,2,1,0:T(8,128)(2,1)S(1)} %pad_maximum_fusion.chip_ref), channel_id=1, source_target_pairs={{7,5},{9,11},{23,21},{25,27}} | collective-permute-start | bytes 24584 | tf_op jit(solution)/shard_map/ppermute | solution.py:230
  6.2 0.0 copy-done.8
  6.2 0.0 copy-done.13
  6.2 0.0 copy-start.12
  6.2 0.7 %copy-done.12 = bf16[128,128]{1,0:T(8,128)(2,1)S(1)} copy-done((bf16[128,128]{1,0:T(8,128)(2,1)S(1)}, bf16[128,128]{1,0:T(8,128)(2,1)}, u32[]{:S(2)}) %copy-start.12) | copy-done | bytes 32792
  7.0 0.7 %shard_map.145 = (bf16[2,2,8,128]{3,2,1,0:T(8,128)(2,1)S(1)}, f32[256,128]{1,0:T(8,128)S(1)}, f32[256,128]{1,0:T(8,128)S(1)}) custom-call(s32[16]{0:T(128)S(1)} %copy-done.8, s32[16]{0:T(128)S(1)} %copy-done.13, bf16[2,2,8,128]{3,2,1,0:T(8,128)(2,1)S(1)} %pad_maximum_fusion.chip_ref, bf16[128,128]{1,0:T(8,128)(2,1)S(1)} %copy-done.12), custom_call_target="tpu_custom_call" | custom-call | flops 1000000000 | bytes 1048576 | tf_op jit(solution)/shard_map/pallas_call | solution.py:264
  7.7 0.0 collective-permute-done.1
  7.7 0.0 collective-permute-done.2
  7.7 0.0 copy-start.6
  7.8 0.0 collective-permute-done.3
  7.8 0.7 %collective-permute-start.6 = (bf16[8,2,8,128]{3,2,1,0:T(8,128)(2,1)S(1)}, bf16[8,2,8,128]{3,2,1,0:T(8,128)(2,1)S(1)}, u32[]{:S(2)}, u32[]{:S(2)}) collective-permute-start(bf16[8,2,8,128]{3,2,1,0:T(8,128)(2,1)S(1)} %constant_dynamic-update-slice_fusion), channel_id=1, source_target_pairs={{5,7},{11,9},{21,23},{27,25}} | collective-permute-start | bytes 98312 | tf_op jit(solution)/shard_map/ppermute | solution.py:230
  8.5 0.7 %collective-permute-start.5 = (bf16[8,2,8,128]{3,2,1,0:T(8,128)(2,1)S(1)}, bf16[8,2,8,128]{3,2,1,0:T(8,128)(2,1)S(1)}, u32[]{:S(2)}, u32[]{:S(2)}) collective-permute-start(bf16[8,2,8,128]{3,2,1,0:T(8,128)(2,1)S(1)} %constant_dynamic-update-slice_fusion), channel_id=1, source_target_pairs={{5,3},{11,13},{21,19},{27,29}} | collective-permute-start | bytes 98312 | tf_op jit(solution)/shard_map/ppermute | solution.py:230
  9.1 0.7 %collective-permute-start.4 = (bf16[8,2,8,128]{3,2,1,0:T(8,128)(2,1)S(1)}, bf16[8,2,8,128]{3,2,1,0:T(8,128)(2,1)S(1)}, u32[]{:S(2)}, u32[]{:S(2)}) collective-permute-start(bf16[8,2,8,128]{3,2,1,0:T(8,128)(2,1)S(1)} %constant_dynamic-update-slice_fusion), channel_id=1, source_target_pairs={{5,1},{11,15},{21,17},{27,31}} | collective-permute-start | bytes 98312 | tf_op jit(solution)/shard_map/ppermute | solution.py:230
  9.8 0.7 %collective-permute-start.10 = (bf16[8,2,8,128]{3,2,1,0:T(8,128)(2,1)S(1)}, bf16[8,2,8,128]{3,2,1,0:T(8,128)(2,1)S(1)}, u32[]{:S(2)}, u32[]{:S(2)}) collective-permute-start(bf16[8,2,8,128]{3,2,1,0:T(8,128)(2,1)S(1)} %constant_dynamic-update-slice_fusion), channel_id=1, source_target_pairs={{5,11},{11,5},{21,27},{27,21}} | collective-permute-start | bytes 98312 | tf_op jit(solution)/shard_map/ppermute | solution.py:230
  10.5 0.7 %collective-permute-start.9 = (bf16[8,2,8,128]{3,2,1,0:T(8,128)(2,1)S(1)}, bf16[8,2,8,128]{3,2,1,0:T(8,128)(2,1)S(1)}, u32[]{:S(2)}, u32[]{:S(2)}) collective-permute-start(bf16[8,2,8,128]{3,2,1,0:T(8,128)(2,1)S(1)} %constant_dynamic-update-slice_fusion), channel_id=1, source_target_pairs={{5,9},{11,7},{21,25},{27,23}} | collective-permute-start | bytes 98312 | tf_op jit(solution)/shard_map/ppermute | solution.py:230
  11.1 0.0 collective-permute-done.6
  11.1 0.7 %collective-permute-start.7 = (bf16[8,2,8,128]{3,2,1,0:T(8,128)(2,1)S(1)}, bf16[8,2,8,128]{3,2,1,0:T(8,128)(2,1)S(1)}, u32[]{:S(2)}, u32[]{:S(2)}) collective-permute-start(bf16[8,2,8,128]{3,2,1,0:T(8,128)(2,1)S(1)} %constant_dynamic-update-slice_fusion), channel_id=1, source_target_pairs={{5,15},{11,1},{21,31},{27,17}} | collective-permute-start | bytes 98312 | tf_op jit(solution)/shard_map/ppermute | solution.py:230
  11.8 0.0 collective-permute-done.5
  11.8 0.7 %collective-permute-start.8 = (bf16[8,2,8,128]{3,2,1,0:T(8,128)(2,1)S(1)}, bf16[8,2,8,128]{3,2,1,0:T(8,128)(2,1)S(1)}, u32[]{:S(2)}, u32[]{:S(2)}) collective-permute-start(bf16[8,2,8,128]{3,2,1,0:T(8,128)(2,1)S(1)} %constant_dynamic-update-slice_fusion), channel_id=1, source_target_pairs={{5,13},{11,3},{21,29},{27,19}} | collective-permute-start | bytes 98312 | tf_op jit(solution)/shard_map/ppermute | solution.py:230
  12.5 0.0 collective-permute-done.4
  12.5 0.0 copy-start.2
  12.5 0.0 copy-start.3
  12.5 0.0 copy-start.4
  12.5 0.0 copy-start.5
  12.6 0.0 copy-start
  12.6 0.0 copy-start.1
  12.6 1.4 %collective-permute-start.11 = (bf16[8,2,8,128]{3,2,1,0:T(8,128)(2,1)S(1)}, bf16[8,2,8,128]{3,2,1,0:T(8,128)(2,1)S(1)}, u32[]{:S(2)}, u32[]{:S(2)}) collective-permute-start(bf16[8,2,8,128]{3,2,1,0:T(8,128)(2,1)S(1)} %add_add_fusion.1.near_ref), channel_id=1, source_target_pairs={{1,0},{3,2},{5,4},{7,6},{9,8},{11,10},{13,12},{15,14},{17,16},{19,... | collective-permute-start | bytes 98312 | tf_op jit(solution)/shard_map/ppermute | solution.py:230
  14.0 0.0 collective-permute-done.10
  14.0 0.0 collective-permute-done.9
  14.1 0.0 collective-permute-done.7
  14.1 0.0 collective-permute-done.8
  14.1 0.0 copy-start.10
  14.1 0.0 copy-start.11
  14.1 1.3 %collective-permute-start.12 = (bf16[8,2,8,128]{3,2,1,0:T(8,128)(2,1)S(1)}, bf16[8,2,8,128]{3,2,1,0:T(8,128)(2,1)S(1)}, u32[]{:S(2)}, u32[]{:S(2)}) collective-permute-start(bf16[8,2,8,128]{3,2,1,0:T(8,128)(2,1)S(1)} %add_add_fusion.far_ref), channel_id=1, source_target_pairs={{1,0},{3,2},{5,4},{7,6},{9,8},{11,10},{13,12},{15,14},{17,16},{19,... | collective-permute-start | bytes 98312 | tf_op jit(solution)/shard_map/ppermute | solution.py:230
  15.4 6.8 %collective-permute-done.11.near_sent_ref = bf16[8,2,8,128]{3,2,1,0:T(8,128)(2,1)S(1)} collective-permute-done((bf16[8,2,8,128]{3,2,1,0:T(8,128)(2,1)S(1)}, bf16[8,2,8,128]{3,2,1,0:T(8,128)(2,1)S(1)}, u32[]{:S(2)}, u32[]{:S(2)}) %collective-permute-start.11) | collective-permute-done | bytes 32800 | tf_op jit(solution)/shard_map/ppermute | solution.py:230
  22.2 6.6 %collective-permute-done.12.far_sent_ref = bf16[8,2,8,128]{3,2,1,0:T(8,128)(2,1)S(1)} collective-permute-done((bf16[8,2,8,128]{3,2,1,0:T(8,128)(2,1)S(1)}, bf16[8,2,8,128]{3,2,1,0:T(8,128)(2,1)S(1)}, u32[]{:S(2)}, u32[]{:S(2)}) %collective-permute-start.12) | collective-permute-done | bytes 32800 | tf_op jit(solution)/shard_map/ppermute | solution.py:230
  28.8 0.0 copy-done.6
  28.8 0.0 copy-done.2
  28.8 0.0 copy-done.3
  28.8 0.0 copy-done.4
  28.8 0.6 %copy-done.7 = bf16[128,4]{0,1:T(4,128)(2,1)S(1)} copy-done((bf16[128,4]{0,1:T(4,128)(2,1)S(1)}, bf16[128,4]{0,1:T(4,128)(2,1)}, u32[]{:S(2)}) %copy-start.7) | copy-done | bytes 1048
  29.4 0.0 copy-done.9
  29.4 2.7 %shard_map.146 = bf16[2,8,128]{2,1,0:T(8,128)(2,1)} custom-call(bf16[8,2,8,128]{3,2,1,0:T(8,128)(2,1)S(1)} %add_add_fusion.1.near_ref, bf16[8,2,8,128]{3,2,1,0:T(8,128)(2,1)S(1)} %add_add_fusion.far_ref, bf16[8,2,8,128]{3,2,1,0:T(8,128)(2,1)S(1)} %collective-permute-done.11.near_sent_ref, bf16[8,2,8,128]{3,2,1,0:T(8,128)(2,1)S(1)} %collective-permute-done.12.far_sent_ref, ...), custom_call_target="tpu_custom_call" | custom-call | tf_op jit(solution)/shard_map/pallas_call | solution.py:283
  (15 shorter events, 0.1 us)
Async XLA Ops:
  0.0 6.2 %copy-start.8 = (s32[16]{0:T(128)S(1)}, s32[16]{0:T(128)}, u32[]{:S(2)}) copy-start(s32[16]{0:T(128)} %mask_ref.3) | copy-start | bytes 196
  0.0 6.2 %copy-start.13 = (s32[16]{0:T(128)S(1)}, s32[16]{0:T(128)}, u32[]{:S(2)}) copy-start(s32[16]{0:T(128)} %pos_ref.1) | copy-start | bytes 196
  0.0 3.5 %collective-permute-start = (bf16[1,2,8,128]{3,2,1,0:T(8,128)(2,1)}, bf16[1,2,8,128]{3,2,1,0:T(8,128)(2,1)S(1)}, u32[]{:S(2)}, u32[]{:S(2)}) collective-permute-start(bf16[1,2,8,128]{3,2,1,0:T(8,128)(2,1)} %bitcast.9), channel_id=1, source_target_pairs={{0,1},{2,3},{4,5},{6,7},{8,9},{10,11},{12,13},{14,15},{16,17},{18,... | collective-permute-start | bytes 12296 | tf_op jit(solution)/shard_map/ppermute | solution.py:230
  4.2 3.5 %collective-permute-start.1 = (bf16[2,2,8,128]{3,2,1,0:T(8,128)(2,1)S(1)}, bf16[2,2,8,128]{3,2,1,0:T(8,128)(2,1)S(1)}, u32[]{:S(2)}, u32[]{:S(2)}) collective-permute-start(bf16[2,2,8,128]{3,2,1,0:T(8,128)(2,1)S(1)} %pad_maximum_fusion.chip_ref), channel_id=1, source_target_pairs={{1,5},{15,11},{17,21},{31,27}} | collective-permute-start | bytes 24584 | tf_op jit(solution)/shard_map/ppermute | solution.py:230
  4.9 2.9 %collective-permute-start.2 = (bf16[2,2,8,128]{3,2,1,0:T(8,128)(2,1)S(1)}, bf16[2,2,8,128]{3,2,1,0:T(8,128)(2,1)S(1)}, u32[]{:S(2)}, u32[]{:S(2)}) collective-permute-start(bf16[2,2,8,128]{3,2,1,0:T(8,128)(2,1)S(1)} %pad_maximum_fusion.chip_ref), channel_id=1, source_target_pairs={{3,5},{13,11},{19,21},{29,27}} | collective-permute-start | bytes 24584 | tf_op jit(solution)/shard_map/ppermute | solution.py:230
  5.5 2.2 %collective-permute-start.3 = (bf16[2,2,8,128]{3,2,1,0:T(8,128)(2,1)S(1)}, bf16[2,2,8,128]{3,2,1,0:T(8,128)(2,1)S(1)}, u32[]{:S(2)}, u32[]{:S(2)}) collective-permute-start(bf16[2,2,8,128]{3,2,1,0:T(8,128)(2,1)S(1)} %pad_maximum_fusion.chip_ref), channel_id=1, source_target_pairs={{7,5},{9,11},{23,21},{25,27}} | collective-permute-start | bytes 24584 | tf_op jit(solution)/shard_map/ppermute | solution.py:230
  6.2 0.8 %copy-start.12 = (bf16[128,128]{1,0:T(8,128)(2,1)S(1)}, bf16[128,128]{1,0:T(8,128)(2,1)}, u32[]{:S(2)}) copy-start(bf16[128,128]{1,0:T(8,128)(2,1)} %table_ref.1) | copy-start | bytes 98308
  7.7 21.0 %copy-start.6 = (bf16[128,128]{1,0:T(8,128)(2,1)S(1)}, bf16[128,128]{1,0:T(8,128)(2,1)}, u32[]{:S(2)}) copy-start(bf16[128,128]{1,0:T(8,128)(2,1)} %att_out_ref.1) | copy-start | bytes 98308
  7.8 3.4 %collective-permute-start.6 = (bf16[8,2,8,128]{3,2,1,0:T(8,128)(2,1)S(1)}, bf16[8,2,8,128]{3,2,1,0:T(8,128)(2,1)S(1)}, u32[]{:S(2)}, u32[]{:S(2)}) collective-permute-start(bf16[8,2,8,128]{3,2,1,0:T(8,128)(2,1)S(1)} %constant_dynamic-update-slice_fusion), channel_id=1, source_target_pairs={{5,7},{11,9},{21,23},{27,25}} | collective-permute-start | bytes 98312 | tf_op jit(solution)/shard_map/ppermute | solution.py:230
  8.5 3.4 %collective-permute-start.5 = (bf16[8,2,8,128]{3,2,1,0:T(8,128)(2,1)S(1)}, bf16[8,2,8,128]{3,2,1,0:T(8,128)(2,1)S(1)}, u32[]{:S(2)}, u32[]{:S(2)}) collective-permute-start(bf16[8,2,8,128]{3,2,1,0:T(8,128)(2,1)S(1)} %constant_dynamic-update-slice_fusion), channel_id=1, source_target_pairs={{5,3},{11,13},{21,19},{27,29}} | collective-permute-start | bytes 98312 | tf_op jit(solution)/shard_map/ppermute | solution.py:230
  9.1 3.4 %collective-permute-start.4 = (bf16[8,2,8,128]{3,2,1,0:T(8,128)(2,1)S(1)}, bf16[8,2,8,128]{3,2,1,0:T(8,128)(2,1)S(1)}, u32[]{:S(2)}, u32[]{:S(2)}) collective-permute-start(bf16[8,2,8,128]{3,2,1,0:T(8,128)(2,1)S(1)} %constant_dynamic-update-slice_fusion), channel_id=1, source_target_pairs={{5,1},{11,15},{21,17},{27,31}} | collective-permute-start | bytes 98312 | tf_op jit(solution)/shard_map/ppermute | solution.py:230
  9.8 4.2 %collective-permute-start.10 = (bf16[8,2,8,128]{3,2,1,0:T(8,128)(2,1)S(1)}, bf16[8,2,8,128]{3,2,1,0:T(8,128)(2,1)S(1)}, u32[]{:S(2)}, u32[]{:S(2)}) collective-permute-start(bf16[8,2,8,128]{3,2,1,0:T(8,128)(2,1)S(1)} %constant_dynamic-update-slice_fusion), channel_id=1, source_target_pairs={{5,11},{11,5},{21,27},{27,21}} | collective-permute-start | bytes 98312 | tf_op jit(solution)/shard_map/ppermute | solution.py:230
  10.5 3.6 %collective-permute-start.9 = (bf16[8,2,8,128]{3,2,1,0:T(8,128)(2,1)S(1)}, bf16[8,2,8,128]{3,2,1,0:T(8,128)(2,1)S(1)}, u32[]{:S(2)}, u32[]{:S(2)}) collective-permute-start(bf16[8,2,8,128]{3,2,1,0:T(8,128)(2,1)S(1)} %constant_dynamic-update-slice_fusion), channel_id=1, source_target_pairs={{5,9},{11,7},{21,25},{27,23}} | collective-permute-start | bytes 98312 | tf_op jit(solution)/shard_map/ppermute | solution.py:230
  11.1 2.9 %collective-permute-start.7 = (bf16[8,2,8,128]{3,2,1,0:T(8,128)(2,1)S(1)}, bf16[8,2,8,128]{3,2,1,0:T(8,128)(2,1)S(1)}, u32[]{:S(2)}, u32[]{:S(2)}) collective-permute-start(bf16[8,2,8,128]{3,2,1,0:T(8,128)(2,1)S(1)} %constant_dynamic-update-slice_fusion), channel_id=1, source_target_pairs={{5,15},{11,1},{21,31},{27,17}} | collective-permute-start | bytes 98312 | tf_op jit(solution)/shard_map/ppermute | solution.py:230
  11.8 2.2 %collective-permute-start.8 = (bf16[8,2,8,128]{3,2,1,0:T(8,128)(2,1)S(1)}, bf16[8,2,8,128]{3,2,1,0:T(8,128)(2,1)S(1)}, u32[]{:S(2)}, u32[]{:S(2)}) collective-permute-start(bf16[8,2,8,128]{3,2,1,0:T(8,128)(2,1)S(1)} %constant_dynamic-update-slice_fusion), channel_id=1, source_target_pairs={{5,13},{11,3},{21,29},{27,19}} | collective-permute-start | bytes 98312 | tf_op jit(solution)/shard_map/ppermute | solution.py:230
  12.5 16.2 %copy-start.2 = (bf16[128,256]{1,0:T(8,128)(2,1)S(1)}, bf16[128,256]{1,0:T(8,128)(2,1)}, u32[]{:S(2)}) copy-start(bf16[128,256]{1,0:T(8,128)(2,1)} %in_gate_ref.1) | copy-start | bytes 196612
  12.5 16.2 %copy-start.3 = (bf16[128,128]{1,0:T(8,128)(2,1)S(1)}, bf16[128,128]{1,0:T(8,128)(2,1)}, u32[]{:S(2)}) copy-start(bf16[128,128]{1,0:T(8,128)(2,1)} %out_gate_ref.1) | copy-start | bytes 98308
  12.5 16.2 %copy-start.4 = (bf16[128,128]{1,0:T(8,128)(2,1)S(1)}, bf16[128,128]{1,0:T(8,128)(2,1)}, u32[]{:S(2)}) copy-start(bf16[128,128]{1,0:T(8,128)(2,1)} %out_weight_ref.1) | copy-start | bytes 98308
  12.5 16.2 %copy-start.5 = (bf16[128,128]{1,0:T(8,128)(2,1)S(1)}, bf16[128,128]{1,0:T(8,128)(2,1)}, u32[]{:S(2)}) copy-start(bf16[128,128]{1,0:T(8,128)(2,1)} %att_gate_ref.1) | copy-start | bytes 98308
  12.6 16.2 %copy-start = (bf16[128,384]{1,0:T(8,128)(2,1)S(1)}, bf16[128,384]{1,0:T(8,128)(2,1)}, u32[]{:S(2)}) copy-start(bf16[128,384]{1,0:T(8,128)(2,1)} %qkv_ref.1) | copy-start | bytes 294916
  12.6 16.2 %copy-start.1 = (bf16[128,256]{1,0:T(8,128)(2,1)S(1)}, bf16[128,256]{1,0:T(8,128)(2,1)}, u32[]{:S(2)}) copy-start(bf16[128,256]{1,0:T(8,128)(2,1)} %in_weight_ref.1) | copy-start | bytes 196612
  12.6 9.6 %collective-permute-start.11 = (bf16[8,2,8,128]{3,2,1,0:T(8,128)(2,1)S(1)}, bf16[8,2,8,128]{3,2,1,0:T(8,128)(2,1)S(1)}, u32[]{:S(2)}, u32[]{:S(2)}) collective-permute-start(bf16[8,2,8,128]{3,2,1,0:T(8,128)(2,1)S(1)} %add_add_fusion.1.near_ref), channel_id=1, source_target_pairs={{1,0},{3,2},{5,4},{7,6},{9,8},{11,10},{13,12},{15,14},{17,16},{19,... | collective-permute-start | bytes 98312 | tf_op jit(solution)/shard_map/ppermute | solution.py:230
  14.1 14.7 %copy-start.10 = (f32[128]{0:T(128)S(1)}, f32[128]{0:T(128)}, u32[]{:S(2)}) copy-start(f32[128]{0:T(128)} %param.23) | copy-start | bytes 1540
  14.1 14.7 %copy-start.11 = (f32[128]{0:T(128)S(1)}, f32[128]{0:T(128)}, u32[]{:S(2)}) copy-start(f32[128]{0:T(128)} %param.25) | copy-start | bytes 1540
  14.1 14.6 %collective-permute-start.12 = (bf16[8,2,8,128]{3,2,1,0:T(8,128)(2,1)S(1)}, bf16[8,2,8,128]{3,2,1,0:T(8,128)(2,1)S(1)}, u32[]{:S(2)}, u32[]{:S(2)}) collective-permute-start(bf16[8,2,8,128]{3,2,1,0:T(8,128)(2,1)S(1)} %add_add_fusion.far_ref), channel_id=1, source_target_pairs={{1,0},{3,2},{5,4},{7,6},{9,8},{11,10},{13,12},{15,14},{17,16},{19,... | collective-permute-start | bytes 98312 | tf_op jit(solution)/shard_map/ppermute | solution.py:230
  28.7 0.7 %copy-start.7 = (bf16[128,4]{0,1:T(4,128)(2,1)S(1)}, bf16[128,4]{0,1:T(4,128)(2,1)}, u32[]{:S(2)}) copy-start(bf16[128,4]{0,1:T(4,128)(2,1)} %param.28) | copy-start | bytes 3076
  28.8 0.7 %copy-start.9 = (f32[128]{0:T(128)S(1)}, f32[128]{0:T(128)}, u32[]{:S(2)}) copy-start(f32[128]{0:T(128)} %param.19) | copy-start | bytes 1540

commit v5 on v3

--- a/solution.py
+++ b/solution.py
@@ -39,7 +39,28 @@
     return values.astype(jnp.bfloat16).astype(jnp.float32)
 
 
-def stage_kernel(cols, mask_ref, pos_ref, table_ref, rel_ref, pair_mask_ref):
+def own_kernel(pair_ref, chip_ref):
+    chip_ref[0] = pair_ref[...]
+
+
+def stage_kernel(
+    cols,
+    mask_ref,
+    pos_ref,
+    table_ref,
+    norm_in_ref,
+    norm_out_ref,
+    att_norm_ref,
+    att_bias_ref,
+    rel_ref,
+    pair_mask_ref,
+    gains_ref,
+    bias_ref,
+):
+    gains_ref[0:1] = norm_in_ref[...]
+    gains_ref[1:2] = norm_out_ref[...]
+    gains_ref[2:3] = att_norm_ref[...]
+    bias_ref[...] = att_bias_ref[...]
     tokens = pos_ref.shape[0]
     bins = table_ref.shape[0]
     sub = lax.broadcasted_iota(jnp.int32, (cols, bins), 0)
@@ -60,28 +81,24 @@
     rel_ref[...] = dot(hot, table_ref[...])
 
 
-def whole_pair_kernel(row_dim, col_dim, heads, pieces, *refs):
-    whole_pair_steps(row_dim, col_dim, heads, refs[:pieces], *refs[pieces:])
-
-
-def whole_pair_steps(
+def whole_pair_kernel(
     row_dim,
-    col_dim,
     heads,
-    piece_refs,
+    held_ref,
+    last_ref,
+    held_sent_ref,
+    last_sent_ref,
     mask_ref,
     rel_ref,
     pair_mask_ref,
-    norm_in_ref,
+    gains_ref,
+    att_bias_ref,
     in_weight_ref,
     in_gate_ref,
     out_gate_ref,
-    norm_out_ref,
     out_weight_ref,
-    att_norm_ref,
     qkv_ref,
     att_gate_ref,
-    att_bias_ref,
     att_out_ref,
     out_ref,
     base_ref,
@@ -91,25 +108,27 @@
     att_ref,
     upd_ref,
 ):
-    rows, cols, width = piece_refs[0].shape[1:]
+    rows, cols, width = held_ref.shape[1:]
     tokens = row_dim * rows
     head_dim = width // heads
     row_first = lax.axis_index("row") * rows
     col_first = pl.multiple_of(lax.axis_index("col") * cols, cols)
     f32, bf16 = jnp.float32, jnp.bfloat16
 
-    me = lax.axis_index("row") * col_dim + lax.axis_index("col")
-    blocks = [piece_ref[at].astype(f32) for piece_ref in piece_refs for at in range(piece_ref.shape[0])]
-    for m, block in enumerate(blocks):
-        owner = me ^ m
+    is_odd = lax.axis_index("col") == 1
+    odd = lax.axis_index("row") * 2 + 1
+    for m in range(2 * row_dim):
+        here, sent = ((held_ref, held_sent_ref), (last_ref, last_sent_ref))[m // row_dim]
+        owner = odd ^ m
+        block = jnp.where(is_odd, here[m % row_dim].astype(f32), sent[m % row_dim].astype(f32))
         for r in range(rows):
-            first = (owner // col_dim * rows + r) * tokens + owner % col_dim * cols
+            first = (owner // 2 * rows + r) * tokens + owner % 2 * cols
             base_ref[pl.ds(pl.multiple_of(first, cols), cols), :] = block[r]
 
     base = base_ref[...] + rel_ref[...]
     base_ref[...] = base
 
-    normed = layer_norm(base, norm_in_ref[...]).astype(bf16)
+    normed = layer_norm(base, gains_ref[0:1]).astype(bf16)
     normed_ref[...] = normed.astype(f32)
     projected = sigmoid(dot(normed, in_gate_ref[...])) * dot(normed, in_weight_ref[...])
     pair_mask = pair_mask_ref[...]
@@ -136,10 +155,10 @@
         own += [ref[pl.ds(row_first + r, tokens, stride=tokens), :] for r in range(rows)]
         return jnp.concatenate(own, axis=0)
 
-    normed_out = layer_norm(products, norm_out_ref[...]).astype(bf16)
+    normed_out = layer_norm(products, gains_ref[1:2]).astype(bf16)
     out_gate = sigmoid(dot(chosen(normed_ref).astype(bf16), out_gate_ref[...]))
     updated = chosen(base_ref) + out_gate * dot(normed_out, out_weight_ref[...])
-    normed_att = layer_norm(updated, att_norm_ref[...]).astype(bf16)
+    normed_att = layer_norm(updated, gains_ref[2:3]).astype(bf16)
     own_pairs = rows * cols
     column_pairs = tokens * cols
     upd_ref[...] = updated[:column_pairs]
@@ -197,7 +216,6 @@
 
 def whole_pair_on_device(
     row_dim,
-    col_dim,
     pair_in,
     token_mask,
     positions,
@@ -215,52 +233,69 @@
     att_out,
 ):
     rows, cols, width = pair_in.shape
-    tokens = row_dim * rows
-    heads = att_bias.shape[1]
-    blocks = row_dim * col_dim
-    pair = [pair_in[None]]
-    step = 1
-    while step < blocks:
-        partners = [(device, device ^ step) for device in range(blocks)]
-        held = jnp.concatenate(pair, axis=0)
-        pair.append(lax.ppermute(held, ("row", "col"), partners))
-        step *= 2
-
     vmem = pl.BlockSpec(memory_space=pltpu.VMEM)
     smem = pl.BlockSpec(memory_space=pltpu.SMEM)
-    weights = (
+    params = pltpu.CompilerParams(vmem_limit_bytes=16 * 1024 * 1024)
+
+    tokens, heads = row_dim * rows, att_bias.shape[1]
+
+    def move(values, step, devices):
+        return lax.ppermute(values, ("row", "col"), [(device, device ^ step) for device in devices])
+
+    blocks = 2 * row_dim
+    chip = pl.pallas_call(
+        own_kernel,
+        out_shape=jax.ShapeDtypeStruct((2,) + pair_in.shape, pair_in.dtype),
+        in_specs=[vmem],
+        out_specs=vmem,
+        compiler_params=params,
+    )(pair_in)
+    held = chip.at[1].set(move(pair_in, 1, range(blocks)))
+    step = 2
+    while True:
+        last = move(held, step, range(1, blocks, 2))
+        step *= 2
+        if step == blocks:
+            break
+        held = jnp.concatenate([held, last], axis=0)
+    held_sent = move(held, 1, range(blocks))
+
+    wide_out = jax.ShapeDtypeStruct((tokens * tokens, width), jnp.float32)
+    staged = pl.pallas_call(
+        functools.partial(stage_kernel, cols),
+        out_shape=[
+            wide_out,
+            wide_out,
+            jax.ShapeDtypeStruct((3, width), jnp.float32),
+            jax.ShapeDtypeStruct((heads, width), att_bias.dtype),
+        ],
+        in_specs=[smem] * 2 + [vmem] * 5,
+        out_specs=[vmem] * 4,
+        compiler_params=params,
+        cost_estimate=pl.CostEstimate(flops=STAGE_FLOPS, bytes_accessed=2**20, transcendentals=0),
+    )(
+        token_mask,
+        positions,
+        relpos_table,
         tri_norm_in.reshape(1, width),
-        tri_in_weight,
-        tri_in_gate,
-        tri_out_gate,
         tri_norm_out.reshape(1, width),
-        tri_out_weight,
         att_norm.reshape(1, width),
-        att_qkv,
-        att_gate,
         att_bias.T,
-        att_out,
-    )
+    )
+    last, *staged = lax.optimization_barrier((last, *staged))
+    gathered = (held, last, held_sent, move(last, 1, range(blocks)))
+
+    weights = (tri_in_weight, tri_in_gate, tri_out_gate, tri_out_weight, att_qkv, att_gate, att_out)
     wide = pltpu.VMEM((tokens * tokens, width), jnp.float32)
     column = pltpu.VMEM((tokens * cols, width), jnp.float32)
-    params = pltpu.CompilerParams(vmem_limit_bytes=16 * 1024 * 1024)
-    wide_out = jax.ShapeDtypeStruct((tokens * tokens, width), jnp.float32)
-    rel, pair_mask = pl.pallas_call(
-        functools.partial(stage_kernel, cols),
-        out_shape=[wide_out] * 2,
-        in_specs=[smem] * 2 + [vmem],
-        out_specs=[vmem] * 2,
-        compiler_params=params,
-        cost_estimate=pl.CostEstimate(flops=STAGE_FLOPS, bytes_accessed=2**20, transcendentals=0),
-    )(token_mask, positions, relpos_table)
     return pl.pallas_call(
-        functools.partial(whole_pair_kernel, row_dim, col_dim, heads, len(pair)),
+        functools.partial(whole_pair_kernel, row_dim, heads),
         out_shape=jax.ShapeDtypeStruct(pair_in.shape, pair_in.dtype),
-        in_specs=[vmem] * len(pair) + [smem] + [vmem] * (2 + len(weights)),
+        in_specs=[vmem] * 4 + [smem] + [vmem] * (4 + len(weights)),
         out_specs=vmem,
         scratch_shapes=[wide] * 4 + [column] * 2,
         compiler_params=params,
-    )(*pair, token_mask, rel, pair_mask, *weights)
+    )(*gathered, token_mask, *staged, *weights)
 
 
 def attend_column(query_col, key_col, value_col, bias_all, key_bias, block_rows):
@@ -386,9 +421,9 @@
     tokens = row_dim * rows
     whole_bytes = tokens * tokens * width * pair_in.dtype.itemsize
     blocks = row_dim * col_dim
-    tiled = cols % 8 == 0 and width % 128 == 0 and blocks & (blocks - 1) == 0
+    tiled = cols % 8 == 0 and width % 128 == 0 and blocks & (blocks - 1) == 0 and blocks >= 4 and col_dim == 2
     if whole_bytes <= WHOLE_PAIR_BYTES and tiled:
-        return whole_pair_on_device(row_dim, col_dim, pair_in, *others)
+        return whole_pair_on_device(row_dim, pair_in, *others)
     return split_pair_on_device(pair_in, *others)
 
 

time: 19.3 us -> 22.1 us (1.15)
  starting transfers between devices: 8.55 us -> 15.2 us
  waiting for transfers between devices: 5.48 us -> 1.47 us
  local copies, waits for them, and re-layouts: 0.68 us -> 1.43 us
  other arithmetic: 0.7 us -> 0.01 us
    ppermute x4 -> x6, starting transfers between devices: 8.55 us -> 15.2 us  [move(): lax.ppermute(values, ('row', 'col'), [(device, device ^ step) for device...]
    ppermute x4 -> x6, waiting for transfers between devices: 5.48 us -> 1.47 us  [move(): lax.ppermute(values, ('row', 'col'), [(device, device ^ step) for device...]
    unnamed x30, local copies, waits for them, and re-layouts: 0.68 us -> 1.43 us
    concatenate x3 -> x2, other arithmetic: 0.7 us -> 0.01 us  [whole_pair_on_device(): held = jnp.concatenate([held, last], axis=0)]
    pallas_call x1 -> x2, Pallas kernels: 2.82 us -> 2.82 us  [the longest x1 2.82 us: whole_pair_on_device(): pl.pallas_call(functools.partial(whole_pair_kernel, row_dim, heads), out_...]
  transfers between devices with their start and end apart: 4 -> 6, of which waited for: 4 -> 3; matrix products, arithmetic and copies ran while one was open for 0% -> 0% of each run, Pallas kernels for 4% -> 3%
where the time goes in v5:
time: 22.1 us; the launch traced here: 21.9 us
  starting transfers between devices  15.2 us (69%)
  Pallas kernels  3.54 us (16%)
  waiting for transfers between devices  1.47 us (7%)
  local copies, waits for them, and re-layouts  1.43 us (6%)
    ppermute x6, starting transfers between devices, move(): lax.ppermute(values, ('row', 'col'), [(device, device ^ step) for device...  15.2 us
    pallas_call x1, Pallas kernels, whole_pair_on_device(): pl.pallas_call(functools.partial(whole_pair_kernel, row_dim, heads), out_...  2.82 us
    ppermute x6, waiting for transfers between devices, move(): lax.ppermute(values, ('row', 'col'), [(device, device ^ step) for device...  1.47 us
    unnamed x30, local copies, waits for them, and re-layouts  1.43 us
    pallas_call x1, Pallas kernels, whole_pair_on_device(): pl.pallas_call(functools.partial(stage_kernel, cols), out_shape=[wide_out...  0.72 us
  transfers between devices with their start and end apart: 6, of which 3 were waited for; matrix products, arithmetic and copies ran while one was open for 0% of the time, Pallas kernels for 3%

profile of v5, /device:TPU:0, one launch (start us, length us, event | category | flops | bytes accessed | tf_op | source)
XLA Modules:
  0.0 21.9 jit_solution(2831161129006660588)
XLA Ops:
  0.0 0.5 %collective-permute-start = (bf16[2,8,128]{2,1,0:T(8,128)(2,1)}, bf16[2,8,128]{2,1,0:T(8,128)(2,1)S(1)}, u32[]{:S(2)}, u32[]{:S(2)}) collective-permute-start(bf16[2,8,128]{2,1,0:T(8,128)(2,1)} %pair_ref.1), channel_id=1, source_target_pairs={{0,1},{1,0},{2,3},{3,2},{4,5},{5,4},{6,7},{7,6},{8,9},{9,8},{10,11... | collective-permute-start | bytes 12296 | tf_op jit(solution)/shard_map/ppermute | solution.py:243
  0.5 0.0 copy-start.7
  0.5 0.7 %copy-done.7 = bf16[2,8,128]{2,1,0:T(8,128)(2,1)S(1)} copy-done((bf16[2,8,128]{2,1,0:T(8,128)(2,1)S(1)}, bf16[2,8,128]{2,1,0:T(8,128)(2,1)}, u32[]{:S(2)}) %copy-start.7) | copy-done | bytes 4120
  1.1 0.3 %collective-permute-done = bf16[2,8,128]{2,1,0:T(8,128)(2,1)S(1)} collective-permute-done((bf16[2,8,128]{2,1,0:T(8,128)(2,1)}, bf16[2,8,128]{2,1,0:T(8,128)(2,1)S(1)}, u32[]{:S(2)}, u32[]{:S(2)}) %collective-permute-start) | collective-permute-done | bytes 4128 | tf_op jit(solution)/shard_map/ppermute | solution.py:243
  1.5 0.6 %collective-permute-start.1 = (bf16[2,2,8,128]{3,2,1,0:T(8,128)(2,1)S(1)}, bf16[2,2,8,128]{3,2,1,0:T(8,128)(2,1)S(1)}, u32[]{:S(2)}, u32[]{:S(2)}) collective-permute-start(bf16[2,2,8,128]{3,2,1,0:T(8,128)(2,1)S(1)} %bitcast_dynamic-update-slice_fusion), channel_id=1, source_target_pairs={{1,3},{3,1},{5,7},{7,5},{9,11},{11,9},{13,15},{15,13},{17,19},{19,... | collective-permute-start | bytes 24584 | tf_op jit(solution)/shard_map/ppermute | solution.py:243
  2.2 0.0 collective-permute-done.1
  2.2 0.0 copy-start.9
  2.2 0.7 %collective-permute-start.2 = (bf16[4,2,8,128]{3,2,1,0:T(8,128)(2,1)S(1)}, bf16[4,2,8,128]{3,2,1,0:T(8,128)(2,1)S(1)}, u32[]{:S(2)}, u32[]{:S(2)}) collective-permute-start(bf16[4,2,8,128]{3,2,1,0:T(8,128)(2,1)S(1)} %pad_maximum_fusion.1), channel_id=1, source_target_pairs={{1,5},{3,7},{5,1},{7,3},{9,13},{11,15},{13,9},{15,11},{17,21},{19,... | collective-permute-start | bytes 49160 | tf_op jit(solution)/shard_map/ppermute | solution.py:243
  2.9 0.0 collective-permute-done.2
  2.9 0.7 %collective-permute-start.3 = (bf16[8,2,8,128]{3,2,1,0:T(8,128)(2,1)S(1)}, bf16[8,2,8,128]{3,2,1,0:T(8,128)(2,1)S(1)}, u32[]{:S(2)}, u32[]{:S(2)}) collective-permute-start(bf16[8,2,8,128]{3,2,1,0:T(8,128)(2,1)S(1)} %pad_maximum_fusion.held_ref), channel_id=1, source_target_pairs={{1,9},{3,11},{5,13},{7,15},{9,1},{11,3},{13,5},{15,7},{17,25},{19,... | collective-permute-start | bytes 98312 | tf_op jit(solution)/shard_map/ppermute | solution.py:243
  3.6 0.0 copy-start.11
  3.6 0.0 copy-start.12
  3.6 0.0 copy-start.13
  3.6 0.0 copy-start.14
  3.6 0.0 copy-start.8
  3.6 0.0 copy-start.10
  3.6 0.0 copy-done.9
  3.6 0.6 %copy-done.11 = s32[16]{0:T(128)S(1)} copy-done((s32[16]{0:T(128)S(1)}, s32[16]{0:T(128)}, u32[]{:S(2)}) %copy-start.11) | copy-done | bytes 88
  4.2 0.0 copy-done.12
  4.2 0.0 copy-done.13
  4.2 0.0 copy-done.14
  4.3 0.0 copy-done.8
  4.3 0.0 copy-done.10
  4.3 0.0 copy-start
  4.3 0.0 copy-start.1
  4.3 0.0 copy-start.2
  4.3 0.0 copy-start.3
  4.3 0.0 copy-start.4
  4.3 0.0 copy-start.5
  4.4 0.0 copy-start.6
  4.4 0.7 %shard_map.146 = (f32[256,128]{1,0:T(8,128)S(1)}, f32[256,128]{1,0:T(8,128)S(1)}, f32[3,128]{1,0:T(4,128)S(1)}, bf16[4,128]{1,0:T(4,128)(2,1)S(1)}) custom-call(s32[16]{0:T(128)S(1)} %copy-done.8, s32[16]{0:T(128)S(1)} %copy-done.11, bf16[128,128]{1,0:T(8,128)(2,1)S(1)} %copy-done.9, f32[1,128]{1,0:T(1,128)S(1)} %bitcast.7, f32[1,128]{1,0:T(1,128)S(1)} %bitcast.8, ...), custom_call_target="tpu_custom_call" | custom-call | flops 1000000000 | bytes 1048576 | tf_op jit(solution)/shard_map/pallas_call | solution.py:264
  5.1 12.7 %collective-permute-start.4 = (bf16[8,2,8,128]{3,2,1,0:T(8,128)(2,1)S(1)}, bf16[8,2,8,128]{3,2,1,0:T(8,128)(2,1)S(1)}, u32[]{:S(2)}, u32[]{:S(2)}) collective-permute-start(bf16[8,2,8,128]{3,2,1,0:T(8,128)(2,1)S(1)} %pad_maximum_fusion.held_ref), channel_id=1, source_target_pairs={{0,1},{1,0},{2,3},{3,2},{4,5},{5,4},{6,7},{7,6},{8,9},{9,8},{10,11... | collective-permute-start | bytes 98312 | tf_op jit(solution)/shard_map/ppermute | solution.py:243
  17.8 0.0 collective-permute-done.3.last_ref
  17.8 0.1 collective-permute-start.5
  17.9 0.8 %collective-permute-done.4.held_sent_ref = bf16[8,2,8,128]{3,2,1,0:T(8,128)(2,1)S(1)} collective-permute-done((bf16[8,2,8,128]{3,2,1,0:T(8,128)(2,1)S(1)}, bf16[8,2,8,128]{3,2,1,0:T(8,128)(2,1)S(1)}, u32[]{:S(2)}, u32[]{:S(2)}) %collective-permute-start.4) | collective-permute-done | bytes 32800 | tf_op jit(solution)/shard_map/ppermute | solution.py:243
  18.7 0.4 %collective-permute-done.5.last_sent_ref = bf16[8,2,8,128]{3,2,1,0:T(8,128)(2,1)S(1)} collective-permute-done((bf16[8,2,8,128]{3,2,1,0:T(8,128)(2,1)S(1)}, bf16[8,2,8,128]{3,2,1,0:T(8,128)(2,1)S(1)}, u32[]{:S(2)}, u32[]{:S(2)}) %collective-permute-start.5) | collective-permute-done | bytes 32800 | tf_op jit(solution)/shard_map/ppermute | solution.py:243
  19.0 0.0 copy-done
  19.0 0.0 copy-done.1
  19.0 0.0 copy-done.2
  19.0 0.0 copy-done.3
  19.0 0.0 copy-done.4
  19.0 0.0 copy-done.5
  19.1 0.0 copy-done.6
  19.1 2.8 %shard_map.147 = bf16[2,8,128]{2,1,0:T(8,128)(2,1)} custom-call(bf16[8,2,8,128]{3,2,1,0:T(8,128)(2,1)S(1)} %pad_maximum_fusion.held_ref, bf16[8,2,8,128]{3,2,1,0:T(8,128)(2,1)S(1)} %collective-permute-done.3.last_ref, bf16[8,2,8,128]{3,2,1,0:T(8,128)(2,1)S(1)} %collective-permute-done.4.held_sent_ref, ...), custom_call_target="tpu_custom_call" | custom-call | tf_op jit(solution)/shard_map/pallas_call | solution.py:291
  (4 shorter events, 0.0 us)
Async XLA Ops:
  0.0 1.5 %collective-permute-start = (bf16[2,8,128]{2,1,0:T(8,128)(2,1)}, bf16[2,8,128]{2,1,0:T(8,128)(2,1)S(1)}, u32[]{:S(2)}, u32[]{:S(2)}) collective-permute-start(bf16[2,8,128]{2,1,0:T(8,128)(2,1)} %pair_ref.1), channel_id=1, source_target_pairs={{0,1},{1,0},{2,3},{3,2},{4,5},{5,4},{6,7},{7,6},{8,9},{9,8},{10,11... | collective-permute-start | bytes 12296 | tf_op jit(solution)/shard_map/ppermute | solution.py:243
  0.5 0.7 %copy-start.7 = (bf16[2,8,128]{2,1,0:T(8,128)(2,1)S(1)}, bf16[2,8,128]{2,1,0:T(8,128)(2,1)}, u32[]{:S(2)}) copy-start(bf16[2,8,128]{2,1,0:T(8,128)(2,1)} %pair_ref.1) | copy-start | bytes 12292
  1.5 0.7 %collective-permute-start.1 = (bf16[2,2,8,128]{3,2,1,0:T(8,128)(2,1)S(1)}, bf16[2,2,8,128]{3,2,1,0:T(8,128)(2,1)S(1)}, u32[]{:S(2)}, u32[]{:S(2)}) collective-permute-start(bf16[2,2,8,128]{3,2,1,0:T(8,128)(2,1)S(1)} %bitcast_dynamic-update-slice_fusion), channel_id=1, source_target_pairs={{1,3},{3,1},{5,7},{7,5},{9,11},{11,9},{13,15},{15,13},{17,19},{19,... | collective-permute-start | bytes 24584 | tf_op jit(solution)/shard_map/ppermute | solution.py:243
  2.2 1.5 %copy-start.9 = (bf16[128,128]{1,0:T(8,128)(2,1)S(1)}, bf16[128,128]{1,0:T(8,128)(2,1)}, u32[]{:S(2)}) copy-start(bf16[128,128]{1,0:T(8,128)(2,1)} %table_ref.1) | copy-start | bytes 98308
  2.2 0.7 %collective-permute-start.2 = (bf16[4,2,8,128]{3,2,1,0:T(8,128)(2,1)S(1)}, bf16[4,2,8,128]{3,2,1,0:T(8,128)(2,1)S(1)}, u32[]{:S(2)}, u32[]{:S(2)}) collective-permute-start(bf16[4,2,8,128]{3,2,1,0:T(8,128)(2,1)S(1)} %pad_maximum_fusion.1), channel_id=1, source_target_pairs={{1,5},{3,7},{5,1},{7,3},{9,13},{11,15},{13,9},{15,11},{17,21},{19,... | collective-permute-start | bytes 49160 | tf_op jit(solution)/shard_map/ppermute | solution.py:243
  2.9 14.9 %collective-permute-start.3 = (bf16[8,2,8,128]{3,2,1,0:T(8,128)(2,1)S(1)}, bf16[8,2,8,128]{3,2,1,0:T(8,128)(2,1)S(1)}, u32[]{:S(2)}, u32[]{:S(2)}) collective-permute-start(bf16[8,2,8,128]{3,2,1,0:T(8,128)(2,1)S(1)} %pad_maximum_fusion.held_ref), channel_id=1, source_target_pairs={{1,9},{3,11},{5,13},{7,15},{9,1},{11,3},{13,5},{15,7},{17,25},{19,... | collective-permute-start | bytes 98312 | tf_op jit(solution)/shard_map/ppermute | solution.py:243
  3.6 0.7 %copy-start.11 = (s32[16]{0:T(128)S(1)}, s32[16]{0:T(128)}, u32[]{:S(2)}) copy-start(s32[16]{0:T(128)} %pos_ref.1) | copy-start | bytes 196
  3.6 0.7 %copy-start.12 = (f32[128]{0:T(128)S(1)}, f32[128]{0:T(128)}, u32[]{:S(2)}) copy-start(f32[128]{0:T(128)} %param.21) | copy-start | bytes 1540
  3.6 0.7 %copy-start.13 = (f32[128]{0:T(128)S(1)}, f32[128]{0:T(128)}, u32[]{:S(2)}) copy-start(f32[128]{0:T(128)} %param.25) | copy-start | bytes 1540
  3.6 0.7 %copy-start.14 = (f32[128]{0:T(128)S(1)}, f32[128]{0:T(128)}, u32[]{:S(2)}) copy-start(f32[128]{0:T(128)} %param.27) | copy-start | bytes 1540
  3.6 0.7 %copy-start.8 = (s32[16]{0:T(128)S(1)}, s32[16]{0:T(128)}, u32[]{:S(2)}) copy-start(s32[16]{0:T(128)} %mask_ref.3) | copy-start | bytes 196
  3.6 0.7 %copy-start.10 = (bf16[128,4]{0,1:T(4,128)(2,1)S(1)}, bf16[128,4]{0,1:T(4,128)(2,1)}, u32[]{:S(2)}) copy-start(bf16[128,4]{0,1:T(4,128)(2,1)} %param.30) | copy-start | bytes 3076
  4.3 14.7 %copy-start = (bf16[128,384]{1,0:T(8,128)(2,1)S(1)}, bf16[128,384]{1,0:T(8,128)(2,1)}, u32[]{:S(2)}) copy-start(bf16[128,384]{1,0:T(8,128)(2,1)} %qkv_ref.1) | copy-start | bytes 294916
  4.3 14.7 %copy-start.1 = (bf16[128,256]{1,0:T(8,128)(2,1)S(1)}, bf16[128,256]{1,0:T(8,128)(2,1)}, u32[]{:S(2)}) copy-start(bf16[128,256]{1,0:T(8,128)(2,1)} %in_weight_ref.1) | copy-start | bytes 196612
  4.3 14.7 %copy-start.2 = (bf16[128,256]{1,0:T(8,128)(2,1)S(1)}, bf16[128,256]{1,0:T(8,128)(2,1)}, u32[]{:S(2)}) copy-start(bf16[128,256]{1,0:T(8,128)(2,1)} %in_gate_ref.1) | copy-start | bytes 196612
  4.3 14.7 %copy-start.3 = (bf16[128,128]{1,0:T(8,128)(2,1)S(1)}, bf16[128,128]{1,0:T(8,128)(2,1)}, u32[]{:S(2)}) copy-start(bf16[128,128]{1,0:T(8,128)(2,1)} %out_gate_ref.1) | copy-start | bytes 98308
  4.3 14.7 %copy-start.4 = (bf16[128,128]{1,0:T(8,128)(2,1)S(1)}, bf16[128,128]{1,0:T(8,128)(2,1)}, u32[]{:S(2)}) copy-start(bf16[128,128]{1,0:T(8,128)(2,1)} %out_weight_ref.1) | copy-start | bytes 98308
  4.3 14.7 %copy-start.5 = (bf16[128,128]{1,0:T(8,128)(2,1)S(1)}, bf16[128,128]{1,0:T(8,128)(2,1)}, u32[]{:S(2)}) copy-start(bf16[128,128]{1,0:T(8,128)(2,1)} %att_gate_ref.1) | copy-start | bytes 98308
  4.4 14.7 %copy-start.6 = (bf16[128,128]{1,0:T(8,128)(2,1)S(1)}, bf16[128,128]{1,0:T(8,128)(2,1)}, u32[]{:S(2)}) copy-start(bf16[128,128]{1,0:T(8,128)(2,1)} %att_out_ref.1) | copy-start | bytes 98308
  5.1 13.6 %collective-permute-start.4 = (bf16[8,2,8,128]{3,2,1,0:T(8,128)(2,1)S(1)}, bf16[8,2,8,128]{3,2,1,0:T(8,128)(2,1)S(1)}, u32[]{:S(2)}, u32[]{:S(2)}) collective-permute-start(bf16[8,2,8,128]{3,2,1,0:T(8,128)(2,1)S(1)} %pad_maximum_fusion.held_ref), channel_id=1, source_target_pairs={{0,1},{1,0},{2,3},{3,2},{4,5},{5,4},{6,7},{7,6},{8,9},{9,8},{10,11... | collective-permute-start | bytes 98312 | tf_op jit(solution)/shard_map/ppermute | solution.py:243
  17.8 1.2 %collective-permute-start.5 = (bf16[8,2,8,128]{3,2,1,0:T(8,128)(2,1)S(1)}, bf16[8,2,8,128]{3,2,1,0:T(8,128)(2,1)S(1)}, u32[]{:S(2)}, u32[]{:S(2)}) collective-permute-start(bf16[8,2,8,128]{3,2,1,0:T(8,128)(2,1)S(1)} %collective-permute-done.3.last_ref), channel_id=1, source_target_pairs={{0,1},{1,0},{2,3},{3,2},{4,5},{5,4},{6,7},{7,6},{8,9},{9,8},{10,11... | collective-permute-start | bytes 98312 | tf_op jit(solution)/shard_map/ppermute | solution.py:243

commit v6 on v5

--- a/solution.py
+++ b/solution.py
@@ -239,8 +239,9 @@
 
     tokens, heads = row_dim * rows, att_bias.shape[1]
 
-    def move(values, step, devices):
-        return lax.ppermute(values, ("row", "col"), [(device, device ^ step) for device in devices])
+    def move(values, step):
+        pairs = [(device, device ^ step if step == 1 or device % 2 else device) for device in range(blocks)]
+        return lax.ppermute(values, ("row", "col"), pairs)
 
     blocks = 2 * row_dim
     chip = pl.pallas_call(
@@ -250,15 +251,15 @@
         out_specs=vmem,
         compiler_params=params,
     )(pair_in)
-    held = chip.at[1].set(move(pair_in, 1, range(blocks)))
+    held = chip.at[1].set(move(pair_in, 1))
     step = 2
     while True:
-        last = move(held, step, range(1, blocks, 2))
+        last = move(held, step)
         step *= 2
         if step == blocks:
             break
         held = jnp.concatenate([held, last], axis=0)
-    held_sent = move(held, 1, range(blocks))
+    held_sent = move(held, 1)
 
     wide_out = jax.ShapeDtypeStruct((tokens * tokens, width), jnp.float32)
     staged = pl.pallas_call(
@@ -283,7 +284,7 @@
         att_bias.T,
     )
     last, *staged = lax.optimization_barrier((last, *staged))
-    gathered = (held, last, held_sent, move(last, 1, range(blocks)))
+    gathered = (held, last, held_sent, move(last, 1))
 
     weights = (tri_in_weight, tri_in_gate, tri_out_gate, tri_out_weight, att_qkv, att_gate, att_out)
     wide = pltpu.VMEM((tokens * tokens, width), jnp.float32)

time: 22.1 us -> 22.1 us (level)
  no operation moved by 1% of the time
where the time goes in v6:
time: 22.1 us; the launch traced here: 21.9 us
  starting transfers between devices  15.2 us (69%)
  Pallas kernels  3.54 us (16%)
  waiting for transfers between devices  1.47 us (7%)
  local copies, waits for them, and re-layouts  1.43 us (6%)
    ppermute x6, starting transfers between devices, move(): return lax.ppermute(values, ('row', 'col'), pairs)  15.2 us
    pallas_call x1, Pallas kernels, whole_pair_on_device(): pl.pallas_call(functools.partial(whole_pair_kernel, row_dim, heads), out_...  2.82 us
    ppermute x6, waiting for transfers between devices, move(): return lax.ppermute(values, ('row', 'col'), pairs)  1.47 us
    unnamed x30, local copies, waits for them, and re-layouts  1.43 us
    pallas_call x1, Pallas kernels, whole_pair_on_device(): pl.pallas_call(functools.partial(stage_kernel, cols), out_shape=[wide_out...  0.72 us
  transfers between devices with their start and end apart: 6, of which 3 were waited for; matrix products, arithmetic and copies ran while one was open for 0% of the time, Pallas kernels for 3%

profile of v6, /device:TPU:0, one launch (start us, length us, event | category | flops | bytes accessed | tf_op | source)
XLA Modules:
  0.0 21.9 jit_solution(9501479788916185822)
XLA Ops:
  0.0 0.5 %collective-permute-start = (bf16[2,8,128]{2,1,0:T(8,128)(2,1)}, bf16[2,8,128]{2,1,0:T(8,128)(2,1)S(1)}, u32[]{:S(2)}, u32[]{:S(2)}) collective-permute-start(bf16[2,8,128]{2,1,0:T(8,128)(2,1)} %pair_ref.1), channel_id=1, source_target_pairs={{0,1},{1,0},{2,3},{3,2},{4,5},{5,4},{6,7},{7,6},{8,9},{9,8},{10,11... | collective-permute-start | bytes 12296 | tf_op jit(solution)/shard_map/ppermute | solution.py:244
  0.5 0.0 copy-start.7
  0.5 0.7 %copy-done.7 = bf16[2,8,128]{2,1,0:T(8,128)(2,1)S(1)} copy-done((bf16[2,8,128]{2,1,0:T(8,128)(2,1)S(1)}, bf16[2,8,128]{2,1,0:T(8,128)(2,1)}, u32[]{:S(2)}) %copy-start.7) | copy-done | bytes 4120
  1.1 0.3 %collective-permute-done = bf16[2,8,128]{2,1,0:T(8,128)(2,1)S(1)} collective-permute-done((bf16[2,8,128]{2,1,0:T(8,128)(2,1)}, bf16[2,8,128]{2,1,0:T(8,128)(2,1)S(1)}, u32[]{:S(2)}, u32[]{:S(2)}) %collective-permute-start) | collective-permute-done | bytes 4128 | tf_op jit(solution)/shard_map/ppermute | solution.py:244
  1.5 0.6 %collective-permute-start.1 = (bf16[2,2,8,128]{3,2,1,0:T(8,128)(2,1)S(1)}, bf16[2,2,8,128]{3,2,1,0:T(8,128)(2,1)S(1)}, u32[]{:S(2)}, u32[]{:S(2)}) collective-permute-start(bf16[2,2,8,128]{3,2,1,0:T(8,128)(2,1)S(1)} %bitcast_dynamic-update-slice_fusion), channel_id=1, source_target_pairs={{0,0},{1,3},{2,2},{3,1},{4,4},{5,7},{6,6},{7,5},{8,8},{9,11},{10,1... | collective-permute-start | bytes 24584 | tf_op jit(solution)/shard_map/ppermute | solution.py:244
  2.2 0.0 collective-permute-done.1
  2.2 0.0 copy-start.9
  2.2 0.7 %collective-permute-start.2 = (bf16[4,2,8,128]{3,2,1,0:T(8,128)(2,1)S(1)}, bf16[4,2,8,128]{3,2,1,0:T(8,128)(2,1)S(1)}, u32[]{:S(2)}, u32[]{:S(2)}) collective-permute-start(bf16[4,2,8,128]{3,2,1,0:T(8,128)(2,1)S(1)} %pad_maximum_fusion.1), channel_id=1, source_target_pairs={{0,0},{1,5},{2,2},{3,7},{4,4},{5,1},{6,6},{7,3},{8,8},{9,13},{10,1... | collective-permute-start | bytes 49160 | tf_op jit(solution)/shard_map/ppermute | solution.py:244
  2.9 0.0 collective-permute-done.2
  2.9 0.7 %collective-permute-start.3 = (bf16[8,2,8,128]{3,2,1,0:T(8,128)(2,1)S(1)}, bf16[8,2,8,128]{3,2,1,0:T(8,128)(2,1)S(1)}, u32[]{:S(2)}, u32[]{:S(2)}) collective-permute-start(bf16[8,2,8,128]{3,2,1,0:T(8,128)(2,1)S(1)} %pad_maximum_fusion.held_ref), channel_id=1, source_target_pairs={{0,0},{1,9},{2,2},{3,11},{4,4},{5,13},{6,6},{7,15},{8,8},{9,1},{10... | collective-permute-start | bytes 98312 | tf_op jit(solution)/shard_map/ppermute | solution.py:244
  3.6 0.0 copy-start.11
  3.6 0.0 copy-start.12
  3.6 0.0 copy-start.13
  3.6 0.0 copy-start.14
  3.6 0.0 copy-start.8
  3.6 0.0 copy-start.10
  3.6 0.0 copy-done.9
  3.6 0.6 %copy-done.11 = s32[16]{0:T(128)S(1)} copy-done((s32[16]{0:T(128)S(1)}, s32[16]{0:T(128)}, u32[]{:S(2)}) %copy-start.11) | copy-done | bytes 88
  4.2 0.0 copy-done.12
  4.2 0.0 copy-done.13
  4.2 0.0 copy-done.14
  4.3 0.0 copy-done.8
  4.3 0.0 copy-done.10
  4.3 0.0 copy-start
  4.3 0.0 copy-start.1
  4.3 0.0 copy-start.2
  4.3 0.0 copy-start.3
  4.3 0.0 copy-start.4
  4.3 0.0 copy-start.5
  4.4 0.0 copy-start.6
  4.4 0.7 %shard_map.146 = (f32[256,128]{1,0:T(8,128)S(1)}, f32[256,128]{1,0:T(8,128)S(1)}, f32[3,128]{1,0:T(4,128)S(1)}, bf16[4,128]{1,0:T(4,128)(2,1)S(1)}) custom-call(s32[16]{0:T(128)S(1)} %copy-done.8, s32[16]{0:T(128)S(1)} %copy-done.11, bf16[128,128]{1,0:T(8,128)(2,1)S(1)} %copy-done.9, f32[1,128]{1,0:T(1,128)S(1)} %bitcast.7, f32[1,128]{1,0:T(1,128)S(1)} %bitcast.8, ...), custom_call_target="tpu_custom_call" | custom-call | flops 1000000000 | bytes 1048576 | tf_op jit(solution)/shard_map/pallas_call | solution.py:265
  5.1 12.7 %collective-permute-start.4 = (bf16[8,2,8,128]{3,2,1,0:T(8,128)(2,1)S(1)}, bf16[8,2,8,128]{3,2,1,0:T(8,128)(2,1)S(1)}, u32[]{:S(2)}, u32[]{:S(2)}) collective-permute-start(bf16[8,2,8,128]{3,2,1,0:T(8,128)(2,1)S(1)} %pad_maximum_fusion.held_ref), channel_id=1, source_target_pairs={{0,1},{1,0},{2,3},{3,2},{4,5},{5,4},{6,7},{7,6},{8,9},{9,8},{10,11... | collective-permute-start | bytes 98312 | tf_op jit(solution)/shard_map/ppermute | solution.py:244
  17.8 0.0 collective-permute-done.3.last_ref
  17.8 0.1 collective-permute-start.5
  17.9 0.8 %collective-permute-done.4.held_sent_ref = bf16[8,2,8,128]{3,2,1,0:T(8,128)(2,1)S(1)} collective-permute-done((bf16[8,2,8,128]{3,2,1,0:T(8,128)(2,1)S(1)}, bf16[8,2,8,128]{3,2,1,0:T(8,128)(2,1)S(1)}, u32[]{:S(2)}, u32[]{:S(2)}) %collective-permute-start.4) | collective-permute-done | bytes 32800 | tf_op jit(solution)/shard_map/ppermute | solution.py:244
  18.7 0.4 %collective-permute-done.5.last_sent_ref = bf16[8,2,8,128]{3,2,1,0:T(8,128)(2,1)S(1)} collective-permute-done((bf16[8,2,8,128]{3,2,1,0:T(8,128)(2,1)S(1)}, bf16[8,2,8,128]{3,2,1,0:T(8,128)(2,1)S(1)}, u32[]{:S(2)}, u32[]{:S(2)}) %collective-permute-start.5) | collective-permute-done | bytes 32800 | tf_op jit(solution)/shard_map/ppermute | solution.py:244
  19.0 0.0 copy-done
  19.0 0.0 copy-done.1
  19.0 0.0 copy-done.2
  19.0 0.0 copy-done.3
  19.0 0.0 copy-done.4
  19.0 0.0 copy-done.5
  19.1 0.0 copy-done.6
  19.1 2.8 %shard_map.147 = bf16[2,8,128]{2,1,0:T(8,128)(2,1)} custom-call(bf16[8,2,8,128]{3,2,1,0:T(8,128)(2,1)S(1)} %pad_maximum_fusion.held_ref, bf16[8,2,8,128]{3,2,1,0:T(8,128)(2,1)S(1)} %collective-permute-done.3.last_ref, bf16[8,2,8,128]{3,2,1,0:T(8,128)(2,1)S(1)} %collective-permute-done.4.held_sent_ref, ...), custom_call_target="tpu_custom_call" | custom-call | tf_op jit(solution)/shard_map/pallas_call | solution.py:292
  (4 shorter events, 0.0 us)
Async XLA Ops:
  0.0 1.5 %collective-permute-start = (bf16[2,8,128]{2,1,0:T(8,128)(2,1)}, bf16[2,8,128]{2,1,0:T(8,128)(2,1)S(1)}, u32[]{:S(2)}, u32[]{:S(2)}) collective-permute-start(bf16[2,8,128]{2,1,0:T(8,128)(2,1)} %pair_ref.1), channel_id=1, source_target_pairs={{0,1},{1,0},{2,3},{3,2},{4,5},{5,4},{6,7},{7,6},{8,9},{9,8},{10,11... | collective-permute-start | bytes 12296 | tf_op jit(solution)/shard_map/ppermute | solution.py:244
  0.5 0.7 %copy-start.7 = (bf16[2,8,128]{2,1,0:T(8,128)(2,1)S(1)}, bf16[2,8,128]{2,1,0:T(8,128)(2,1)}, u32[]{:S(2)}) copy-start(bf16[2,8,128]{2,1,0:T(8,128)(2,1)} %pair_ref.1) | copy-start | bytes 12292
  1.5 0.7 %collective-permute-start.1 = (bf16[2,2,8,128]{3,2,1,0:T(8,128)(2,1)S(1)}, bf16[2,2,8,128]{3,2,1,0:T(8,128)(2,1)S(1)}, u32[]{:S(2)}, u32[]{:S(2)}) collective-permute-start(bf16[2,2,8,128]{3,2,1,0:T(8,128)(2,1)S(1)} %bitcast_dynamic-update-slice_fusion), channel_id=1, source_target_pairs={{0,0},{1,3},{2,2},{3,1},{4,4},{5,7},{6,6},{7,5},{8,8},{9,11},{10,1... | collective-permute-start | bytes 24584 | tf_op jit(solution)/shard_map/ppermute | solution.py:244
  2.2 1.5 %copy-start.9 = (bf16[128,128]{1,0:T(8,128)(2,1)S(1)}, bf16[128,128]{1,0:T(8,128)(2,1)}, u32[]{:S(2)}) copy-start(bf16[128,128]{1,0:T(8,128)(2,1)} %table_ref.1) | copy-start | bytes 98308
  2.2 0.7 %collective-permute-start.2 = (bf16[4,2,8,128]{3,2,1,0:T(8,128)(2,1)S(1)}, bf16[4,2,8,128]{3,2,1,0:T(8,128)(2,1)S(1)}, u32[]{:S(2)}, u32[]{:S(2)}) collective-permute-start(bf16[4,2,8,128]{3,2,1,0:T(8,128)(2,1)S(1)} %pad_maximum_fusion.1), channel_id=1, source_target_pairs={{0,0},{1,5},{2,2},{3,7},{4,4},{5,1},{6,6},{7,3},{8,8},{9,13},{10,1... | collective-permute-start | bytes 49160 | tf_op jit(solution)/shard_map/ppermute | solution.py:244
  2.9 14.9 %collective-permute-start.3 = (bf16[8,2,8,128]{3,2,1,0:T(8,128)(2,1)S(1)}, bf16[8,2,8,128]{3,2,1,0:T(8,128)(2,1)S(1)}, u32[]{:S(2)}, u32[]{:S(2)}) collective-permute-start(bf16[8,2,8,128]{3,2,1,0:T(8,128)(2,1)S(1)} %pad_maximum_fusion.held_ref), channel_id=1, source_target_pairs={{0,0},{1,9},{2,2},{3,11},{4,4},{5,13},{6,6},{7,15},{8,8},{9,1},{10... | collective-permute-start | bytes 98312 | tf_op jit(solution)/shard_map/ppermute | solution.py:244
  3.6 0.7 %copy-start.11 = (s32[16]{0:T(128)S(1)}, s32[16]{0:T(128)}, u32[]{:S(2)}) copy-start(s32[16]{0:T(128)} %pos_ref.1) | copy-start | bytes 196
  3.6 0.7 %copy-start.12 = (f32[128]{0:T(128)S(1)}, f32[128]{0:T(128)}, u32[]{:S(2)}) copy-start(f32[128]{0:T(128)} %param.21) | copy-start | bytes 1540
  3.6 0.7 %copy-start.13 = (f32[128]{0:T(128)S(1)}, f32[128]{0:T(128)}, u32[]{:S(2)}) copy-start(f32[128]{0:T(128)} %param.25) | copy-start | bytes 1540
  3.6 0.7 %copy-start.14 = (f32[128]{0:T(128)S(1)}, f32[128]{0:T(128)}, u32[]{:S(2)}) copy-start(f32[128]{0:T(128)} %param.27) | copy-start | bytes 1540
  3.6 0.7 %copy-start.8 = (s32[16]{0:T(128)S(1)}, s32[16]{0:T(128)}, u32[]{:S(2)}) copy-start(s32[16]{0:T(128)} %mask_ref.3) | copy-start | bytes 196
  3.6 0.7 %copy-start.10 = (bf16[128,4]{0,1:T(4,128)(2,1)S(1)}, bf16[128,4]{0,1:T(4,128)(2,1)}, u32[]{:S(2)}) copy-start(bf16[128,4]{0,1:T(4,128)(2,1)} %param.30) | copy-start | bytes 3076
  4.3 14.7 %copy-start = (bf16[128,384]{1,0:T(8,128)(2,1)S(1)}, bf16[128,384]{1,0:T(8,128)(2,1)}, u32[]{:S(2)}) copy-start(bf16[128,384]{1,0:T(8,128)(2,1)} %qkv_ref.1) | copy-start | bytes 294916
  4.3 14.7 %copy-start.1 = (bf16[128,256]{1,0:T(8,128)(2,1)S(1)}, bf16[128,256]{1,0:T(8,128)(2,1)}, u32[]{:S(2)}) copy-start(bf16[128,256]{1,0:T(8,128)(2,1)} %in_weight_ref.1) | copy-start | bytes 196612
  4.3 14.7 %copy-start.2 = (bf16[128,256]{1,0:T(8,128)(2,1)S(1)}, bf16[128,256]{1,0:T(8,128)(2,1)}, u32[]{:S(2)}) copy-start(bf16[128,256]{1,0:T(8,128)(2,1)} %in_gate_ref.1) | copy-start | bytes 196612
  4.3 14.7 %copy-start.3 = (bf16[128,128]{1,0:T(8,128)(2,1)S(1)}, bf16[128,128]{1,0:T(8,128)(2,1)}, u32[]{:S(2)}) copy-start(bf16[128,128]{1,0:T(8,128)(2,1)} %out_gate_ref.1) | copy-start | bytes 98308
  4.3 14.7 %copy-start.4 = (bf16[128,128]{1,0:T(8,128)(2,1)S(1)}, bf16[128,128]{1,0:T(8,128)(2,1)}, u32[]{:S(2)}) copy-start(bf16[128,128]{1,0:T(8,128)(2,1)} %out_weight_ref.1) | copy-start | bytes 98308
  4.3 14.7 %copy-start.5 = (bf16[128,128]{1,0:T(8,128)(2,1)S(1)}, bf16[128,128]{1,0:T(8,128)(2,1)}, u32[]{:S(2)}) copy-start(bf16[128,128]{1,0:T(8,128)(2,1)} %att_gate_ref.1) | copy-start | bytes 98308
  4.4 14.7 %copy-start.6 = (bf16[128,128]{1,0:T(8,128)(2,1)S(1)}, bf16[128,128]{1,0:T(8,128)(2,1)}, u32[]{:S(2)}) copy-start(bf16[128,128]{1,0:T(8,128)(2,1)} %att_out_ref.1) | copy-start | bytes 98308
  5.1 13.6 %collective-permute-start.4 = (bf16[8,2,8,128]{3,2,1,0:T(8,128)(2,1)S(1)}, bf16[8,2,8,128]{3,2,1,0:T(8,128)(2,1)S(1)}, u32[]{:S(2)}, u32[]{:S(2)}) collective-permute-start(bf16[8,2,8,128]{3,2,1,0:T(8,128)(2,1)S(1)} %pad_maximum_fusion.held_ref), channel_id=1, source_target_pairs={{0,1},{1,0},{2,3},{3,2},{4,5},{5,4},{6,7},{7,6},{8,9},{9,8},{10,11... | collective-permute-start | bytes 98312 | tf_op jit(solution)/shard_map/ppermute | solution.py:244
  17.8 1.2 %collective-permute-start.5 = (bf16[8,2,8,128]{3,2,1,0:T(8,128)(2,1)S(1)}, bf16[8,2,8,128]{3,2,1,0:T(8,128)(2,1)S(1)}, u32[]{:S(2)}, u32[]{:S(2)}) collective-permute-start(bf16[8,2,8,128]{3,2,1,0:T(8,128)(2,1)S(1)} %collective-permute-done.3.last_ref), channel_id=1, source_target_pairs={{0,1},{1,0},{2,3},{3,2},{4,5},{5,4},{6,7},{7,6},{8,9},{9,8},{10,11... | collective-permute-start | bytes 98312 | tf_op jit(solution)/shard_map/ppermute | solution.py:244

commit v7 on v6

--- a/solution.py
+++ b/solution.py
@@ -84,10 +84,9 @@
 def whole_pair_kernel(
     row_dim,
     heads,
+    order,
     held_ref,
-    last_ref,
-    held_sent_ref,
-    last_sent_ref,
+    other_ref,
     mask_ref,
     rel_ref,
     pair_mask_ref,
@@ -115,15 +114,14 @@
     col_first = pl.multiple_of(lax.axis_index("col") * cols, cols)
     f32, bf16 = jnp.float32, jnp.bfloat16
 
-    is_odd = lax.axis_index("col") == 1
-    odd = lax.axis_index("row") * 2 + 1
-    for m in range(2 * row_dim):
-        here, sent = ((held_ref, held_sent_ref), (last_ref, last_sent_ref))[m // row_dim]
-        owner = odd ^ m
-        block = jnp.where(is_odd, here[m % row_dim].astype(f32), sent[m % row_dim].astype(f32))
-        for r in range(rows):
-            first = (owner // 2 * rows + r) * tokens + owner % 2 * cols
-            base_ref[pl.ds(pl.multiple_of(first, cols), cols), :] = block[r]
+    me = lax.axis_index("row") * 2 + lax.axis_index("col")
+    for ref, flip in ((held_ref, 0), (other_ref, 1)):
+        for at, place in enumerate(order):
+            owner = me ^ (place ^ flip)
+            block = ref[at].astype(f32)
+            for r in range(rows):
+                first = (owner // 2 * rows + r) * tokens + owner % 2 * cols
+                base_ref[pl.ds(pl.multiple_of(first, cols), cols), :] = block[r]
 
     base = base_ref[...] + rel_ref[...]
     base_ref[...] = base
@@ -236,30 +234,25 @@
     vmem = pl.BlockSpec(memory_space=pltpu.VMEM)
     smem = pl.BlockSpec(memory_space=pltpu.SMEM)
     params = pltpu.CompilerParams(vmem_limit_bytes=16 * 1024 * 1024)
-
     tokens, heads = row_dim * rows, att_bias.shape[1]
 
+    blocks = 2 * row_dim
+
     def move(values, step):
-        pairs = [(device, device ^ step if step == 1 or device % 2 else device) for device in range(blocks)]
-        return lax.ppermute(values, ("row", "col"), pairs)
-
-    blocks = 2 * row_dim
-    chip = pl.pallas_call(
+        return lax.ppermute(values, ("row", "col"), [(device, device ^ step) for device in range(blocks)])
+
+    held = pl.pallas_call(
         own_kernel,
         out_shape=jax.ShapeDtypeStruct((2,) + pair_in.shape, pair_in.dtype),
         in_specs=[vmem],
         out_specs=vmem,
         compiler_params=params,
     )(pair_in)
-    held = chip.at[1].set(move(pair_in, 1))
-    step = 2
-    while True:
-        last = move(held, step)
-        step *= 2
-        if step == blocks:
-            break
-        held = jnp.concatenate([held, last], axis=0)
-    held_sent = move(held, 1)
+    held, order = held.at[1].set(move(pair_in, 3)), (0, 3)
+    while len(order) < row_dim:
+        step = 2 * len(order) + 1
+        held = jnp.concatenate([held, move(held, step)], axis=0)
+        order += tuple(place ^ step for place in order)
 
     wide_out = jax.ShapeDtypeStruct((tokens * tokens, width), jnp.float32)
     staged = pl.pallas_call(
@@ -283,16 +276,16 @@
         att_norm.reshape(1, width),
         att_bias.T,
     )
-    last, *staged = lax.optimization_barrier((last, *staged))
-    gathered = (held, last, held_sent, move(last, 1))
+    held, *staged = lax.optimization_barrier((held, *staged))
+    gathered = (held, move(held, 1))
 
     weights = (tri_in_weight, tri_in_gate, tri_out_gate, tri_out_weight, att_qkv, att_gate, att_out)
     wide = pltpu.VMEM((tokens * tokens, width), jnp.float32)
     column = pltpu.VMEM((tokens * cols, width), jnp.float32)
     return pl.pallas_call(
-        functools.partial(whole_pair_kernel, row_dim, heads),
+        functools.partial(whole_pair_kernel, row_dim, heads, order),
         out_shape=jax.ShapeDtypeStruct(pair_in.shape, pair_in.dtype),
-        in_specs=[vmem] * 4 + [smem] + [vmem] * (4 + len(weights)),
+        in_specs=[vmem] * 2 + [smem] + [vmem] * (4 + len(weights)),
         out_specs=vmem,
         scratch_shapes=[wide] * 4 + [column] * 2,
         compiler_params=params,

time: 22.1 us -> 16 us (0.72)
  starting transfers between devices: 15.2 us -> 7.63 us
  waiting for transfers between devices: 1.47 us -> 3.04 us
    ppermute x6 -> x4, starting transfers between devices: 15.2 us -> 7.63 us  [move(): lax.ppermute(values, ('row', 'col'), [(device, device ^ step) for device...]
    ppermute x6 -> x4, waiting for transfers between devices: 1.47 us -> 3.04 us  [move(): lax.ppermute(values, ('row', 'col'), [(device, device ^ step) for device...]
  transfers between devices with their start and end apart: 6 -> 4, of which waited for: 3 -> 3; matrix products, arithmetic and copies ran while one was open for 0% -> 0% of each run, Pallas kernels for 3% -> 5%
where the time goes in v7:
time: 16 us; the launch traced here: 15.8 us
  starting transfers between devices  7.63 us (48%)
  Pallas kernels  3.54 us (22%)
  waiting for transfers between devices  3.04 us (19%)
  local copies, waits for them, and re-layouts  1.49 us (9%)
    ppermute x4, starting transfers between devices, move(): lax.ppermute(values, ('row', 'col'), [(device, device ^ step) for device...  7.63 us
    ppermute x4, waiting for transfers between devices, move(): lax.ppermute(values, ('row', 'col'), [(device, device ^ step) for device...  3.04 us
    pallas_call x1, Pallas kernels, whole_pair_on_device(): pl.pallas_call(functools.partial(whole_pair_kernel, row_dim, heads, order...  2.82 us
    unnamed x30, local copies, waits for them, and re-layouts  1.48 us
    pallas_call x1, Pallas kernels, whole_pair_on_device(): pl.pallas_call(functools.partial(stage_kernel, cols), out_shape=[wide_out...  0.72 us
  transfers between devices with their start and end apart: 4, of which 3 were waited for; matrix products, arithmetic and copies ran while one was open for 0% of the time, Pallas kernels for 5%

profile of v7, /device:TPU:0, one launch (start us, length us, event | category | flops | bytes accessed | tf_op | source)
XLA Modules:
  0.0 15.8 jit_solution(14043798986983058779)
XLA Ops:
  0.0 2.4 %collective-permute-start = (bf16[2,8,128]{2,1,0:T(8,128)(2,1)}, bf16[2,8,128]{2,1,0:T(8,128)(2,1)S(1)}, u32[]{:S(2)}, u32[]{:S(2)}) collective-permute-start(bf16[2,8,128]{2,1,0:T(8,128)(2,1)} %pair_ref.1), channel_id=1, source_target_pairs={{0,3},{1,2},{2,1},{3,0},{4,7},{5,6},{6,5},{7,4},{8,11},{9,10},{10,... | collective-permute-start | bytes 12296 | tf_op jit(solution)/shard_map/ppermute | solution.py:242
  2.4 0.0 copy-start.7
  2.4 0.7 %copy-done.7 = bf16[2,8,128]{2,1,0:T(8,128)(2,1)S(1)} copy-done((bf16[2,8,128]{2,1,0:T(8,128)(2,1)S(1)}, bf16[2,8,128]{2,1,0:T(8,128)(2,1)}, u32[]{:S(2)}) %copy-start.7) | copy-done | bytes 4120
  3.1 0.0 copy-start.9
  3.1 0.8 %collective-permute-done = bf16[2,8,128]{2,1,0:T(8,128)(2,1)S(1)} collective-permute-done((bf16[2,8,128]{2,1,0:T(8,128)(2,1)}, bf16[2,8,128]{2,1,0:T(8,128)(2,1)S(1)}, u32[]{:S(2)}, u32[]{:S(2)}) %collective-permute-start) | collective-permute-done | bytes 4128 | tf_op jit(solution)/shard_map/ppermute | solution.py:242
  3.9 2.1 %collective-permute-start.1 = (bf16[2,2,8,128]{3,2,1,0:T(8,128)(2,1)S(1)}, bf16[2,2,8,128]{3,2,1,0:T(8,128)(2,1)S(1)}, u32[]{:S(2)}, u32[]{:S(2)}) collective-permute-start(bf16[2,2,8,128]{3,2,1,0:T(8,128)(2,1)S(1)} %bitcast_dynamic-update-slice_fusion), channel_id=1, source_target_pairs={{0,5},{1,4},{2,7},{3,6},{4,1},{5,0},{6,3},{7,2},{8,13},{9,12},{10,... | collective-permute-start | bytes 24584 | tf_op jit(solution)/shard_map/ppermute | solution.py:242
  6.0 1.4 %collective-permute-done.1 = bf16[2,2,8,128]{3,2,1,0:T(8,128)(2,1)S(1)} collective-permute-done((bf16[2,2,8,128]{3,2,1,0:T(8,128)(2,1)S(1)}, bf16[2,2,8,128]{3,2,1,0:T(8,128)(2,1)S(1)}, u32[]{:S(2)}, u32[]{:S(2)}) %collective-permute-start.1) | collective-permute-done | bytes 8224 | tf_op jit(solution)/shard_map/ppermute | solution.py:242
  7.4 2.7 %collective-permute-start.2 = (bf16[4,2,8,128]{3,2,1,0:T(8,128)(2,1)S(1)}, bf16[4,2,8,128]{3,2,1,0:T(8,128)(2,1)S(1)}, u32[]{:S(2)}, u32[]{:S(2)}) collective-permute-start(bf16[4,2,8,128]{3,2,1,0:T(8,128)(2,1)S(1)} %pad_maximum_fusion.1), channel_id=1, source_target_pairs={{0,9},{1,8},{2,11},{3,10},{4,13},{5,12},{6,15},{7,14},{8,1},{9,0},... | collective-permute-start | bytes 49160 | tf_op jit(solution)/shard_map/ppermute | solution.py:242
  10.1 0.0 copy-start.11
  10.1 0.0 copy-start.12
  10.1 0.0 copy-start.13
  10.1 0.0 copy-start.14
  10.1 0.0 copy-start.8
  10.1 0.0 copy-start.10
  10.1 0.0 copy-done.9
  10.1 0.6 %copy-done.11 = s32[16]{0:T(128)S(1)} copy-done((s32[16]{0:T(128)S(1)}, s32[16]{0:T(128)}, u32[]{:S(2)}) %copy-start.11) | copy-done | bytes 88
  10.7 0.0 copy-done.12
  10.8 0.0 copy-done.13
  10.8 0.0 copy-done.14
  10.8 0.0 copy-done.8
  10.8 0.0 copy-done.10
  10.8 0.0 copy-start
  10.8 0.0 copy-start.2
  10.9 0.0 copy-start.3
  10.9 0.0 copy-start.4
  10.9 0.0 copy-start.5
  10.9 0.0 copy-start.6
  10.9 0.7 %shard_map.146 = (f32[256,128]{1,0:T(8,128)S(1)}, f32[256,128]{1,0:T(8,128)S(1)}, f32[3,128]{1,0:T(4,128)S(1)}, bf16[4,128]{1,0:T(4,128)(2,1)S(1)}) custom-call(s32[16]{0:T(128)S(1)} %copy-done.8, s32[16]{0:T(128)S(1)} %copy-done.11, bf16[128,128]{1,0:T(8,128)(2,1)S(1)} %copy-done.9, f32[1,128]{1,0:T(1,128)S(1)} %bitcast.7, f32[1,128]{1,0:T(1,128)S(1)} %bitcast.8, ...), custom_call_target="tpu_custom_call" | custom-call | flops 1000000000 | bytes 1048576 | tf_op jit(solution)/shard_map/pallas_call | solution.py:258
  11.6 0.0 copy-start.1
  11.6 0.0 collective-permute-done.2
  11.6 0.5 %collective-permute-start.3 = (bf16[8,2,8,128]{3,2,1,0:T(8,128)(2,1)S(1)}, bf16[8,2,8,128]{3,2,1,0:T(8,128)(2,1)S(1)}, u32[]{:S(2)}, u32[]{:S(2)}) collective-permute-start(bf16[8,2,8,128]{3,2,1,0:T(8,128)(2,1)S(1)} %pad_maximum_fusion.held_ref), channel_id=1, source_target_pairs={{0,1},{1,0},{2,3},{3,2},{4,5},{5,4},{6,7},{7,6},{8,9},{9,8},{10,11... | collective-permute-start | bytes 98312 | tf_op jit(solution)/shard_map/ppermute | solution.py:242
  12.1 0.9 %collective-permute-done.3.other_ref = bf16[8,2,8,128]{3,2,1,0:T(8,128)(2,1)S(1)} collective-permute-done((bf16[8,2,8,128]{3,2,1,0:T(8,128)(2,1)S(1)}, bf16[8,2,8,128]{3,2,1,0:T(8,128)(2,1)S(1)}, u32[]{:S(2)}, u32[]{:S(2)}) %collective-permute-start.3) | collective-permute-done | bytes 32800 | tf_op jit(solution)/shard_map/ppermute | solution.py:242
  13.0 0.0 copy-done
  13.0 0.0 copy-done.2
  13.0 0.0 copy-done.3
  13.0 0.0 copy-done.4
  13.0 0.0 copy-done.5
  13.0 0.0 copy-done.6
  13.0 0.0 copy-done.1
  13.0 2.8 %shard_map.147 = bf16[2,8,128]{2,1,0:T(8,128)(2,1)} custom-call(bf16[8,2,8,128]{3,2,1,0:T(8,128)(2,1)S(1)} %pad_maximum_fusion.held_ref, bf16[8,2,8,128]{3,2,1,0:T(8,128)(2,1)S(1)} %collective-permute-done.3.other_ref, s32[16]{0:T(128)S(1)} %copy-done.8, f32[256,128]{1,0:T(8,128)S(1)} %get-tuple-element.31.rel_ref, ...), custom_call_target="tpu_custom_call" | custom-call | tf_op jit(solution)/shard_map/pallas_call | solution.py:285
  (4 shorter events, 0.0 us)
Async XLA Ops:
  0.0 3.9 %collective-permute-start = (bf16[2,8,128]{2,1,0:T(8,128)(2,1)}, bf16[2,8,128]{2,1,0:T(8,128)(2,1)S(1)}, u32[]{:S(2)}, u32[]{:S(2)}) collective-permute-start(bf16[2,8,128]{2,1,0:T(8,128)(2,1)} %pair_ref.1), channel_id=1, source_target_pairs={{0,3},{1,2},{2,1},{3,0},{4,7},{5,6},{6,5},{7,4},{8,11},{9,10},{10,... | collective-permute-start | bytes 12296 | tf_op jit(solution)/shard_map/ppermute | solution.py:242
  2.4 0.7 %copy-start.7 = (bf16[2,8,128]{2,1,0:T(8,128)(2,1)S(1)}, bf16[2,8,128]{2,1,0:T(8,128)(2,1)}, u32[]{:S(2)}) copy-start(bf16[2,8,128]{2,1,0:T(8,128)(2,1)} %pair_ref.1) | copy-start | bytes 12292
  3.1 7.0 %copy-start.9 = (bf16[128,128]{1,0:T(8,128)(2,1)S(1)}, bf16[128,128]{1,0:T(8,128)(2,1)}, u32[]{:S(2)}) copy-start(bf16[128,128]{1,0:T(8,128)(2,1)} %table_ref.1) | copy-start | bytes 98308
  3.9 3.4 %collective-permute-start.1 = (bf16[2,2,8,128]{3,2,1,0:T(8,128)(2,1)S(1)}, bf16[2,2,8,128]{3,2,1,0:T(8,128)(2,1)S(1)}, u32[]{:S(2)}, u32[]{:S(2)}) collective-permute-start(bf16[2,2,8,128]{3,2,1,0:T(8,128)(2,1)S(1)} %bitcast_dynamic-update-slice_fusion), channel_id=1, source_target_pairs={{0,5},{1,4},{2,7},{3,6},{4,1},{5,0},{6,3},{7,2},{8,13},{9,12},{10,... | collective-permute-start | bytes 24584 | tf_op jit(solution)/shard_map/ppermute | solution.py:242
  7.4 4.2 %collective-permute-start.2 = (bf16[4,2,8,128]{3,2,1,0:T(8,128)(2,1)S(1)}, bf16[4,2,8,128]{3,2,1,0:T(8,128)(2,1)S(1)}, u32[]{:S(2)}, u32[]{:S(2)}) collective-permute-start(bf16[4,2,8,128]{3,2,1,0:T(8,128)(2,1)S(1)} %pad_maximum_fusion.1), channel_id=1, source_target_pairs={{0,9},{1,8},{2,11},{3,10},{4,13},{5,12},{6,15},{7,14},{8,1},{9,0},... | collective-permute-start | bytes 49160 | tf_op jit(solution)/shard_map/ppermute | solution.py:242
  10.1 0.7 %copy-start.11 = (s32[16]{0:T(128)S(1)}, s32[16]{0:T(128)}, u32[]{:S(2)}) copy-start(s32[16]{0:T(128)} %pos_ref.1) | copy-start | bytes 196
  10.1 0.7 %copy-start.12 = (f32[128]{0:T(128)S(1)}, f32[128]{0:T(128)}, u32[]{:S(2)}) copy-start(f32[128]{0:T(128)} %param.21) | copy-start | bytes 1540
  10.1 0.7 %copy-start.13 = (f32[128]{0:T(128)S(1)}, f32[128]{0:T(128)}, u32[]{:S(2)}) copy-start(f32[128]{0:T(128)} %param.25) | copy-start | bytes 1540
  10.1 0.7 %copy-start.14 = (f32[128]{0:T(128)S(1)}, f32[128]{0:T(128)}, u32[]{:S(2)}) copy-start(f32[128]{0:T(128)} %param.27) | copy-start | bytes 1540
  10.1 0.7 %copy-start.8 = (s32[16]{0:T(128)S(1)}, s32[16]{0:T(128)}, u32[]{:S(2)}) copy-start(s32[16]{0:T(128)} %mask_ref.3) | copy-start | bytes 196
  10.1 0.7 %copy-start.10 = (bf16[128,4]{0,1:T(4,128)(2,1)S(1)}, bf16[128,4]{0,1:T(4,128)(2,1)}, u32[]{:S(2)}) copy-start(bf16[128,4]{0,1:T(4,128)(2,1)} %param.30) | copy-start | bytes 3076
  10.8 2.1 %copy-start = (bf16[128,384]{1,0:T(8,128)(2,1)S(1)}, bf16[128,384]{1,0:T(8,128)(2,1)}, u32[]{:S(2)}) copy-start(bf16[128,384]{1,0:T(8,128)(2,1)} %qkv_ref.1) | copy-start | bytes 294916
  10.8 2.1 %copy-start.2 = (bf16[128,256]{1,0:T(8,128)(2,1)S(1)}, bf16[128,256]{1,0:T(8,128)(2,1)}, u32[]{:S(2)}) copy-start(bf16[128,256]{1,0:T(8,128)(2,1)} %in_gate_ref.1) | copy-start | bytes 196612
  10.9 2.1 %copy-start.3 = (bf16[128,128]{1,0:T(8,128)(2,1)S(1)}, bf16[128,128]{1,0:T(8,128)(2,1)}, u32[]{:S(2)}) copy-start(bf16[128,128]{1,0:T(8,128)(2,1)} %out_gate_ref.1) | copy-start | bytes 98308
  10.9 2.1 %copy-start.4 = (bf16[128,128]{1,0:T(8,128)(2,1)S(1)}, bf16[128,128]{1,0:T(8,128)(2,1)}, u32[]{:S(2)}) copy-start(bf16[128,128]{1,0:T(8,128)(2,1)} %out_weight_ref.1) | copy-start | bytes 98308
  10.9 2.1 %copy-start.5 = (bf16[128,128]{1,0:T(8,128)(2,1)S(1)}, bf16[128,128]{1,0:T(8,128)(2,1)}, u32[]{:S(2)}) copy-start(bf16[128,128]{1,0:T(8,128)(2,1)} %att_gate_ref.1) | copy-start | bytes 98308
  10.9 2.1 %copy-start.6 = (bf16[128,128]{1,0:T(8,128)(2,1)S(1)}, bf16[128,128]{1,0:T(8,128)(2,1)}, u32[]{:S(2)}) copy-start(bf16[128,128]{1,0:T(8,128)(2,1)} %att_out_ref.1) | copy-start | bytes 98308
  11.6 1.4 %copy-start.1 = (bf16[128,256]{1,0:T(8,128)(2,1)S(1)}, bf16[128,256]{1,0:T(8,128)(2,1)}, u32[]{:S(2)}) copy-start(bf16[128,256]{1,0:T(8,128)(2,1)} %in_weight_ref.1) | copy-start | bytes 196612
  11.6 1.3 %collective-permute-start.3 = (bf16[8,2,8,128]{3,2,1,0:T(8,128)(2,1)S(1)}, bf16[8,2,8,128]{3,2,1,0:T(8,128)(2,1)S(1)}, u32[]{:S(2)}, u32[]{:S(2)}) collective-permute-start(bf16[8,2,8,128]{3,2,1,0:T(8,128)(2,1)S(1)} %pad_maximum_fusion.held_ref), channel_id=1, source_target_pairs={{0,1},{1,0},{2,3},{3,2},{4,5},{5,4},{6,7},{7,6},{8,9},{9,8},{10,11... | collective-permute-start | bytes 98312 | tf_op jit(solution)/shard_map/ppermute | solution.py:242

commit v8 on v7

--- a/solution.py
+++ b/solution.py
@@ -37,10 +37,6 @@
 
 def round_bf16(values):
     return values.astype(jnp.bfloat16).astype(jnp.float32)
-
-
-def own_kernel(pair_ref, chip_ref):
-    chip_ref[0] = pair_ref[...]
 
 
 def stage_kernel(
@@ -114,13 +110,13 @@
     col_first = pl.multiple_of(lax.axis_index("col") * cols, cols)
     f32, bf16 = jnp.float32, jnp.bfloat16
 
-    me = lax.axis_index("row") * 2 + lax.axis_index("col")
-    for ref, flip in ((held_ref, 0), (other_ref, 1)):
-        for at, place in enumerate(order):
-            owner = me ^ (place ^ flip)
+    row, col = lax.axis_index("row"), lax.axis_index("col")
+    for ref, other in ((held_ref, 0), (other_ref, 1)):
+        for at, (back, flip) in enumerate(order):
+            owner = lax.rem(row + row_dim - back, row_dim)
             block = ref[at].astype(f32)
             for r in range(rows):
-                first = (owner // 2 * rows + r) * tokens + owner % 2 * cols
+                first = (owner * rows + r) * tokens + (col ^ flip ^ other) * cols
                 base_ref[pl.ds(pl.multiple_of(first, cols), cols), :] = block[r]
 
     base = base_ref[...] + rel_ref[...]
@@ -236,23 +232,25 @@
     params = pltpu.CompilerParams(vmem_limit_bytes=16 * 1024 * 1024)
     tokens, heads = row_dim * rows, att_bias.shape[1]
 
-    blocks = 2 * row_dim
-
-    def move(values, step):
-        return lax.ppermute(values, ("row", "col"), [(device, device ^ step) for device in range(blocks)])
-
-    held = pl.pallas_call(
-        own_kernel,
-        out_shape=jax.ShapeDtypeStruct((2,) + pair_in.shape, pair_in.dtype),
-        in_specs=[vmem],
-        out_specs=vmem,
-        compiler_params=params,
-    )(pair_in)
-    held, order = held.at[1].set(move(pair_in, 3)), (0, 3)
-    while len(order) < row_dim:
-        step = 2 * len(order) + 1
-        held = jnp.concatenate([held, move(held, step)], axis=0)
-        order += tuple(place ^ step for place in order)
+    def shift(values, back):
+        pairs = [
+            (row * 2 + core, (row + back) % row_dim * 2 + 1 - core) for row in range(row_dim) for core in range(2)
+        ]
+        return lax.ppermute(values, ("row", "col"), pairs)
+
+    pieces = [pair_in[None]]
+    places = [((0, 0),)]
+    while sum(len(piece) for piece in places) < row_dim:
+        ready = max(1, len(pieces) - 1)
+        known = tuple(place for piece in places for place in piece)
+        back = len(known)
+        wanted = min(sum(len(piece) for piece in places[:ready]), row_dim - back)
+        sent = jnp.concatenate(pieces[:ready], axis=0)[:wanted]
+        pieces.append(shift(sent, back))
+        places.append(tuple((back + rows_back, 1 - flip) for rows_back, flip in known[:wanted]))
+    pieces[-2], positions = lax.optimization_barrier((pieces[-2], positions))
+    held = jnp.concatenate(pieces, axis=0)
+    order = tuple(place for piece in places for place in piece)
 
     wide_out = jax.ShapeDtypeStruct((tokens * tokens, width), jnp.float32)
     staged = pl.pallas_call(
@@ -277,7 +275,8 @@
         att_bias.T,
     )
     held, *staged = lax.optimization_barrier((held, *staged))
-    gathered = (held, move(held, 1))
+    swap = [(device, device ^ 1) for device in range(2 * row_dim)]
+    gathered = (held, lax.ppermute(held, ("row", "col"), swap))
 
     weights = (tri_in_weight, tri_in_gate, tri_out_gate, tri_out_weight, att_qkv, att_gate, att_out)
     wide = pltpu.VMEM((tokens * tokens, width), jnp.float32)

time: 16 us -> 19.5 us (1.22)
  waiting for transfers between devices: 3.04 us -> 5.57 us
  starting transfers between devices: 7.63 us -> 8.61 us
    ppermute x4 -> x5, waiting for transfers between devices: 3.04 us -> 5.57 us  [the longest x4 4.71 us: shift(): return lax.ppermute(values, ('row', 'col'), pairs)]
    ppermute x4 -> x5, starting transfers between devices: 7.63 us -> 8.61 us  [the longest x4 7.88 us: shift(): return lax.ppermute(values, ('row', 'col'), pairs)]
    unnamed x30 -> x34, local copies, waits for them, and re-layouts: 1.48 us -> 1.5 us
  transfers between devices with their start and end apart: 4 -> 5, of which waited for: 3 -> 3; matrix products, arithmetic and copies ran while one was open for 0% -> 4% of each run, Pallas kernels for 5% -> 4%
where the time goes in v8:
time: 19.5 us; the launch traced here: 19.3 us
  starting transfers between devices  8.61 us (44%)
  waiting for transfers between devices  5.57 us (29%)
  Pallas kernels  3.47 us (18%)
  local copies, waits for them, and re-layouts  1.51 us (8%)
    ppermute x4, starting transfers between devices, shift(): return lax.ppermute(values, ('row', 'col'), pairs)  7.88 us
    ppermute x4, waiting for transfers between devices, shift(): return lax.ppermute(values, ('row', 'col'), pairs)  4.71 us
    pallas_call x1, Pallas kernels, whole_pair_on_device(): pl.pallas_call(functools.partial(whole_pair_kernel, row_dim, heads, order...  2.75 us
    unnamed x34, local copies, waits for them, and re-layouts  1.5 us
    ppermute x1, waiting for transfers between devices, whole_pair_on_device(): gathered = (held, lax.ppermute(held, ('row', 'col'), swap))  0.86 us
    ppermute x1, starting transfers between devices, whole_pair_on_device(): gathered = (held, lax.ppermute(held, ('row', 'col'), swap))  0.73 us
    pallas_call x1, Pallas kernels, whole_pair_on_device(): pl.pallas_call(functools.partial(stage_kernel, cols), out_shape=[wide_out...  0.72 us
  transfers between devices with their start and end apart: 5, of which 3 were waited for; matrix products, arithmetic and copies ran while one was open for 4% of the time, Pallas kernels for 4%

profile of v8, /device:TPU:0, one launch (start us, length us, event | category | flops | bytes accessed | tf_op | source)
XLA Modules:
  0.0 19.3 jit_solution(8504508846134132836)
XLA Ops:
  0.0 0.0 copy-start.14
  0.0 2.5 %collective-permute-start.1 = (bf16[1,2,8,128]{3,2,1,0:T(8,128)(2,1)}, bf16[1,2,8,128]{3,2,1,0:T(8,128)(2,1)S(1)}, u32[]{:S(2)}, u32[]{:S(2)}) collective-permute-start(bf16[1,2,8,128]{3,2,1,0:T(8,128)(2,1)} %bitcast.10), channel_id=1, source_target_pairs={{0,5},{1,4},{2,7},{3,6},{4,9},{5,8},{6,11},{7,10},{8,13},{9,12},{1... | collective-permute-start | bytes 12296 | tf_op jit(solution)/shard_map/ppermute | solution.py:239
  2.5 1.8 %collective-permute-start = (bf16[1,2,8,128]{3,2,1,0:T(8,128)(2,1)}, bf16[1,2,8,128]{3,2,1,0:T(8,128)(2,1)S(1)}, u32[]{:S(2)}, u32[]{:S(2)}) collective-permute-start(bf16[1,2,8,128]{3,2,1,0:T(8,128)(2,1)} %bitcast.11), channel_id=1, source_target_pairs={{0,3},{1,2},{2,5},{3,4},{4,7},{5,6},{6,9},{7,8},{8,11},{9,10},{10,... | collective-permute-start | bytes 12296 | tf_op jit(solution)/shard_map/ppermute | solution.py:239
  4.2 0.7 %constant_dynamic-update-slice_fusion.4 = bf16[8,2,8,128]{3,2,1,0:T(8,128)(2,1)S(1)} fusion(bf16[2,8,128]{2,1,0:T(8,128)(2,1)} %param.15), kind=kLoop, calls=%fused_computation.5 | loop fusion | bytes 8192
  5.0 3.4 %collective-permute-done = bf16[1,2,8,128]{3,2,1,0:T(8,128)(2,1)S(1)} collective-permute-done((bf16[1,2,8,128]{3,2,1,0:T(8,128)(2,1)}, bf16[1,2,8,128]{3,2,1,0:T(8,128)(2,1)S(1)}, u32[]{:S(2)}, u32[]{:S(2)}) %collective-permute-start) | collective-permute-done | bytes 4128 | tf_op jit(solution)/shard_map/ppermute | solution.py:239
  8.4 0.0 copy-done.14
  8.4 0.0 copy-start.8
  8.4 0.1 collective-permute-start.2
  8.6 0.0 collective-permute-done.1
  8.6 3.5 %collective-permute-start.3 = (bf16[3,2,8,128]{3,2,1,0:T(8,128)(2,1)S(1)}, bf16[3,2,8,128]{3,2,1,0:T(8,128)(2,1)S(1)}, u32[]{:S(2)}, u32[]{:S(2)}) collective-permute-start(bf16[3,2,8,128]{3,2,1,0:T(8,128)(2,1)S(1)} %pad_maximum_fusion), channel_id=1, source_target_pairs={{0,11},{1,10},{2,13},{3,12},{4,15},{5,14},{6,1},{7,0},{8,3},{9,2},... | collective-permute-start | bytes 36872 | tf_op jit(solution)/shard_map/ppermute | solution.py:239
  12.1 1.3 %collective-permute-done.2 = bf16[2,2,8,128]{3,2,1,0:T(8,128)(2,1)S(1)} collective-permute-done((bf16[2,2,8,128]{3,2,1,0:T(8,128)(2,1)S(1)}, bf16[2,2,8,128]{3,2,1,0:T(8,128)(2,1)S(1)}, u32[]{:S(2)}, u32[]{:S(2)}) %collective-permute-start.2) | collective-permute-done | bytes 8224 | tf_op jit(solution)/shard_map/ppermute | solution.py:239
  13.4 0.0 copy-start.10
  13.4 0.0 copy-start.11
  13.4 0.0 copy-start.12
  13.4 0.0 copy-start.13
  13.4 0.0 copy-start.7
  13.4 0.0 copy-start.9
  13.4 0.0 copy-done.8
  13.4 0.6 %copy-done.10 = s32[16]{0:T(128)S(1)} copy-done((s32[16]{0:T(128)S(1)}, s32[16]{0:T(128)}, u32[]{:S(2)}) %copy-start.10) | copy-done | bytes 88
  14.0 0.0 copy-done.11
  14.0 0.0 copy-done.12
  14.1 0.0 copy-done.13
  14.1 0.0 copy-done.7
  14.1 0.0 copy-done.9
  14.1 0.0 copy-start
  14.1 0.0 copy-start.1
  14.1 0.0 copy-start.2
  14.1 0.0 copy-start.3
  14.1 0.0 copy-start.4
  14.1 0.0 copy-start.5
  14.2 0.0 copy-start.6
  14.2 0.7 %shard_map.145 = (f32[256,128]{1,0:T(8,128)S(1)}, f32[256,128]{1,0:T(8,128)S(1)}, f32[3,128]{1,0:T(4,128)S(1)}, bf16[4,128]{1,0:T(4,128)(2,1)S(1)}) custom-call(s32[16]{0:T(128)S(1)} %copy-done.7, s32[16]{0:T(128)S(1)} %copy-done.10, bf16[128,128]{1,0:T(8,128)(2,1)S(1)} %copy-done.8, f32[1,128]{1,0:T(1,128)S(1)} %bitcast.7, f32[1,128]{1,0:T(1,128)S(1)} %bitcast.8, ...), custom_call_target="tpu_custom_call" | custom-call | flops 1000000000 | bytes 1048576 | tf_op jit(solution)/shard_map/pallas_call | solution.py:256
  14.9 0.0 collective-permute-done.3
  14.9 0.7 %collective-permute-start.4 = (bf16[8,2,8,128]{3,2,1,0:T(8,128)(2,1)S(1)}, bf16[8,2,8,128]{3,2,1,0:T(8,128)(2,1)S(1)}, u32[]{:S(2)}, u32[]{:S(2)}) collective-permute-start(bf16[8,2,8,128]{3,2,1,0:T(8,128)(2,1)S(1)} %constant_dynamic-update-slice_fusion.held_ref), channel_id=1, source_target_pairs={{0,1},{1,0},{2,3},{3,2},{4,5},{5,4},{6,7},{7,6},{8,9},{9,8},{10,11... | collective-permute-start | bytes 98312 | tf_op jit(solution)/shard_map/ppermute | solution.py:279
  15.6 0.9 %collective-permute-done.4.other_ref = bf16[8,2,8,128]{3,2,1,0:T(8,128)(2,1)S(1)} collective-permute-done((bf16[8,2,8,128]{3,2,1,0:T(8,128)(2,1)S(1)}, bf16[8,2,8,128]{3,2,1,0:T(8,128)(2,1)S(1)}, u32[]{:S(2)}, u32[]{:S(2)}) %collective-permute-start.4) | collective-permute-done | bytes 32800 | tf_op jit(solution)/shard_map/ppermute | solution.py:279
  16.5 0.0 copy-done
  16.5 0.0 copy-done.1
  16.5 0.0 copy-done.2
  16.5 0.0 copy-done.3
  16.5 0.0 copy-done.4
  16.5 0.0 copy-done.5
  16.5 0.0 copy-done.6
  16.5 2.7 %shard_map.146 = bf16[2,8,128]{2,1,0:T(8,128)(2,1)} custom-call(bf16[8,2,8,128]{3,2,1,0:T(8,128)(2,1)S(1)} %constant_dynamic-update-slice_fusion.held_ref, bf16[8,2,8,128]{3,2,1,0:T(8,128)(2,1)S(1)} %collective-permute-done.4.other_ref, s32[16]{0:T(128)S(1)} %copy-done.7, f32[256,128]{1,0:T(8,128)S(1)} %get-tuple-element.23.rel_ref, ...), custom_call_target="tpu_custom_call" | custom-call | tf_op jit(solution)/shard_map/pallas_call | solution.py:284
  (6 shorter events, 0.0 us)
Async XLA Ops:
  0.0 8.4 %copy-start.14 = (bf16[2,8,128]{2,1,0:T(8,128)(2,1)S(1)}, bf16[2,8,128]{2,1,0:T(8,128)(2,1)}, u32[]{:S(2)}) copy-start(bf16[2,8,128]{2,1,0:T(8,128)(2,1)} %param.15) | copy-start | bytes 12292
  0.0 8.6 %collective-permute-start.1 = (bf16[1,2,8,128]{3,2,1,0:T(8,128)(2,1)}, bf16[1,2,8,128]{3,2,1,0:T(8,128)(2,1)S(1)}, u32[]{:S(2)}, u32[]{:S(2)}) collective-permute-start(bf16[1,2,8,128]{3,2,1,0:T(8,128)(2,1)} %bitcast.10), channel_id=1, source_target_pairs={{0,5},{1,4},{2,7},{3,6},{4,9},{5,8},{6,11},{7,10},{8,13},{9,12},{1... | collective-permute-start | bytes 12296 | tf_op jit(solution)/shard_map/ppermute | solution.py:239
  2.5 5.9 %collective-permute-start = (bf16[1,2,8,128]{3,2,1,0:T(8,128)(2,1)}, bf16[1,2,8,128]{3,2,1,0:T(8,128)(2,1)S(1)}, u32[]{:S(2)}, u32[]{:S(2)}) collective-permute-start(bf16[1,2,8,128]{3,2,1,0:T(8,128)(2,1)} %bitcast.11), channel_id=1, source_target_pairs={{0,3},{1,2},{2,5},{3,4},{4,7},{5,6},{6,9},{7,8},{8,11},{9,10},{10,... | collective-permute-start | bytes 12296 | tf_op jit(solution)/shard_map/ppermute | solution.py:239
  8.4 5.0 %copy-start.8 = (bf16[128,128]{1,0:T(8,128)(2,1)S(1)}, bf16[128,128]{1,0:T(8,128)(2,1)}, u32[]{:S(2)}) copy-start(bf16[128,128]{1,0:T(8,128)(2,1)} %table_ref.1) | copy-start | bytes 98308
  8.4 4.9 %collective-permute-start.2 = (bf16[2,2,8,128]{3,2,1,0:T(8,128)(2,1)S(1)}, bf16[2,2,8,128]{3,2,1,0:T(8,128)(2,1)S(1)}, u32[]{:S(2)}, u32[]{:S(2)}) collective-permute-start(bf16[2,2,8,128]{3,2,1,0:T(8,128)(2,1)S(1)} %pad_maximum_fusion.1), channel_id=1, source_target_pairs={{0,7},{1,6},{2,9},{3,8},{4,11},{5,10},{6,13},{7,12},{8,15},{9,14},... | collective-permute-start | bytes 24584 | tf_op jit(solution)/shard_map/ppermute | solution.py:239
  8.6 6.3 %collective-permute-start.3 = (bf16[3,2,8,128]{3,2,1,0:T(8,128)(2,1)S(1)}, bf16[3,2,8,128]{3,2,1,0:T(8,128)(2,1)S(1)}, u32[]{:S(2)}, u32[]{:S(2)}) collective-permute-start(bf16[3,2,8,128]{3,2,1,0:T(8,128)(2,1)S(1)} %pad_maximum_fusion), channel_id=1, source_target_pairs={{0,11},{1,10},{2,13},{3,12},{4,15},{5,14},{6,1},{7,0},{8,3},{9,2},... | collective-permute-start | bytes 36872 | tf_op jit(solution)/shard_map/ppermute | solution.py:239
  13.4 0.7 %copy-start.10 = (s32[16]{0:T(128)S(1)}, s32[16]{0:T(128)}, u32[]{:S(2)}) copy-start(s32[16]{0:T(128)} %pos_ref) | copy-start | bytes 196
  13.4 0.7 %copy-start.11 = (f32[128]{0:T(128)S(1)}, f32[128]{0:T(128)}, u32[]{:S(2)}) copy-start(f32[128]{0:T(128)} %param.19) | copy-start | bytes 1540
  13.4 0.7 %copy-start.12 = (f32[128]{0:T(128)S(1)}, f32[128]{0:T(128)}, u32[]{:S(2)}) copy-start(f32[128]{0:T(128)} %param.23) | copy-start | bytes 1540
  13.4 0.7 %copy-start.13 = (f32[128]{0:T(128)S(1)}, f32[128]{0:T(128)}, u32[]{:S(2)}) copy-start(f32[128]{0:T(128)} %param.25) | copy-start | bytes 1540
  13.4 0.7 %copy-start.7 = (s32[16]{0:T(128)S(1)}, s32[16]{0:T(128)}, u32[]{:S(2)}) copy-start(s32[16]{0:T(128)} %mask_ref.3) | copy-start | bytes 196
  13.4 0.7 %copy-start.9 = (bf16[128,4]{0,1:T(4,128)(2,1)S(1)}, bf16[128,4]{0,1:T(4,128)(2,1)}, u32[]{:S(2)}) copy-start(bf16[128,4]{0,1:T(4,128)(2,1)} %param.28) | copy-start | bytes 3076
  14.1 2.4 %copy-start = (bf16[128,384]{1,0:T(8,128)(2,1)S(1)}, bf16[128,384]{1,0:T(8,128)(2,1)}, u32[]{:S(2)}) copy-start(bf16[128,384]{1,0:T(8,128)(2,1)} %qkv_ref.1) | copy-start | bytes 294916
  14.1 2.4 %copy-start.1 = (bf16[128,256]{1,0:T(8,128)(2,1)S(1)}, bf16[128,256]{1,0:T(8,128)(2,1)}, u32[]{:S(2)}) copy-start(bf16[128,256]{1,0:T(8,128)(2,1)} %in_weight_ref.1) | copy-start | bytes 196612
  14.1 2.4 %copy-start.2 = (bf16[128,256]{1,0:T(8,128)(2,1)S(1)}, bf16[128,256]{1,0:T(8,128)(2,1)}, u32[]{:S(2)}) copy-start(bf16[128,256]{1,0:T(8,128)(2,1)} %in_gate_ref.1) | copy-start | bytes 196612
  14.1 2.4 %copy-start.3 = (bf16[128,128]{1,0:T(8,128)(2,1)S(1)}, bf16[128,128]{1,0:T(8,128)(2,1)}, u32[]{:S(2)}) copy-start(bf16[128,128]{1,0:T(8,128)(2,1)} %out_gate_ref.1) | copy-start | bytes 98308
  14.1 2.4 %copy-start.4 = (bf16[128,128]{1,0:T(8,128)(2,1)S(1)}, bf16[128,128]{1,0:T(8,128)(2,1)}, u32[]{:S(2)}) copy-start(bf16[128,128]{1,0:T(8,128)(2,1)} %out_weight_ref.1) | copy-start | bytes 98308
  14.1 2.4 %copy-start.5 = (bf16[128,128]{1,0:T(8,128)(2,1)S(1)}, bf16[128,128]{1,0:T(8,128)(2,1)}, u32[]{:S(2)}) copy-start(bf16[128,128]{1,0:T(8,128)(2,1)} %att_gate_ref.1) | copy-start | bytes 98308
  14.2 2.4 %copy-start.6 = (bf16[128,128]{1,0:T(8,128)(2,1)S(1)}, bf16[128,128]{1,0:T(8,128)(2,1)}, u32[]{:S(2)}) copy-start(bf16[128,128]{1,0:T(8,128)(2,1)} %att_out_ref.1) | copy-start | bytes 98308
  14.9 1.6 %collective-permute-start.4 = (bf16[8,2,8,128]{3,2,1,0:T(8,128)(2,1)S(1)}, bf16[8,2,8,128]{3,2,1,0:T(8,128)(2,1)S(1)}, u32[]{:S(2)}, u32[]{:S(2)}) collective-permute-start(bf16[8,2,8,128]{3,2,1,0:T(8,128)(2,1)S(1)} %constant_dynamic-update-slice_fusion.held_ref), channel_id=1, source_target_pairs={{0,1},{1,0},{2,3},{3,2},{4,5},{5,4},{6,7},{7,6},{8,9},{9,8},{10,11... | collective-permute-start | bytes 98312 | tf_op jit(solution)/shard_map/ppermute | solution.py:279

commit v9 on v7

--- a/solution.py
+++ b/solution.py
@@ -56,6 +56,7 @@
     pair_mask_ref,
     gains_ref,
     bias_ref,
+    key_bias_ref,
 ):
     gains_ref[0:1] = norm_in_ref[...]
     gains_ref[1:2] = norm_out_ref[...]
@@ -77,6 +78,13 @@
             bucket = jnp.clip(pos_ref[i] - pos_vec, -(bins // 2), bins // 2 - 1) + bins // 2
             hot[at] = (bucket == lane).astype(jnp.float32)
             pair_mask_ref[at * cols : (at + 1) * cols, :] = (mask_vec * mask_ref[i]).astype(jnp.float32)
+    key_sub = lax.broadcasted_iota(jnp.int32, key_bias_ref.shape, 0)
+    key_lane = lax.broadcasted_iota(jnp.int32, key_bias_ref.shape, 1)
+    key_mask = jnp.zeros(key_bias_ref.shape, jnp.int32)
+    for k in range(tokens):
+        key_mask = jnp.where(key_lane // cols == k, mask_ref[k], key_mask)
+    key_bias = (key_mask.astype(jnp.float32) - 1.0) * 1000000000.0
+    key_bias_ref[...] = jnp.where(key_lane % cols == key_sub, key_bias, -jnp.inf)
     hot = jnp.concatenate(hot, axis=0).astype(jnp.bfloat16)
     rel_ref[...] = dot(hot, table_ref[...])
 
@@ -87,11 +95,11 @@
     order,
     held_ref,
     other_ref,
-    mask_ref,
     rel_ref,
     pair_mask_ref,
     gains_ref,
     att_bias_ref,
+    key_bias_ref,
     in_weight_ref,
     in_gate_ref,
     out_gate_ref,
@@ -189,17 +197,8 @@
         [jnp.broadcast_to(bias[r][h : h + 1], (cols, column_pairs)) for h in range(heads) for r in range(rows)],
         axis=0,
     )
-    lane_row = lax.broadcasted_iota(jnp.int32, (1, column_pairs), 1)
-    key_mask = jnp.zeros((1, column_pairs), jnp.int32)
-    for k in range(tokens):
-        key_mask = jnp.where(lane_row // cols == k, mask_ref[k], key_mask)
-    key_bias = (key_mask.astype(f32) - 1.0) * 1000000000.0
+    key_bias = jnp.concatenate([key_bias_ref[...]] * (heads * rows), axis=0)
     scores = scores + biases + key_bias
-    same = (
-        lax.broadcasted_iota(jnp.int32, scores.shape, 1) % cols
-        == lax.broadcasted_iota(jnp.int32, scores.shape, 0) % cols
-    )
-    scores = jnp.where(same, scores, -jnp.inf)
     expo = jnp.exp(scores - jnp.max(scores, axis=-1, keepdims=True))
     totals = jnp.sum(expo, axis=-1, keepdims=True)
     mixed = dot(expo.astype(bf16), values) / totals
@@ -262,9 +261,10 @@
             wide_out,
             jax.ShapeDtypeStruct((3, width), jnp.float32),
             jax.ShapeDtypeStruct((heads, width), att_bias.dtype),
+            jax.ShapeDtypeStruct((cols, tokens * cols), jnp.float32),
         ],
         in_specs=[smem] * 2 + [vmem] * 5,
-        out_specs=[vmem] * 4,
+        out_specs=[vmem] * 5,
         compiler_params=params,
         cost_estimate=pl.CostEstimate(flops=STAGE_FLOPS, bytes_accessed=2**20, transcendentals=0),
     )(
@@ -285,11 +285,11 @@
     return pl.pallas_call(
         functools.partial(whole_pair_kernel, row_dim, heads, order),
         out_shape=jax.ShapeDtypeStruct(pair_in.shape, pair_in.dtype),
-        in_specs=[vmem] * 2 + [smem] + [vmem] * (4 + len(weights)),
+        in_specs=[vmem] * (7 + len(weights)),
         out_specs=vmem,
         scratch_shapes=[wide] * 4 + [column] * 2,
         compiler_params=params,
-    )(*gathered, token_mask, *staged, *weights)
+    )(*gathered, *staged, *weights)
 
 
 def attend_column(query_col, key_col, value_col, bias_all, key_bias, block_rows):

time: 16 us -> 15.5 us (0.969)
  Pallas kernels: 3.54 us -> 3 us
    pallas_call x1, Pallas kernels: 2.82 us -> 2.28 us  [whole_pair_on_device(): pl.pallas_call(functools.partial(whole_pair_kernel, row_dim, heads, order...]
where the time goes in v9:
time: 15.5 us; the launch traced here: 15.3 us
  starting transfers between devices  7.63 us (49%)
  waiting for transfers between devices  3.04 us (20%)
  Pallas kernels  3 us (19%)
  local copies, waits for them, and re-layouts  1.48 us (10%)
    ppermute x4, starting transfers between devices, move(): lax.ppermute(values, ('row', 'col'), [(device, device ^ step) for device...  7.63 us
    ppermute x4, waiting for transfers between devices, move(): lax.ppermute(values, ('row', 'col'), [(device, device ^ step) for device...  3.04 us
    pallas_call x1, Pallas kernels, whole_pair_on_device(): pl.pallas_call(functools.partial(whole_pair_kernel, row_dim, heads, order...  2.28 us
    unnamed x30, local copies, waits for them, and re-layouts  1.47 us
    pallas_call x1, Pallas kernels, whole_pair_on_device(): pl.pallas_call(functools.partial(stage_kernel, cols), out_shape=[wide_out...  0.72 us
  transfers between devices with their start and end apart: 4, of which 3 were waited for; matrix products, arithmetic and copies ran while one was open for 0% of the time, Pallas kernels for 5%

profile of v9, /device:TPU:0, one launch (start us, length us, event | category | flops | bytes accessed | tf_op | source)
XLA Modules:
  0.0 15.3 jit_solution(11560704607335354972)
XLA Ops:
  0.0 2.4 %collective-permute-start = (bf16[2,8,128]{2,1,0:T(8,128)(2,1)}, bf16[2,8,128]{2,1,0:T(8,128)(2,1)S(1)}, u32[]{:S(2)}, u32[]{:S(2)}) collective-permute-start(bf16[2,8,128]{2,1,0:T(8,128)(2,1)} %pair_ref.1), channel_id=1, source_target_pairs={{0,3},{1,2},{2,1},{3,0},{4,7},{5,6},{6,5},{7,4},{8,11},{9,10},{10,... | collective-permute-start | bytes 12296 | tf_op jit(solution)/shard_map/ppermute | solution.py:241
  2.4 0.0 copy-start.7
  2.4 0.7 %copy-done.7 = bf16[2,8,128]{2,1,0:T(8,128)(2,1)S(1)} copy-done((bf16[2,8,128]{2,1,0:T(8,128)(2,1)S(1)}, bf16[2,8,128]{2,1,0:T(8,128)(2,1)}, u32[]{:S(2)}) %copy-start.7) | copy-done | bytes 4120
  3.1 0.0 copy-start.8
  3.1 0.8 %collective-permute-done = bf16[2,8,128]{2,1,0:T(8,128)(2,1)S(1)} collective-permute-done((bf16[2,8,128]{2,1,0:T(8,128)(2,1)}, bf16[2,8,128]{2,1,0:T(8,128)(2,1)S(1)}, u32[]{:S(2)}, u32[]{:S(2)}) %collective-permute-start) | collective-permute-done | bytes 4128 | tf_op jit(solution)/shard_map/ppermute | solution.py:241
  3.9 2.1 %collective-permute-start.1 = (bf16[2,2,8,128]{3,2,1,0:T(8,128)(2,1)S(1)}, bf16[2,2,8,128]{3,2,1,0:T(8,128)(2,1)S(1)}, u32[]{:S(2)}, u32[]{:S(2)}) collective-permute-start(bf16[2,2,8,128]{3,2,1,0:T(8,128)(2,1)S(1)} %bitcast_dynamic-update-slice_fusion), channel_id=1, source_target_pairs={{0,5},{1,4},{2,7},{3,6},{4,1},{5,0},{6,3},{7,2},{8,13},{9,12},{10,... | collective-permute-start | bytes 24584 | tf_op jit(solution)/shard_map/ppermute | solution.py:241
  6.0 1.4 %collective-permute-done.1 = bf16[2,2,8,128]{3,2,1,0:T(8,128)(2,1)S(1)} collective-permute-done((bf16[2,2,8,128]{3,2,1,0:T(8,128)(2,1)S(1)}, bf16[2,2,8,128]{3,2,1,0:T(8,128)(2,1)S(1)}, u32[]{:S(2)}, u32[]{:S(2)}) %collective-permute-start.1) | collective-permute-done | bytes 8224 | tf_op jit(solution)/shard_map/ppermute | solution.py:241
  7.4 2.7 %collective-permute-start.2 = (bf16[4,2,8,128]{3,2,1,0:T(8,128)(2,1)S(1)}, bf16[4,2,8,128]{3,2,1,0:T(8,128)(2,1)S(1)}, u32[]{:S(2)}, u32[]{:S(2)}) collective-permute-start(bf16[4,2,8,128]{3,2,1,0:T(8,128)(2,1)S(1)} %pad_maximum_fusion.1), channel_id=1, source_target_pairs={{0,9},{1,8},{2,11},{3,10},{4,13},{5,12},{6,15},{7,14},{8,1},{9,0},... | collective-permute-start | bytes 49160 | tf_op jit(solution)/shard_map/ppermute | solution.py:241
  10.1 0.0 copy-start.11
  10.1 0.0 copy-start.12
  10.1 0.0 copy-start.13
  10.1 0.0 copy-start.14
  10.1 0.0 copy-start.9
  10.1 0.0 copy-start.10
  10.1 0.0 copy-done.8
  10.1 0.6 %copy-done.11 = s32[16]{0:T(128)S(1)} copy-done((s32[16]{0:T(128)S(1)}, s32[16]{0:T(128)}, u32[]{:S(2)}) %copy-start.11) | copy-done | bytes 88
  10.7 0.0 copy-done.12
  10.8 0.0 copy-done.13
  10.8 0.0 copy-done.14
  10.8 0.0 copy-done.9
  10.8 0.0 copy-done.10
  10.8 0.0 copy-start
  10.8 0.0 copy-start.2
  10.8 0.0 copy-start.3
  10.8 0.0 copy-start.4
  10.9 0.0 copy-start.5
  10.9 0.0 copy-start.6
  10.9 0.7 %shard_map.146 = (f32[256,128]{1,0:T(8,128)S(1)}, f32[256,128]{1,0:T(8,128)S(1)}, f32[3,128]{1,0:T(4,128)S(1)}, bf16[4,128]{1,0:T(4,128)(2,1)S(1)}, f32[8,128]{1,0:T(8,128)S(1)}) custom-call(s32[16]{0:T(128)S(1)} %copy-done.10, s32[16]{0:T(128)S(1)} %copy-done.11, bf16[128,128]{1,0:T(8,128)(2,1)S(1)} %copy-done.8, f32[1,128]{1,0:T(1,128)S(1)} %bitcast.7, ...), custom_call_target="tpu_custom_call" | custom-call | flops 1000000000 | bytes 1048576 | tf_op jit(solution)/shard_map/pallas_call | solution.py:257
  11.6 0.0 copy-start.1
  11.6 0.0 collective-permute-done.2
  11.6 0.5 %collective-permute-start.3 = (bf16[8,2,8,128]{3,2,1,0:T(8,128)(2,1)S(1)}, bf16[8,2,8,128]{3,2,1,0:T(8,128)(2,1)S(1)}, u32[]{:S(2)}, u32[]{:S(2)}) collective-permute-start(bf16[8,2,8,128]{3,2,1,0:T(8,128)(2,1)S(1)} %pad_maximum_fusion.held_ref), channel_id=1, source_target_pairs={{0,1},{1,0},{2,3},{3,2},{4,5},{5,4},{6,7},{7,6},{8,9},{9,8},{10,11... | collective-permute-start | bytes 98312 | tf_op jit(solution)/shard_map/ppermute | solution.py:241
  12.1 0.9 %collective-permute-done.3.other_ref = bf16[8,2,8,128]{3,2,1,0:T(8,128)(2,1)S(1)} collective-permute-done((bf16[8,2,8,128]{3,2,1,0:T(8,128)(2,1)S(1)}, bf16[8,2,8,128]{3,2,1,0:T(8,128)(2,1)S(1)}, u32[]{:S(2)}, u32[]{:S(2)}) %collective-permute-start.3) | collective-permute-done | bytes 32800 | tf_op jit(solution)/shard_map/ppermute | solution.py:241
  13.0 0.0 copy-done
  13.0 0.0 copy-done.2
  13.0 0.0 copy-done.3
  13.0 0.0 copy-done.4
  13.0 0.0 copy-done.5
  13.0 0.0 copy-done.6
  13.0 0.0 copy-done.1
  13.0 2.3 %shard_map.147 = bf16[2,8,128]{2,1,0:T(8,128)(2,1)} custom-call(bf16[8,2,8,128]{3,2,1,0:T(8,128)(2,1)S(1)} %pad_maximum_fusion.held_ref, bf16[8,2,8,128]{3,2,1,0:T(8,128)(2,1)S(1)} %collective-permute-done.3.other_ref, f32[256,128]{1,0:T(8,128)S(1)} %get-tuple-element.34.rel_ref, f32[256,128]{1,0:T(8,128)S(1)} %get-tuple-element.35.pair_mask_ref, ...), custom_call_target="tpu_custom_call" | custom-call | tf_op jit(solution)/shard_map/pallas_call | solution.py:285
  (4 shorter events, 0.0 us)
Async XLA Ops:
  0.0 3.9 %collective-permute-start = (bf16[2,8,128]{2,1,0:T(8,128)(2,1)}, bf16[2,8,128]{2,1,0:T(8,128)(2,1)S(1)}, u32[]{:S(2)}, u32[]{:S(2)}) collective-permute-start(bf16[2,8,128]{2,1,0:T(8,128)(2,1)} %pair_ref.1), channel_id=1, source_target_pairs={{0,3},{1,2},{2,1},{3,0},{4,7},{5,6},{6,5},{7,4},{8,11},{9,10},{10,... | collective-permute-start | bytes 12296 | tf_op jit(solution)/shard_map/ppermute | solution.py:241
  2.4 0.7 %copy-start.7 = (bf16[2,8,128]{2,1,0:T(8,128)(2,1)S(1)}, bf16[2,8,128]{2,1,0:T(8,128)(2,1)}, u32[]{:S(2)}) copy-start(bf16[2,8,128]{2,1,0:T(8,128)(2,1)} %pair_ref.1) | copy-start | bytes 12292
  3.1 7.0 %copy-start.8 = (bf16[128,128]{1,0:T(8,128)(2,1)S(1)}, bf16[128,128]{1,0:T(8,128)(2,1)}, u32[]{:S(2)}) copy-start(bf16[128,128]{1,0:T(8,128)(2,1)} %table_ref.1) | copy-start | bytes 98308
  3.9 3.4 %collective-permute-start.1 = (bf16[2,2,8,128]{3,2,1,0:T(8,128)(2,1)S(1)}, bf16[2,2,8,128]{3,2,1,0:T(8,128)(2,1)S(1)}, u32[]{:S(2)}, u32[]{:S(2)}) collective-permute-start(bf16[2,2,8,128]{3,2,1,0:T(8,128)(2,1)S(1)} %bitcast_dynamic-update-slice_fusion), channel_id=1, source_target_pairs={{0,5},{1,4},{2,7},{3,6},{4,1},{5,0},{6,3},{7,2},{8,13},{9,12},{10,... | collective-permute-start | bytes 24584 | tf_op jit(solution)/shard_map/ppermute | solution.py:241
  7.4 4.2 %collective-permute-start.2 = (bf16[4,2,8,128]{3,2,1,0:T(8,128)(2,1)S(1)}, bf16[4,2,8,128]{3,2,1,0:T(8,128)(2,1)S(1)}, u32[]{:S(2)}, u32[]{:S(2)}) collective-permute-start(bf16[4,2,8,128]{3,2,1,0:T(8,128)(2,1)S(1)} %pad_maximum_fusion.1), channel_id=1, source_target_pairs={{0,9},{1,8},{2,11},{3,10},{4,13},{5,12},{6,15},{7,14},{8,1},{9,0},... | collective-permute-start | bytes 49160 | tf_op jit(solution)/shard_map/ppermute | solution.py:241
  10.1 0.7 %copy-start.11 = (s32[16]{0:T(128)S(1)}, s32[16]{0:T(128)}, u32[]{:S(2)}) copy-start(s32[16]{0:T(128)} %pos_ref.1) | copy-start | bytes 196
  10.1 0.7 %copy-start.12 = (f32[128]{0:T(128)S(1)}, f32[128]{0:T(128)}, u32[]{:S(2)}) copy-start(f32[128]{0:T(128)} %param.21) | copy-start | bytes 1540
  10.1 0.7 %copy-start.13 = (f32[128]{0:T(128)S(1)}, f32[128]{0:T(128)}, u32[]{:S(2)}) copy-start(f32[128]{0:T(128)} %param.25) | copy-start | bytes 1540
  10.1 0.7 %copy-start.14 = (f32[128]{0:T(128)S(1)}, f32[128]{0:T(128)}, u32[]{:S(2)}) copy-start(f32[128]{0:T(128)} %param.27) | copy-start | bytes 1540
  10.1 0.7 %copy-start.9 = (bf16[128,4]{0,1:T(4,128)(2,1)S(1)}, bf16[128,4]{0,1:T(4,128)(2,1)}, u32[]{:S(2)}) copy-start(bf16[128,4]{0,1:T(4,128)(2,1)} %param.30) | copy-start | bytes 3076
  10.1 0.7 %copy-start.10 = (s32[16]{0:T(128)S(1)}, s32[16]{0:T(128)}, u32[]{:S(2)}) copy-start(s32[16]{0:T(128)} %mask_ref.1) | copy-start | bytes 196
  10.8 2.1 %copy-start = (bf16[128,384]{1,0:T(8,128)(2,1)S(1)}, bf16[128,384]{1,0:T(8,128)(2,1)}, u32[]{:S(2)}) copy-start(bf16[128,384]{1,0:T(8,128)(2,1)} %qkv_ref.1) | copy-start | bytes 294916
  10.8 2.1 %copy-start.2 = (bf16[128,256]{1,0:T(8,128)(2,1)S(1)}, bf16[128,256]{1,0:T(8,128)(2,1)}, u32[]{:S(2)}) copy-start(bf16[128,256]{1,0:T(8,128)(2,1)} %in_gate_ref.1) | copy-start | bytes 196612
  10.8 2.1 %copy-start.3 = (bf16[128,128]{1,0:T(8,128)(2,1)S(1)}, bf16[128,128]{1,0:T(8,128)(2,1)}, u32[]{:S(2)}) copy-start(bf16[128,128]{1,0:T(8,128)(2,1)} %out_gate_ref.1) | copy-start | bytes 98308
  10.8 2.1 %copy-start.4 = (bf16[128,128]{1,0:T(8,128)(2,1)S(1)}, bf16[128,128]{1,0:T(8,128)(2,1)}, u32[]{:S(2)}) copy-start(bf16[128,128]{1,0:T(8,128)(2,1)} %out_weight_ref.1) | copy-start | bytes 98308
  10.9 2.1 %copy-start.5 = (bf16[128,128]{1,0:T(8,128)(2,1)S(1)}, bf16[128,128]{1,0:T(8,128)(2,1)}, u32[]{:S(2)}) copy-start(bf16[128,128]{1,0:T(8,128)(2,1)} %att_gate_ref.1) | copy-start | bytes 98308
  10.9 2.1 %copy-start.6 = (bf16[128,128]{1,0:T(8,128)(2,1)S(1)}, bf16[128,128]{1,0:T(8,128)(2,1)}, u32[]{:S(2)}) copy-start(bf16[128,128]{1,0:T(8,128)(2,1)} %att_out_ref.1) | copy-start | bytes 98308
  11.6 1.4 %copy-start.1 = (bf16[128,256]{1,0:T(8,128)(2,1)S(1)}, bf16[128,256]{1,0:T(8,128)(2,1)}, u32[]{:S(2)}) copy-start(bf16[128,256]{1,0:T(8,128)(2,1)} %in_weight_ref.1) | copy-start | bytes 196612
  11.6 1.3 %collective-permute-start.3 = (bf16[8,2,8,128]{3,2,1,0:T(8,128)(2,1)S(1)}, bf16[8,2,8,128]{3,2,1,0:T(8,128)(2,1)S(1)}, u32[]{:S(2)}, u32[]{:S(2)}) collective-permute-start(bf16[8,2,8,128]{3,2,1,0:T(8,128)(2,1)S(1)} %pad_maximum_fusion.held_ref), channel_id=1, source_target_pairs={{0,1},{1,0},{2,3},{3,2},{4,5},{5,4},{6,7},{7,6},{8,9},{9,8},{10,11... | collective-permute-start | bytes 98312 | tf_op jit(solution)/shard_map/ppermute | solution.py:241

commit v10 on v9

--- a/solution.py
+++ b/solution.py
@@ -39,52 +39,46 @@
     return values.astype(jnp.bfloat16).astype(jnp.float32)
 
 
-def own_kernel(pair_ref, chip_ref):
+def token_column(ref, first, shape):
+    sub = lax.broadcasted_iota(jnp.int32, shape, 0)
+    column = jnp.zeros(shape, jnp.int32)
+    for s in range(shape[0]):
+        column = jnp.where(sub == s, ref[first + s], column)
+    return column
+
+
+def own_kernel(mask_ref, pair_ref, att_bias_ref, chip_ref, bias_ref, pair_mask_ref, key_bias_ref):
     chip_ref[0] = pair_ref[...]
-
-
-def stage_kernel(
-    cols,
-    mask_ref,
-    pos_ref,
-    table_ref,
-    norm_in_ref,
-    norm_out_ref,
-    att_norm_ref,
-    att_bias_ref,
-    rel_ref,
-    pair_mask_ref,
-    gains_ref,
-    bias_ref,
-    key_bias_ref,
-):
+    bias_ref[...] = att_bias_ref[...]
+    tokens = mask_ref.shape[0]
+    cols, width = key_bias_ref.shape[0], pair_mask_ref.shape[1]
+    for half in range(tokens // cols):
+        column = token_column(mask_ref, half * cols, (cols, width))
+        for i in range(tokens):
+            first = i * tokens + half * cols
+            pair_mask_ref[first : first + cols, :] = (column * mask_ref[i]).astype(jnp.float32)
+    sub = lax.broadcasted_iota(jnp.int32, key_bias_ref.shape, 0)
+    lane = lax.broadcasted_iota(jnp.int32, key_bias_ref.shape, 1)
+    key_mask = jnp.zeros(key_bias_ref.shape, jnp.int32)
+    for k in range(tokens):
+        key_mask = jnp.where(lane // cols == k, mask_ref[k], key_mask)
+    key_bias = (key_mask.astype(jnp.float32) - 1.0) * 1000000000.0
+    key_bias_ref[...] = jnp.where(lane % cols == sub, key_bias, -jnp.inf)
+
+
+def stage_kernel(cols, pos_ref, table_ref, norm_in_ref, norm_out_ref, att_norm_ref, rel_ref, gains_ref):
     gains_ref[0:1] = norm_in_ref[...]
     gains_ref[1:2] = norm_out_ref[...]
     gains_ref[2:3] = att_norm_ref[...]
-    bias_ref[...] = att_bias_ref[...]
     tokens = pos_ref.shape[0]
     bins = table_ref.shape[0]
-    sub = lax.broadcasted_iota(jnp.int32, (cols, bins), 0)
     lane = lax.broadcasted_iota(jnp.int32, (cols, bins), 1)
     hot = [None] * (tokens * tokens // cols)
     for half in range(tokens // cols):
-        pos_vec = jnp.zeros((cols, bins), jnp.int32)
-        mask_vec = jnp.zeros((cols, bins), jnp.int32)
-        for c in range(cols):
-            pos_vec = jnp.where(sub == c, pos_ref[half * cols + c], pos_vec)
-            mask_vec = jnp.where(sub == c, mask_ref[half * cols + c], mask_vec)
+        column = token_column(pos_ref, half * cols, (cols, bins))
         for i in range(tokens):
-            at = i * (tokens // cols) + half
-            bucket = jnp.clip(pos_ref[i] - pos_vec, -(bins // 2), bins // 2 - 1) + bins // 2
-            hot[at] = (bucket == lane).astype(jnp.float32)
-            pair_mask_ref[at * cols : (at + 1) * cols, :] = (mask_vec * mask_ref[i]).astype(jnp.float32)
-    key_sub = lax.broadcasted_iota(jnp.int32, key_bias_ref.shape, 0)
-    key_lane = lax.broadcasted_iota(jnp.int32, key_bias_ref.shape, 1)
-    key_mask = jnp.zeros(key_bias_ref.shape, jnp.int32)
-    for k in range(tokens):
-        key_mask = jnp.where(key_lane // cols == k, mask_ref[k], key_mask)
-    key_bias = (key_mask.astype(jnp.float32) - 1.0) * 1000000000.0
-    key_bias_ref[...] = jnp.where(key_lane % cols == key_sub, key_bias, -jnp.inf)
+            bucket = jnp.clip(pos_ref[i] - column, -(bins // 2), bins // 2 - 1) + bins // 2
+            hot[i * (tokens // cols) + half] = (bucket == lane).astype(jnp.float32)
     hot = jnp.concatenate(hot, axis=0).astype(jnp.bfloat16)
     rel_ref[...] = dot(hot, table_ref[...])
 
@@ -235,48 +229,48 @@
     params = pltpu.CompilerParams(vmem_limit_bytes=16 * 1024 * 1024)
     tokens, heads = row_dim * rows, att_bias.shape[1]
 
-    blocks = 2 * row_dim
-
-    def move(values, step):
-        return lax.ppermute(values, ("row", "col"), [(device, device ^ step) for device in range(blocks)])
-
-    held = pl.pallas_call(
-        own_kernel,
-        out_shape=jax.ShapeDtypeStruct((2,) + pair_in.shape, pair_in.dtype),
-        in_specs=[vmem],
-        out_specs=vmem,
+    beside = pl.CostEstimate(flops=STAGE_FLOPS, bytes_accessed=2**20, transcendentals=0)
+    wide_out = jax.ShapeDtypeStruct((tokens * tokens, width), jnp.float32)
+    rel, gains = pl.pallas_call(
+        functools.partial(stage_kernel, cols),
+        out_shape=[wide_out, jax.ShapeDtypeStruct((3, width), jnp.float32)],
+        in_specs=[smem] + [vmem] * 4,
+        out_specs=[vmem] * 2,
         compiler_params=params,
-    )(pair_in)
-    held, order = held.at[1].set(move(pair_in, 3)), (0, 3)
-    while len(order) < row_dim:
-        step = 2 * len(order) + 1
-        held = jnp.concatenate([held, move(held, step)], axis=0)
-        order += tuple(place ^ step for place in order)
-
-    wide_out = jax.ShapeDtypeStruct((tokens * tokens, width), jnp.float32)
-    staged = pl.pallas_call(
-        functools.partial(stage_kernel, cols),
-        out_shape=[
-            wide_out,
-            wide_out,
-            jax.ShapeDtypeStruct((3, width), jnp.float32),
-            jax.ShapeDtypeStruct((heads, width), att_bias.dtype),
-            jax.ShapeDtypeStruct((cols, tokens * cols), jnp.float32),
-        ],
-        in_specs=[smem] * 2 + [vmem] * 5,
-        out_specs=[vmem] * 5,
-        compiler_params=params,
-        cost_estimate=pl.CostEstimate(flops=STAGE_FLOPS, bytes_accessed=2**20, transcendentals=0),
+        cost_estimate=beside,
     )(
-        token_mask,
         positions,
         relpos_table,
         tri_norm_in.reshape(1, width),
         tri_norm_out.reshape(1, width),
         att_norm.reshape(1, width),
-        att_bias.T,
-    )
-    held, *staged = lax.optimization_barrier((held, *staged))
+    )
+
+    blocks = 2 * row_dim
+
+    def move(values, step):
+        return lax.ppermute(values, ("row", "col"), [(device, device ^ step) for device in range(blocks)])
+
+    line = tuple(range(blocks - 3, 1, -4))
+    held, bias, pair_mask, key_bias = pl.pallas_call(
+        own_kernel,
+        out_shape=[
+            jax.ShapeDtypeStruct((1 + len(line),) + pair_in.shape, pair_in.dtype),
+            jax.ShapeDtypeStruct((heads, width), att_bias.dtype),
+            wide_out,
+            jax.ShapeDtypeStruct((cols, tokens * cols), jnp.float32),
+        ],
+        in_specs=[smem] + [vmem] * 2,
+        out_specs=[vmem] * 4,
+        compiler_params=params,
+        cost_estimate=beside,
+    )(token_mask, pair_in, att_bias.T)
+    for at, step in enumerate(line):
+        held = held.at[1 + at].set(move(pair_in, step))
+    order = (0,) + line
+    held = jnp.concatenate([held, move(held, 3)], axis=0)
+    order += tuple(place ^ 3 for place in order)
+    held, rel, gains = lax.optimization_barrier((held, rel, gains))
     gathered = (held, move(held, 1))
 
     weights = (tri_in_weight, tri_in_gate, tri_out_gate, tri_out_weight, att_qkv, att_gate, att_out)
@@ -289,7 +283,7 @@
         out_specs=vmem,
         scratch_shapes=[wide] * 4 + [column] * 2,
         compiler_params=params,
-    )(*gathered, *staged, *weights)
+    )(*gathered, rel, pair_mask, gains, bias, key_bias, *weights)
 
 
 def attend_column(query_col, key_col, value_col, bias_all, key_bias, block_rows):

time: 15.5 us -> 15.9 us (1.026)
  Pallas kernels: 3 us -> 3.55 us
  waiting for transfers between devices: 3.04 us -> 2.78 us
  starting transfers between devices: 7.63 us -> 7.85 us
    pallas_call x1, Pallas kernels: 0.01 us -> 0.57 us  [whole_pair_on_device(): pl.pallas_call(own_kernel, out_shape=[jax.ShapeDtypeStruct((1 + len(line)...]
    ppermute x4 -> x5, waiting for transfers between devices: 3.04 us -> 2.78 us  [move(): lax.ppermute(values, ('row', 'col'), [(device, device ^ step) for device...]
    ppermute x4 -> x5, starting transfers between devices: 7.63 us -> 7.85 us  [move(): lax.ppermute(values, ('row', 'col'), [(device, device ^ step) for device...]
  transfers between devices with their start and end apart: 4 -> 5, of which waited for: 3 -> 2; matrix products, arithmetic and copies ran while one was open for 0% -> 0% of each run, Pallas kernels for 5% -> 8%
where the time goes in v10:
time: 15.9 us; the launch traced here: 15.8 us
  starting transfers between devices  7.85 us (49%)
  Pallas kernels  3.55 us (22%)
  waiting for transfers between devices  2.78 us (17%)
  local copies, waits for them, and re-layouts  1.45 us (9%)
    ppermute x5, starting transfers between devices, move(): lax.ppermute(values, ('row', 'col'), [(device, device ^ step) for device...  7.85 us
    ppermute x5, waiting for transfers between devices, move(): lax.ppermute(values, ('row', 'col'), [(device, device ^ step) for device...  2.78 us
    pallas_call x1, Pallas kernels, whole_pair_on_device(): pl.pallas_call(functools.partial(whole_pair_kernel, row_dim, heads, order...  2.28 us
    unnamed x30, local copies, waits for them, and re-layouts  1.43 us
    pallas_call x1, Pallas kernels, whole_pair_on_device(): pl.pallas_call(functools.partial(stage_kernel, cols), out_shape=[wide_out...  0.7 us
    pallas_call x1, Pallas kernels, whole_pair_on_device(): pl.pallas_call(own_kernel, out_shape=[jax.ShapeDtypeStruct((1 + len(line)...  0.57 us
  transfers between devices with their start and end apart: 5, of which 2 were waited for; matrix products, arithmetic and copies ran while one was open for 0% of the time, Pallas kernels for 8%

profile of v10, /device:TPU:0, one launch (start us, length us, event | category | flops | bytes accessed | tf_op | source)
XLA Modules:
  0.0 15.8 jit_solution(12904781371071259230)
XLA Ops:
  0.0 0.0 copy-start.9
  0.0 0.0 copy-start.10
  0.0 4.5 %collective-permute-start = (bf16[2,8,128]{2,1,0:T(8,128)(2,1)}, bf16[2,8,128]{2,1,0:T(8,128)(2,1)S(1)}, u32[]{:S(2)}, u32[]{:S(2)}) collective-permute-start(bf16[2,8,128]{2,1,0:T(8,128)(2,1)} %pair_ref.1), channel_id=1, source_target_pairs={{0,13},{1,12},{2,15},{3,14},{4,9},{5,8},{6,11},{7,10},{8,5},{9,4},... | collective-permute-start | bytes 12296 | tf_op jit(solution)/shard_map/ppermute | solution.py:252
  4.5 0.0 collective-permute-start.2
  4.5 0.9 %collective-permute-start.1 = (bf16[2,8,128]{2,1,0:T(8,128)(2,1)}, bf16[2,8,128]{2,1,0:T(8,128)(2,1)S(1)}, u32[]{:S(2)}, u32[]{:S(2)}) collective-permute-start(bf16[2,8,128]{2,1,0:T(8,128)(2,1)} %pair_ref.1), channel_id=1, source_target_pairs={{0,9},{1,8},{2,11},{3,10},{4,13},{5,12},{6,15},{7,14},{8,1},{9,0},... | collective-permute-start | bytes 12296 | tf_op jit(solution)/shard_map/ppermute | solution.py:252
  5.4 0.0 copy-done.9
  5.4 0.0 copy-done.10
  5.4 0.0 copy-start.8
  5.4 0.7 %copy-done.8 = bf16[2,8,128]{2,1,0:T(8,128)(2,1)S(1)} copy-done((bf16[2,8,128]{2,1,0:T(8,128)(2,1)S(1)}, bf16[2,8,128]{2,1,0:T(8,128)(2,1)}, u32[]{:S(2)}) %copy-start.8) | copy-done | bytes 4120
  6.1 0.0 copy-start.7
  6.1 0.0 copy-start.14
  6.1 0.6 %shard_map.145 = (bf16[4,2,8,128]{3,2,1,0:T(8,128)(2,1)S(1)}, bf16[4,128]{1,0:T(4,128)(2,1)S(1)}, f32[256,128]{1,0:T(8,128)S(1)}, f32[8,128]{1,0:T(8,128)S(1)}) custom-call(s32[16]{0:T(128)S(1)} %copy-done.10, bf16[2,8,128]{2,1,0:T(8,128)(2,1)S(1)} %copy-done.8, bf16[4,128]{1,0:T(4,128)(2,1)S(1)} %bitcast.10), custom_call_target="tpu_custom_call" | custom-call | flops 1000000000 | bytes 1048576 | tf_op jit(solution)/shard_map/pallas_call | solution.py:255
  6.7 0.0 collective-permute-done
  6.7 1.9 %collective-permute-done.1 = bf16[2,8,128]{2,1,0:T(8,128)(2,1)S(1)} collective-permute-done((bf16[2,8,128]{2,1,0:T(8,128)(2,1)}, bf16[2,8,128]{2,1,0:T(8,128)(2,1)S(1)}, u32[]{:S(2)}, u32[]{:S(2)}) %collective-permute-start.1) | collective-permute-done | bytes 4128 | tf_op jit(solution)/shard_map/ppermute | solution.py:252
  8.6 0.0 collective-permute-done.2
  8.7 1.8 %collective-permute-start.3 = (bf16[4,2,8,128]{3,2,1,0:T(8,128)(2,1)S(1)}, bf16[4,2,8,128]{3,2,1,0:T(8,128)(2,1)S(1)}, u32[]{:S(2)}, u32[]{:S(2)}) collective-permute-start(bf16[4,2,8,128]{3,2,1,0:T(8,128)(2,1)S(1)} %bitcast_dynamic-update-slice_fusion), channel_id=1, source_target_pairs={{0,3},{1,2},{2,1},{3,0},{4,7},{5,6},{6,5},{7,4},{8,11},{9,10},{10,... | collective-permute-start | bytes 49160 | tf_op jit(solution)/shard_map/ppermute | solution.py:252
  10.5 0.0 copy-start.11
  10.5 0.0 copy-start.12
  10.5 0.0 copy-start.13
  10.5 0.0 copy-done.7
  10.5 0.0 copy-done.14
  10.5 0.6 %copy-done.11 = s32[16]{0:T(128)S(1)} copy-done((s32[16]{0:T(128)S(1)}, s32[16]{0:T(128)}, u32[]{:S(2)}) %copy-start.11) | copy-done | bytes 88
  11.1 0.0 copy-done.12
  11.2 0.0 copy-done.13
  11.2 0.0 copy-start
  11.2 0.0 copy-start.2
  11.2 0.0 copy-start.3
  11.2 0.0 copy-start.4
  11.2 0.0 copy-start.5
  11.2 0.0 copy-start.6
  11.2 0.7 %shard_map.146 = (f32[256,128]{1,0:T(8,128)S(1)}, f32[3,128]{1,0:T(4,128)S(1)}) custom-call(s32[16]{0:T(128)S(1)} %copy-done.11, bf16[128,128]{1,0:T(8,128)(2,1)S(1)} %copy-done.7, f32[1,128]{1,0:T(1,128)S(1)} %bitcast.11, f32[1,128]{1,0:T(1,128)S(1)} %bitcast.12, f32[1,128]{1,0:T(1,128)S(1)} %bitcast.13), custom_call_target="tpu_custom_call" | custom-call | flops 1000000000 | bytes 1048576 | tf_op jit(solution)/shard_map/pallas_call | solution.py:234
  11.9 0.0 copy-start.1
  11.9 0.0 collective-permute-done.3
  11.9 0.6 %collective-permute-start.4 = (bf16[8,2,8,128]{3,2,1,0:T(8,128)(2,1)S(1)}, bf16[8,2,8,128]{3,2,1,0:T(8,128)(2,1)S(1)}, u32[]{:S(2)}, u32[]{:S(2)}) collective-permute-start(bf16[8,2,8,128]{3,2,1,0:T(8,128)(2,1)S(1)} %pad_maximum_fusion.held_ref), channel_id=1, source_target_pairs={{0,1},{1,0},{2,3},{3,2},{4,5},{5,4},{6,7},{7,6},{8,9},{9,8},{10,11... | collective-permute-start | bytes 98312 | tf_op jit(solution)/shard_map/ppermute | solution.py:252
  12.6 0.9 %collective-permute-done.4.other_ref = bf16[8,2,8,128]{3,2,1,0:T(8,128)(2,1)S(1)} collective-permute-done((bf16[8,2,8,128]{3,2,1,0:T(8,128)(2,1)S(1)}, bf16[8,2,8,128]{3,2,1,0:T(8,128)(2,1)S(1)}, u32[]{:S(2)}, u32[]{:S(2)}) %collective-permute-start.4) | collective-permute-done | bytes 32800 | tf_op jit(solution)/shard_map/ppermute | solution.py:252
  13.4 0.0 copy-done
  13.4 0.0 copy-done.2
  13.4 0.0 copy-done.3
  13.4 0.0 copy-done.4
  13.4 0.0 copy-done.5
  13.4 0.0 copy-done.6
  13.5 0.0 copy-done.1
  13.5 2.3 %shard_map.147 = bf16[2,8,128]{2,1,0:T(8,128)(2,1)} custom-call(bf16[8,2,8,128]{3,2,1,0:T(8,128)(2,1)S(1)} %pad_maximum_fusion.held_ref, bf16[8,2,8,128]{3,2,1,0:T(8,128)(2,1)S(1)} %collective-permute-done.4.other_ref, f32[256,128]{1,0:T(8,128)S(1)} %get-tuple-element.54.rel_ref, f32[256,128]{1,0:T(8,128)S(1)} %get-tuple-element.55.pair_mask_ref, ...), custom_call_target="tpu_custom_call" | custom-call | tf_op jit(solution)/shard_map/pallas_call | solution.py:279
  (4 shorter events, 0.0 us)
Async XLA Ops:
  0.0 5.4 %copy-start.9 = (bf16[128,4]{0,1:T(4,128)(2,1)S(1)}, bf16[128,4]{0,1:T(4,128)(2,1)}, u32[]{:S(2)}) copy-start(bf16[128,4]{0,1:T(4,128)(2,1)} %param.34) | copy-start | bytes 3076
  0.0 5.4 %copy-start.10 = (s32[16]{0:T(128)S(1)}, s32[16]{0:T(128)}, u32[]{:S(2)}) copy-start(s32[16]{0:T(128)} %mask_ref.1) | copy-start | bytes 196
  0.0 6.7 %collective-permute-start = (bf16[2,8,128]{2,1,0:T(8,128)(2,1)}, bf16[2,8,128]{2,1,0:T(8,128)(2,1)S(1)}, u32[]{:S(2)}, u32[]{:S(2)}) collective-permute-start(bf16[2,8,128]{2,1,0:T(8,128)(2,1)} %pair_ref.1), channel_id=1, source_target_pairs={{0,13},{1,12},{2,15},{3,14},{4,9},{5,8},{6,11},{7,10},{8,5},{9,4},... | collective-permute-start | bytes 12296 | tf_op jit(solution)/shard_map/ppermute | solution.py:252
  4.5 4.2 %collective-permute-start.2 = (bf16[2,8,128]{2,1,0:T(8,128)(2,1)}, bf16[2,8,128]{2,1,0:T(8,128)(2,1)S(1)}, u32[]{:S(2)}, u32[]{:S(2)}) collective-permute-start(bf16[2,8,128]{2,1,0:T(8,128)(2,1)} %pair_ref.1), channel_id=1, source_target_pairs={{0,5},{1,4},{2,7},{3,6},{4,1},{5,0},{6,3},{7,2},{8,13},{9,12},{10,... | collective-permute-start | bytes 12296 | tf_op jit(solution)/shard_map/ppermute | solution.py:252
  4.5 4.1 %collective-permute-start.1 = (bf16[2,8,128]{2,1,0:T(8,128)(2,1)}, bf16[2,8,128]{2,1,0:T(8,128)(2,1)S(1)}, u32[]{:S(2)}, u32[]{:S(2)}) collective-permute-start(bf16[2,8,128]{2,1,0:T(8,128)(2,1)} %pair_ref.1), channel_id=1, source_target_pairs={{0,9},{1,8},{2,11},{3,10},{4,13},{5,12},{6,15},{7,14},{8,1},{9,0},... | collective-permute-start | bytes 12296 | tf_op jit(solution)/shard_map/ppermute | solution.py:252
  5.4 0.7 %copy-start.8 = (bf16[2,8,128]{2,1,0:T(8,128)(2,1)S(1)}, bf16[2,8,128]{2,1,0:T(8,128)(2,1)}, u32[]{:S(2)}) copy-start(bf16[2,8,128]{2,1,0:T(8,128)(2,1)} %pair_ref.1) | copy-start | bytes 12292
  6.1 4.4 %copy-start.7 = (bf16[128,128]{1,0:T(8,128)(2,1)S(1)}, bf16[128,128]{1,0:T(8,128)(2,1)}, u32[]{:S(2)}) copy-start(bf16[128,128]{1,0:T(8,128)(2,1)} %table_ref.1) | copy-start | bytes 98308
  6.1 4.4 %copy-start.14 = (f32[128]{0:T(128)S(1)}, f32[128]{0:T(128)}, u32[]{:S(2)}) copy-start(f32[128]{0:T(128)} %param.31) | copy-start | bytes 1540
  8.7 3.3 %collective-permute-start.3 = (bf16[4,2,8,128]{3,2,1,0:T(8,128)(2,1)S(1)}, bf16[4,2,8,128]{3,2,1,0:T(8,128)(2,1)S(1)}, u32[]{:S(2)}, u32[]{:S(2)}) collective-permute-start(bf16[4,2,8,128]{3,2,1,0:T(8,128)(2,1)S(1)} %bitcast_dynamic-update-slice_fusion), channel_id=1, source_target_pairs={{0,3},{1,2},{2,1},{3,0},{4,7},{5,6},{6,5},{7,4},{8,11},{9,10},{10,... | collective-permute-start | bytes 49160 | tf_op jit(solution)/shard_map/ppermute | solution.py:252
  10.5 0.7 %copy-start.11 = (s32[16]{0:T(128)S(1)}, s32[16]{0:T(128)}, u32[]{:S(2)}) copy-start(s32[16]{0:T(128)} %pos_ref.1) | copy-start | bytes 196
  10.5 0.7 %copy-start.12 = (f32[128]{0:T(128)S(1)}, f32[128]{0:T(128)}, u32[]{:S(2)}) copy-start(f32[128]{0:T(128)} %param.25) | copy-start | bytes 1540
  10.5 0.7 %copy-start.13 = (f32[128]{0:T(128)S(1)}, f32[128]{0:T(128)}, u32[]{:S(2)}) copy-start(f32[128]{0:T(128)} %param.29) | copy-start | bytes 1540
  11.2 2.2 %copy-start = (bf16[128,384]{1,0:T(8,128)(2,1)S(1)}, bf16[128,384]{1,0:T(8,128)(2,1)}, u32[]{:S(2)}) copy-start(bf16[128,384]{1,0:T(8,128)(2,1)} %qkv_ref.1) | copy-start | bytes 294916
  11.2 2.2 %copy-start.2 = (bf16[128,256]{1,0:T(8,128)(2,1)S(1)}, bf16[128,256]{1,0:T(8,128)(2,1)}, u32[]{:S(2)}) copy-start(bf16[128,256]{1,0:T(8,128)(2,1)} %in_gate_ref.1) | copy-start | bytes 196612
  11.2 2.3 %copy-start.3 = (bf16[128,128]{1,0:T(8,128)(2,1)S(1)}, bf16[128,128]{1,0:T(8,128)(2,1)}, u32[]{:S(2)}) copy-start(bf16[128,128]{1,0:T(8,128)(2,1)} %out_gate_ref.1) | copy-start | bytes 98308
  11.2 2.3 %copy-start.4 = (bf16[128,128]{1,0:T(8,128)(2,1)S(1)}, bf16[128,128]{1,0:T(8,128)(2,1)}, u32[]{:S(2)}) copy-start(bf16[128,128]{1,0:T(8,128)(2,1)} %out_weight_ref.1) | copy-start | bytes 98308
  11.2 2.3 %copy-start.5 = (bf16[128,128]{1,0:T(8,128)(2,1)S(1)}, bf16[128,128]{1,0:T(8,128)(2,1)}, u32[]{:S(2)}) copy-start(bf16[128,128]{1,0:T(8,128)(2,1)} %att_gate_ref.1) | copy-start | bytes 98308
  11.2 2.2 %copy-start.6 = (bf16[128,128]{1,0:T(8,128)(2,1)S(1)}, bf16[128,128]{1,0:T(8,128)(2,1)}, u32[]{:S(2)}) copy-start(bf16[128,128]{1,0:T(8,128)(2,1)} %att_out_ref.1) | copy-start | bytes 98308
  11.9 1.5 %copy-start.1 = (bf16[128,256]{1,0:T(8,128)(2,1)S(1)}, bf16[128,256]{1,0:T(8,128)(2,1)}, u32[]{:S(2)}) copy-start(bf16[128,256]{1,0:T(8,128)(2,1)} %in_weight_ref.1) | copy-start | bytes 196612
  11.9 1.5 %collective-permute-start.4 = (bf16[8,2,8,128]{3,2,1,0:T(8,128)(2,1)S(1)}, bf16[8,2,8,128]{3,2,1,0:T(8,128)(2,1)S(1)}, u32[]{:S(2)}, u32[]{:S(2)}) collective-permute-start(bf16[8,2,8,128]{3,2,1,0:T(8,128)(2,1)S(1)} %pad_maximum_fusion.held_ref), channel_id=1, source_target_pairs={{0,1},{1,0},{2,3},{3,2},{4,5},{5,4},{6,7},{7,6},{8,9},{9,8},{10,11... | collective-permute-start | bytes 98312 | tf_op jit(solution)/shard_map/ppermute | solution.py:252

commit v11 on v10

--- a/solution.py
+++ b/solution.py
@@ -251,11 +251,11 @@
     def move(values, step):
         return lax.ppermute(values, ("row", "col"), [(device, device ^ step) for device in range(blocks)])
 
-    line = tuple(range(blocks - 3, 1, -4))
+    square = (7, 4, 3)
     held, bias, pair_mask, key_bias = pl.pallas_call(
         own_kernel,
         out_shape=[
-            jax.ShapeDtypeStruct((1 + len(line),) + pair_in.shape, pair_in.dtype),
+            jax.ShapeDtypeStruct((1 + len(square),) + pair_in.shape, pair_in.dtype),
             jax.ShapeDtypeStruct((heads, width), att_bias.dtype),
             wide_out,
             jax.ShapeDtypeStruct((cols, tokens * cols), jnp.float32),
@@ -265,11 +265,13 @@
         compiler_params=params,
         cost_estimate=beside,
     )(token_mask, pair_in, att_bias.T)
-    for at, step in enumerate(line):
+    for at, step in enumerate(square):
         held = held.at[1 + at].set(move(pair_in, step))
-    order = (0,) + line
-    held = jnp.concatenate([held, move(held, 3)], axis=0)
-    order += tuple(place ^ 3 for place in order)
+    order = (0,) + square
+    while len(order) < row_dim:
+        step = 2 * len(order) + 1
+        held = jnp.concatenate([held, move(held, step)], axis=0)
+        order += tuple(place ^ step for place in order)
     held, rel, gains = lax.optimization_barrier((held, rel, gains))
     gathered = (held, move(held, 1))
 
@@ -409,7 +411,7 @@
     tokens = row_dim * rows
     whole_bytes = tokens * tokens * width * pair_in.dtype.itemsize
     blocks = row_dim * col_dim
-    tiled = cols % 8 == 0 and width % 128 == 0 and blocks & (blocks - 1) == 0 and blocks >= 4 and col_dim == 2
+    tiled = cols % 8 == 0 and width % 128 == 0 and blocks & (blocks - 1) == 0 and blocks >= 8 and col_dim == 2
     if whole_bytes <= WHOLE_PAIR_BYTES and tiled:
         return whole_pair_on_device(row_dim, pair_in, *others)
     return split_pair_on_device(pair_in, *others)

time: 15.9 us -> 15.9 us (level)
  starting transfers between devices: 7.85 us -> 5.84 us
  waiting for transfers between devices: 2.78 us -> 4.75 us
    ppermute x5, starting transfers between devices: 7.85 us -> 5.84 us  [move(): lax.ppermute(values, ('row', 'col'), [(device, device ^ step) for device...]
    ppermute x5, waiting for transfers between devices: 2.78 us -> 4.75 us  [move(): lax.ppermute(values, ('row', 'col'), [(device, device ^ step) for device...]
  transfers between devices with their start and end apart: 5 -> 5, of which waited for: 2 -> 3; matrix products, arithmetic and copies ran while one was open for 0% -> 0% of each run, Pallas kernels for 8% -> 8%
where the time goes in v11:
time: 15.9 us; the launch traced here: 15.7 us
  starting transfers between devices  5.84 us (37%)
  waiting for transfers between devices  4.75 us (30%)
  Pallas kernels  3.55 us (22%)
  local copies, waits for them, and re-layouts  1.48 us (9%)
    ppermute x5, starting transfers between devices, move(): lax.ppermute(values, ('row', 'col'), [(device, device ^ step) for device...  5.84 us
    ppermute x5, waiting for transfers between devices, move(): lax.ppermute(values, ('row', 'col'), [(device, device ^ step) for device...  4.75 us
    pallas_call x1, Pallas kernels, whole_pair_on_device(): pl.pallas_call(functools.partial(whole_pair_kernel, row_dim, heads, order...  2.28 us
    unnamed x30, local copies, waits for them, and re-layouts  1.45 us
    pallas_call x1, Pallas kernels, whole_pair_on_device(): pl.pallas_call(functools.partial(stage_kernel, cols), out_shape=[wide_out...  0.7 us
    pallas_call x1, Pallas kernels, whole_pair_on_device(): pl.pallas_call(own_kernel, out_shape=[jax.ShapeDtypeStruct((1 + len(squar...  0.57 us
  transfers between devices with their start and end apart: 5, of which 3 were waited for; matrix products, arithmetic and copies ran while one was open for 0% of the time, Pallas kernels for 8%

profile of v11, /device:TPU:0, one launch (start us, length us, event | category | flops | bytes accessed | tf_op | source)
XLA Modules:
  0.0 15.7 jit_solution(5060392061580302868)
XLA Ops:
  0.0 0.0 copy-start.9
  0.0 0.0 copy-start.10
  0.0 3.4 %collective-permute-start = (bf16[2,8,128]{2,1,0:T(8,128)(2,1)}, bf16[2,8,128]{2,1,0:T(8,128)(2,1)S(1)}, u32[]{:S(2)}, u32[]{:S(2)}) collective-permute-start(bf16[2,8,128]{2,1,0:T(8,128)(2,1)} %pair_ref.1), channel_id=1, source_target_pairs={{0,7},{1,6},{2,5},{3,4},{4,3},{5,2},{6,1},{7,0},{8,15},{9,14},{10,... | collective-permute-start | bytes 12296 | tf_op jit(solution)/shard_map/ppermute | solution.py:252
  3.4 0.8 %collective-permute-start.2 = (bf16[2,8,128]{2,1,0:T(8,128)(2,1)}, bf16[2,8,128]{2,1,0:T(8,128)(2,1)S(1)}, u32[]{:S(2)}, u32[]{:S(2)}) collective-permute-start(bf16[2,8,128]{2,1,0:T(8,128)(2,1)} %pair_ref.1), channel_id=1, source_target_pairs={{0,3},{1,2},{2,1},{3,0},{4,7},{5,6},{6,5},{7,4},{8,11},{9,10},{10,... | collective-permute-start | bytes 12296 | tf_op jit(solution)/shard_map/ppermute | solution.py:252
  4.2 0.0 collective-permute-start.1
  4.2 0.0 copy-done.9
  4.2 0.0 copy-done.10
  4.2 0.0 copy-start.8
  4.2 0.7 %copy-done.8 = bf16[2,8,128]{2,1,0:T(8,128)(2,1)S(1)} copy-done((bf16[2,8,128]{2,1,0:T(8,128)(2,1)S(1)}, bf16[2,8,128]{2,1,0:T(8,128)(2,1)}, u32[]{:S(2)}) %copy-start.8) | copy-done | bytes 4120
  5.0 0.0 copy-start.7
  5.0 0.0 copy-start.14
  5.0 0.6 %shard_map.145 = (bf16[4,2,8,128]{3,2,1,0:T(8,128)(2,1)S(1)}, bf16[4,128]{1,0:T(4,128)(2,1)S(1)}, f32[256,128]{1,0:T(8,128)S(1)}, f32[8,128]{1,0:T(8,128)S(1)}) custom-call(s32[16]{0:T(128)S(1)} %copy-done.10, bf16[2,8,128]{2,1,0:T(8,128)(2,1)S(1)} %copy-done.8, bf16[4,128]{1,0:T(4,128)(2,1)S(1)} %bitcast.10), custom_call_target="tpu_custom_call" | custom-call | flops 1000000000 | bytes 1048576 | tf_op jit(solution)/shard_map/pallas_call | solution.py:255
  5.5 0.0 collective-permute-done
  5.6 2.5 %collective-permute-done.1 = bf16[2,8,128]{2,1,0:T(8,128)(2,1)S(1)} collective-permute-done((bf16[2,8,128]{2,1,0:T(8,128)(2,1)}, bf16[2,8,128]{2,1,0:T(8,128)(2,1)S(1)}, u32[]{:S(2)}, u32[]{:S(2)}) %collective-permute-start.1) | collective-permute-done | bytes 4128 | tf_op jit(solution)/shard_map/ppermute | solution.py:252
  8.0 0.0 collective-permute-done.2
  8.0 1.5 %collective-permute-start.3 = (bf16[4,2,8,128]{3,2,1,0:T(8,128)(2,1)S(1)}, bf16[4,2,8,128]{3,2,1,0:T(8,128)(2,1)S(1)}, u32[]{:S(2)}, u32[]{:S(2)}) collective-permute-start(bf16[4,2,8,128]{3,2,1,0:T(8,128)(2,1)S(1)} %bitcast_dynamic-update-slice_fusion), channel_id=1, source_target_pairs={{0,9},{1,8},{2,11},{3,10},{4,13},{5,12},{6,15},{7,14},{8,1},{9,0},... | collective-permute-start | bytes 49160 | tf_op jit(solution)/shard_map/ppermute | solution.py:252
  9.5 0.0 copy-start.11
  9.5 0.0 copy-start.12
  9.5 0.0 copy-start.13
  9.5 0.0 copy-done.7
  9.5 0.0 copy-done.14
  9.5 0.6 %copy-done.11 = s32[16]{0:T(128)S(1)} copy-done((s32[16]{0:T(128)S(1)}, s32[16]{0:T(128)}, u32[]{:S(2)}) %copy-start.11) | copy-done | bytes 88
  10.2 0.0 copy-done.12
  10.2 0.0 copy-done.13
  10.2 0.0 copy-start
  10.2 0.0 copy-start.2
  10.2 0.0 copy-start.3
  10.2 0.0 copy-start.4
  10.2 0.0 copy-start.5
  10.2 0.0 copy-start.6
  10.2 0.7 %shard_map.146 = (f32[256,128]{1,0:T(8,128)S(1)}, f32[3,128]{1,0:T(4,128)S(1)}) custom-call(s32[16]{0:T(128)S(1)} %copy-done.11, bf16[128,128]{1,0:T(8,128)(2,1)S(1)} %copy-done.7, f32[1,128]{1,0:T(1,128)S(1)} %bitcast.11, f32[1,128]{1,0:T(1,128)S(1)} %bitcast.12, f32[1,128]{1,0:T(1,128)S(1)} %bitcast.13), custom_call_target="tpu_custom_call" | custom-call | flops 1000000000 | bytes 1048576 | tf_op jit(solution)/shard_map/pallas_call | solution.py:234
  10.9 0.0 copy-start.1
  10.9 1.2 %collective-permute-done.3 = bf16[4,2,8,128]{3,2,1,0:T(8,128)(2,1)S(1)} collective-permute-done((bf16[4,2,8,128]{3,2,1,0:T(8,128)(2,1)S(1)}, bf16[4,2,8,128]{3,2,1,0:T(8,128)(2,1)S(1)}, u32[]{:S(2)}, u32[]{:S(2)}) %collective-permute-start.3) | collective-permute-done | bytes 16416 | tf_op jit(solution)/shard_map/ppermute | solution.py:252
  12.2 0.2 %collective-permute-start.4 = (bf16[8,2,8,128]{3,2,1,0:T(8,128)(2,1)S(1)}, bf16[8,2,8,128]{3,2,1,0:T(8,128)(2,1)S(1)}, u32[]{:S(2)}, u32[]{:S(2)}) collective-permute-start(bf16[8,2,8,128]{3,2,1,0:T(8,128)(2,1)S(1)} %pad_maximum_fusion.held_ref), channel_id=1, source_target_pairs={{0,1},{1,0},{2,3},{3,2},{4,5},{5,4},{6,7},{7,6},{8,9},{9,8},{10,11... | collective-permute-start | bytes 98312 | tf_op jit(solution)/shard_map/ppermute | solution.py:252
  12.3 1.0 %collective-permute-done.4.other_ref = bf16[8,2,8,128]{3,2,1,0:T(8,128)(2,1)S(1)} collective-permute-done((bf16[8,2,8,128]{3,2,1,0:T(8,128)(2,1)S(1)}, bf16[8,2,8,128]{3,2,1,0:T(8,128)(2,1)S(1)}, u32[]{:S(2)}, u32[]{:S(2)}) %collective-permute-start.4) | collective-permute-done | bytes 32800 | tf_op jit(solution)/shard_map/ppermute | solution.py:252
  13.4 0.0 copy-done
  13.4 0.0 copy-done.2
  13.4 0.0 copy-done.3
  13.4 0.0 copy-done.4
  13.4 0.0 copy-done.5
  13.4 0.0 copy-done.6
  13.4 0.0 copy-done.1
  13.4 2.3 %shard_map.147 = bf16[2,8,128]{2,1,0:T(8,128)(2,1)} custom-call(bf16[8,2,8,128]{3,2,1,0:T(8,128)(2,1)S(1)} %pad_maximum_fusion.held_ref, bf16[8,2,8,128]{3,2,1,0:T(8,128)(2,1)S(1)} %collective-permute-done.4.other_ref, f32[256,128]{1,0:T(8,128)S(1)} %get-tuple-element.54.rel_ref, f32[256,128]{1,0:T(8,128)S(1)} %get-tuple-element.55.pair_mask_ref, ...), custom_call_target="tpu_custom_call" | custom-call | tf_op jit(solution)/shard_map/pallas_call | solution.py:281
  (4 shorter events, 0.0 us)
Async XLA Ops:
  0.0 4.2 %copy-start.9 = (bf16[128,4]{0,1:T(4,128)(2,1)S(1)}, bf16[128,4]{0,1:T(4,128)(2,1)}, u32[]{:S(2)}) copy-start(bf16[128,4]{0,1:T(4,128)(2,1)} %param.34) | copy-start | bytes 3076
  0.0 4.2 %copy-start.10 = (s32[16]{0:T(128)S(1)}, s32[16]{0:T(128)}, u32[]{:S(2)}) copy-start(s32[16]{0:T(128)} %mask_ref.1) | copy-start | bytes 196
  0.0 5.5 %collective-permute-start = (bf16[2,8,128]{2,1,0:T(8,128)(2,1)}, bf16[2,8,128]{2,1,0:T(8,128)(2,1)S(1)}, u32[]{:S(2)}, u32[]{:S(2)}) collective-permute-start(bf16[2,8,128]{2,1,0:T(8,128)(2,1)} %pair_ref.1), channel_id=1, source_target_pairs={{0,7},{1,6},{2,5},{3,4},{4,3},{5,2},{6,1},{7,0},{8,15},{9,14},{10,... | collective-permute-start | bytes 12296 | tf_op jit(solution)/shard_map/ppermute | solution.py:252
  3.4 4.6 %collective-permute-start.2 = (bf16[2,8,128]{2,1,0:T(8,128)(2,1)}, bf16[2,8,128]{2,1,0:T(8,128)(2,1)S(1)}, u32[]{:S(2)}, u32[]{:S(2)}) collective-permute-start(bf16[2,8,128]{2,1,0:T(8,128)(2,1)} %pair_ref.1), channel_id=1, source_target_pairs={{0,3},{1,2},{2,1},{3,0},{4,7},{5,6},{6,5},{7,4},{8,11},{9,10},{10,... | collective-permute-start | bytes 12296 | tf_op jit(solution)/shard_map/ppermute | solution.py:252
  4.2 3.8 %collective-permute-start.1 = (bf16[2,8,128]{2,1,0:T(8,128)(2,1)}, bf16[2,8,128]{2,1,0:T(8,128)(2,1)S(1)}, u32[]{:S(2)}, u32[]{:S(2)}) collective-permute-start(bf16[2,8,128]{2,1,0:T(8,128)(2,1)} %pair_ref.1), channel_id=1, source_target_pairs={{0,4},{1,5},{2,6},{3,7},{4,0},{5,1},{6,2},{7,3},{8,12},{9,13},{10,... | collective-permute-start | bytes 12296 | tf_op jit(solution)/shard_map/ppermute | solution.py:252
  4.2 0.7 %copy-start.8 = (bf16[2,8,128]{2,1,0:T(8,128)(2,1)S(1)}, bf16[2,8,128]{2,1,0:T(8,128)(2,1)}, u32[]{:S(2)}) copy-start(bf16[2,8,128]{2,1,0:T(8,128)(2,1)} %pair_ref.1) | copy-start | bytes 12292
  5.0 4.6 %copy-start.7 = (bf16[128,128]{1,0:T(8,128)(2,1)S(1)}, bf16[128,128]{1,0:T(8,128)(2,1)}, u32[]{:S(2)}) copy-start(bf16[128,128]{1,0:T(8,128)(2,1)} %table_ref.1) | copy-start | bytes 98308
  5.0 4.6 %copy-start.14 = (f32[128]{0:T(128)S(1)}, f32[128]{0:T(128)}, u32[]{:S(2)}) copy-start(f32[128]{0:T(128)} %param.31) | copy-start | bytes 1540
  8.0 4.1 %collective-permute-start.3 = (bf16[4,2,8,128]{3,2,1,0:T(8,128)(2,1)S(1)}, bf16[4,2,8,128]{3,2,1,0:T(8,128)(2,1)S(1)}, u32[]{:S(2)}, u32[]{:S(2)}) collective-permute-start(bf16[4,2,8,128]{3,2,1,0:T(8,128)(2,1)S(1)} %bitcast_dynamic-update-slice_fusion), channel_id=1, source_target_pairs={{0,9},{1,8},{2,11},{3,10},{4,13},{5,12},{6,15},{7,14},{8,1},{9,0},... | collective-permute-start | bytes 49160 | tf_op jit(solution)/shard_map/ppermute | solution.py:252
  9.5 0.7 %copy-start.11 = (s32[16]{0:T(128)S(1)}, s32[16]{0:T(128)}, u32[]{:S(2)}) copy-start(s32[16]{0:T(128)} %pos_ref.1) | copy-start | bytes 196
  9.5 0.7 %copy-start.12 = (f32[128]{0:T(128)S(1)}, f32[128]{0:T(128)}, u32[]{:S(2)}) copy-start(f32[128]{0:T(128)} %param.25) | copy-start | bytes 1540
  9.5 0.7 %copy-start.13 = (f32[128]{0:T(128)S(1)}, f32[128]{0:T(128)}, u32[]{:S(2)}) copy-start(f32[128]{0:T(128)} %param.29) | copy-start | bytes 1540
  10.2 3.2 %copy-start = (bf16[128,384]{1,0:T(8,128)(2,1)S(1)}, bf16[128,384]{1,0:T(8,128)(2,1)}, u32[]{:S(2)}) copy-start(bf16[128,384]{1,0:T(8,128)(2,1)} %qkv_ref.1) | copy-start | bytes 294916
  10.2 3.2 %copy-start.2 = (bf16[128,256]{1,0:T(8,128)(2,1)S(1)}, bf16[128,256]{1,0:T(8,128)(2,1)}, u32[]{:S(2)}) copy-start(bf16[128,256]{1,0:T(8,128)(2,1)} %in_gate_ref.1) | copy-start | bytes 196612
  10.2 3.2 %copy-start.3 = (bf16[128,128]{1,0:T(8,128)(2,1)S(1)}, bf16[128,128]{1,0:T(8,128)(2,1)}, u32[]{:S(2)}) copy-start(bf16[128,128]{1,0:T(8,128)(2,1)} %out_gate_ref.1) | copy-start | bytes 98308
  10.2 3.2 %copy-start.4 = (bf16[128,128]{1,0:T(8,128)(2,1)S(1)}, bf16[128,128]{1,0:T(8,128)(2,1)}, u32[]{:S(2)}) copy-start(bf16[128,128]{1,0:T(8,128)(2,1)} %out_weight_ref.1) | copy-start | bytes 98308
  10.2 3.2 %copy-start.5 = (bf16[128,128]{1,0:T(8,128)(2,1)S(1)}, bf16[128,128]{1,0:T(8,128)(2,1)}, u32[]{:S(2)}) copy-start(bf16[128,128]{1,0:T(8,128)(2,1)} %att_gate_ref.1) | copy-start | bytes 98308
  10.2 3.2 %copy-start.6 = (bf16[128,128]{1,0:T(8,128)(2,1)S(1)}, bf16[128,128]{1,0:T(8,128)(2,1)}, u32[]{:S(2)}) copy-start(bf16[128,128]{1,0:T(8,128)(2,1)} %att_out_ref.1) | copy-start | bytes 98308
  10.9 2.5 %copy-start.1 = (bf16[128,256]{1,0:T(8,128)(2,1)S(1)}, bf16[128,256]{1,0:T(8,128)(2,1)}, u32[]{:S(2)}) copy-start(bf16[128,256]{1,0:T(8,128)(2,1)} %in_weight_ref.1) | copy-start | bytes 196612
  12.2 1.2 %collective-permute-start.4 = (bf16[8,2,8,128]{3,2,1,0:T(8,128)(2,1)S(1)}, bf16[8,2,8,128]{3,2,1,0:T(8,128)(2,1)S(1)}, u32[]{:S(2)}, u32[]{:S(2)}) collective-permute-start(bf16[8,2,8,128]{3,2,1,0:T(8,128)(2,1)S(1)} %pad_maximum_fusion.held_ref), channel_id=1, source_target_pairs={{0,1},{1,0},{2,3},{3,2},{4,5},{5,4},{6,7},{7,6},{8,9},{9,8},{10,11... | collective-permute-start | bytes 98312 | tf_op jit(solution)/shard_map/ppermute | solution.py:252

commit v12 on v9

--- a/solution.py
+++ b/solution.py
@@ -37,6 +37,14 @@
 
 def round_bf16(values):
     return values.astype(jnp.bfloat16).astype(jnp.float32)
+
+
+def token_column(ref, first, shape):
+    sub = lax.broadcasted_iota(jnp.int32, shape, 0)
+    column = jnp.zeros(shape, jnp.int32)
+    for s in range(shape[0]):
+        column = jnp.where(sub == s, ref[first + s], column)
+    return column
 
 
 def own_kernel(pair_ref, chip_ref):
@@ -64,37 +72,36 @@
     bias_ref[...] = att_bias_ref[...]
     tokens = pos_ref.shape[0]
     bins = table_ref.shape[0]
-    sub = lax.broadcasted_iota(jnp.int32, (cols, bins), 0)
     lane = lax.broadcasted_iota(jnp.int32, (cols, bins), 1)
     hot = [None] * (tokens * tokens // cols)
     for half in range(tokens // cols):
-        pos_vec = jnp.zeros((cols, bins), jnp.int32)
-        mask_vec = jnp.zeros((cols, bins), jnp.int32)
-        for c in range(cols):
-            pos_vec = jnp.where(sub == c, pos_ref[half * cols + c], pos_vec)
-            mask_vec = jnp.where(sub == c, mask_ref[half * cols + c], mask_vec)
+        column = token_column(pos_ref, half * cols, (cols, bins))
+        column_mask = token_column(mask_ref, half * cols, (cols, bins))
         for i in range(tokens):
-            at = i * (tokens // cols) + half
-            bucket = jnp.clip(pos_ref[i] - pos_vec, -(bins // 2), bins // 2 - 1) + bins // 2
-            hot[at] = (bucket == lane).astype(jnp.float32)
-            pair_mask_ref[at * cols : (at + 1) * cols, :] = (mask_vec * mask_ref[i]).astype(jnp.float32)
-    key_sub = lax.broadcasted_iota(jnp.int32, key_bias_ref.shape, 0)
-    key_lane = lax.broadcasted_iota(jnp.int32, key_bias_ref.shape, 1)
+            first = i * tokens + half * cols
+            pair_mask_ref[first : first + cols, :] = (column_mask * mask_ref[i]).astype(jnp.float32)
+            bucket = jnp.clip(pos_ref[i] - column, -(bins // 2), bins // 2 - 1) + bins // 2
+            hot[i * (tokens // cols) + half] = (bucket == lane).astype(jnp.float32)
+    sub = lax.broadcasted_iota(jnp.int32, key_bias_ref.shape, 0)
+    lane = lax.broadcasted_iota(jnp.int32, key_bias_ref.shape, 1)
     key_mask = jnp.zeros(key_bias_ref.shape, jnp.int32)
     for k in range(tokens):
-        key_mask = jnp.where(key_lane // cols == k, mask_ref[k], key_mask)
+        key_mask = jnp.where(lane // cols == k, mask_ref[k], key_mask)
     key_bias = (key_mask.astype(jnp.float32) - 1.0) * 1000000000.0
-    key_bias_ref[...] = jnp.where(key_lane % cols == key_sub, key_bias, -jnp.inf)
+    key_bias_ref[...] = jnp.where(lane % cols == sub, key_bias, -jnp.inf)
     hot = jnp.concatenate(hot, axis=0).astype(jnp.bfloat16)
     rel_ref[...] = dot(hot, table_ref[...])
 
 
-def whole_pair_kernel(
+def whole_pair_kernel(row_dim, heads, orders, *refs):
+    whole_pair_steps(row_dim, heads, orders, refs[: len(orders)], *refs[len(orders) :])
+
+
+def whole_pair_steps(
     row_dim,
     heads,
-    order,
-    held_ref,
-    other_ref,
+    orders,
+    piece_refs,
     rel_ref,
     pair_mask_ref,
     gains_ref,
@@ -115,7 +122,7 @@
     att_ref,
     upd_ref,
 ):
-    rows, cols, width = held_ref.shape[1:]
+    rows, cols, width = piece_refs[0].shape[1:]
     tokens = row_dim * rows
     head_dim = width // heads
     row_first = lax.axis_index("row") * rows
@@ -123,9 +130,9 @@
     f32, bf16 = jnp.float32, jnp.bfloat16
 
     me = lax.axis_index("row") * 2 + lax.axis_index("col")
-    for ref, flip in ((held_ref, 0), (other_ref, 1)):
+    for ref, order in zip(piece_refs, orders):
         for at, place in enumerate(order):
-            owner = me ^ (place ^ flip)
+            owner = me ^ place
             block = ref[at].astype(f32)
             for r in range(rows):
                 first = (owner // 2 * rows + r) * tokens + owner % 2 * cols
@@ -235,24 +242,7 @@
     params = pltpu.CompilerParams(vmem_limit_bytes=16 * 1024 * 1024)
     tokens, heads = row_dim * rows, att_bias.shape[1]
 
-    blocks = 2 * row_dim
-
-    def move(values, step):
-        return lax.ppermute(values, ("row", "col"), [(device, device ^ step) for device in range(blocks)])
-
-    held = pl.pallas_call(
-        own_kernel,
-        out_shape=jax.ShapeDtypeStruct((2,) + pair_in.shape, pair_in.dtype),
-        in_specs=[vmem],
-        out_specs=vmem,
-        compiler_params=params,
-    )(pair_in)
-    held, order = held.at[1].set(move(pair_in, 3)), (0, 3)
-    while len(order) < row_dim:
-        step = 2 * len(order) + 1
-        held = jnp.concatenate([held, move(held, step)], axis=0)
-        order += tuple(place ^ step for place in order)
-
+    beside = pl.CostEstimate(flops=STAGE_FLOPS, bytes_accessed=2**20, transcendentals=0)
     wide_out = jax.ShapeDtypeStruct((tokens * tokens, width), jnp.float32)
     staged = pl.pallas_call(
         functools.partial(stage_kernel, cols),
@@ -266,7 +256,7 @@
         in_specs=[smem] * 2 + [vmem] * 5,
         out_specs=[vmem] * 5,
         compiler_params=params,
-        cost_estimate=pl.CostEstimate(flops=STAGE_FLOPS, bytes_accessed=2**20, transcendentals=0),
+        cost_estimate=beside,
     )(
         token_mask,
         positions,
@@ -276,16 +266,38 @@
         att_norm.reshape(1, width),
         att_bias.T,
     )
-    held, *staged = lax.optimization_barrier((held, *staged))
-    gathered = (held, move(held, 1))
+
+    blocks = 2 * row_dim
+
+    def move(piece, step):
+        values, order = piece
+        values = lax.ppermute(values, ("row", "col"), [(device, device ^ step) for device in range(blocks)])
+        return values, tuple(place ^ step for place in order)
+
+    chip = pl.pallas_call(
+        own_kernel,
+        out_shape=jax.ShapeDtypeStruct((2,) + pair_in.shape, pair_in.dtype),
+        in_specs=[vmem],
+        out_specs=vmem,
+        compiler_params=params,
+        cost_estimate=beside,
+    )(pair_in)
+    other, _ = move((pair_in, (0,)), 1)
+    pieces = [(chip.at[1].set(other), (0, 1))]
+    first = move(pieces[0], 9)
+    pieces += [first, move(pieces[0], 7), move(pieces[0], 15)]
+    both = jnp.concatenate([pieces[0][0], first[0]], axis=0), pieces[0][1] + first[1]
+    pieces += [move(both, 5), move(both, 3)]
+    gathered = [values for values, _ in pieces]
+    orders = [order for _, order in pieces]
 
     weights = (tri_in_weight, tri_in_gate, tri_out_gate, tri_out_weight, att_qkv, att_gate, att_out)
     wide = pltpu.VMEM((tokens * tokens, width), jnp.float32)
     column = pltpu.VMEM((tokens * cols, width), jnp.float32)
     return pl.pallas_call(
-        functools.partial(whole_pair_kernel, row_dim, heads, order),
+        functools.partial(whole_pair_kernel, row_dim, heads, orders),
         out_shape=jax.ShapeDtypeStruct(pair_in.shape, pair_in.dtype),
-        in_specs=[vmem] * (7 + len(weights)),
+        in_specs=[vmem] * (len(gathered) + 5 + len(weights)),
         out_specs=vmem,
         scratch_shapes=[wide] * 4 + [column] * 2,
         compiler_params=params,
@@ -415,7 +427,7 @@
     tokens = row_dim * rows
     whole_bytes = tokens * tokens * width * pair_in.dtype.itemsize
     blocks = row_dim * col_dim
-    tiled = cols % 8 == 0 and width % 128 == 0 and blocks & (blocks - 1) == 0 and blocks >= 4 and col_dim == 2
+    tiled = cols % 8 == 0 and width % 128 == 0 and blocks == 16 and col_dim == 2
     if whole_bytes <= WHOLE_PAIR_BYTES and tiled:
         return whole_pair_on_device(row_dim, pair_in, *others)
     return split_pair_on_device(pair_in, *others)

time: 15.5 us -> 14.6 us (0.942)
  waiting for transfers between devices: 3.04 us -> 0.36 us
  starting transfers between devices: 7.63 us -> 9.42 us
    ppermute x4 -> x6, waiting for transfers between devices: 3.04 us -> 0.36 us  [move(): lax.ppermute(values, ('row', 'col'), [(device, device ^ step) for device...]
    ppermute x4 -> x6, starting transfers between devices: 7.63 us -> 9.42 us  [move(): lax.ppermute(values, ('row', 'col'), [(device, device ^ step) for device...]
  transfers between devices with their start and end apart: 4 -> 6, of which waited for: 3 -> 1; matrix products, arithmetic and copies ran while one was open for 0% -> 0% of each run, Pallas kernels for 5% -> 5%
where the time goes in v12:
time: 14.6 us; the launch traced here: 14.4 us
  starting transfers between devices  9.42 us (65%)
  Pallas kernels  3.01 us (21%)
  local copies, waits for them, and re-layouts  1.49 us (10%)
  waiting for transfers between devices  0.36 us (2%)
    ppermute x6, starting transfers between devices, move(): lax.ppermute(values, ('row', 'col'), [(device, device ^ step) for device...  9.42 us
    pallas_call x1, Pallas kernels, whole_pair_on_device(): pl.pallas_call(functools.partial(whole_pair_kernel, row_dim, heads, order...  2.28 us
    unnamed x30, local copies, waits for them, and re-layouts  1.48 us
    pallas_call x1, Pallas kernels, whole_pair_on_device(): pl.pallas_call(functools.partial(stage_kernel, cols), out_shape=[wide_out...  0.72 us
    ppermute x6, waiting for transfers between devices, move(): lax.ppermute(values, ('row', 'col'), [(device, device ^ step) for device...  0.36 us
  transfers between devices with their start and end apart: 6, of which 1 were waited for; matrix products, arithmetic and copies ran while one was open for 0% of the time, Pallas kernels for 5%

profile of v12, /device:TPU:0, one launch (start us, length us, event | category | flops | bytes accessed | tf_op | source)
XLA Modules:
  0.0 14.4 jit_solution(14847141138038795612)
XLA Ops:
  0.0 0.5 %collective-permute-start = (bf16[2,8,128]{2,1,0:T(8,128)(2,1)}, bf16[2,8,128]{2,1,0:T(8,128)(2,1)S(1)}, u32[]{:S(2)}, u32[]{:S(2)}) collective-permute-start(bf16[2,8,128]{2,1,0:T(8,128)(2,1)} %pair_ref.1), channel_id=1, source_target_pairs={{0,1},{1,0},{2,3},{3,2},{4,5},{5,4},{6,7},{7,6},{8,9},{9,8},{10,11... | collective-permute-start | bytes 12296 | tf_op jit(solution)/shard_map/ppermute | solution.py:274
  0.5 0.0 copy-start.8
  0.5 0.7 %copy-done.8 = bf16[2,8,128]{2,1,0:T(8,128)(2,1)S(1)} copy-done((bf16[2,8,128]{2,1,0:T(8,128)(2,1)S(1)}, bf16[2,8,128]{2,1,0:T(8,128)(2,1)}, u32[]{:S(2)}) %copy-start.8) | copy-done | bytes 4120
  1.1 0.0 copy-start.7
  1.1 0.3 %collective-permute-done = bf16[2,8,128]{2,1,0:T(8,128)(2,1)S(1)} collective-permute-done((bf16[2,8,128]{2,1,0:T(8,128)(2,1)}, bf16[2,8,128]{2,1,0:T(8,128)(2,1)S(1)}, u32[]{:S(2)}, u32[]{:S(2)}) %collective-permute-start) | collective-permute-done | bytes 4128 | tf_op jit(solution)/shard_map/ppermute | solution.py:274
  1.5 3.7 %collective-permute-start.1 = (bf16[2,2,8,128]{3,2,1,0:T(8,128)(2,1)S(1)}, bf16[2,2,8,128]{3,2,1,0:T(8,128)(2,1)S(1)}, u32[]{:S(2)}, u32[]{:S(2)}) collective-permute-start(bf16[2,2,8,128]{3,2,1,0:T(8,128)(2,1)S(1)} %bitcast_dynamic-update-slice_fusion.refs_0_), channel_id=1, source_target_pairs={{0,9},{1,8},{2,11},{3,10},{4,13},{5,12},{6,15},{7,14},{8,1},{9,0},... | collective-permute-start | bytes 24584 | tf_op jit(solution)/shard_map/ppermute | solution.py:274
  5.2 2.2 %collective-permute-start.3 = (bf16[2,2,8,128]{3,2,1,0:T(8,128)(2,1)S(1)}, bf16[2,2,8,128]{3,2,1,0:T(8,128)(2,1)S(1)}, u32[]{:S(2)}, u32[]{:S(2)}) collective-permute-start(bf16[2,2,8,128]{3,2,1,0:T(8,128)(2,1)S(1)} %bitcast_dynamic-update-slice_fusion.refs_0_), channel_id=1, source_target_pairs={{0,15},{1,14},{2,13},{3,12},{4,11},{5,10},{6,9},{7,8},{8,7},{9,6},... | collective-permute-start | bytes 24584 | tf_op jit(solution)/shard_map/ppermute | solution.py:274
  7.4 0.2 %collective-permute-start.2 = (bf16[2,2,8,128]{3,2,1,0:T(8,128)(2,1)S(1)}, bf16[2,2,8,128]{3,2,1,0:T(8,128)(2,1)S(1)}, u32[]{:S(2)}, u32[]{:S(2)}) collective-permute-start(bf16[2,2,8,128]{3,2,1,0:T(8,128)(2,1)S(1)} %bitcast_dynamic-update-slice_fusion.refs_0_), channel_id=1, source_target_pairs={{0,7},{1,6},{2,5},{3,4},{4,3},{5,2},{6,1},{7,0},{8,15},{9,14},{10,... | collective-permute-start | bytes 24584 | tf_op jit(solution)/shard_map/ppermute | solution.py:274
  7.7 0.0 collective-permute-done.1.refs_1_
  7.7 0.0 copy-start.11
  7.7 0.0 copy-start.12
  7.7 0.0 copy-start.13
  7.7 0.0 copy-start.14
  7.7 0.6 %collective-permute-start.5 = (bf16[4,2,8,128]{3,2,1,0:T(8,128)(2,1)S(1)}, bf16[4,2,8,128]{3,2,1,0:T(8,128)(2,1)S(1)}, u32[]{:S(2)}, u32[]{:S(2)}) collective-permute-start(bf16[4,2,8,128]{3,2,1,0:T(8,128)(2,1)S(1)} %pad_maximum_fusion), channel_id=1, source_target_pairs={{0,3},{1,2},{2,1},{3,0},{4,7},{5,6},{6,5},{7,4},{8,11},{9,10},{10,... | collective-permute-start | bytes 49160 | tf_op jit(solution)/shard_map/ppermute | solution.py:274
  8.3 2.2 %collective-permute-start.4 = (bf16[4,2,8,128]{3,2,1,0:T(8,128)(2,1)S(1)}, bf16[4,2,8,128]{3,2,1,0:T(8,128)(2,1)S(1)}, u32[]{:S(2)}, u32[]{:S(2)}) collective-permute-start(bf16[4,2,8,128]{3,2,1,0:T(8,128)(2,1)S(1)} %pad_maximum_fusion), channel_id=1, source_target_pairs={{0,5},{1,4},{2,7},{3,6},{4,1},{5,0},{6,3},{7,2},{8,13},{9,12},{10,... | collective-permute-start | bytes 49160 | tf_op jit(solution)/shard_map/ppermute | solution.py:274
  10.5 0.0 copy-start.9
  10.5 0.0 copy-start.10
  10.5 0.0 copy-done.7
  10.5 0.0 copy-done.11
  10.5 0.0 copy-done.12
  10.5 0.0 copy-done.13
  10.5 0.0 copy-done.14
  10.5 0.6 %copy-done.9 = bf16[128,4]{0,1:T(4,128)(2,1)S(1)} copy-done((bf16[128,4]{0,1:T(4,128)(2,1)S(1)}, bf16[128,4]{0,1:T(4,128)(2,1)}, u32[]{:S(2)}) %copy-start.9) | copy-done | bytes 1048
  11.2 0.0 copy-done.10
  11.2 0.0 copy-start
  11.2 0.0 copy-start.1
  11.2 0.0 copy-start.2
  11.2 0.0 copy-start.3
  11.2 0.0 copy-start.4
  11.2 0.0 copy-start.5
  11.2 0.0 copy-start.6
  11.2 0.7 %shard_map.146 = (f32[256,128]{1,0:T(8,128)S(1)}, f32[256,128]{1,0:T(8,128)S(1)}, f32[3,128]{1,0:T(4,128)S(1)}, bf16[4,128]{1,0:T(4,128)(2,1)S(1)}, f32[8,128]{1,0:T(8,128)S(1)}) custom-call(s32[16]{0:T(128)S(1)} %copy-done.10, s32[16]{0:T(128)S(1)} %copy-done.11, bf16[128,128]{1,0:T(8,128)(2,1)S(1)} %copy-done.7, f32[1,128]{1,0:T(1,128)S(1)} %bitcast.7, ...), custom_call_target="tpu_custom_call" | custom-call | flops 1000000000 | bytes 1048576 | tf_op jit(solution)/shard_map/pallas_call | solution.py:247
  12.0 0.0 collective-permute-done.3.refs_3_
  12.0 0.0 collective-permute-done.2.refs_2_
  12.0 0.0 collective-permute-done.5.refs_5_
  12.0 0.0 collective-permute-done.4.refs_4_
  12.0 0.1 copy-done
  12.1 0.0 copy-done.1
  12.1 0.0 copy-done.2
  12.1 0.0 copy-done.3
  12.1 0.0 copy-done.4
  12.1 0.0 copy-done.5
  12.1 0.0 copy-done.6
  12.1 2.3 %shard_map.147 = bf16[2,8,128]{2,1,0:T(8,128)(2,1)} custom-call(bf16[2,2,8,128]{3,2,1,0:T(8,128)(2,1)S(1)} %bitcast_dynamic-update-slice_fusion.refs_0_, bf16[2,2,8,128]{3,2,1,0:T(8,128)(2,1)S(1)} %collective-permute-done.1.refs_1_, bf16[2,2,8,128]{3,2,1,0:T(8,128)(2,1)S(1)} %collective-permute-done.2.refs_2_, ...), custom_call_target="tpu_custom_call" | custom-call | tf_op jit(solution)/shard_map/pallas_call | solution.py:297
  (3 shorter events, 0.0 us)
Async XLA Ops:
  0.0 1.5 %collective-permute-start = (bf16[2,8,128]{2,1,0:T(8,128)(2,1)}, bf16[2,8,128]{2,1,0:T(8,128)(2,1)S(1)}, u32[]{:S(2)}, u32[]{:S(2)}) collective-permute-start(bf16[2,8,128]{2,1,0:T(8,128)(2,1)} %pair_ref.1), channel_id=1, source_target_pairs={{0,1},{1,0},{2,3},{3,2},{4,5},{5,4},{6,7},{7,6},{8,9},{9,8},{10,11... | collective-permute-start | bytes 12296 | tf_op jit(solution)/shard_map/ppermute | solution.py:274
  0.5 0.7 %copy-start.8 = (bf16[2,8,128]{2,1,0:T(8,128)(2,1)S(1)}, bf16[2,8,128]{2,1,0:T(8,128)(2,1)}, u32[]{:S(2)}) copy-start(bf16[2,8,128]{2,1,0:T(8,128)(2,1)} %pair_ref.1) | copy-start | bytes 12292
  1.1 9.4 %copy-start.7 = (bf16[128,128]{1,0:T(8,128)(2,1)S(1)}, bf16[128,128]{1,0:T(8,128)(2,1)}, u32[]{:S(2)}) copy-start(bf16[128,128]{1,0:T(8,128)(2,1)} %table_ref.1) | copy-start | bytes 98308
  1.5 6.2 %collective-permute-start.1 = (bf16[2,2,8,128]{3,2,1,0:T(8,128)(2,1)S(1)}, bf16[2,2,8,128]{3,2,1,0:T(8,128)(2,1)S(1)}, u32[]{:S(2)}, u32[]{:S(2)}) collective-permute-start(bf16[2,2,8,128]{3,2,1,0:T(8,128)(2,1)S(1)} %bitcast_dynamic-update-slice_fusion.refs_0_), channel_id=1, source_target_pairs={{0,9},{1,8},{2,11},{3,10},{4,13},{5,12},{6,15},{7,14},{8,1},{9,0},... | collective-permute-start | bytes 24584 | tf_op jit(solution)/shard_map/ppermute | solution.py:274
  5.2 6.8 %collective-permute-start.3 = (bf16[2,2,8,128]{3,2,1,0:T(8,128)(2,1)S(1)}, bf16[2,2,8,128]{3,2,1,0:T(8,128)(2,1)S(1)}, u32[]{:S(2)}, u32[]{:S(2)}) collective-permute-start(bf16[2,2,8,128]{3,2,1,0:T(8,128)(2,1)S(1)} %bitcast_dynamic-update-slice_fusion.refs_0_), channel_id=1, source_target_pairs={{0,15},{1,14},{2,13},{3,12},{4,11},{5,10},{6,9},{7,8},{8,7},{9,6},... | collective-permute-start | bytes 24584 | tf_op jit(solution)/shard_map/ppermute | solution.py:274
  7.4 4.6 %collective-permute-start.2 = (bf16[2,2,8,128]{3,2,1,0:T(8,128)(2,1)S(1)}, bf16[2,2,8,128]{3,2,1,0:T(8,128)(2,1)S(1)}, u32[]{:S(2)}, u32[]{:S(2)}) collective-permute-start(bf16[2,2,8,128]{3,2,1,0:T(8,128)(2,1)S(1)} %bitcast_dynamic-update-slice_fusion.refs_0_), channel_id=1, source_target_pairs={{0,7},{1,6},{2,5},{3,4},{4,3},{5,2},{6,1},{7,0},{8,15},{9,14},{10,... | collective-permute-start | bytes 24584 | tf_op jit(solution)/shard_map/ppermute | solution.py:274
  7.7 2.9 %copy-start.11 = (s32[16]{0:T(128)S(1)}, s32[16]{0:T(128)}, u32[]{:S(2)}) copy-start(s32[16]{0:T(128)} %pos_ref.1) | copy-start | bytes 196
  7.7 2.9 %copy-start.12 = (f32[128]{0:T(128)S(1)}, f32[128]{0:T(128)}, u32[]{:S(2)}) copy-start(f32[128]{0:T(128)} %param.21) | copy-start | bytes 1540
  7.7 2.9 %copy-start.13 = (f32[128]{0:T(128)S(1)}, f32[128]{0:T(128)}, u32[]{:S(2)}) copy-start(f32[128]{0:T(128)} %param.25) | copy-start | bytes 1540
  7.7 2.9 %copy-start.14 = (f32[128]{0:T(128)S(1)}, f32[128]{0:T(128)}, u32[]{:S(2)}) copy-start(f32[128]{0:T(128)} %param.27) | copy-start | bytes 1540
  7.7 4.3 %collective-permute-start.5 = (bf16[4,2,8,128]{3,2,1,0:T(8,128)(2,1)S(1)}, bf16[4,2,8,128]{3,2,1,0:T(8,128)(2,1)S(1)}, u32[]{:S(2)}, u32[]{:S(2)}) collective-permute-start(bf16[4,2,8,128]{3,2,1,0:T(8,128)(2,1)S(1)} %pad_maximum_fusion), channel_id=1, source_target_pairs={{0,3},{1,2},{2,1},{3,0},{4,7},{5,6},{6,5},{7,4},{8,11},{9,10},{10,... | collective-permute-start | bytes 49160 | tf_op jit(solution)/shard_map/ppermute | solution.py:274
  8.3 3.7 %collective-permute-start.4 = (bf16[4,2,8,128]{3,2,1,0:T(8,128)(2,1)S(1)}, bf16[4,2,8,128]{3,2,1,0:T(8,128)(2,1)S(1)}, u32[]{:S(2)}, u32[]{:S(2)}) collective-permute-start(bf16[4,2,8,128]{3,2,1,0:T(8,128)(2,1)S(1)} %pad_maximum_fusion), channel_id=1, source_target_pairs={{0,5},{1,4},{2,7},{3,6},{4,1},{5,0},{6,3},{7,2},{8,13},{9,12},{10,... | collective-permute-start | bytes 49160 | tf_op jit(solution)/shard_map/ppermute | solution.py:274
  10.5 0.7 %copy-start.9 = (bf16[128,4]{0,1:T(4,128)(2,1)S(1)}, bf16[128,4]{0,1:T(4,128)(2,1)}, u32[]{:S(2)}) copy-start(bf16[128,4]{0,1:T(4,128)(2,1)} %param.30) | copy-start | bytes 3076
  10.5 0.7 %copy-start.10 = (s32[16]{0:T(128)S(1)}, s32[16]{0:T(128)}, u32[]{:S(2)}) copy-start(s32[16]{0:T(128)} %mask_ref.1) | copy-start | bytes 196
  11.2 0.9 %copy-start = (bf16[128,384]{1,0:T(8,128)(2,1)S(1)}, bf16[128,384]{1,0:T(8,128)(2,1)}, u32[]{:S(2)}) copy-start(bf16[128,384]{1,0:T(8,128)(2,1)} %refs_15_.1) | copy-start | bytes 294916
  11.2 0.9 %copy-start.1 = (bf16[128,256]{1,0:T(8,128)(2,1)S(1)}, bf16[128,256]{1,0:T(8,128)(2,1)}, u32[]{:S(2)}) copy-start(bf16[128,256]{1,0:T(8,128)(2,1)} %refs_11_.1) | copy-start | bytes 196612
  11.2 0.9 %copy-start.2 = (bf16[128,256]{1,0:T(8,128)(2,1)S(1)}, bf16[128,256]{1,0:T(8,128)(2,1)}, u32[]{:S(2)}) copy-start(bf16[128,256]{1,0:T(8,128)(2,1)} %refs_12_.1) | copy-start | bytes 196612
  11.2 0.9 %copy-start.3 = (bf16[128,128]{1,0:T(8,128)(2,1)S(1)}, bf16[128,128]{1,0:T(8,128)(2,1)}, u32[]{:S(2)}) copy-start(bf16[128,128]{1,0:T(8,128)(2,1)} %refs_13_.1) | copy-start | bytes 98308
  11.2 0.9 %copy-start.4 = (bf16[128,128]{1,0:T(8,128)(2,1)S(1)}, bf16[128,128]{1,0:T(8,128)(2,1)}, u32[]{:S(2)}) copy-start(bf16[128,128]{1,0:T(8,128)(2,1)} %refs_14_.1) | copy-start | bytes 98308
  11.2 0.9 %copy-start.5 = (bf16[128,128]{1,0:T(8,128)(2,1)S(1)}, bf16[128,128]{1,0:T(8,128)(2,1)}, u32[]{:S(2)}) copy-start(bf16[128,128]{1,0:T(8,128)(2,1)} %refs_16_.1) | copy-start | bytes 98308
  11.2 0.9 %copy-start.6 = (bf16[128,128]{1,0:T(8,128)(2,1)S(1)}, bf16[128,128]{1,0:T(8,128)(2,1)}, u32[]{:S(2)}) copy-start(bf16[128,128]{1,0:T(8,128)(2,1)} %refs_17_.1) | copy-start | bytes 98308

commit v13 on v12

--- a/solution.py
+++ b/solution.py
@@ -19,6 +19,21 @@
     centred = values - mean_val
     var_val = jnp.mean(centred * centred, axis=-1, keepdims=True)
     return centred * lax.rsqrt(var_val + epsilon) * gain
+
+
+def lane_mean(values, terms):
+    parts = []
+    for _ in range(terms):
+        parts.append(values.astype(jnp.bfloat16))
+        values = values - parts[-1].astype(jnp.float32)
+    width = values.shape[1]
+    share = jnp.full((terms * width, width), 1.0 / width, jnp.bfloat16)
+    return dot(jnp.concatenate(parts, axis=1), share)
+
+
+def lane_norm(values, gain):
+    centred = values - lane_mean(values, 3)
+    return centred * lax.rsqrt(lane_mean(centred * centred, 2) + epsilon) * gain
 
 
 def sigmoid(values):
@@ -141,7 +156,7 @@
     base = base_ref[...] + rel_ref[...]
     base_ref[...] = base
 
-    normed = layer_norm(base, gains_ref[0:1]).astype(bf16)
+    normed = lane_norm(base, gains_ref[0:1]).astype(bf16)
     normed_ref[...] = normed.astype(f32)
     projected = sigmoid(dot(normed, in_gate_ref[...])) * dot(normed, in_weight_ref[...])
     pair_mask = pair_mask_ref[...]
@@ -168,10 +183,10 @@
         own += [ref[pl.ds(row_first + r, tokens, stride=tokens), :] for r in range(rows)]
         return jnp.concatenate(own, axis=0)
 
-    normed_out = layer_norm(products, gains_ref[1:2]).astype(bf16)
+    normed_out = lane_norm(products, gains_ref[1:2]).astype(bf16)
     out_gate = sigmoid(dot(chosen(normed_ref).astype(bf16), out_gate_ref[...]))
     updated = chosen(base_ref) + out_gate * dot(normed_out, out_weight_ref[...])
-    normed_att = layer_norm(updated, gains_ref[2:3]).astype(bf16)
+    normed_att = lane_norm(updated, gains_ref[2:3]).astype(bf16)
     own_pairs = rows * cols
     column_pairs = tokens * cols
     upd_ref[...] = updated[:column_pairs]
@@ -207,8 +222,8 @@
     key_bias = jnp.concatenate([key_bias_ref[...]] * (heads * rows), axis=0)
     scores = scores + biases + key_bias
     expo = jnp.exp(scores - jnp.max(scores, axis=-1, keepdims=True))
-    totals = jnp.sum(expo, axis=-1, keepdims=True)
-    mixed = dot(expo.astype(bf16), values) / totals
+    shares = 1.0 / jnp.sum(expo, axis=-1, keepdims=True)
+    mixed = dot(expo.astype(bf16), values) * shares
     attended = jnp.zeros((own_pairs, width), f32)
     for h in range(heads):
         attended = jnp.where(head_of == h, mixed[h * own_pairs : (h + 1) * own_pairs], attended)
@@ -427,7 +442,7 @@
     tokens = row_dim * rows
     whole_bytes = tokens * tokens * width * pair_in.dtype.itemsize
     blocks = row_dim * col_dim
-    tiled = cols % 8 == 0 and width % 128 == 0 and blocks == 16 and col_dim == 2
+    tiled = cols % 8 == 0 and width == 128 and blocks == 16 and col_dim == 2
     if whole_bytes <= WHOLE_PAIR_BYTES and tiled:
         return whole_pair_on_device(row_dim, pair_in, *others)
     return split_pair_on_device(pair_in, *others)

time: 14.6 us -> 14.9 us (1.021)
  Pallas kernels: 3.01 us -> 3.32 us
    pallas_call x1, Pallas kernels: 2.28 us -> 2.6 us  [whole_pair_on_device(): pl.pallas_call(functools.partial(whole_pair_kernel, row_dim, heads, order...]
where the time goes in v13:
time: 14.9 us; the launch traced here: 14.7 us
  starting transfers between devices  9.42 us (63%)
  Pallas kernels  3.32 us (22%)
  local copies, waits for them, and re-layouts  1.49 us (10%)
  waiting for transfers between devices  0.36 us (2%)
    ppermute x6, starting transfers between devices, move(): lax.ppermute(values, ('row', 'col'), [(device, device ^ step) for device...  9.42 us
    pallas_call x1, Pallas kernels, whole_pair_on_device(): pl.pallas_call(functools.partial(whole_pair_kernel, row_dim, heads, order...  2.6 us
    unnamed x30, local copies, waits for them, and re-layouts  1.48 us
    pallas_call x1, Pallas kernels, whole_pair_on_device(): pl.pallas_call(functools.partial(stage_kernel, cols), out_shape=[wide_out...  0.72 us
    ppermute x6, waiting for transfers between devices, move(): lax.ppermute(values, ('row', 'col'), [(device, device ^ step) for device...  0.36 us
  transfers between devices with their start and end apart: 6, of which 1 were waited for; matrix products, arithmetic and copies ran while one was open for 0% of the time, Pallas kernels for 5%

profile of v13, /device:TPU:0, one launch (start us, length us, event | category | flops | bytes accessed | tf_op | source)
XLA Modules:
  0.0 14.7 jit_solution(11439193937522420774)
XLA Ops:
  0.0 0.5 %collective-permute-start = (bf16[2,8,128]{2,1,0:T(8,128)(2,1)}, bf16[2,8,128]{2,1,0:T(8,128)(2,1)S(1)}, u32[]{:S(2)}, u32[]{:S(2)}) collective-permute-start(bf16[2,8,128]{2,1,0:T(8,128)(2,1)} %pair_ref.1), channel_id=1, source_target_pairs={{0,1},{1,0},{2,3},{3,2},{4,5},{5,4},{6,7},{7,6},{8,9},{9,8},{10,11... | collective-permute-start | bytes 12296 | tf_op jit(solution)/shard_map/ppermute | solution.py:289
  0.5 0.0 copy-start.8
  0.5 0.7 %copy-done.8 = bf16[2,8,128]{2,1,0:T(8,128)(2,1)S(1)} copy-done((bf16[2,8,128]{2,1,0:T(8,128)(2,1)S(1)}, bf16[2,8,128]{2,1,0:T(8,128)(2,1)}, u32[]{:S(2)}) %copy-start.8) | copy-done | bytes 4120
  1.1 0.0 copy-start.7
  1.1 0.3 %collective-permute-done = bf16[2,8,128]{2,1,0:T(8,128)(2,1)S(1)} collective-permute-done((bf16[2,8,128]{2,1,0:T(8,128)(2,1)}, bf16[2,8,128]{2,1,0:T(8,128)(2,1)S(1)}, u32[]{:S(2)}, u32[]{:S(2)}) %collective-permute-start) | collective-permute-done | bytes 4128 | tf_op jit(solution)/shard_map/ppermute | solution.py:289
  1.5 3.7 %collective-permute-start.1 = (bf16[2,2,8,128]{3,2,1,0:T(8,128)(2,1)S(1)}, bf16[2,2,8,128]{3,2,1,0:T(8,128)(2,1)S(1)}, u32[]{:S(2)}, u32[]{:S(2)}) collective-permute-start(bf16[2,2,8,128]{3,2,1,0:T(8,128)(2,1)S(1)} %bitcast_dynamic-update-slice_fusion.refs_0_), channel_id=1, source_target_pairs={{0,9},{1,8},{2,11},{3,10},{4,13},{5,12},{6,15},{7,14},{8,1},{9,0},... | collective-permute-start | bytes 24584 | tf_op jit(solution)/shard_map/ppermute | solution.py:289
  5.2 2.2 %collective-permute-start.3 = (bf16[2,2,8,128]{3,2,1,0:T(8,128)(2,1)S(1)}, bf16[2,2,8,128]{3,2,1,0:T(8,128)(2,1)S(1)}, u32[]{:S(2)}, u32[]{:S(2)}) collective-permute-start(bf16[2,2,8,128]{3,2,1,0:T(8,128)(2,1)S(1)} %bitcast_dynamic-update-slice_fusion.refs_0_), channel_id=1, source_target_pairs={{0,15},{1,14},{2,13},{3,12},{4,11},{5,10},{6,9},{7,8},{8,7},{9,6},... | collective-permute-start | bytes 24584 | tf_op jit(solution)/shard_map/ppermute | solution.py:289
  7.4 0.2 %collective-permute-start.2 = (bf16[2,2,8,128]{3,2,1,0:T(8,128)(2,1)S(1)}, bf16[2,2,8,128]{3,2,1,0:T(8,128)(2,1)S(1)}, u32[]{:S(2)}, u32[]{:S(2)}) collective-permute-start(bf16[2,2,8,128]{3,2,1,0:T(8,128)(2,1)S(1)} %bitcast_dynamic-update-slice_fusion.refs_0_), channel_id=1, source_target_pairs={{0,7},{1,6},{2,5},{3,4},{4,3},{5,2},{6,1},{7,0},{8,15},{9,14},{10,... | collective-permute-start | bytes 24584 | tf_op jit(solution)/shard_map/ppermute | solution.py:289
  7.7 0.0 collective-permute-done.1.refs_1_
  7.7 0.0 copy-start.11
  7.7 0.0 copy-start.12
  7.7 0.0 copy-start.13
  7.7 0.0 copy-start.14
  7.7 0.6 %collective-permute-start.5 = (bf16[4,2,8,128]{3,2,1,0:T(8,128)(2,1)S(1)}, bf16[4,2,8,128]{3,2,1,0:T(8,128)(2,1)S(1)}, u32[]{:S(2)}, u32[]{:S(2)}) collective-permute-start(bf16[4,2,8,128]{3,2,1,0:T(8,128)(2,1)S(1)} %pad_maximum_fusion), channel_id=1, source_target_pairs={{0,3},{1,2},{2,1},{3,0},{4,7},{5,6},{6,5},{7,4},{8,11},{9,10},{10,... | collective-permute-start | bytes 49160 | tf_op jit(solution)/shard_map/ppermute | solution.py:289
  8.3 2.2 %collective-permute-start.4 = (bf16[4,2,8,128]{3,2,1,0:T(8,128)(2,1)S(1)}, bf16[4,2,8,128]{3,2,1,0:T(8,128)(2,1)S(1)}, u32[]{:S(2)}, u32[]{:S(2)}) collective-permute-start(bf16[4,2,8,128]{3,2,1,0:T(8,128)(2,1)S(1)} %pad_maximum_fusion), channel_id=1, source_target_pairs={{0,5},{1,4},{2,7},{3,6},{4,1},{5,0},{6,3},{7,2},{8,13},{9,12},{10,... | collective-permute-start | bytes 49160 | tf_op jit(solution)/shard_map/ppermute | solution.py:289
  10.5 0.0 copy-start.9
  10.5 0.0 copy-start.10
  10.5 0.0 copy-done.7
  10.5 0.0 copy-done.11
  10.5 0.0 copy-done.12
  10.5 0.0 copy-done.13
  10.5 0.0 copy-done.14
  10.5 0.6 %copy-done.9 = bf16[128,4]{0,1:T(4,128)(2,1)S(1)} copy-done((bf16[128,4]{0,1:T(4,128)(2,1)S(1)}, bf16[128,4]{0,1:T(4,128)(2,1)}, u32[]{:S(2)}) %copy-start.9) | copy-done | bytes 1048
  11.2 0.0 copy-done.10
  11.2 0.0 copy-start
  11.2 0.0 copy-start.1
  11.2 0.0 copy-start.2
  11.2 0.0 copy-start.3
  11.2 0.0 copy-start.4
  11.2 0.0 copy-start.5
  11.2 0.0 copy-start.6
  11.2 0.7 %shard_map.146 = (f32[256,128]{1,0:T(8,128)S(1)}, f32[256,128]{1,0:T(8,128)S(1)}, f32[3,128]{1,0:T(4,128)S(1)}, bf16[4,128]{1,0:T(4,128)(2,1)S(1)}, f32[8,128]{1,0:T(8,128)S(1)}) custom-call(s32[16]{0:T(128)S(1)} %copy-done.10, s32[16]{0:T(128)S(1)} %copy-done.11, bf16[128,128]{1,0:T(8,128)(2,1)S(1)} %copy-done.7, f32[1,128]{1,0:T(1,128)S(1)} %bitcast.7, ...), custom_call_target="tpu_custom_call" | custom-call | flops 1000000000 | bytes 1048576 | tf_op jit(solution)/shard_map/pallas_call | solution.py:262
  12.0 0.0 collective-permute-done.3.refs_3_
  12.0 0.0 collective-permute-done.2.refs_2_
  12.0 0.0 collective-permute-done.5.refs_5_
  12.0 0.0 collective-permute-done.4.refs_4_
  12.0 0.1 copy-done
  12.1 0.0 copy-done.1
  12.1 0.0 copy-done.2
  12.1 0.0 copy-done.3
  12.1 0.0 copy-done.4
  12.1 0.0 copy-done.5
  12.1 0.0 copy-done.6
  12.1 2.6 %shard_map.147 = bf16[2,8,128]{2,1,0:T(8,128)(2,1)} custom-call(bf16[2,2,8,128]{3,2,1,0:T(8,128)(2,1)S(1)} %bitcast_dynamic-update-slice_fusion.refs_0_, bf16[2,2,8,128]{3,2,1,0:T(8,128)(2,1)S(1)} %collective-permute-done.1.refs_1_, bf16[2,2,8,128]{3,2,1,0:T(8,128)(2,1)S(1)} %collective-permute-done.2.refs_2_, ...), custom_call_target="tpu_custom_call" | custom-call | tf_op jit(solution)/shard_map/pallas_call | solution.py:312
  (3 shorter events, 0.0 us)
Async XLA Ops:
  0.0 1.5 %collective-permute-start = (bf16[2,8,128]{2,1,0:T(8,128)(2,1)}, bf16[2,8,128]{2,1,0:T(8,128)(2,1)S(1)}, u32[]{:S(2)}, u32[]{:S(2)}) collective-permute-start(bf16[2,8,128]{2,1,0:T(8,128)(2,1)} %pair_ref.1), channel_id=1, source_target_pairs={{0,1},{1,0},{2,3},{3,2},{4,5},{5,4},{6,7},{7,6},{8,9},{9,8},{10,11... | collective-permute-start | bytes 12296 | tf_op jit(solution)/shard_map/ppermute | solution.py:289
  0.5 0.7 %copy-start.8 = (bf16[2,8,128]{2,1,0:T(8,128)(2,1)S(1)}, bf16[2,8,128]{2,1,0:T(8,128)(2,1)}, u32[]{:S(2)}) copy-start(bf16[2,8,128]{2,1,0:T(8,128)(2,1)} %pair_ref.1) | copy-start | bytes 12292
  1.1 9.4 %copy-start.7 = (bf16[128,128]{1,0:T(8,128)(2,1)S(1)}, bf16[128,128]{1,0:T(8,128)(2,1)}, u32[]{:S(2)}) copy-start(bf16[128,128]{1,0:T(8,128)(2,1)} %table_ref.1) | copy-start | bytes 98308
  1.5 6.2 %collective-permute-start.1 = (bf16[2,2,8,128]{3,2,1,0:T(8,128)(2,1)S(1)}, bf16[2,2,8,128]{3,2,1,0:T(8,128)(2,1)S(1)}, u32[]{:S(2)}, u32[]{:S(2)}) collective-permute-start(bf16[2,2,8,128]{3,2,1,0:T(8,128)(2,1)S(1)} %bitcast_dynamic-update-slice_fusion.refs_0_), channel_id=1, source_target_pairs={{0,9},{1,8},{2,11},{3,10},{4,13},{5,12},{6,15},{7,14},{8,1},{9,0},... | collective-permute-start | bytes 24584 | tf_op jit(solution)/shard_map/ppermute | solution.py:289
  5.2 6.8 %collective-permute-start.3 = (bf16[2,2,8,128]{3,2,1,0:T(8,128)(2,1)S(1)}, bf16[2,2,8,128]{3,2,1,0:T(8,128)(2,1)S(1)}, u32[]{:S(2)}, u32[]{:S(2)}) collective-permute-start(bf16[2,2,8,128]{3,2,1,0:T(8,128)(2,1)S(1)} %bitcast_dynamic-update-slice_fusion.refs_0_), channel_id=1, source_target_pairs={{0,15},{1,14},{2,13},{3,12},{4,11},{5,10},{6,9},{7,8},{8,7},{9,6},... | collective-permute-start | bytes 24584 | tf_op jit(solution)/shard_map/ppermute | solution.py:289
  7.4 4.6 %collective-permute-start.2 = (bf16[2,2,8,128]{3,2,1,0:T(8,128)(2,1)S(1)}, bf16[2,2,8,128]{3,2,1,0:T(8,128)(2,1)S(1)}, u32[]{:S(2)}, u32[]{:S(2)}) collective-permute-start(bf16[2,2,8,128]{3,2,1,0:T(8,128)(2,1)S(1)} %bitcast_dynamic-update-slice_fusion.refs_0_), channel_id=1, source_target_pairs={{0,7},{1,6},{2,5},{3,4},{4,3},{5,2},{6,1},{7,0},{8,15},{9,14},{10,... | collective-permute-start | bytes 24584 | tf_op jit(solution)/shard_map/ppermute | solution.py:289
  7.7 2.9 %copy-start.11 = (s32[16]{0:T(128)S(1)}, s32[16]{0:T(128)}, u32[]{:S(2)}) copy-start(s32[16]{0:T(128)} %pos_ref.1) | copy-start | bytes 196
  7.7 2.9 %copy-start.12 = (f32[128]{0:T(128)S(1)}, f32[128]{0:T(128)}, u32[]{:S(2)}) copy-start(f32[128]{0:T(128)} %param.21) | copy-start | bytes 1540
  7.7 2.9 %copy-start.13 = (f32[128]{0:T(128)S(1)}, f32[128]{0:T(128)}, u32[]{:S(2)}) copy-start(f32[128]{0:T(128)} %param.25) | copy-start | bytes 1540
  7.7 2.9 %copy-start.14 = (f32[128]{0:T(128)S(1)}, f32[128]{0:T(128)}, u32[]{:S(2)}) copy-start(f32[128]{0:T(128)} %param.27) | copy-start | bytes 1540
  7.7 4.3 %collective-permute-start.5 = (bf16[4,2,8,128]{3,2,1,0:T(8,128)(2,1)S(1)}, bf16[4,2,8,128]{3,2,1,0:T(8,128)(2,1)S(1)}, u32[]{:S(2)}, u32[]{:S(2)}) collective-permute-start(bf16[4,2,8,128]{3,2,1,0:T(8,128)(2,1)S(1)} %pad_maximum_fusion), channel_id=1, source_target_pairs={{0,3},{1,2},{2,1},{3,0},{4,7},{5,6},{6,5},{7,4},{8,11},{9,10},{10,... | collective-permute-start | bytes 49160 | tf_op jit(solution)/shard_map/ppermute | solution.py:289
  8.3 3.7 %collective-permute-start.4 = (bf16[4,2,8,128]{3,2,1,0:T(8,128)(2,1)S(1)}, bf16[4,2,8,128]{3,2,1,0:T(8,128)(2,1)S(1)}, u32[]{:S(2)}, u32[]{:S(2)}) collective-permute-start(bf16[4,2,8,128]{3,2,1,0:T(8,128)(2,1)S(1)} %pad_maximum_fusion), channel_id=1, source_target_pairs={{0,5},{1,4},{2,7},{3,6},{4,1},{5,0},{6,3},{7,2},{8,13},{9,12},{10,... | collective-permute-start | bytes 49160 | tf_op jit(solution)/shard_map/ppermute | solution.py:289
  10.5 0.7 %copy-start.9 = (bf16[128,4]{0,1:T(4,128)(2,1)S(1)}, bf16[128,4]{0,1:T(4,128)(2,1)}, u32[]{:S(2)}) copy-start(bf16[128,4]{0,1:T(4,128)(2,1)} %param.30) | copy-start | bytes 3076
  10.5 0.7 %copy-start.10 = (s32[16]{0:T(128)S(1)}, s32[16]{0:T(128)}, u32[]{:S(2)}) copy-start(s32[16]{0:T(128)} %mask_ref.1) | copy-start | bytes 196
  11.2 0.9 %copy-start = (bf16[128,384]{1,0:T(8,128)(2,1)S(1)}, bf16[128,384]{1,0:T(8,128)(2,1)}, u32[]{:S(2)}) copy-start(bf16[128,384]{1,0:T(8,128)(2,1)} %refs_15_.1) | copy-start | bytes 294916
  11.2 0.9 %copy-start.1 = (bf16[128,256]{1,0:T(8,128)(2,1)S(1)}, bf16[128,256]{1,0:T(8,128)(2,1)}, u32[]{:S(2)}) copy-start(bf16[128,256]{1,0:T(8,128)(2,1)} %refs_11_.1) | copy-start | bytes 196612
  11.2 0.9 %copy-start.2 = (bf16[128,256]{1,0:T(8,128)(2,1)S(1)}, bf16[128,256]{1,0:T(8,128)(2,1)}, u32[]{:S(2)}) copy-start(bf16[128,256]{1,0:T(8,128)(2,1)} %refs_12_.1) | copy-start | bytes 196612
  11.2 0.9 %copy-start.3 = (bf16[128,128]{1,0:T(8,128)(2,1)S(1)}, bf16[128,128]{1,0:T(8,128)(2,1)}, u32[]{:S(2)}) copy-start(bf16[128,128]{1,0:T(8,128)(2,1)} %refs_13_.1) | copy-start | bytes 98308
  11.2 0.9 %copy-start.4 = (bf16[128,128]{1,0:T(8,128)(2,1)S(1)}, bf16[128,128]{1,0:T(8,128)(2,1)}, u32[]{:S(2)}) copy-start(bf16[128,128]{1,0:T(8,128)(2,1)} %refs_14_.1) | copy-start | bytes 98308
  11.2 0.9 %copy-start.5 = (bf16[128,128]{1,0:T(8,128)(2,1)S(1)}, bf16[128,128]{1,0:T(8,128)(2,1)}, u32[]{:S(2)}) copy-start(bf16[128,128]{1,0:T(8,128)(2,1)} %refs_16_.1) | copy-start | bytes 98308
  11.2 0.9 %copy-start.6 = (bf16[128,128]{1,0:T(8,128)(2,1)S(1)}, bf16[128,128]{1,0:T(8,128)(2,1)}, u32[]{:S(2)}) copy-start(bf16[128,128]{1,0:T(8,128)(2,1)} %refs_17_.1) | copy-start | bytes 98308

commit v14 on v12

--- a/solution.py
+++ b/solution.py
@@ -39,20 +39,14 @@
     return values.astype(jnp.bfloat16).astype(jnp.float32)
 
 
-def token_column(ref, first, shape):
-    sub = lax.broadcasted_iota(jnp.int32, shape, 0)
-    column = jnp.zeros(shape, jnp.int32)
-    for s in range(shape[0]):
-        column = jnp.where(sub == s, ref[first + s], column)
-    return column
-
-
-def own_kernel(pair_ref, chip_ref):
-    chip_ref[0] = pair_ref[...]
+def column_kernel(other_columns_ref):
+    sub = lax.broadcasted_iota(jnp.int32, other_columns_ref.shape, 0)
+    lane = lax.broadcasted_iota(jnp.int32, other_columns_ref.shape, 1)
+    other_columns_ref[...] = jnp.where(lane % other_columns_ref.shape[0] == sub, 0.0, -jnp.inf)
 
 
 def stage_kernel(
-    cols,
+    pair_ref,
     mask_ref,
     pos_ref,
     table_ref,
@@ -60,48 +54,96 @@
     norm_out_ref,
     att_norm_ref,
     att_bias_ref,
+    other_columns_ref,
+    chip_ref,
     rel_ref,
     pair_mask_ref,
     gains_ref,
     bias_ref,
     key_bias_ref,
 ):
+    chip_ref[0] = pair_ref[...]
     gains_ref[0:1] = norm_in_ref[...]
     gains_ref[1:2] = norm_out_ref[...]
     gains_ref[2:3] = att_norm_ref[...]
     bias_ref[...] = att_bias_ref[...]
-    tokens = pos_ref.shape[0]
-    bins = table_ref.shape[0]
-    lane = lax.broadcasted_iota(jnp.int32, (cols, bins), 1)
-    hot = [None] * (tokens * tokens // cols)
-    for half in range(tokens // cols):
-        column = token_column(pos_ref, half * cols, (cols, bins))
-        column_mask = token_column(mask_ref, half * cols, (cols, bins))
-        for i in range(tokens):
-            first = i * tokens + half * cols
-            pair_mask_ref[first : first + cols, :] = (column_mask * mask_ref[i]).astype(jnp.float32)
-            bucket = jnp.clip(pos_ref[i] - column, -(bins // 2), bins // 2 - 1) + bins // 2
-            hot[i * (tokens // cols) + half] = (bucket == lane).astype(jnp.float32)
-    sub = lax.broadcasted_iota(jnp.int32, key_bias_ref.shape, 0)
-    lane = lax.broadcasted_iota(jnp.int32, key_bias_ref.shape, 1)
-    key_mask = jnp.zeros(key_bias_ref.shape, jnp.int32)
-    for k in range(tokens):
-        key_mask = jnp.where(lane // cols == k, mask_ref[k], key_mask)
-    key_bias = (key_mask.astype(jnp.float32) - 1.0) * 1000000000.0
-    key_bias_ref[...] = jnp.where(lane % cols == sub, key_bias, -jnp.inf)
-    hot = jnp.concatenate(hot, axis=0).astype(jnp.bfloat16)
-    rel_ref[...] = dot(hot, table_ref[...])
-
-
-def whole_pair_kernel(row_dim, heads, orders, *refs):
-    whole_pair_steps(row_dim, heads, orders, refs[: len(orders)], *refs[len(orders) :])
+    tokens, (cols, lanes) = pos_ref.shape[1], key_bias_ref.shape
+    bins, width = table_ref.shape
+    f32 = jnp.float32
+
+    def by_row(ref):
+        sub = lax.broadcasted_iota(jnp.int32, (tokens, tokens), 0)
+        lane = lax.broadcasted_iota(jnp.int32, (tokens, tokens), 1)
+        spread = jnp.where(sub == lane, jnp.broadcast_to(ref[...].astype(f32), (tokens, tokens)), 0.0)
+        return jnp.broadcast_to(jnp.sum(spread, axis=1, keepdims=True), (tokens, bins))
+
+    pos, mask = by_row(pos_ref), by_row(mask_ref)
+    lane = lax.broadcasted_iota(jnp.int32, (cols, bins), 1).astype(f32)
+    centre = float(bins // 2)
+    hot = []
+    for i in range(tokens):
+        for first in range(0, tokens, cols):
+            bucket = jnp.clip(pos[i : i + 1] - pos[first : first + cols], -centre, centre - 1.0) + centre
+            hot.append((bucket == lane).astype(f32))
+            at = i * tokens + first
+            pair_mask_ref[at : at + cols, :] = mask[first : first + cols, :width] * mask[i : i + 1, :width]
+    rel_ref[...] = dot(jnp.concatenate(hot, axis=0).astype(jnp.bfloat16), table_ref[...])
+    key_of = lax.broadcasted_iota(jnp.int32, (tokens, lanes), 1) // cols
+    own_key = key_of == lax.broadcasted_iota(jnp.int32, (tokens, lanes), 0)
+    key_mask = jnp.sum(jnp.where(own_key, mask[:, :1], 0.0), axis=0, keepdims=True)
+    key_bias_ref[...] = (key_mask - 1.0) * 1000000000.0 + other_columns_ref[...]
+
+
+def tile_places(row_dim, rows, cols, order):
+    me = lax.axis_index("row") * 2 + lax.axis_index("col")
+    places = []
+    for place in order:
+        owner = me ^ place
+        for r in range(rows):
+            first = (owner // 2 * rows + r) * row_dim * rows + owner % 2 * cols
+            places.append(pl.ds(pl.multiple_of(first, cols), cols))
+    return places
+
+
+def edge_operands(pieces, places, rel_ref, pair_mask_ref, gain, in_gate, in_weight):
+    width = rel_ref.shape[1]
+    blocks = [piece[at].astype(jnp.float32) for piece in pieces for at in range(piece.shape[0])]
+    rows = len(places) // len(blocks)
+    tiles = [block[r] for block in blocks for r in range(rows)]
+    base = jnp.concatenate([tile + rel_ref[place, :] for tile, place in zip(tiles, places)], axis=0)
+    pair_mask = jnp.concatenate([pair_mask_ref[place, :] for place in places], axis=0)
+    normed = layer_norm(base, gain).astype(jnp.bfloat16)
+    projected = sigmoid(dot(normed, in_gate)) * dot(normed, in_weight)
+    left = round_bf16(projected[:, :width] * pair_mask)
+    right = round_bf16(projected[:, width:] * pair_mask)
+    return left, right, base, normed.astype(jnp.float32)
+
+
+def early_kernel(row_dim, orders, *refs):
+    piece_refs, (rel_ref, pair_mask_ref, gains_ref, in_weight_ref, in_gate_ref) = refs[:-9], refs[-9:-4]
+    rows, cols = piece_refs[0].shape[1:3]
+    places = tile_places(row_dim, rows, cols, sum(orders, ()))
+    found = edge_operands(
+        piece_refs, places, rel_ref, pair_mask_ref, gains_ref[0:1], in_gate_ref[...], in_weight_ref[...]
+    )
+    for ref, values in zip(refs[-4:], found):
+        ref[...] = values
+
+
+def whole_pair_kernel(row_dim, heads, early, orders, *refs):
+    whole_pair_steps(row_dim, heads, early, orders, refs[: len(orders)], *refs[len(orders) :])
 
 
 def whole_pair_steps(
     row_dim,
     heads,
+    early,
     orders,
     piece_refs,
+    early_left_ref,
+    early_right_ref,
+    early_base_ref,
+    early_normed_ref,
     rel_ref,
     pair_mask_ref,
     gains_ref,
@@ -129,24 +171,20 @@
     col_first = pl.multiple_of(lax.axis_index("col") * cols, cols)
     f32, bf16 = jnp.float32, jnp.bfloat16
 
-    me = lax.axis_index("row") * 2 + lax.axis_index("col")
-    for ref, order in zip(piece_refs, orders):
-        for at, place in enumerate(order):
-            owner = me ^ place
-            block = ref[at].astype(f32)
-            for r in range(rows):
-                first = (owner // 2 * rows + r) * tokens + owner % 2 * cols
-                base_ref[pl.ds(pl.multiple_of(first, cols), cols), :] = block[r]
-
-    base = base_ref[...] + rel_ref[...]
-    base_ref[...] = base
-
-    normed = layer_norm(base, gains_ref[0:1]).astype(bf16)
-    normed_ref[...] = normed.astype(f32)
-    projected = sigmoid(dot(normed, in_gate_ref[...])) * dot(normed, in_weight_ref[...])
-    pair_mask = pair_mask_ref[...]
-    left_ref[...] = round_bf16(projected[:, :width] * pair_mask)
-    right_ref[...] = round_bf16(projected[:, width:] * pair_mask)
+    def stored(places, found):
+        for ref, values in zip((left_ref, right_ref, base_ref, normed_ref), found):
+            for at, place in enumerate(places):
+                ref[place, :] = values[at * cols : (at + 1) * cols]
+
+    places = tile_places(row_dim, rows, cols, sum(orders, ()))
+    found = edge_operands(
+        piece_refs, places, rel_ref, pair_mask_ref, gains_ref[0:1], in_gate_ref[...], in_weight_ref[...]
+    )
+    stored(
+        tile_places(row_dim, rows, cols, sum(early, ())),
+        [ref[...] for ref in (early_left_ref, early_right_ref, early_base_ref, early_normed_ref)],
+    )
+    stored(places, found)
 
     right_at = [right_ref[pl.ds(col_first * tokens + m, cols, stride=tokens), :] for m in range(tokens)]
     products = []
@@ -207,8 +245,8 @@
     key_bias = jnp.concatenate([key_bias_ref[...]] * (heads * rows), axis=0)
     scores = scores + biases + key_bias
     expo = jnp.exp(scores - jnp.max(scores, axis=-1, keepdims=True))
-    totals = jnp.sum(expo, axis=-1, keepdims=True)
-    mixed = dot(expo.astype(bf16), values) / totals
+    shares = 1.0 / jnp.sum(expo, axis=-1, keepdims=True)
+    mixed = dot(expo.astype(bf16), values) * shares
     attended = jnp.zeros((own_pairs, width), f32)
     for h in range(heads):
         attended = jnp.where(head_of == h, mixed[h * own_pairs : (h + 1) * own_pairs], attended)
@@ -238,33 +276,43 @@
 ):
     rows, cols, width = pair_in.shape
     vmem = pl.BlockSpec(memory_space=pltpu.VMEM)
-    smem = pl.BlockSpec(memory_space=pltpu.SMEM)
     params = pltpu.CompilerParams(vmem_limit_bytes=16 * 1024 * 1024)
     tokens, heads = row_dim * rows, att_bias.shape[1]
 
     beside = pl.CostEstimate(flops=STAGE_FLOPS, bytes_accessed=2**20, transcendentals=0)
     wide_out = jax.ShapeDtypeStruct((tokens * tokens, width), jnp.float32)
-    staged = pl.pallas_call(
-        functools.partial(stage_kernel, cols),
+    key_shape = jax.ShapeDtypeStruct((cols, tokens * cols), jnp.float32)
+    other_columns = pl.pallas_call(
+        column_kernel,
+        out_shape=key_shape,
+        out_specs=vmem,
+        compiler_params=params,
+        cost_estimate=beside,
+    )()
+    chip, *staged = pl.pallas_call(
+        stage_kernel,
         out_shape=[
+            jax.ShapeDtypeStruct((2,) + pair_in.shape, pair_in.dtype),
             wide_out,
             wide_out,
             jax.ShapeDtypeStruct((3, width), jnp.float32),
             jax.ShapeDtypeStruct((heads, width), att_bias.dtype),
-            jax.ShapeDtypeStruct((cols, tokens * cols), jnp.float32),
+            key_shape,
         ],
-        in_specs=[smem] * 2 + [vmem] * 5,
-        out_specs=[vmem] * 5,
+        in_specs=[vmem] * 9,
+        out_specs=[vmem] * 6,
         compiler_params=params,
         cost_estimate=beside,
     )(
-        token_mask,
-        positions,
+        pair_in,
+        token_mask.reshape(1, tokens),
+        positions.reshape(1, tokens),
         relpos_table,
         tri_norm_in.reshape(1, width),
         tri_norm_out.reshape(1, width),
         att_norm.reshape(1, width),
         att_bias.T,
+        other_columns,
     )
 
     blocks = 2 * row_dim
@@ -274,34 +322,36 @@
         values = lax.ppermute(values, ("row", "col"), [(device, device ^ step) for device in range(blocks)])
         return values, tuple(place ^ step for place in order)
 
-    chip = pl.pallas_call(
-        own_kernel,
-        out_shape=jax.ShapeDtypeStruct((2,) + pair_in.shape, pair_in.dtype),
-        in_specs=[vmem],
-        out_specs=vmem,
-        compiler_params=params,
-        cost_estimate=beside,
-    )(pair_in)
     other, _ = move((pair_in, (0,)), 1)
     pieces = [(chip.at[1].set(other), (0, 1))]
     first = move(pieces[0], 9)
-    pieces += [first, move(pieces[0], 7), move(pieces[0], 15)]
+    pieces += [first, move(pieces[0], 15), move(pieces[0], 7)]
     both = jnp.concatenate([pieces[0][0], first[0]], axis=0), pieces[0][1] + first[1]
-    pieces += [move(both, 5), move(both, 3)]
-    gathered = [values for values, _ in pieces]
-    orders = [order for _, order in pieces]
-
+    pieces += [move(both, 3), move(both, 5)]
+    rel, pair_mask, gains, *_ = staged
+    early = [order for _, order in pieces[:4]]
+    half = jax.ShapeDtypeStruct((tokens * tokens // 2, width), jnp.float32)
+    halves = pl.pallas_call(
+        functools.partial(early_kernel, row_dim, early),
+        out_shape=[half] * 4,
+        in_specs=[vmem] * 9,
+        out_specs=[vmem] * 4,
+        compiler_params=params,
+        cost_estimate=beside,
+    )(*[values for values, _ in pieces[:4]], rel, pair_mask, gains, tri_in_weight, tri_in_gate)
+    late = [order for _, order in pieces[4:]]
+    gathered = [values for values, _ in pieces[4:]]
     weights = (tri_in_weight, tri_in_gate, tri_out_gate, tri_out_weight, att_qkv, att_gate, att_out)
     wide = pltpu.VMEM((tokens * tokens, width), jnp.float32)
     column = pltpu.VMEM((tokens * cols, width), jnp.float32)
     return pl.pallas_call(
-        functools.partial(whole_pair_kernel, row_dim, heads, orders),
+        functools.partial(whole_pair_kernel, row_dim, heads, early, late),
         out_shape=jax.ShapeDtypeStruct(pair_in.shape, pair_in.dtype),
-        in_specs=[vmem] * (len(gathered) + 5 + len(weights)),
+        in_specs=[vmem] * (len(gathered) + 9 + len(weights)),
         out_specs=vmem,
         scratch_shapes=[wide] * 4 + [column] * 2,
         compiler_params=params,
-    )(*gathered, *staged, *weights)
+    )(*gathered, *halves, *staged, *weights)
 
 
 def attend_column(query_col, key_col, value_col, bias_all, key_bias, block_rows):
@@ -427,7 +477,7 @@
     tokens = row_dim * rows
     whole_bytes = tokens * tokens * width * pair_in.dtype.itemsize
     blocks = row_dim * col_dim
-    tiled = cols % 8 == 0 and width % 128 == 0 and blocks == 16 and col_dim == 2
+    tiled = cols % 8 == 0 and width == 128 and blocks == 16 and col_dim == 2
     if whole_bytes <= WHOLE_PAIR_BYTES and tiled:
         return whole_pair_on_device(row_dim, pair_in, *others)
     return split_pair_on_device(pair_in, *others)

time: 14.6 us -> 14.7 us (level)
  waiting for transfers between devices: 0.36 us -> 1.04 us
  local copies, waits for them, and re-layouts: 1.49 us -> 1.16 us
  Pallas kernels: 3.01 us -> 2.74 us
    ppermute x6, waiting for transfers between devices: 0.36 us -> 1.04 us  [move(): lax.ppermute(values, ('row', 'col'), [(device, device ^ step) for device...]
    unnamed x30, local copies, waits for them, and re-layouts: 1.48 us -> 1.15 us
    pallas_call x3 -> x4, Pallas kernels: 3.01 us -> 2.74 us  [the longest x1 2.13 us: whole_pair_on_device(): pl.pallas_call(functools.partial(whole_pair_kernel, row_dim, heads, early...]
  transfers between devices with their start and end apart: 6 -> 6, of which waited for: 1 -> 3; matrix products, arithmetic and copies ran while one was open for 0% -> 0% of each run, Pallas kernels for 5% -> 4%
where the time goes in v14:
time: 14.7 us; the launch traced here: 14.4 us
  starting transfers between devices  9.4 us (64%)
  Pallas kernels  2.74 us (19%)
  local copies, waits for them, and re-layouts  1.16 us (8%)
  waiting for transfers between devices  1.04 us (7%)
    ppermute x6, starting transfers between devices, move(): lax.ppermute(values, ('row', 'col'), [(device, device ^ step) for device...  9.4 us
    pallas_call x1, Pallas kernels, whole_pair_on_device(): pl.pallas_call(functools.partial(whole_pair_kernel, row_dim, heads, early...  2.13 us
    unnamed x30, local copies, waits for them, and re-layouts  1.15 us
    ppermute x6, waiting for transfers between devices, move(): lax.ppermute(values, ('row', 'col'), [(device, device ^ step) for device...  1.04 us
    pallas_call x1, Pallas kernels, whole_pair_on_device(): pl.pallas_call(functools.partial(early_kernel, row_dim, early), out_shape...  0.38 us
  transfers between devices with their start and end apart: 6, of which 3 were waited for; matrix products, arithmetic and copies ran while one was open for 0% of the time, Pallas kernels for 4%

profile of v14, /device:TPU:0, one launch (start us, length us, event | category | flops | bytes accessed | tf_op | source)
XLA Modules:
  0.0 14.4 jit_solution(3658531717672315369)
XLA Ops:
  0.0 0.0 copy-start.7
  0.0 0.5 %collective-permute-start = (bf16[2,8,128]{2,1,0:T(8,128)(2,1)}, bf16[2,8,128]{2,1,0:T(8,128)(2,1)S(1)}, u32[]{:S(2)}, u32[]{:S(2)}) collective-permute-start(bf16[2,8,128]{2,1,0:T(8,128)(2,1)} %pair_ref.1), channel_id=1, source_target_pairs={{0,1},{1,0},{2,3},{3,2},{4,5},{5,4},{6,7},{7,6},{8,9},{9,8},{10,11... | collective-permute-start | bytes 12296 | tf_op jit(solution)/shard_map/ppermute | solution.py:322
  0.5 0.0 copy-start.11
  0.5 0.0 copy-start.12
  0.5 0.0 copy-start.13
  0.5 0.0 copy-start.14
  0.5 0.0 copy-start.8
  0.5 0.0 copy-start.9
  0.5 0.0 copy-start.10
  0.5 0.2 %copy-done.7 = bf16[128,128]{1,0:T(8,128)(2,1)S(1)} copy-done((bf16[128,128]{1,0:T(8,128)(2,1)S(1)}, bf16[128,128]{1,0:T(8,128)(2,1)}, u32[]{:S(2)}) %copy-start.7) | copy-done | bytes 32792
  0.8 0.4 %copy-done.11 = s32[16]{0:T(128)S(1)} copy-done((s32[16]{0:T(128)S(1)}, s32[16]{0:T(128)}, u32[]{:S(2)}) %copy-start.11) | copy-done | bytes 88
  1.1 0.0 copy-done.12
  1.1 0.0 copy-done.13
  1.1 0.0 copy-done.14
  1.2 0.0 copy-done.8
  1.2 0.0 copy-done.9
  1.2 0.0 copy-done.10
  1.2 0.0 copy-start.1
  1.2 0.0 copy-start.2
  1.2 0.2 %shard_map.146 = (bf16[2,2,8,128]{3,2,1,0:T(8,128)(2,1)S(1)}, f32[256,128]{1,0:T(8,128)S(1)}, f32[256,128]{1,0:T(8,128)S(1)}, f32[3,128]{1,0:T(4,128)S(1)}, bf16...) custom-call(bf16[2,8,128]{2,1,0:T(8,128)(2,1)S(1)} %copy-done.8, s32[1,16]{1,0:T(1,128)S(1)} %bitcast.9, ...), custom_call_target="tpu_custom_call" | custom-call | flops 1000000000 | bytes 1048576 | tf_op jit(solution)/shard_map/pallas_call | solution.py:292
  1.5 0.0 collective-permute-done
  1.5 3.7 %collective-permute-start.1 = (bf16[2,2,8,128]{3,2,1,0:T(8,128)(2,1)S(1)}, bf16[2,2,8,128]{3,2,1,0:T(8,128)(2,1)S(1)}, u32[]{:S(2)}, u32[]{:S(2)}) collective-permute-start(bf16[2,2,8,128]{3,2,1,0:T(8,128)(2,1)S(1)} %bitcast_dynamic-update-slice_fusion.refs_0_), channel_id=1, source_target_pairs={{0,9},{1,8},{2,11},{3,10},{4,13},{5,12},{6,15},{7,14},{8,1},{9,0},... | collective-permute-start | bytes 24584 | tf_op jit(solution)/shard_map/ppermute | solution.py:322
  5.2 2.2 %collective-permute-start.4 = (bf16[2,2,8,128]{3,2,1,0:T(8,128)(2,1)S(1)}, bf16[2,2,8,128]{3,2,1,0:T(8,128)(2,1)S(1)}, u32[]{:S(2)}, u32[]{:S(2)}) collective-permute-start(bf16[2,2,8,128]{3,2,1,0:T(8,128)(2,1)S(1)} %bitcast_dynamic-update-slice_fusion.refs_0_), channel_id=1, source_target_pairs={{0,15},{1,14},{2,13},{3,12},{4,11},{5,10},{6,9},{7,8},{8,7},{9,6},... | collective-permute-start | bytes 24584 | tf_op jit(solution)/shard_map/ppermute | solution.py:322
  7.4 0.2 %collective-permute-start.5 = (bf16[2,2,8,128]{3,2,1,0:T(8,128)(2,1)S(1)}, bf16[2,2,8,128]{3,2,1,0:T(8,128)(2,1)S(1)}, u32[]{:S(2)}, u32[]{:S(2)}) collective-permute-start(bf16[2,2,8,128]{3,2,1,0:T(8,128)(2,1)S(1)} %bitcast_dynamic-update-slice_fusion.refs_0_), channel_id=1, source_target_pairs={{0,7},{1,6},{2,5},{3,4},{4,3},{5,2},{6,1},{7,0},{8,15},{9,14},{10,... | collective-permute-start | bytes 24584 | tf_op jit(solution)/shard_map/ppermute | solution.py:322
  7.7 0.0 collective-permute-done.1.refs_1_
  7.7 0.5 %collective-permute-start.2 = (bf16[4,2,8,128]{3,2,1,0:T(8,128)(2,1)S(1)}, bf16[4,2,8,128]{3,2,1,0:T(8,128)(2,1)S(1)}, u32[]{:S(2)}, u32[]{:S(2)}) collective-permute-start(bf16[4,2,8,128]{3,2,1,0:T(8,128)(2,1)S(1)} %pad_maximum_fusion), channel_id=1, source_target_pairs={{0,3},{1,2},{2,1},{3,0},{4,7},{5,6},{6,5},{7,4},{8,11},{9,10},{10,... | collective-permute-start | bytes 49160 | tf_op jit(solution)/shard_map/ppermute | solution.py:322
  8.2 2.3 %collective-permute-start.3 = (bf16[4,2,8,128]{3,2,1,0:T(8,128)(2,1)S(1)}, bf16[4,2,8,128]{3,2,1,0:T(8,128)(2,1)S(1)}, u32[]{:S(2)}, u32[]{:S(2)}) collective-permute-start(bf16[4,2,8,128]{3,2,1,0:T(8,128)(2,1)S(1)} %pad_maximum_fusion), channel_id=1, source_target_pairs={{0,5},{1,4},{2,7},{3,6},{4,1},{5,0},{6,3},{7,2},{8,13},{9,12},{10,... | collective-permute-start | bytes 49160 | tf_op jit(solution)/shard_map/ppermute | solution.py:322
  10.5 0.6 %collective-permute-done.4.refs_2_ = bf16[2,2,8,128]{3,2,1,0:T(8,128)(2,1)S(1)} collective-permute-done((bf16[2,2,8,128]{3,2,1,0:T(8,128)(2,1)S(1)}, bf16[2,2,8,128]{3,2,1,0:T(8,128)(2,1)S(1)}, u32[]{:S(2)}, u32[]{:S(2)}) %collective-permute-start.4) | collective-permute-done | bytes 8224 | tf_op jit(solution)/shard_map/ppermute | solution.py:322
  11.0 0.4 %collective-permute-done.5.refs_3_ = bf16[2,2,8,128]{3,2,1,0:T(8,128)(2,1)S(1)} collective-permute-done((bf16[2,2,8,128]{3,2,1,0:T(8,128)(2,1)S(1)}, bf16[2,2,8,128]{3,2,1,0:T(8,128)(2,1)S(1)}, u32[]{:S(2)}, u32[]{:S(2)}) %collective-permute-start.5) | collective-permute-done | bytes 8224 | tf_op jit(solution)/shard_map/ppermute | solution.py:322
  11.4 0.0 copy-done.1
  11.4 0.0 copy-done.2
  11.4 0.0 copy-start
  11.4 0.0 copy-start.3
  11.4 0.0 copy-start.4
  11.4 0.0 copy-start.5
  11.4 0.0 copy-start.6
  11.4 0.4 %shard_map.147 = (f32[128,128]{1,0:T(8,128)S(1)}, f32[128,128]{1,0:T(8,128)S(1)}, f32[128,128]{1,0:T(8,128)S(1)}, f32[128,128]{1,0:T(8,128)S(1)}) custom-call(bf16[2,2,8,128]{3,2,1,0:T(8,128)(2,1)S(1)} %bitcast_dynamic-update-slice_fusion.refs_0_, bf16[2,2,8,128]{3,2,1,0:T(8,128)(2,1)S(1)} %collective-permute-done.1.refs_1_, ...), custom_call_target="tpu_custom_call" | custom-call | flops 1000000000 | bytes 1048576 | tf_op jit(solution)/shard_map/pallas_call | solution.py:334
  11.8 0.0 collective-permute-done.2.refs_0_
  11.8 0.1 collective-permute-done.3.refs_1_
  11.9 0.4 %copy-done = bf16[128,384]{1,0:T(8,128)(2,1)S(1)} copy-done((bf16[128,384]{1,0:T(8,128)(2,1)S(1)}, bf16[128,384]{1,0:T(8,128)(2,1)}, u32[]{:S(2)}) %copy-start) | copy-done | bytes 98328
  12.3 0.0 copy-done.3
  12.3 0.0 copy-done.4
  12.3 0.0 copy-done.5
  12.3 0.0 copy-done.6
  12.3 2.1 %shard_map.148 = bf16[2,8,128]{2,1,0:T(8,128)(2,1)} custom-call(bf16[4,2,8,128]{3,2,1,0:T(8,128)(2,1)S(1)} %collective-permute-done.2.refs_0_, bf16[4,2,8,128]{3,2,1,0:T(8,128)(2,1)S(1)} %collective-permute-done.3.refs_1_, f32[128,128]{1,0:T(8,128)S(1)} %get-tuple-element.31.refs_2_, f32[128,128]{1,0:T(8,128)S(1)} %get-tuple-element.32.refs_3_, ...), custom_call_target="tpu_custom_call" | custom-call | tf_op jit(solution)/shard_map/pallas_call | solution.py:347
  (3 shorter events, 0.0 us)
Async XLA Ops:
  0.0 0.8 %copy-start.7 = (bf16[128,128]{1,0:T(8,128)(2,1)S(1)}, bf16[128,128]{1,0:T(8,128)(2,1)}, u32[]{:S(2)}) copy-start(bf16[128,128]{1,0:T(8,128)(2,1)} %table_ref.1) | copy-start | bytes 98308
  0.0 1.5 %collective-permute-start = (bf16[2,8,128]{2,1,0:T(8,128)(2,1)}, bf16[2,8,128]{2,1,0:T(8,128)(2,1)S(1)}, u32[]{:S(2)}, u32[]{:S(2)}) collective-permute-start(bf16[2,8,128]{2,1,0:T(8,128)(2,1)} %pair_ref.1), channel_id=1, source_target_pairs={{0,1},{1,0},{2,3},{3,2},{4,5},{5,4},{6,7},{7,6},{8,9},{9,8},{10,11... | collective-permute-start | bytes 12296 | tf_op jit(solution)/shard_map/ppermute | solution.py:322
  0.5 0.7 %copy-start.11 = (s32[16]{0:T(128)S(1)}, s32[16]{0:T(128)}, u32[]{:S(2)}) copy-start(s32[16]{0:T(128)} %param.19) | copy-start | bytes 196
  0.5 0.7 %copy-start.12 = (f32[128]{0:T(128)S(1)}, f32[128]{0:T(128)}, u32[]{:S(2)}) copy-start(f32[128]{0:T(128)} %param.21) | copy-start | bytes 1540
  0.5 0.7 %copy-start.13 = (f32[128]{0:T(128)S(1)}, f32[128]{0:T(128)}, u32[]{:S(2)}) copy-start(f32[128]{0:T(128)} %param.25) | copy-start | bytes 1540
  0.5 0.7 %copy-start.14 = (f32[128]{0:T(128)S(1)}, f32[128]{0:T(128)}, u32[]{:S(2)}) copy-start(f32[128]{0:T(128)} %param.27) | copy-start | bytes 1540
  0.5 0.7 %copy-start.8 = (bf16[2,8,128]{2,1,0:T(8,128)(2,1)S(1)}, bf16[2,8,128]{2,1,0:T(8,128)(2,1)}, u32[]{:S(2)}) copy-start(bf16[2,8,128]{2,1,0:T(8,128)(2,1)} %pair_ref.1) | copy-start | bytes 12292
  0.5 0.7 %copy-start.9 = (bf16[128,4]{0,1:T(4,128)(2,1)S(1)}, bf16[128,4]{0,1:T(4,128)(2,1)}, u32[]{:S(2)}) copy-start(bf16[128,4]{0,1:T(4,128)(2,1)} %param.30) | copy-start | bytes 3076
  0.5 0.7 %copy-start.10 = (s32[16]{0:T(128)S(1)}, s32[16]{0:T(128)}, u32[]{:S(2)}) copy-start(s32[16]{0:T(128)} %param.18) | copy-start | bytes 196
  1.2 10.2 %copy-start.1 = (bf16[128,256]{1,0:T(8,128)(2,1)S(1)}, bf16[128,256]{1,0:T(8,128)(2,1)}, u32[]{:S(2)}) copy-start(bf16[128,256]{1,0:T(8,128)(2,1)} %refs_11_.1) | copy-start | bytes 196612
  1.2 10.2 %copy-start.2 = (bf16[128,256]{1,0:T(8,128)(2,1)S(1)}, bf16[128,256]{1,0:T(8,128)(2,1)}, u32[]{:S(2)}) copy-start(bf16[128,256]{1,0:T(8,128)(2,1)} %refs_12_.1) | copy-start | bytes 196612
  1.5 6.2 %collective-permute-start.1 = (bf16[2,2,8,128]{3,2,1,0:T(8,128)(2,1)S(1)}, bf16[2,2,8,128]{3,2,1,0:T(8,128)(2,1)S(1)}, u32[]{:S(2)}, u32[]{:S(2)}) collective-permute-start(bf16[2,2,8,128]{3,2,1,0:T(8,128)(2,1)S(1)} %bitcast_dynamic-update-slice_fusion.refs_0_), channel_id=1, source_target_pairs={{0,9},{1,8},{2,11},{3,10},{4,13},{5,12},{6,15},{7,14},{8,1},{9,0},... | collective-permute-start | bytes 24584 | tf_op jit(solution)/shard_map/ppermute | solution.py:322
  5.2 5.8 %collective-permute-start.4 = (bf16[2,2,8,128]{3,2,1,0:T(8,128)(2,1)S(1)}, bf16[2,2,8,128]{3,2,1,0:T(8,128)(2,1)S(1)}, u32[]{:S(2)}, u32[]{:S(2)}) collective-permute-start(bf16[2,2,8,128]{3,2,1,0:T(8,128)(2,1)S(1)} %bitcast_dynamic-update-slice_fusion.refs_0_), channel_id=1, source_target_pairs={{0,15},{1,14},{2,13},{3,12},{4,11},{5,10},{6,9},{7,8},{8,7},{9,6},... | collective-permute-start | bytes 24584 | tf_op jit(solution)/shard_map/ppermute | solution.py:322
  7.4 4.0 %collective-permute-start.5 = (bf16[2,2,8,128]{3,2,1,0:T(8,128)(2,1)S(1)}, bf16[2,2,8,128]{3,2,1,0:T(8,128)(2,1)S(1)}, u32[]{:S(2)}, u32[]{:S(2)}) collective-permute-start(bf16[2,2,8,128]{3,2,1,0:T(8,128)(2,1)S(1)} %bitcast_dynamic-update-slice_fusion.refs_0_), channel_id=1, source_target_pairs={{0,7},{1,6},{2,5},{3,4},{4,3},{5,2},{6,1},{7,0},{8,15},{9,14},{10,... | collective-permute-start | bytes 24584 | tf_op jit(solution)/shard_map/ppermute | solution.py:322
  7.7 4.2 %collective-permute-start.2 = (bf16[4,2,8,128]{3,2,1,0:T(8,128)(2,1)S(1)}, bf16[4,2,8,128]{3,2,1,0:T(8,128)(2,1)S(1)}, u32[]{:S(2)}, u32[]{:S(2)}) collective-permute-start(bf16[4,2,8,128]{3,2,1,0:T(8,128)(2,1)S(1)} %pad_maximum_fusion), channel_id=1, source_target_pairs={{0,3},{1,2},{2,1},{3,0},{4,7},{5,6},{6,5},{7,4},{8,11},{9,10},{10,... | collective-permute-start | bytes 49160 | tf_op jit(solution)/shard_map/ppermute | solution.py:322
  8.2 3.7 %collective-permute-start.3 = (bf16[4,2,8,128]{3,2,1,0:T(8,128)(2,1)S(1)}, bf16[4,2,8,128]{3,2,1,0:T(8,128)(2,1)S(1)}, u32[]{:S(2)}, u32[]{:S(2)}) collective-permute-start(bf16[4,2,8,128]{3,2,1,0:T(8,128)(2,1)S(1)} %pad_maximum_fusion), channel_id=1, source_target_pairs={{0,5},{1,4},{2,7},{3,6},{4,1},{5,0},{6,3},{7,2},{8,13},{9,12},{10,... | collective-permute-start | bytes 49160 | tf_op jit(solution)/shard_map/ppermute | solution.py:322
  11.4 0.9 %copy-start = (bf16[128,384]{1,0:T(8,128)(2,1)S(1)}, bf16[128,384]{1,0:T(8,128)(2,1)}, u32[]{:S(2)}) copy-start(bf16[128,384]{1,0:T(8,128)(2,1)} %refs_15_.1) | copy-start | bytes 294916
  11.4 0.9 %copy-start.3 = (bf16[128,128]{1,0:T(8,128)(2,1)S(1)}, bf16[128,128]{1,0:T(8,128)(2,1)}, u32[]{:S(2)}) copy-start(bf16[128,128]{1,0:T(8,128)(2,1)} %refs_13_.1) | copy-start | bytes 98308
  11.4 0.9 %copy-start.4 = (bf16[128,128]{1,0:T(8,128)(2,1)S(1)}, bf16[128,128]{1,0:T(8,128)(2,1)}, u32[]{:S(2)}) copy-start(bf16[128,128]{1,0:T(8,128)(2,1)} %refs_14_.1) | copy-start | bytes 98308
  11.4 0.9 %copy-start.5 = (bf16[128,128]{1,0:T(8,128)(2,1)S(1)}, bf16[128,128]{1,0:T(8,128)(2,1)}, u32[]{:S(2)}) copy-start(bf16[128,128]{1,0:T(8,128)(2,1)} %refs_16_.1) | copy-start | bytes 98308
  11.4 0.9 %copy-start.6 = (bf16[128,128]{1,0:T(8,128)(2,1)S(1)}, bf16[128,128]{1,0:T(8,128)(2,1)}, u32[]{:S(2)}) copy-start(bf16[128,128]{1,0:T(8,128)(2,1)} %refs_17_.1) | copy-start | bytes 98308

commit v15 on v14

--- a/solution.py
+++ b/solution.py
@@ -120,7 +120,8 @@
 
 
 def early_kernel(row_dim, orders, *refs):
-    piece_refs, (rel_ref, pair_mask_ref, gains_ref, in_weight_ref, in_gate_ref) = refs[:-9], refs[-9:-4]
+    piece_refs = refs[: len(orders)]
+    rel_ref, pair_mask_ref, gains_ref, in_weight_ref, in_gate_ref = refs[len(orders) : len(orders) + 5]
     rows, cols = piece_refs[0].shape[1:3]
     places = tile_places(row_dim, rows, cols, sum(orders, ()))
     found = edge_operands(
@@ -328,20 +329,20 @@
     pieces += [first, move(pieces[0], 15), move(pieces[0], 7)]
     both = jnp.concatenate([pieces[0][0], first[0]], axis=0), pieces[0][1] + first[1]
     pieces += [move(both, 3), move(both, 5)]
+    weights = (tri_in_weight, tri_in_gate, tri_out_gate, tri_out_weight, att_qkv, att_gate, att_out)
     rel, pair_mask, gains, *_ = staged
     early = [order for _, order in pieces[:4]]
     half = jax.ShapeDtypeStruct((tokens * tokens // 2, width), jnp.float32)
     halves = pl.pallas_call(
         functools.partial(early_kernel, row_dim, early),
         out_shape=[half] * 4,
-        in_specs=[vmem] * 9,
+        in_specs=[vmem] * (7 + len(weights)),
         out_specs=[vmem] * 4,
         compiler_params=params,
         cost_estimate=beside,
-    )(*[values for values, _ in pieces[:4]], rel, pair_mask, gains, tri_in_weight, tri_in_gate)
+    )(*[values for values, _ in pieces[:4]], rel, pair_mask, gains, *weights)
     late = [order for _, order in pieces[4:]]
     gathered = [values for values, _ in pieces[4:]]
-    weights = (tri_in_weight, tri_in_gate, tri_out_gate, tri_out_weight, att_qkv, att_gate, att_out)
     wide = pltpu.VMEM((tokens * tokens, width), jnp.float32)
     column = pltpu.VMEM((tokens * cols, width), jnp.float32)
     return pl.pallas_call(

time: 14.7 us -> 14.3 us (0.973)
  local copies, waits for them, and re-layouts: 1.16 us -> 0.77 us
    unnamed x30, local copies, waits for them, and re-layouts: 1.15 us -> 0.76 us
where the time goes in v15:
time: 14.3 us; the launch traced here: 14.1 us
  starting transfers between devices  9.42 us (66%)
  Pallas kernels  2.71 us (19%)
  waiting for transfers between devices  1.01 us (7%)
  local copies, waits for them, and re-layouts  0.77 us (5%)
  between operations  0.15 us (1%)
    ppermute x6, starting transfers between devices, move(): lax.ppermute(values, ('row', 'col'), [(device, device ^ step) for device...  9.42 us
    pallas_call x1, Pallas kernels, whole_pair_on_device(): pl.pallas_call(functools.partial(whole_pair_kernel, row_dim, heads, early...  2.1 us
    ppermute x6, waiting for transfers between devices, move(): lax.ppermute(values, ('row', 'col'), [(device, device ^ step) for device...  1.01 us
    unnamed x30, local copies, waits for them, and re-layouts  0.76 us
    pallas_call x1, Pallas kernels, whole_pair_on_device(): pl.pallas_call(functools.partial(early_kernel, row_dim, early), out_shape...  0.38 us
  transfers between devices with their start and end apart: 6, of which 3 were waited for; matrix products, arithmetic and copies ran while one was open for 0% of the time, Pallas kernels for 4%

profile of v15, /device:TPU:0, one launch (start us, length us, event | category | flops | bytes accessed | tf_op | source)
XLA Modules:
  0.0 14.1 jit_solution(14258936494146977341)
XLA Ops:
  0.0 0.0 copy-start.7
  0.0 0.5 %collective-permute-start = (bf16[2,8,128]{2,1,0:T(8,128)(2,1)}, bf16[2,8,128]{2,1,0:T(8,128)(2,1)S(1)}, u32[]{:S(2)}, u32[]{:S(2)}) collective-permute-start(bf16[2,8,128]{2,1,0:T(8,128)(2,1)} %pair_ref.1), channel_id=1, source_target_pairs={{0,1},{1,0},{2,3},{3,2},{4,5},{5,4},{6,7},{7,6},{8,9},{9,8},{10,11... | collective-permute-start | bytes 12296 | tf_op jit(solution)/shard_map/ppermute | solution.py:323
  0.5 0.0 copy-start.11
  0.5 0.0 copy-start.12
  0.5 0.0 copy-start.13
  0.5 0.0 copy-start.14
  0.5 0.0 copy-start.8
  0.5 0.0 copy-start.9
  0.5 0.0 copy-start.10
  0.5 0.2 %copy-done.7 = bf16[128,128]{1,0:T(8,128)(2,1)S(1)} copy-done((bf16[128,128]{1,0:T(8,128)(2,1)S(1)}, bf16[128,128]{1,0:T(8,128)(2,1)}, u32[]{:S(2)}) %copy-start.7) | copy-done | bytes 32792
  0.8 0.4 %copy-done.11 = s32[16]{0:T(128)S(1)} copy-done((s32[16]{0:T(128)S(1)}, s32[16]{0:T(128)}, u32[]{:S(2)}) %copy-start.11) | copy-done | bytes 88
  1.1 0.0 copy-done.12
  1.1 0.0 copy-done.13
  1.1 0.0 copy-done.14
  1.2 0.0 copy-done.8
  1.2 0.0 copy-done.9
  1.2 0.0 copy-done.10
  1.2 0.0 copy-start
  1.2 0.0 copy-start.1
  1.2 0.0 copy-start.2
  1.2 0.0 copy-start.4
  1.2 0.0 copy-start.5
  1.3 0.0 copy-start.6
  1.3 0.2 %shard_map.146 = (bf16[2,2,8,128]{3,2,1,0:T(8,128)(2,1)S(1)}, f32[256,128]{1,0:T(8,128)S(1)}, f32[256,128]{1,0:T(8,128)S(1)}, f32[3,128]{1,0:T(4,128)S(1)}, bf16...) custom-call(bf16[2,8,128]{2,1,0:T(8,128)(2,1)S(1)} %copy-done.8, s32[1,16]{1,0:T(1,128)S(1)} %bitcast.9, ...), custom_call_target="tpu_custom_call" | custom-call | flops 1000000000 | bytes 1048576 | tf_op jit(solution)/shard_map/pallas_call | solution.py:293
  1.5 0.0 copy-start.3
  1.5 0.0 collective-permute-done
  1.5 3.8 %collective-permute-start.1 = (bf16[2,2,8,128]{3,2,1,0:T(8,128)(2,1)S(1)}, bf16[2,2,8,128]{3,2,1,0:T(8,128)(2,1)S(1)}, u32[]{:S(2)}, u32[]{:S(2)}) collective-permute-start(bf16[2,2,8,128]{3,2,1,0:T(8,128)(2,1)S(1)} %bitcast_dynamic-update-slice_fusion.refs_0_), channel_id=1, source_target_pairs={{0,9},{1,8},{2,11},{3,10},{4,13},{5,12},{6,15},{7,14},{8,1},{9,0},... | collective-permute-start | bytes 24584 | tf_op jit(solution)/shard_map/ppermute | solution.py:323
  5.3 2.1 %collective-permute-start.4 = (bf16[2,2,8,128]{3,2,1,0:T(8,128)(2,1)S(1)}, bf16[2,2,8,128]{3,2,1,0:T(8,128)(2,1)S(1)}, u32[]{:S(2)}, u32[]{:S(2)}) collective-permute-start(bf16[2,2,8,128]{3,2,1,0:T(8,128)(2,1)S(1)} %bitcast_dynamic-update-slice_fusion.refs_0_), channel_id=1, source_target_pairs={{0,15},{1,14},{2,13},{3,12},{4,11},{5,10},{6,9},{7,8},{8,7},{9,6},... | collective-permute-start | bytes 24584 | tf_op jit(solution)/shard_map/ppermute | solution.py:323
  7.4 0.2 %collective-permute-start.5 = (bf16[2,2,8,128]{3,2,1,0:T(8,128)(2,1)S(1)}, bf16[2,2,8,128]{3,2,1,0:T(8,128)(2,1)S(1)}, u32[]{:S(2)}, u32[]{:S(2)}) collective-permute-start(bf16[2,2,8,128]{3,2,1,0:T(8,128)(2,1)S(1)} %bitcast_dynamic-update-slice_fusion.refs_0_), channel_id=1, source_target_pairs={{0,7},{1,6},{2,5},{3,4},{4,3},{5,2},{6,1},{7,0},{8,15},{9,14},{10,... | collective-permute-start | bytes 24584 | tf_op jit(solution)/shard_map/ppermute | solution.py:323
  7.7 0.0 collective-permute-done.1.refs_1_
  7.7 0.5 %collective-permute-start.2 = (bf16[4,2,8,128]{3,2,1,0:T(8,128)(2,1)S(1)}, bf16[4,2,8,128]{3,2,1,0:T(8,128)(2,1)S(1)}, u32[]{:S(2)}, u32[]{:S(2)}) collective-permute-start(bf16[4,2,8,128]{3,2,1,0:T(8,128)(2,1)S(1)} %pad_maximum_fusion), channel_id=1, source_target_pairs={{0,3},{1,2},{2,1},{3,0},{4,7},{5,6},{6,5},{7,4},{8,11},{9,10},{10,... | collective-permute-start | bytes 49160 | tf_op jit(solution)/shard_map/ppermute | solution.py:323
  8.2 2.3 %collective-permute-start.3 = (bf16[4,2,8,128]{3,2,1,0:T(8,128)(2,1)S(1)}, bf16[4,2,8,128]{3,2,1,0:T(8,128)(2,1)S(1)}, u32[]{:S(2)}, u32[]{:S(2)}) collective-permute-start(bf16[4,2,8,128]{3,2,1,0:T(8,128)(2,1)S(1)} %pad_maximum_fusion), channel_id=1, source_target_pairs={{0,5},{1,4},{2,7},{3,6},{4,1},{5,0},{6,3},{7,2},{8,13},{9,12},{10,... | collective-permute-start | bytes 49160 | tf_op jit(solution)/shard_map/ppermute | solution.py:323
  10.5 0.6 %collective-permute-done.4.refs_2_ = bf16[2,2,8,128]{3,2,1,0:T(8,128)(2,1)S(1)} collective-permute-done((bf16[2,2,8,128]{3,2,1,0:T(8,128)(2,1)S(1)}, bf16[2,2,8,128]{3,2,1,0:T(8,128)(2,1)S(1)}, u32[]{:S(2)}, u32[]{:S(2)}) %collective-permute-start.4) | collective-permute-done | bytes 8224 | tf_op jit(solution)/shard_map/ppermute | solution.py:323
  11.1 0.3 %collective-permute-done.5.refs_3_ = bf16[2,2,8,128]{3,2,1,0:T(8,128)(2,1)S(1)} collective-permute-done((bf16[2,2,8,128]{3,2,1,0:T(8,128)(2,1)S(1)}, bf16[2,2,8,128]{3,2,1,0:T(8,128)(2,1)S(1)}, u32[]{:S(2)}, u32[]{:S(2)}) %collective-permute-start.5) | collective-permute-done | bytes 8224 | tf_op jit(solution)/shard_map/ppermute | solution.py:323
  11.4 0.0 copy-done
  11.4 0.0 copy-done.1
  11.4 0.0 copy-done.2
  11.4 0.0 copy-done.4
  11.4 0.0 copy-done.5
  11.4 0.0 copy-done.6
  11.4 0.0 copy-done.3
  11.4 0.4 %shard_map.147 = (f32[128,128]{1,0:T(8,128)S(1)}, f32[128,128]{1,0:T(8,128)S(1)}, f32[128,128]{1,0:T(8,128)S(1)}, f32[128,128]{1,0:T(8,128)S(1)}) custom-call(bf16[2,2,8,128]{3,2,1,0:T(8,128)(2,1)S(1)} %bitcast_dynamic-update-slice_fusion.refs_0_, bf16[2,2,8,128]{3,2,1,0:T(8,128)(2,1)S(1)} %collective-permute-done.1.refs_1_, ...), custom_call_target="tpu_custom_call" | custom-call | flops 1000000000 | bytes 1048576 | tf_op jit(solution)/shard_map/pallas_call | solution.py:336
  11.8 0.0 collective-permute-done.2.refs_0_
  11.8 0.1 collective-permute-done.3.refs_1_
  12.0 2.1 %shard_map.148 = bf16[2,8,128]{2,1,0:T(8,128)(2,1)} custom-call(bf16[4,2,8,128]{3,2,1,0:T(8,128)(2,1)S(1)} %collective-permute-done.2.refs_0_, bf16[4,2,8,128]{3,2,1,0:T(8,128)(2,1)S(1)} %collective-permute-done.3.refs_1_, f32[128,128]{1,0:T(8,128)S(1)} %get-tuple-element.31.refs_2_, f32[128,128]{1,0:T(8,128)S(1)} %get-tuple-element.32.refs_3_, ...), custom_call_target="tpu_custom_call" | custom-call | tf_op jit(solution)/shard_map/pallas_call | solution.py:348
  (3 shorter events, 0.0 us)
Async XLA Ops:
  0.0 0.8 %copy-start.7 = (bf16[128,128]{1,0:T(8,128)(2,1)S(1)}, bf16[128,128]{1,0:T(8,128)(2,1)}, u32[]{:S(2)}) copy-start(bf16[128,128]{1,0:T(8,128)(2,1)} %table_ref.1) | copy-start | bytes 98308
  0.0 1.5 %collective-permute-start = (bf16[2,8,128]{2,1,0:T(8,128)(2,1)}, bf16[2,8,128]{2,1,0:T(8,128)(2,1)S(1)}, u32[]{:S(2)}, u32[]{:S(2)}) collective-permute-start(bf16[2,8,128]{2,1,0:T(8,128)(2,1)} %pair_ref.1), channel_id=1, source_target_pairs={{0,1},{1,0},{2,3},{3,2},{4,5},{5,4},{6,7},{7,6},{8,9},{9,8},{10,11... | collective-permute-start | bytes 12296 | tf_op jit(solution)/shard_map/ppermute | solution.py:323
  0.5 0.7 %copy-start.11 = (s32[16]{0:T(128)S(1)}, s32[16]{0:T(128)}, u32[]{:S(2)}) copy-start(s32[16]{0:T(128)} %param.19) | copy-start | bytes 196
  0.5 0.7 %copy-start.12 = (f32[128]{0:T(128)S(1)}, f32[128]{0:T(128)}, u32[]{:S(2)}) copy-start(f32[128]{0:T(128)} %param.21) | copy-start | bytes 1540
  0.5 0.7 %copy-start.13 = (f32[128]{0:T(128)S(1)}, f32[128]{0:T(128)}, u32[]{:S(2)}) copy-start(f32[128]{0:T(128)} %param.25) | copy-start | bytes 1540
  0.5 0.7 %copy-start.14 = (f32[128]{0:T(128)S(1)}, f32[128]{0:T(128)}, u32[]{:S(2)}) copy-start(f32[128]{0:T(128)} %param.27) | copy-start | bytes 1540
  0.5 0.7 %copy-start.8 = (bf16[2,8,128]{2,1,0:T(8,128)(2,1)S(1)}, bf16[2,8,128]{2,1,0:T(8,128)(2,1)}, u32[]{:S(2)}) copy-start(bf16[2,8,128]{2,1,0:T(8,128)(2,1)} %pair_ref.1) | copy-start | bytes 12292
  0.5 0.7 %copy-start.9 = (bf16[128,4]{0,1:T(4,128)(2,1)S(1)}, bf16[128,4]{0,1:T(4,128)(2,1)}, u32[]{:S(2)}) copy-start(bf16[128,4]{0,1:T(4,128)(2,1)} %param.30) | copy-start | bytes 3076
  0.5 0.7 %copy-start.10 = (s32[16]{0:T(128)S(1)}, s32[16]{0:T(128)}, u32[]{:S(2)}) copy-start(s32[16]{0:T(128)} %param.18) | copy-start | bytes 196
  1.2 10.2 %copy-start = (bf16[128,384]{1,0:T(8,128)(2,1)S(1)}, bf16[128,384]{1,0:T(8,128)(2,1)}, u32[]{:S(2)}) copy-start(bf16[128,384]{1,0:T(8,128)(2,1)} %refs_15_.1) | copy-start | bytes 294916
  1.2 10.2 %copy-start.1 = (bf16[128,256]{1,0:T(8,128)(2,1)S(1)}, bf16[128,256]{1,0:T(8,128)(2,1)}, u32[]{:S(2)}) copy-start(bf16[128,256]{1,0:T(8,128)(2,1)} %refs_11_.3) | copy-start | bytes 196612
  1.2 10.2 %copy-start.2 = (bf16[128,256]{1,0:T(8,128)(2,1)S(1)}, bf16[128,256]{1,0:T(8,128)(2,1)}, u32[]{:S(2)}) copy-start(bf16[128,256]{1,0:T(8,128)(2,1)} %refs_12_.3) | copy-start | bytes 196612
  1.2 10.2 %copy-start.4 = (bf16[128,128]{1,0:T(8,128)(2,1)S(1)}, bf16[128,128]{1,0:T(8,128)(2,1)}, u32[]{:S(2)}) copy-start(bf16[128,128]{1,0:T(8,128)(2,1)} %refs_14_.1) | copy-start | bytes 98308
  1.2 10.2 %copy-start.5 = (bf16[128,128]{1,0:T(8,128)(2,1)S(1)}, bf16[128,128]{1,0:T(8,128)(2,1)}, u32[]{:S(2)}) copy-start(bf16[128,128]{1,0:T(8,128)(2,1)} %refs_16_.1) | copy-start | bytes 98308
  1.3 10.2 %copy-start.6 = (bf16[128,128]{1,0:T(8,128)(2,1)S(1)}, bf16[128,128]{1,0:T(8,128)(2,1)}, u32[]{:S(2)}) copy-start(bf16[128,128]{1,0:T(8,128)(2,1)} %refs_17_.1) | copy-start | bytes 98308
  1.5 9.9 %copy-start.3 = (bf16[128,128]{1,0:T(8,128)(2,1)S(1)}, bf16[128,128]{1,0:T(8,128)(2,1)}, u32[]{:S(2)}) copy-start(bf16[128,128]{1,0:T(8,128)(2,1)} %refs_13_.3) | copy-start | bytes 98308
  1.5 6.1 %collective-permute-start.1 = (bf16[2,2,8,128]{3,2,1,0:T(8,128)(2,1)S(1)}, bf16[2,2,8,128]{3,2,1,0:T(8,128)(2,1)S(1)}, u32[]{:S(2)}, u32[]{:S(2)}) collective-permute-start(bf16[2,2,8,128]{3,2,1,0:T(8,128)(2,1)S(1)} %bitcast_dynamic-update-slice_fusion.refs_0_), channel_id=1, source_target_pairs={{0,9},{1,8},{2,11},{3,10},{4,13},{5,12},{6,15},{7,14},{8,1},{9,0},... | collective-permute-start | bytes 24584 | tf_op jit(solution)/shard_map/ppermute | solution.py:323
  5.3 5.8 %collective-permute-start.4 = (bf16[2,2,8,128]{3,2,1,0:T(8,128)(2,1)S(1)}, bf16[2,2,8,128]{3,2,1,0:T(8,128)(2,1)S(1)}, u32[]{:S(2)}, u32[]{:S(2)}) collective-permute-start(bf16[2,2,8,128]{3,2,1,0:T(8,128)(2,1)S(1)} %bitcast_dynamic-update-slice_fusion.refs_0_), channel_id=1, source_target_pairs={{0,15},{1,14},{2,13},{3,12},{4,11},{5,10},{6,9},{7,8},{8,7},{9,6},... | collective-permute-start | bytes 24584 | tf_op jit(solution)/shard_map/ppermute | solution.py:323
  7.4 4.0 %collective-permute-start.5 = (bf16[2,2,8,128]{3,2,1,0:T(8,128)(2,1)S(1)}, bf16[2,2,8,128]{3,2,1,0:T(8,128)(2,1)S(1)}, u32[]{:S(2)}, u32[]{:S(2)}) collective-permute-start(bf16[2,2,8,128]{3,2,1,0:T(8,128)(2,1)S(1)} %bitcast_dynamic-update-slice_fusion.refs_0_), channel_id=1, source_target_pairs={{0,7},{1,6},{2,5},{3,4},{4,3},{5,2},{6,1},{7,0},{8,15},{9,14},{10,... | collective-permute-start | bytes 24584 | tf_op jit(solution)/shard_map/ppermute | solution.py:323
  7.7 4.2 %collective-permute-start.2 = (bf16[4,2,8,128]{3,2,1,0:T(8,128)(2,1)S(1)}, bf16[4,2,8,128]{3,2,1,0:T(8,128)(2,1)S(1)}, u32[]{:S(2)}, u32[]{:S(2)}) collective-permute-start(bf16[4,2,8,128]{3,2,1,0:T(8,128)(2,1)S(1)} %pad_maximum_fusion), channel_id=1, source_target_pairs={{0,3},{1,2},{2,1},{3,0},{4,7},{5,6},{6,5},{7,4},{8,11},{9,10},{10,... | collective-permute-start | bytes 49160 | tf_op jit(solution)/shard_map/ppermute | solution.py:323
  8.2 3.8 %collective-permute-start.3 = (bf16[4,2,8,128]{3,2,1,0:T(8,128)(2,1)S(1)}, bf16[4,2,8,128]{3,2,1,0:T(8,128)(2,1)S(1)}, u32[]{:S(2)}, u32[]{:S(2)}) collective-permute-start(bf16[4,2,8,128]{3,2,1,0:T(8,128)(2,1)S(1)} %pad_maximum_fusion), channel_id=1, source_target_pairs={{0,5},{1,4},{2,7},{3,6},{4,1},{5,0},{6,3},{7,2},{8,13},{9,12},{10,... | collective-permute-start | bytes 49160 | tf_op jit(solution)/shard_map/ppermute | solution.py:323

commit v16 on v15

--- a/solution.py
+++ b/solution.py
@@ -42,7 +42,8 @@
 def column_kernel(other_columns_ref):
     sub = lax.broadcasted_iota(jnp.int32, other_columns_ref.shape, 0)
     lane = lax.broadcasted_iota(jnp.int32, other_columns_ref.shape, 1)
-    other_columns_ref[...] = jnp.where(lane % other_columns_ref.shape[0] == sub, 0.0, -jnp.inf)
+    cols, lanes = other_columns_ref.shape
+    other_columns_ref[...] = jnp.where(lane // (lanes // cols) == sub, 0.0, -jnp.inf)
 
 
 def stage_kernel(
@@ -88,7 +89,7 @@
             at = i * tokens + first
             pair_mask_ref[at : at + cols, :] = mask[first : first + cols, :width] * mask[i : i + 1, :width]
     rel_ref[...] = dot(jnp.concatenate(hot, axis=0).astype(jnp.bfloat16), table_ref[...])
-    key_of = lax.broadcasted_iota(jnp.int32, (tokens, lanes), 1) // cols
+    key_of = lax.broadcasted_iota(jnp.int32, (tokens, lanes), 1) % tokens
     own_key = key_of == lax.broadcasted_iota(jnp.int32, (tokens, lanes), 0)
     key_mask = jnp.sum(jnp.where(own_key, mask[:, :1], 0.0), axis=0, keepdims=True)
     key_bias_ref[...] = (key_mask - 1.0) * 1000000000.0 + other_columns_ref[...]
@@ -187,25 +188,17 @@
     )
     stored(places, found)
 
-    right_at = [right_ref[pl.ds(col_first * tokens + m, cols, stride=tokens), :] for m in range(tokens)]
-    products = []
-    for i in range(tokens):
-        total = left_ref[pl.ds(i * tokens, 1), :] * right_at[0]
-        for m in range(1, tokens):
-            total = total + left_ref[pl.ds(i * tokens + m, 1), :] * right_at[m]
-        products.append(total)
-    extra = [None] * rows
+    seconds = [col_first + c for c in range(cols)] + [row_first + r for r in range(rows)]
+    products = [None] * len(seconds)
     for m in range(tokens):
         left_at = left_ref[pl.ds(m, tokens, stride=tokens), :]
-        for r in range(rows):
-            term = left_at * right_ref[pl.ds((row_first + r) * tokens + m, 1), :]
-            extra[r] = term if m == 0 else extra[r] + term
-    products = round_bf16(jnp.concatenate(products + extra, axis=0))
+        for at, second in enumerate(seconds):
+            term = left_at * right_ref[pl.ds(second * tokens + m, 1), :]
+            products[at] = term if m == 0 else products[at] + term
+    products = round_bf16(jnp.concatenate(products, axis=0))
 
     def chosen(ref):
-        own = [ref[pl.ds(i * tokens + col_first, cols), :] for i in range(tokens)]
-        own += [ref[pl.ds(row_first + r, tokens, stride=tokens), :] for r in range(rows)]
-        return jnp.concatenate(own, axis=0)
+        return jnp.concatenate([ref[pl.ds(second, tokens, stride=tokens), :] for second in seconds], axis=0)
 
     normed_out = layer_norm(products, gains_ref[1:2]).astype(bf16)
     out_gate = sigmoid(dot(chosen(normed_ref).astype(bf16), out_gate_ref[...]))
@@ -214,11 +207,12 @@
     own_pairs = rows * cols
     column_pairs = tokens * cols
     upd_ref[...] = updated[:column_pairs]
-    att_f = normed_att.astype(f32)
-    att_ref[...] = att_f[:column_pairs]
-
-    own_at = pl.ds(pl.multiple_of(row_first * cols, own_pairs), own_pairs)
-    own = att_ref[own_at, :].astype(bf16)
+    att_ref[...] = normed_att[:column_pairs].astype(f32)
+
+    def own_rows(ref):
+        return jnp.concatenate([ref[pl.ds(row_first + r, cols, stride=tokens), :] for r in range(rows)], axis=0)
+
+    own = own_rows(att_ref).astype(bf16)
     column = normed_att[:column_pairs]
     queries = dot(own, qkv_ref[:, :width])
     keys = dot(column, qkv_ref[:, width : 2 * width]).astype(bf16)
@@ -227,11 +221,8 @@
 
     bias = []
     for r in range(rows):
-        part = att_f[column_pairs + r * tokens : column_pairs + (r + 1) * tokens]
-        spread = jnp.concatenate(
-            [jnp.broadcast_to(part[k : k + 1], (cols, width)) for k in range(tokens)], axis=0
-        )
-        bias.append(round_bf16(dot_t(att_bias_ref[...], spread.astype(bf16))))
+        part = normed_att[column_pairs + r * tokens : column_pairs + (r + 1) * tokens]
+        bias.append(round_bf16(dot_t(att_bias_ref[...], jnp.concatenate([part] * cols, axis=0))))
 
     head_of = lax.broadcasted_iota(jnp.int32, (own_pairs, width), 1) // head_dim
     queries = round_bf16(queries)
@@ -253,7 +244,7 @@
         attended = jnp.where(head_of == h, mixed[h * own_pairs : (h + 1) * own_pairs], attended)
 
     gated = (own_gate * attended).astype(bf16)
-    result = upd_ref[own_at, :] + dot(gated, att_out_ref[...])
+    result = own_rows(upd_ref) + dot(gated, att_out_ref[...])
     out_ref[...] = result.reshape(rows, cols, width).astype(bf16)
 
 

time: 14.3 us -> 14.3 us (level)
  no operation moved by 1% of the time
where the time goes in v16:
time: 14.3 us; the launch traced here: 14.1 us
  starting transfers between devices  9.42 us (66%)
  Pallas kernels  2.72 us (19%)
  waiting for transfers between devices  1.01 us (7%)
  local copies, waits for them, and re-layouts  0.77 us (5%)
  between operations  0.15 us (1%)
    ppermute x6, starting transfers between devices, move(): lax.ppermute(values, ('row', 'col'), [(device, device ^ step) for device...  9.42 us
    pallas_call x1, Pallas kernels, whole_pair_on_device(): pl.pallas_call(functools.partial(whole_pair_kernel, row_dim, heads, early...  2.1 us
    ppermute x6, waiting for transfers between devices, move(): lax.ppermute(values, ('row', 'col'), [(device, device ^ step) for device...  1.01 us
    unnamed x30, local copies, waits for them, and re-layouts  0.76 us
    pallas_call x1, Pallas kernels, whole_pair_on_device(): pl.pallas_call(functools.partial(early_kernel, row_dim, early), out_shape...  0.38 us
  transfers between devices with their start and end apart: 6, of which 3 were waited for; matrix products, arithmetic and copies ran while one was open for 0% of the time, Pallas kernels for 4%

profile of v16, /device:TPU:0, one launch (start us, length us, event | category | flops | bytes accessed | tf_op | source)
XLA Modules:
  0.0 14.1 jit_solution(12698768235451841846)
XLA Ops:
  0.0 0.0 copy-start.7
  0.0 0.5 %collective-permute-start = (bf16[2,8,128]{2,1,0:T(8,128)(2,1)}, bf16[2,8,128]{2,1,0:T(8,128)(2,1)S(1)}, u32[]{:S(2)}, u32[]{:S(2)}) collective-permute-start(bf16[2,8,128]{2,1,0:T(8,128)(2,1)} %pair_ref.1), channel_id=1, source_target_pairs={{0,1},{1,0},{2,3},{3,2},{4,5},{5,4},{6,7},{7,6},{8,9},{9,8},{10,11... | collective-permute-start | bytes 12296 | tf_op jit(solution)/shard_map/ppermute | solution.py:314
  0.5 0.0 copy-start.11
  0.5 0.0 copy-start.12
  0.5 0.0 copy-start.13
  0.5 0.0 copy-start.14
  0.5 0.0 copy-start.8
  0.5 0.0 copy-start.9
  0.5 0.0 copy-start.10
  0.5 0.2 %copy-done.7 = bf16[128,128]{1,0:T(8,128)(2,1)S(1)} copy-done((bf16[128,128]{1,0:T(8,128)(2,1)S(1)}, bf16[128,128]{1,0:T(8,128)(2,1)}, u32[]{:S(2)}) %copy-start.7) | copy-done | bytes 32792
  0.8 0.4 %copy-done.11 = s32[16]{0:T(128)S(1)} copy-done((s32[16]{0:T(128)S(1)}, s32[16]{0:T(128)}, u32[]{:S(2)}) %copy-start.11) | copy-done | bytes 88
  1.1 0.0 copy-done.12
  1.1 0.0 copy-done.13
  1.1 0.0 copy-done.14
  1.2 0.0 copy-done.8
  1.2 0.0 copy-done.9
  1.2 0.0 copy-done.10
  1.2 0.0 copy-start
  1.2 0.0 copy-start.1
  1.2 0.0 copy-start.2
  1.2 0.0 copy-start.4
  1.2 0.0 copy-start.5
  1.3 0.0 copy-start.6
  1.3 0.2 %shard_map.146 = (bf16[2,2,8,128]{3,2,1,0:T(8,128)(2,1)S(1)}, f32[256,128]{1,0:T(8,128)S(1)}, f32[256,128]{1,0:T(8,128)S(1)}, f32[3,128]{1,0:T(4,128)S(1)}, bf16...) custom-call(bf16[2,8,128]{2,1,0:T(8,128)(2,1)S(1)} %copy-done.8, s32[1,16]{1,0:T(1,128)S(1)} %bitcast.9, ...), custom_call_target="tpu_custom_call" | custom-call | flops 1000000000 | bytes 1048576 | tf_op jit(solution)/shard_map/pallas_call | solution.py:284
  1.5 0.0 copy-start.3
  1.5 0.0 collective-permute-done
  1.5 3.8 %collective-permute-start.1 = (bf16[2,2,8,128]{3,2,1,0:T(8,128)(2,1)S(1)}, bf16[2,2,8,128]{3,2,1,0:T(8,128)(2,1)S(1)}, u32[]{:S(2)}, u32[]{:S(2)}) collective-permute-start(bf16[2,2,8,128]{3,2,1,0:T(8,128)(2,1)S(1)} %bitcast_dynamic-update-slice_fusion.refs_0_), channel_id=1, source_target_pairs={{0,9},{1,8},{2,11},{3,10},{4,13},{5,12},{6,15},{7,14},{8,1},{9,0},... | collective-permute-start | bytes 24584 | tf_op jit(solution)/shard_map/ppermute | solution.py:314
  5.3 2.1 %collective-permute-start.4 = (bf16[2,2,8,128]{3,2,1,0:T(8,128)(2,1)S(1)}, bf16[2,2,8,128]{3,2,1,0:T(8,128)(2,1)S(1)}, u32[]{:S(2)}, u32[]{:S(2)}) collective-permute-start(bf16[2,2,8,128]{3,2,1,0:T(8,128)(2,1)S(1)} %bitcast_dynamic-update-slice_fusion.refs_0_), channel_id=1, source_target_pairs={{0,15},{1,14},{2,13},{3,12},{4,11},{5,10},{6,9},{7,8},{8,7},{9,6},... | collective-permute-start | bytes 24584 | tf_op jit(solution)/shard_map/ppermute | solution.py:314
  7.4 0.2 %collective-permute-start.5 = (bf16[2,2,8,128]{3,2,1,0:T(8,128)(2,1)S(1)}, bf16[2,2,8,128]{3,2,1,0:T(8,128)(2,1)S(1)}, u32[]{:S(2)}, u32[]{:S(2)}) collective-permute-start(bf16[2,2,8,128]{3,2,1,0:T(8,128)(2,1)S(1)} %bitcast_dynamic-update-slice_fusion.refs_0_), channel_id=1, source_target_pairs={{0,7},{1,6},{2,5},{3,4},{4,3},{5,2},{6,1},{7,0},{8,15},{9,14},{10,... | collective-permute-start | bytes 24584 | tf_op jit(solution)/shard_map/ppermute | solution.py:314
  7.7 0.0 collective-permute-done.1.refs_1_
  7.7 0.5 %collective-permute-start.2 = (bf16[4,2,8,128]{3,2,1,0:T(8,128)(2,1)S(1)}, bf16[4,2,8,128]{3,2,1,0:T(8,128)(2,1)S(1)}, u32[]{:S(2)}, u32[]{:S(2)}) collective-permute-start(bf16[4,2,8,128]{3,2,1,0:T(8,128)(2,1)S(1)} %pad_maximum_fusion), channel_id=1, source_target_pairs={{0,3},{1,2},{2,1},{3,0},{4,7},{5,6},{6,5},{7,4},{8,11},{9,10},{10,... | collective-permute-start | bytes 49160 | tf_op jit(solution)/shard_map/ppermute | solution.py:314
  8.2 2.3 %collective-permute-start.3 = (bf16[4,2,8,128]{3,2,1,0:T(8,128)(2,1)S(1)}, bf16[4,2,8,128]{3,2,1,0:T(8,128)(2,1)S(1)}, u32[]{:S(2)}, u32[]{:S(2)}) collective-permute-start(bf16[4,2,8,128]{3,2,1,0:T(8,128)(2,1)S(1)} %pad_maximum_fusion), channel_id=1, source_target_pairs={{0,5},{1,4},{2,7},{3,6},{4,1},{5,0},{6,3},{7,2},{8,13},{9,12},{10,... | collective-permute-start | bytes 49160 | tf_op jit(solution)/shard_map/ppermute | solution.py:314
  10.5 0.6 %collective-permute-done.4.refs_2_ = bf16[2,2,8,128]{3,2,1,0:T(8,128)(2,1)S(1)} collective-permute-done((bf16[2,2,8,128]{3,2,1,0:T(8,128)(2,1)S(1)}, bf16[2,2,8,128]{3,2,1,0:T(8,128)(2,1)S(1)}, u32[]{:S(2)}, u32[]{:S(2)}) %collective-permute-start.4) | collective-permute-done | bytes 8224 | tf_op jit(solution)/shard_map/ppermute | solution.py:314
  11.1 0.3 %collective-permute-done.5.refs_3_ = bf16[2,2,8,128]{3,2,1,0:T(8,128)(2,1)S(1)} collective-permute-done((bf16[2,2,8,128]{3,2,1,0:T(8,128)(2,1)S(1)}, bf16[2,2,8,128]{3,2,1,0:T(8,128)(2,1)S(1)}, u32[]{:S(2)}, u32[]{:S(2)}) %collective-permute-start.5) | collective-permute-done | bytes 8224 | tf_op jit(solution)/shard_map/ppermute | solution.py:314
  11.4 0.0 copy-done
  11.4 0.0 copy-done.1
  11.4 0.0 copy-done.2
  11.4 0.0 copy-done.4
  11.4 0.0 copy-done.5
  11.4 0.0 copy-done.6
  11.4 0.0 copy-done.3
  11.4 0.4 %shard_map.147 = (f32[128,128]{1,0:T(8,128)S(1)}, f32[128,128]{1,0:T(8,128)S(1)}, f32[128,128]{1,0:T(8,128)S(1)}, f32[128,128]{1,0:T(8,128)S(1)}) custom-call(bf16[2,2,8,128]{3,2,1,0:T(8,128)(2,1)S(1)} %bitcast_dynamic-update-slice_fusion.refs_0_, bf16[2,2,8,128]{3,2,1,0:T(8,128)(2,1)S(1)} %collective-permute-done.1.refs_1_, ...), custom_call_target="tpu_custom_call" | custom-call | flops 1000000000 | bytes 1048576 | tf_op jit(solution)/shard_map/pallas_call | solution.py:327
  11.8 0.0 collective-permute-done.2.refs_0_
  11.8 0.1 collective-permute-done.3.refs_1_
  12.0 2.1 %shard_map.148 = bf16[2,8,128]{2,1,0:T(8,128)(2,1)} custom-call(bf16[4,2,8,128]{3,2,1,0:T(8,128)(2,1)S(1)} %collective-permute-done.2.refs_0_, bf16[4,2,8,128]{3,2,1,0:T(8,128)(2,1)S(1)} %collective-permute-done.3.refs_1_, f32[128,128]{1,0:T(8,128)S(1)} %get-tuple-element.31.refs_2_, f32[128,128]{1,0:T(8,128)S(1)} %get-tuple-element.32.refs_3_, ...), custom_call_target="tpu_custom_call" | custom-call | tf_op jit(solution)/shard_map/pallas_call | solution.py:339
  (3 shorter events, 0.0 us)
Async XLA Ops:
  0.0 0.8 %copy-start.7 = (bf16[128,128]{1,0:T(8,128)(2,1)S(1)}, bf16[128,128]{1,0:T(8,128)(2,1)}, u32[]{:S(2)}) copy-start(bf16[128,128]{1,0:T(8,128)(2,1)} %table_ref.1) | copy-start | bytes 98308
  0.0 1.5 %collective-permute-start = (bf16[2,8,128]{2,1,0:T(8,128)(2,1)}, bf16[2,8,128]{2,1,0:T(8,128)(2,1)S(1)}, u32[]{:S(2)}, u32[]{:S(2)}) collective-permute-start(bf16[2,8,128]{2,1,0:T(8,128)(2,1)} %pair_ref.1), channel_id=1, source_target_pairs={{0,1},{1,0},{2,3},{3,2},{4,5},{5,4},{6,7},{7,6},{8,9},{9,8},{10,11... | collective-permute-start | bytes 12296 | tf_op jit(solution)/shard_map/ppermute | solution.py:314
  0.5 0.7 %copy-start.11 = (s32[16]{0:T(128)S(1)}, s32[16]{0:T(128)}, u32[]{:S(2)}) copy-start(s32[16]{0:T(128)} %param.19) | copy-start | bytes 196
  0.5 0.7 %copy-start.12 = (f32[128]{0:T(128)S(1)}, f32[128]{0:T(128)}, u32[]{:S(2)}) copy-start(f32[128]{0:T(128)} %param.21) | copy-start | bytes 1540
  0.5 0.7 %copy-start.13 = (f32[128]{0:T(128)S(1)}, f32[128]{0:T(128)}, u32[]{:S(2)}) copy-start(f32[128]{0:T(128)} %param.25) | copy-start | bytes 1540
  0.5 0.7 %copy-start.14 = (f32[128]{0:T(128)S(1)}, f32[128]{0:T(128)}, u32[]{:S(2)}) copy-start(f32[128]{0:T(128)} %param.27) | copy-start | bytes 1540
  0.5 0.7 %copy-start.8 = (bf16[2,8,128]{2,1,0:T(8,128)(2,1)S(1)}, bf16[2,8,128]{2,1,0:T(8,128)(2,1)}, u32[]{:S(2)}) copy-start(bf16[2,8,128]{2,1,0:T(8,128)(2,1)} %pair_ref.1) | copy-start | bytes 12292
  0.5 0.7 %copy-start.9 = (bf16[128,4]{0,1:T(4,128)(2,1)S(1)}, bf16[128,4]{0,1:T(4,128)(2,1)}, u32[]{:S(2)}) copy-start(bf16[128,4]{0,1:T(4,128)(2,1)} %param.30) | copy-start | bytes 3076
  0.5 0.7 %copy-start.10 = (s32[16]{0:T(128)S(1)}, s32[16]{0:T(128)}, u32[]{:S(2)}) copy-start(s32[16]{0:T(128)} %param.18) | copy-start | bytes 196
  1.2 10.2 %copy-start = (bf16[128,384]{1,0:T(8,128)(2,1)S(1)}, bf16[128,384]{1,0:T(8,128)(2,1)}, u32[]{:S(2)}) copy-start(bf16[128,384]{1,0:T(8,128)(2,1)} %refs_15_.1) | copy-start | bytes 294916
  1.2 10.2 %copy-start.1 = (bf16[128,256]{1,0:T(8,128)(2,1)S(1)}, bf16[128,256]{1,0:T(8,128)(2,1)}, u32[]{:S(2)}) copy-start(bf16[128,256]{1,0:T(8,128)(2,1)} %refs_11_.3) | copy-start | bytes 196612
  1.2 10.2 %copy-start.2 = (bf16[128,256]{1,0:T(8,128)(2,1)S(1)}, bf16[128,256]{1,0:T(8,128)(2,1)}, u32[]{:S(2)}) copy-start(bf16[128,256]{1,0:T(8,128)(2,1)} %refs_12_.3) | copy-start | bytes 196612
  1.2 10.2 %copy-start.4 = (bf16[128,128]{1,0:T(8,128)(2,1)S(1)}, bf16[128,128]{1,0:T(8,128)(2,1)}, u32[]{:S(2)}) copy-start(bf16[128,128]{1,0:T(8,128)(2,1)} %refs_14_.1) | copy-start | bytes 98308
  1.2 10.2 %copy-start.5 = (bf16[128,128]{1,0:T(8,128)(2,1)S(1)}, bf16[128,128]{1,0:T(8,128)(2,1)}, u32[]{:S(2)}) copy-start(bf16[128,128]{1,0:T(8,128)(2,1)} %refs_16_.1) | copy-start | bytes 98308
  1.3 10.2 %copy-start.6 = (bf16[128,128]{1,0:T(8,128)(2,1)S(1)}, bf16[128,128]{1,0:T(8,128)(2,1)}, u32[]{:S(2)}) copy-start(bf16[128,128]{1,0:T(8,128)(2,1)} %refs_17_.1) | copy-start | bytes 98308
  1.5 9.9 %copy-start.3 = (bf16[128,128]{1,0:T(8,128)(2,1)S(1)}, bf16[128,128]{1,0:T(8,128)(2,1)}, u32[]{:S(2)}) copy-start(bf16[128,128]{1,0:T(8,128)(2,1)} %refs_13_.3) | copy-start | bytes 98308
  1.5 6.1 %collective-permute-start.1 = (bf16[2,2,8,128]{3,2,1,0:T(8,128)(2,1)S(1)}, bf16[2,2,8,128]{3,2,1,0:T(8,128)(2,1)S(1)}, u32[]{:S(2)}, u32[]{:S(2)}) collective-permute-start(bf16[2,2,8,128]{3,2,1,0:T(8,128)(2,1)S(1)} %bitcast_dynamic-update-slice_fusion.refs_0_), channel_id=1, source_target_pairs={{0,9},{1,8},{2,11},{3,10},{4,13},{5,12},{6,15},{7,14},{8,1},{9,0},... | collective-permute-start | bytes 24584 | tf_op jit(solution)/shard_map/ppermute | solution.py:314
  5.3 5.8 %collective-permute-start.4 = (bf16[2,2,8,128]{3,2,1,0:T(8,128)(2,1)S(1)}, bf16[2,2,8,128]{3,2,1,0:T(8,128)(2,1)S(1)}, u32[]{:S(2)}, u32[]{:S(2)}) collective-permute-start(bf16[2,2,8,128]{3,2,1,0:T(8,128)(2,1)S(1)} %bitcast_dynamic-update-slice_fusion.refs_0_), channel_id=1, source_target_pairs={{0,15},{1,14},{2,13},{3,12},{4,11},{5,10},{6,9},{7,8},{8,7},{9,6},... | collective-permute-start | bytes 24584 | tf_op jit(solution)/shard_map/ppermute | solution.py:314
  7.4 4.0 %collective-permute-start.5 = (bf16[2,2,8,128]{3,2,1,0:T(8,128)(2,1)S(1)}, bf16[2,2,8,128]{3,2,1,0:T(8,128)(2,1)S(1)}, u32[]{:S(2)}, u32[]{:S(2)}) collective-permute-start(bf16[2,2,8,128]{3,2,1,0:T(8,128)(2,1)S(1)} %bitcast_dynamic-update-slice_fusion.refs_0_), channel_id=1, source_target_pairs={{0,7},{1,6},{2,5},{3,4},{4,3},{5,2},{6,1},{7,0},{8,15},{9,14},{10,... | collective-permute-start | bytes 24584 | tf_op jit(solution)/shard_map/ppermute | solution.py:314
  7.7 4.2 %collective-permute-start.2 = (bf16[4,2,8,128]{3,2,1,0:T(8,128)(2,1)S(1)}, bf16[4,2,8,128]{3,2,1,0:T(8,128)(2,1)S(1)}, u32[]{:S(2)}, u32[]{:S(2)}) collective-permute-start(bf16[4,2,8,128]{3,2,1,0:T(8,128)(2,1)S(1)} %pad_maximum_fusion), channel_id=1, source_target_pairs={{0,3},{1,2},{2,1},{3,0},{4,7},{5,6},{6,5},{7,4},{8,11},{9,10},{10,... | collective-permute-start | bytes 49160 | tf_op jit(solution)/shard_map/ppermute | solution.py:314
  8.2 3.8 %collective-permute-start.3 = (bf16[4,2,8,128]{3,2,1,0:T(8,128)(2,1)S(1)}, bf16[4,2,8,128]{3,2,1,0:T(8,128)(2,1)S(1)}, u32[]{:S(2)}, u32[]{:S(2)}) collective-permute-start(bf16[4,2,8,128]{3,2,1,0:T(8,128)(2,1)S(1)} %pad_maximum_fusion), channel_id=1, source_target_pairs={{0,5},{1,4},{2,7},{3,6},{4,1},{5,0},{6,3},{7,2},{8,13},{9,12},{10,... | collective-permute-start | bytes 49160 | tf_op jit(solution)/shard_map/ppermute | solution.py:314

commit v17 on v15

--- a/solution.py
+++ b/solution.py
@@ -45,7 +45,13 @@
     other_columns_ref[...] = jnp.where(lane % other_columns_ref.shape[0] == sub, 0.0, -jnp.inf)
 
 
+def token_rows(chips, rows):
+    return [(lax.axis_index("row") ^ chip) * rows + r for chip in chips for r in range(rows)]
+
+
 def stage_kernel(
+    chips,
+    rows,
     pair_ref,
     mask_ref,
     pos_ref,
@@ -61,6 +67,8 @@
     gains_ref,
     bias_ref,
     key_bias_ref,
+    pos_rows_ref,
+    mask_rows_ref,
 ):
     chip_ref[0] = pair_ref[...]
     gains_ref[0:1] = norm_in_ref[...]
@@ -77,41 +85,34 @@
         spread = jnp.where(sub == lane, jnp.broadcast_to(ref[...].astype(f32), (tokens, tokens)), 0.0)
         return jnp.broadcast_to(jnp.sum(spread, axis=1, keepdims=True), (tokens, bins))
 
-    pos, mask = by_row(pos_ref), by_row(mask_ref)
+    pos_rows_ref[...] = by_row(pos_ref)
+    mask_rows_ref[...] = by_row(mask_ref)
+    own_half = lax.axis_index("col")
+    halves = [pl.ds(pl.multiple_of((own_half ^ half) * cols, cols), cols) for half in range(tokens // cols)]
     lane = lax.broadcasted_iota(jnp.int32, (cols, bins), 1).astype(f32)
+    key_of = lax.broadcasted_iota(jnp.int32, (1, lanes), 1) // cols
+    key_mask = jnp.zeros((1, lanes), f32)
     centre = float(bins // 2)
     hot = []
-    for i in range(tokens):
-        for first in range(0, tokens, cols):
-            bucket = jnp.clip(pos[i : i + 1] - pos[first : first + cols], -centre, centre - 1.0) + centre
+    for at, token in enumerate(token_rows(chips, rows)):
+        pos, mask = pos_rows_ref[pl.ds(token, 1), :], mask_rows_ref[pl.ds(token, 1), :]
+        for half in halves:
+            bucket = jnp.clip(pos - pos_rows_ref[half, :], -centre, centre - 1.0) + centre
+            first = len(hot) * cols
+            pair_mask_ref[first : first + cols, :] = mask_rows_ref[half, :] * mask
             hot.append((bucket == lane).astype(f32))
-            at = i * tokens + first
-            pair_mask_ref[at : at + cols, :] = mask[first : first + cols, :width] * mask[i : i + 1, :width]
+        key_mask = jnp.where(key_of == at, mask, key_mask)
     rel_ref[...] = dot(jnp.concatenate(hot, axis=0).astype(jnp.bfloat16), table_ref[...])
-    key_of = lax.broadcasted_iota(jnp.int32, (tokens, lanes), 1) // cols
-    own_key = key_of == lax.broadcasted_iota(jnp.int32, (tokens, lanes), 0)
-    key_mask = jnp.sum(jnp.where(own_key, mask[:, :1], 0.0), axis=0, keepdims=True)
     key_bias_ref[...] = (key_mask - 1.0) * 1000000000.0 + other_columns_ref[...]
 
 
-def tile_places(row_dim, rows, cols, order):
-    me = lax.axis_index("row") * 2 + lax.axis_index("col")
-    places = []
-    for place in order:
-        owner = me ^ place
-        for r in range(rows):
-            first = (owner // 2 * rows + r) * row_dim * rows + owner % 2 * cols
-            places.append(pl.ds(pl.multiple_of(first, cols), cols))
-    return places
-
-
-def edge_operands(pieces, places, rel_ref, pair_mask_ref, gain, in_gate, in_weight):
-    width = rel_ref.shape[1]
-    blocks = [piece[at].astype(jnp.float32) for piece in pieces for at in range(piece.shape[0])]
-    rows = len(places) // len(blocks)
-    tiles = [block[r] for block in blocks for r in range(rows)]
-    base = jnp.concatenate([tile + rel_ref[place, :] for tile, place in zip(tiles, places)], axis=0)
-    pair_mask = jnp.concatenate([pair_mask_ref[place, :] for place in places], axis=0)
+def edge_operands(pieces, orders, rows, rel, pair_mask, gain, in_gate, in_weight):
+    width = rel.shape[1]
+    blocks = {
+        place: piece[at].astype(jnp.float32) for piece, order in zip(pieces, orders) for at, place in enumerate(order)
+    }
+    tiles = [blocks[2 * chip + half][r] for chip in chips_of(orders) for r in range(rows) for half in range(2)]
+    base = jnp.concatenate(tiles, axis=0) + rel
     normed = layer_norm(base, gain).astype(jnp.bfloat16)
     projected = sigmoid(dot(normed, in_gate)) * dot(normed, in_weight)
     left = round_bf16(projected[:, :width] * pair_mask)
@@ -119,27 +120,37 @@
     return left, right, base, normed.astype(jnp.float32)
 
 
-def early_kernel(row_dim, orders, *refs):
+def chips_of(orders):
+    return list(dict.fromkeys(place // 2 for order in orders for place in order))
+
+
+def early_kernel(orders, *refs):
     piece_refs = refs[: len(orders)]
     rel_ref, pair_mask_ref, gains_ref, in_weight_ref, in_gate_ref = refs[len(orders) : len(orders) + 5]
-    rows, cols = piece_refs[0].shape[1:3]
-    places = tile_places(row_dim, rows, cols, sum(orders, ()))
+    here = refs[-1].shape[0]
     found = edge_operands(
-        piece_refs, places, rel_ref, pair_mask_ref, gains_ref[0:1], in_gate_ref[...], in_weight_ref[...]
+        piece_refs,
+        orders,
+        piece_refs[0].shape[1],
+        rel_ref[:here],
+        pair_mask_ref[:here],
+        gains_ref[0:1],
+        in_gate_ref[...],
+        in_weight_ref[...],
     )
     for ref, values in zip(refs[-4:], found):
         ref[...] = values
 
 
-def whole_pair_kernel(row_dim, heads, early, orders, *refs):
-    whole_pair_steps(row_dim, heads, early, orders, refs[: len(orders)], *refs[len(orders) :])
+def whole_pair_kernel(row_dim, heads, early, late, *refs):
+    whole_pair_steps(row_dim, heads, early, late, refs[: len(late)], *refs[len(late) :])
 
 
 def whole_pair_steps(
     row_dim,
     heads,
     early,
-    orders,
+    late,
     piece_refs,
     early_left_ref,
     early_right_ref,
@@ -158,67 +169,68 @@
     att_gate_ref,
     att_out_ref,
     out_ref,
-    base_ref,
-    normed_ref,
-    left_ref,
+    late_left_ref,
+    late_base_ref,
+    late_normed_ref,
     right_ref,
-    att_ref,
-    upd_ref,
 ):
     rows, cols, width = piece_refs[0].shape[1:]
     tokens = row_dim * rows
     head_dim = width // heads
-    row_first = lax.axis_index("row") * rows
-    col_first = pl.multiple_of(lax.axis_index("col") * cols, cols)
+    row, col = lax.axis_index("row"), lax.axis_index("col")
     f32, bf16 = jnp.float32, jnp.bfloat16
 
-    def stored(places, found):
-        for ref, values in zip((left_ref, right_ref, base_ref, normed_ref), found):
-            for at, place in enumerate(places):
-                ref[place, :] = values[at * cols : (at + 1) * cols]
-
-    places = tile_places(row_dim, rows, cols, sum(orders, ()))
-    found = edge_operands(
-        piece_refs, places, rel_ref, pair_mask_ref, gains_ref[0:1], in_gate_ref[...], in_weight_ref[...]
-    )
-    stored(
-        tile_places(row_dim, rows, cols, sum(early, ())),
-        [ref[...] for ref in (early_left_ref, early_right_ref, early_base_ref, early_normed_ref)],
-    )
-    stored(places, found)
-
-    right_at = [right_ref[pl.ds(col_first * tokens + m, cols, stride=tokens), :] for m in range(tokens)]
+    here = early_left_ref.shape[0]
+    left, right, base, normed = edge_operands(
+        piece_refs, late, rows, rel_ref[here:], pair_mask_ref[here:], gains_ref[0:1], in_gate_ref[...], in_weight_ref[...]
+    )
+    late_left_ref[...] = left
+    late_base_ref[...] = base
+    late_normed_ref[...] = normed
+    lefts = (early_left_ref, late_left_ref)
+
+    for at, token in enumerate(token_rows(chips_of(early + late), rows)):
+        place = pl.ds(pl.multiple_of(token * tokens, tokens), tokens)
+        first = at * tokens
+        if first < here:
+            right_ref[place, :] = early_right_ref[first : first + tokens]
+        else:
+            right_ref[place, :] = right[first - here : first - here + tokens]
+
+    right_at = [right_ref[pl.ds(col * cols * tokens + m, cols, stride=tokens), :] for m in range(tokens)]
     products = []
     for i in range(tokens):
-        total = left_ref[pl.ds(i * tokens, 1), :] * right_at[0]
+        ref, first = lefts[i * tokens // here], i * tokens % here
+        total = ref[first : first + 1] * right_at[0]
         for m in range(1, tokens):
-            total = total + left_ref[pl.ds(i * tokens + m, 1), :] * right_at[m]
+            total = total + ref[first + m : first + m + 1] * right_at[m]
         products.append(total)
     extra = [None] * rows
     for m in range(tokens):
-        left_at = left_ref[pl.ds(m, tokens, stride=tokens), :]
+        left_at = jnp.concatenate([ref[pl.ds(m, here // tokens, stride=tokens), :] for ref in lefts], axis=0)
         for r in range(rows):
-            term = left_at * right_ref[pl.ds((row_first + r) * tokens + m, 1), :]
+            term = left_at * early_right_ref[r * tokens + m : r * tokens + m + 1]
             extra[r] = term if m == 0 else extra[r] + term
     products = round_bf16(jnp.concatenate(products + extra, axis=0))
 
-    def chosen(ref):
-        own = [ref[pl.ds(i * tokens + col_first, cols), :] for i in range(tokens)]
-        own += [ref[pl.ds(row_first + r, tokens, stride=tokens), :] for r in range(rows)]
+    own_token = row * rows
+    own_column = ((own_token // cols) ^ col) * cols + own_token % cols
+
+    def chosen(early_ref, late_ref):
+        pair = (early_ref, late_ref)
+        own = [pair[i * tokens // here][i * tokens % here : i * tokens % here + cols] for i in range(tokens)]
+        for r in range(rows):
+            own += [ref[pl.ds(own_column + r, here // tokens, stride=tokens), :] for ref in pair]
         return jnp.concatenate(own, axis=0)
 
     normed_out = layer_norm(products, gains_ref[1:2]).astype(bf16)
-    out_gate = sigmoid(dot(chosen(normed_ref).astype(bf16), out_gate_ref[...]))
-    updated = chosen(base_ref) + out_gate * dot(normed_out, out_weight_ref[...])
+    out_gate = sigmoid(dot(chosen(early_normed_ref, late_normed_ref).astype(bf16), out_gate_ref[...]))
+    updated = chosen(early_base_ref, late_base_ref) + out_gate * dot(normed_out, out_weight_ref[...])
     normed_att = layer_norm(updated, gains_ref[2:3]).astype(bf16)
     own_pairs = rows * cols
     column_pairs = tokens * cols
-    upd_ref[...] = updated[:column_pairs]
-    att_f = normed_att.astype(f32)
-    att_ref[...] = att_f[:column_pairs]
-
-    own_at = pl.ds(pl.multiple_of(row_first * cols, own_pairs), own_pairs)
-    own = att_ref[own_at, :].astype(bf16)
+
+    own = normed_att[:own_pairs]
     column = normed_att[:column_pairs]
     queries = dot(own, qkv_ref[:, :width])
     keys = dot(column, qkv_ref[:, width : 2 * width]).astype(bf16)
@@ -226,8 +238,9 @@
     own_gate = sigmoid(dot(own, att_gate_ref[...]))
 
     bias = []
+    att_f = normed_att[column_pairs:].astype(f32)
     for r in range(rows):
-        part = att_f[column_pairs + r * tokens : column_pairs + (r + 1) * tokens]
+        part = att_f[r * tokens : (r + 1) * tokens]
         spread = jnp.concatenate(
             [jnp.broadcast_to(part[k : k + 1], (cols, width)) for k in range(tokens)], axis=0
         )
@@ -253,7 +266,7 @@
         attended = jnp.where(head_of == h, mixed[h * own_pairs : (h + 1) * own_pairs], attended)
 
     gated = (own_gate * attended).astype(bf16)
-    result = upd_ref[own_at, :] + dot(gated, att_out_ref[...])
+    result = updated[:own_pairs] + dot(gated, att_out_ref[...])
     out_ref[...] = result.reshape(rows, cols, width).astype(bf16)
 
 
@@ -280,6 +293,18 @@
     params = pltpu.CompilerParams(vmem_limit_bytes=16 * 1024 * 1024)
     tokens, heads = row_dim * rows, att_bias.shape[1]
 
+    blocks = 2 * row_dim
+
+    def moved(order, step):
+        return tuple(place ^ step for place in order)
+
+    def move(values, step):
+        return lax.ppermute(values, ("row", "col"), [(device, device ^ step) for device in range(blocks)])
+
+    own_order = (0, 1)
+    early = [own_order] + [moved(own_order, step) for step in (9, 15, 7)]
+    late = [moved(own_order + early[1], step) for step in (3, 5)]
+
     beside = pl.CostEstimate(flops=STAGE_FLOPS, bytes_accessed=2**20, transcendentals=0)
     wide_out = jax.ShapeDtypeStruct((tokens * tokens, width), jnp.float32)
     key_shape = jax.ShapeDtypeStruct((cols, tokens * cols), jnp.float32)
@@ -291,7 +316,7 @@
         cost_estimate=beside,
     )()
     chip, *staged = pl.pallas_call(
-        stage_kernel,
+        functools.partial(stage_kernel, chips_of(early + late), rows),
         out_shape=[
             jax.ShapeDtypeStruct((2,) + pair_in.shape, pair_in.dtype),
             wide_out,
@@ -302,6 +327,7 @@
         ],
         in_specs=[vmem] * 9,
         out_specs=[vmem] * 6,
+        scratch_shapes=[pltpu.VMEM((tokens, relpos_table.shape[0]), jnp.float32)] * 2,
         compiler_params=params,
         cost_estimate=beside,
     )(
@@ -316,43 +342,30 @@
         other_columns,
     )
 
-    blocks = 2 * row_dim
-
-    def move(piece, step):
-        values, order = piece
-        values = lax.ppermute(values, ("row", "col"), [(device, device ^ step) for device in range(blocks)])
-        return values, tuple(place ^ step for place in order)
-
-    other, _ = move((pair_in, (0,)), 1)
-    pieces = [(chip.at[1].set(other), (0, 1))]
-    first = move(pieces[0], 9)
-    pieces += [first, move(pieces[0], 15), move(pieces[0], 7)]
-    both = jnp.concatenate([pieces[0][0], first[0]], axis=0), pieces[0][1] + first[1]
-    pieces += [move(both, 3), move(both, 5)]
+    chip = chip.at[1].set(move(pair_in, 1))
+    first = move(chip, 9)
+    pieces = [chip, first, move(chip, 15), move(chip, 7)]
+    both = jnp.concatenate([chip, first], axis=0)
+    last = [move(both, 3), move(both, 5)]
     weights = (tri_in_weight, tri_in_gate, tri_out_gate, tri_out_weight, att_qkv, att_gate, att_out)
     rel, pair_mask, gains, *_ = staged
-    early = [order for _, order in pieces[:4]]
     half = jax.ShapeDtypeStruct((tokens * tokens // 2, width), jnp.float32)
     halves = pl.pallas_call(
-        functools.partial(early_kernel, row_dim, early),
+        functools.partial(early_kernel, early),
         out_shape=[half] * 4,
         in_specs=[vmem] * (7 + len(weights)),
         out_specs=[vmem] * 4,
         compiler_params=params,
         cost_estimate=beside,
-    )(*[values for values, _ in pieces[:4]], rel, pair_mask, gains, *weights)
-    late = [order for _, order in pieces[4:]]
-    gathered = [values for values, _ in pieces[4:]]
-    wide = pltpu.VMEM((tokens * tokens, width), jnp.float32)
-    column = pltpu.VMEM((tokens * cols, width), jnp.float32)
+    )(*pieces, rel, pair_mask, gains, *weights)
     return pl.pallas_call(
         functools.partial(whole_pair_kernel, row_dim, heads, early, late),
         out_shape=jax.ShapeDtypeStruct(pair_in.shape, pair_in.dtype),
-        in_specs=[vmem] * (len(gathered) + 9 + len(weights)),
+        in_specs=[vmem] * (len(last) + 9 + len(weights)),
         out_specs=vmem,
-        scratch_shapes=[wide] * 4 + [column] * 2,
+        scratch_shapes=[pltpu.VMEM(half.shape, half.dtype)] * 3 + [pltpu.VMEM(wide_out.shape, wide_out.dtype)],
         compiler_params=params,
-    )(*gathered, *halves, *staged, *weights)
+    )(*last, *halves, *staged, *weights)
 
 
 def attend_column(query_col, key_col, value_col, bias_all, key_bias, block_rows):
@@ -477,9 +490,9 @@
     rows, cols, width = pair_in.shape
     tokens = row_dim * rows
     whole_bytes = tokens * tokens * width * pair_in.dtype.itemsize
-    blocks = row_dim * col_dim
-    tiled = cols % 8 == 0 and width == 128 and blocks == 16 and col_dim == 2
-    if whole_bytes <= WHOLE_PAIR_BYTES and tiled:
+    bins = others[2].shape[0]
+    tiled = cols % 8 == 0 and cols % rows == 0 and width == bins == tokens * cols == 128
+    if whole_bytes <= WHOLE_PAIR_BYTES and tiled and (row_dim, col_dim) == (8, 2):
         return whole_pair_on_device(row_dim, pair_in, *others)
     return split_pair_on_device(pair_in, *others)
 

time: 14.3 us -> 14.2 us (level)
  no operation moved by 1% of the time
where the time goes in v17:
time: 14.2 us; the launch traced here: 14 us
  starting transfers between devices  9.42 us (66%)
  Pallas kernels  2.67 us (19%)
  waiting for transfers between devices  1.03 us (7%)
  local copies, waits for them, and re-layouts  0.77 us (5%)
    ppermute x6, starting transfers between devices, move(): lax.ppermute(values, ('row', 'col'), [(device, device ^ step) for device...  9.42 us
    pallas_call x1, Pallas kernels, whole_pair_on_device(): pl.pallas_call(functools.partial(whole_pair_kernel, row_dim, heads, early...  2.08 us
    ppermute x6, waiting for transfers between devices, move(): lax.ppermute(values, ('row', 'col'), [(device, device ^ step) for device...  1.03 us
    unnamed x30, local copies, waits for them, and re-layouts  0.76 us
    pallas_call x1, Pallas kernels, whole_pair_on_device(): pl.pallas_call(functools.partial(early_kernel, early), out_shape=[half] *...  0.35 us
  transfers between devices with their start and end apart: 6, of which 3 were waited for; matrix products, arithmetic and copies ran while one was open for 0% of the time, Pallas kernels for 4%

profile of v17, /device:TPU:0, one launch (start us, length us, event | category | flops | bytes accessed | tf_op | source)
XLA Modules:
  0.0 14.0 jit_solution(11555591956990744360)
XLA Ops:
  0.0 0.0 copy-start.7
  0.0 0.5 %collective-permute-start = (bf16[2,8,128]{2,1,0:T(8,128)(2,1)}, bf16[2,8,128]{2,1,0:T(8,128)(2,1)S(1)}, u32[]{:S(2)}, u32[]{:S(2)}) collective-permute-start(bf16[2,8,128]{2,1,0:T(8,128)(2,1)} %pair_ref.1), channel_id=1, source_target_pairs={{0,1},{1,0},{2,3},{3,2},{4,5},{5,4},{6,7},{7,6},{8,9},{9,8},{10,11... | collective-permute-start | bytes 12296 | tf_op jit(solution)/shard_map/ppermute | solution.py:302
  0.5 0.0 copy-start.11
  0.5 0.0 copy-start.12
  0.5 0.0 copy-start.13
  0.5 0.0 copy-start.14
  0.5 0.0 copy-start.8
  0.5 0.0 copy-start.9
  0.5 0.0 copy-start.10
  0.5 0.2 %copy-done.7 = bf16[128,128]{1,0:T(8,128)(2,1)S(1)} copy-done((bf16[128,128]{1,0:T(8,128)(2,1)S(1)}, bf16[128,128]{1,0:T(8,128)(2,1)}, u32[]{:S(2)}) %copy-start.7) | copy-done | bytes 32792
  0.8 0.4 %copy-done.11 = s32[16]{0:T(128)S(1)} copy-done((s32[16]{0:T(128)S(1)}, s32[16]{0:T(128)}, u32[]{:S(2)}) %copy-start.11) | copy-done | bytes 88
  1.1 0.0 copy-done.12
  1.1 0.0 copy-done.13
  1.1 0.0 copy-done.14
  1.2 0.0 copy-done.8
  1.2 0.0 copy-done.9
  1.2 0.0 copy-done.10
  1.2 0.0 copy-start
  1.2 0.0 copy-start.1
  1.2 0.0 copy-start.2
  1.2 0.0 copy-start.4
  1.2 0.0 copy-start.5
  1.3 0.0 copy-start.6
  1.3 0.2 %shard_map.146 = (bf16[2,2,8,128]{3,2,1,0:T(8,128)(2,1)S(1)}, f32[256,128]{1,0:T(8,128)S(1)}, f32[256,128]{1,0:T(8,128)S(1)}, f32[3,128]{1,0:T(4,128)S(1)}, bf16...) custom-call(bf16[2,8,128]{2,1,0:T(8,128)(2,1)S(1)} %copy-done.8, s32[1,16]{1,0:T(1,128)S(1)} %bitcast.9, ...), custom_call_target="tpu_custom_call" | custom-call | flops 1000000000 | bytes 1048576 | tf_op jit(solution)/shard_map/pallas_call | solution.py:318
  1.5 0.0 copy-start.3
  1.5 0.0 collective-permute-done
  1.5 3.8 %collective-permute-start.1 = (bf16[2,2,8,128]{3,2,1,0:T(8,128)(2,1)S(1)}, bf16[2,2,8,128]{3,2,1,0:T(8,128)(2,1)S(1)}, u32[]{:S(2)}, u32[]{:S(2)}) collective-permute-start(bf16[2,2,8,128]{3,2,1,0:T(8,128)(2,1)S(1)} %bitcast_dynamic-update-slice_fusion.refs_0_), channel_id=1, source_target_pairs={{0,9},{1,8},{2,11},{3,10},{4,13},{5,12},{6,15},{7,14},{8,1},{9,0},... | collective-permute-start | bytes 24584 | tf_op jit(solution)/shard_map/ppermute | solution.py:302
  5.3 2.1 %collective-permute-start.4 = (bf16[2,2,8,128]{3,2,1,0:T(8,128)(2,1)S(1)}, bf16[2,2,8,128]{3,2,1,0:T(8,128)(2,1)S(1)}, u32[]{:S(2)}, u32[]{:S(2)}) collective-permute-start(bf16[2,2,8,128]{3,2,1,0:T(8,128)(2,1)S(1)} %bitcast_dynamic-update-slice_fusion.refs_0_), channel_id=1, source_target_pairs={{0,15},{1,14},{2,13},{3,12},{4,11},{5,10},{6,9},{7,8},{8,7},{9,6},... | collective-permute-start | bytes 24584 | tf_op jit(solution)/shard_map/ppermute | solution.py:302
  7.4 0.2 %collective-permute-start.5 = (bf16[2,2,8,128]{3,2,1,0:T(8,128)(2,1)S(1)}, bf16[2,2,8,128]{3,2,1,0:T(8,128)(2,1)S(1)}, u32[]{:S(2)}, u32[]{:S(2)}) collective-permute-start(bf16[2,2,8,128]{3,2,1,0:T(8,128)(2,1)S(1)} %bitcast_dynamic-update-slice_fusion.refs_0_), channel_id=1, source_target_pairs={{0,7},{1,6},{2,5},{3,4},{4,3},{5,2},{6,1},{7,0},{8,15},{9,14},{10,... | collective-permute-start | bytes 24584 | tf_op jit(solution)/shard_map/ppermute | solution.py:302
  7.7 0.0 collective-permute-done.1.refs_1_
  7.7 0.5 %collective-permute-start.2 = (bf16[4,2,8,128]{3,2,1,0:T(8,128)(2,1)S(1)}, bf16[4,2,8,128]{3,2,1,0:T(8,128)(2,1)S(1)}, u32[]{:S(2)}, u32[]{:S(2)}) collective-permute-start(bf16[4,2,8,128]{3,2,1,0:T(8,128)(2,1)S(1)} %pad_maximum_fusion), channel_id=1, source_target_pairs={{0,3},{1,2},{2,1},{3,0},{4,7},{5,6},{6,5},{7,4},{8,11},{9,10},{10,... | collective-permute-start | bytes 49160 | tf_op jit(solution)/shard_map/ppermute | solution.py:302
  8.2 2.3 %collective-permute-start.3 = (bf16[4,2,8,128]{3,2,1,0:T(8,128)(2,1)S(1)}, bf16[4,2,8,128]{3,2,1,0:T(8,128)(2,1)S(1)}, u32[]{:S(2)}, u32[]{:S(2)}) collective-permute-start(bf16[4,2,8,128]{3,2,1,0:T(8,128)(2,1)S(1)} %pad_maximum_fusion), channel_id=1, source_target_pairs={{0,5},{1,4},{2,7},{3,6},{4,1},{5,0},{6,3},{7,2},{8,13},{9,12},{10,... | collective-permute-start | bytes 49160 | tf_op jit(solution)/shard_map/ppermute | solution.py:302
  10.5 0.6 %collective-permute-done.4.refs_2_ = bf16[2,2,8,128]{3,2,1,0:T(8,128)(2,1)S(1)} collective-permute-done((bf16[2,2,8,128]{3,2,1,0:T(8,128)(2,1)S(1)}, bf16[2,2,8,128]{3,2,1,0:T(8,128)(2,1)S(1)}, u32[]{:S(2)}, u32[]{:S(2)}) %collective-permute-start.4) | collective-permute-done | bytes 8224 | tf_op jit(solution)/shard_map/ppermute | solution.py:302
  11.1 0.3 %collective-permute-done.5.refs_3_ = bf16[2,2,8,128]{3,2,1,0:T(8,128)(2,1)S(1)} collective-permute-done((bf16[2,2,8,128]{3,2,1,0:T(8,128)(2,1)S(1)}, bf16[2,2,8,128]{3,2,1,0:T(8,128)(2,1)S(1)}, u32[]{:S(2)}, u32[]{:S(2)}) %collective-permute-start.5) | collective-permute-done | bytes 8224 | tf_op jit(solution)/shard_map/ppermute | solution.py:302
  11.4 0.0 copy-done
  11.4 0.0 copy-done.1
  11.4 0.0 copy-done.2
  11.4 0.0 copy-done.4
  11.4 0.0 copy-done.5
  11.4 0.0 copy-done.6
  11.4 0.0 copy-done.3
  11.4 0.3 %shard_map.147 = (f32[128,128]{1,0:T(8,128)S(1)}, f32[128,128]{1,0:T(8,128)S(1)}, f32[128,128]{1,0:T(8,128)S(1)}, f32[128,128]{1,0:T(8,128)S(1)}) custom-call(bf16[2,2,8,128]{3,2,1,0:T(8,128)(2,1)S(1)} %bitcast_dynamic-update-slice_fusion.refs_0_, bf16[2,2,8,128]{3,2,1,0:T(8,128)(2,1)S(1)} %collective-permute-done.1.refs_1_, ...), custom_call_target="tpu_custom_call" | custom-call | flops 1000000000 | bytes 1048576 | tf_op jit(solution)/shard_map/pallas_call | solution.py:353
  11.8 0.0 collective-permute-done.2.refs_0_
  11.8 0.1 %collective-permute-done.3.refs_1_ = bf16[4,2,8,128]{3,2,1,0:T(8,128)(2,1)S(1)} collective-permute-done((bf16[4,2,8,128]{3,2,1,0:T(8,128)(2,1)S(1)}, bf16[4,2,8,128]{3,2,1,0:T(8,128)(2,1)S(1)}, u32[]{:S(2)}, u32[]{:S(2)}) %collective-permute-start.3) | collective-permute-done | bytes 16416 | tf_op jit(solution)/shard_map/ppermute | solution.py:302
  12.0 2.1 %shard_map.148 = bf16[2,8,128]{2,1,0:T(8,128)(2,1)} custom-call(bf16[4,2,8,128]{3,2,1,0:T(8,128)(2,1)S(1)} %collective-permute-done.2.refs_0_, bf16[4,2,8,128]{3,2,1,0:T(8,128)(2,1)S(1)} %collective-permute-done.3.refs_1_, f32[128,128]{1,0:T(8,128)S(1)} %get-tuple-element.31.refs_2_, f32[128,128]{1,0:T(8,128)S(1)} %get-tuple-element.32.refs_3_, ...), custom_call_target="tpu_custom_call" | custom-call | tf_op jit(solution)/shard_map/pallas_call | solution.py:361
  (3 shorter events, 0.0 us)
Async XLA Ops:
  0.0 0.8 %copy-start.7 = (bf16[128,128]{1,0:T(8,128)(2,1)S(1)}, bf16[128,128]{1,0:T(8,128)(2,1)}, u32[]{:S(2)}) copy-start(bf16[128,128]{1,0:T(8,128)(2,1)} %table_ref.1) | copy-start | bytes 98308
  0.0 1.5 %collective-permute-start = (bf16[2,8,128]{2,1,0:T(8,128)(2,1)}, bf16[2,8,128]{2,1,0:T(8,128)(2,1)S(1)}, u32[]{:S(2)}, u32[]{:S(2)}) collective-permute-start(bf16[2,8,128]{2,1,0:T(8,128)(2,1)} %pair_ref.1), channel_id=1, source_target_pairs={{0,1},{1,0},{2,3},{3,2},{4,5},{5,4},{6,7},{7,6},{8,9},{9,8},{10,11... | collective-permute-start | bytes 12296 | tf_op jit(solution)/shard_map/ppermute | solution.py:302
  0.5 0.7 %copy-start.11 = (s32[16]{0:T(128)S(1)}, s32[16]{0:T(128)}, u32[]{:S(2)}) copy-start(s32[16]{0:T(128)} %param.19) | copy-start | bytes 196
  0.5 0.7 %copy-start.12 = (f32[128]{0:T(128)S(1)}, f32[128]{0:T(128)}, u32[]{:S(2)}) copy-start(f32[128]{0:T(128)} %param.21) | copy-start | bytes 1540
  0.5 0.7 %copy-start.13 = (f32[128]{0:T(128)S(1)}, f32[128]{0:T(128)}, u32[]{:S(2)}) copy-start(f32[128]{0:T(128)} %param.25) | copy-start | bytes 1540
  0.5 0.7 %copy-start.14 = (f32[128]{0:T(128)S(1)}, f32[128]{0:T(128)}, u32[]{:S(2)}) copy-start(f32[128]{0:T(128)} %param.27) | copy-start | bytes 1540
  0.5 0.7 %copy-start.8 = (bf16[2,8,128]{2,1,0:T(8,128)(2,1)S(1)}, bf16[2,8,128]{2,1,0:T(8,128)(2,1)}, u32[]{:S(2)}) copy-start(bf16[2,8,128]{2,1,0:T(8,128)(2,1)} %pair_ref.1) | copy-start | bytes 12292
  0.5 0.7 %copy-start.9 = (bf16[128,4]{0,1:T(4,128)(2,1)S(1)}, bf16[128,4]{0,1:T(4,128)(2,1)}, u32[]{:S(2)}) copy-start(bf16[128,4]{0,1:T(4,128)(2,1)} %param.30) | copy-start | bytes 3076
  0.5 0.7 %copy-start.10 = (s32[16]{0:T(128)S(1)}, s32[16]{0:T(128)}, u32[]{:S(2)}) copy-start(s32[16]{0:T(128)} %param.18) | copy-start | bytes 196
  1.2 10.2 %copy-start = (bf16[128,384]{1,0:T(8,128)(2,1)S(1)}, bf16[128,384]{1,0:T(8,128)(2,1)}, u32[]{:S(2)}) copy-start(bf16[128,384]{1,0:T(8,128)(2,1)} %refs_15_.1) | copy-start | bytes 294916
  1.2 10.2 %copy-start.1 = (bf16[128,256]{1,0:T(8,128)(2,1)S(1)}, bf16[128,256]{1,0:T(8,128)(2,1)}, u32[]{:S(2)}) copy-start(bf16[128,256]{1,0:T(8,128)(2,1)} %refs_11_.3) | copy-start | bytes 196612
  1.2 10.2 %copy-start.2 = (bf16[128,256]{1,0:T(8,128)(2,1)S(1)}, bf16[128,256]{1,0:T(8,128)(2,1)}, u32[]{:S(2)}) copy-start(bf16[128,256]{1,0:T(8,128)(2,1)} %refs_12_.3) | copy-start | bytes 196612
  1.2 10.2 %copy-start.4 = (bf16[128,128]{1,0:T(8,128)(2,1)S(1)}, bf16[128,128]{1,0:T(8,128)(2,1)}, u32[]{:S(2)}) copy-start(bf16[128,128]{1,0:T(8,128)(2,1)} %refs_14_.1) | copy-start | bytes 98308
  1.2 10.2 %copy-start.5 = (bf16[128,128]{1,0:T(8,128)(2,1)S(1)}, bf16[128,128]{1,0:T(8,128)(2,1)}, u32[]{:S(2)}) copy-start(bf16[128,128]{1,0:T(8,128)(2,1)} %refs_16_.1) | copy-start | bytes 98308
  1.3 10.2 %copy-start.6 = (bf16[128,128]{1,0:T(8,128)(2,1)S(1)}, bf16[128,128]{1,0:T(8,128)(2,1)}, u32[]{:S(2)}) copy-start(bf16[128,128]{1,0:T(8,128)(2,1)} %refs_17_.1) | copy-start | bytes 98308
  1.5 9.9 %copy-start.3 = (bf16[128,128]{1,0:T(8,128)(2,1)S(1)}, bf16[128,128]{1,0:T(8,128)(2,1)}, u32[]{:S(2)}) copy-start(bf16[128,128]{1,0:T(8,128)(2,1)} %refs_13_.3) | copy-start | bytes 98308
  1.5 6.1 %collective-permute-start.1 = (bf16[2,2,8,128]{3,2,1,0:T(8,128)(2,1)S(1)}, bf16[2,2,8,128]{3,2,1,0:T(8,128)(2,1)S(1)}, u32[]{:S(2)}, u32[]{:S(2)}) collective-permute-start(bf16[2,2,8,128]{3,2,1,0:T(8,128)(2,1)S(1)} %bitcast_dynamic-update-slice_fusion.refs_0_), channel_id=1, source_target_pairs={{0,9},{1,8},{2,11},{3,10},{4,13},{5,12},{6,15},{7,14},{8,1},{9,0},... | collective-permute-start | bytes 24584 | tf_op jit(solution)/shard_map/ppermute | solution.py:302
  5.3 5.8 %collective-permute-start.4 = (bf16[2,2,8,128]{3,2,1,0:T(8,128)(2,1)S(1)}, bf16[2,2,8,128]{3,2,1,0:T(8,128)(2,1)S(1)}, u32[]{:S(2)}, u32[]{:S(2)}) collective-permute-start(bf16[2,2,8,128]{3,2,1,0:T(8,128)(2,1)S(1)} %bitcast_dynamic-update-slice_fusion.refs_0_), channel_id=1, source_target_pairs={{0,15},{1,14},{2,13},{3,12},{4,11},{5,10},{6,9},{7,8},{8,7},{9,6},... | collective-permute-start | bytes 24584 | tf_op jit(solution)/shard_map/ppermute | solution.py:302
  7.4 4.0 %collective-permute-start.5 = (bf16[2,2,8,128]{3,2,1,0:T(8,128)(2,1)S(1)}, bf16[2,2,8,128]{3,2,1,0:T(8,128)(2,1)S(1)}, u32[]{:S(2)}, u32[]{:S(2)}) collective-permute-start(bf16[2,2,8,128]{3,2,1,0:T(8,128)(2,1)S(1)} %bitcast_dynamic-update-slice_fusion.refs_0_), channel_id=1, source_target_pairs={{0,7},{1,6},{2,5},{3,4},{4,3},{5,2},{6,1},{7,0},{8,15},{9,14},{10,... | collective-permute-start | bytes 24584 | tf_op jit(solution)/shard_map/ppermute | solution.py:302
  7.7 4.1 %collective-permute-start.2 = (bf16[4,2,8,128]{3,2,1,0:T(8,128)(2,1)S(1)}, bf16[4,2,8,128]{3,2,1,0:T(8,128)(2,1)S(1)}, u32[]{:S(2)}, u32[]{:S(2)}) collective-permute-start(bf16[4,2,8,128]{3,2,1,0:T(8,128)(2,1)S(1)} %pad_maximum_fusion), channel_id=1, source_target_pairs={{0,3},{1,2},{2,1},{3,0},{4,7},{5,6},{6,5},{7,4},{8,11},{9,10},{10,... | collective-permute-start | bytes 49160 | tf_op jit(solution)/shard_map/ppermute | solution.py:302
  8.2 3.8 %collective-permute-start.3 = (bf16[4,2,8,128]{3,2,1,0:T(8,128)(2,1)S(1)}, bf16[4,2,8,128]{3,2,1,0:T(8,128)(2,1)S(1)}, u32[]{:S(2)}, u32[]{:S(2)}) collective-permute-start(bf16[4,2,8,128]{3,2,1,0:T(8,128)(2,1)S(1)} %pad_maximum_fusion), channel_id=1, source_target_pairs={{0,5},{1,4},{2,7},{3,6},{4,1},{5,0},{6,3},{7,2},{8,13},{9,12},{10,... | collective-permute-start | bytes 49160 | tf_op jit(solution)/shard_map/ppermute | solution.py:302

commit v18 on v17

--- a/solution.py
+++ b/solution.py
@@ -11,6 +11,7 @@
 epsilon = 1e-05
 
 WHOLE_PAIR_BYTES = 256 * 1024
+SPARE_ROWS = 16
 STAGE_FLOPS = 10**9
 
 
@@ -127,7 +128,7 @@
 def early_kernel(orders, *refs):
     piece_refs = refs[: len(orders)]
     rel_ref, pair_mask_ref, gains_ref, in_weight_ref, in_gate_ref = refs[len(orders) : len(orders) + 5]
-    here = refs[-1].shape[0]
+    here = refs[-1].shape[0] - SPARE_ROWS
     found = edge_operands(
         piece_refs,
         orders,
@@ -139,7 +140,7 @@
         in_weight_ref[...],
     )
     for ref, values in zip(refs[-4:], found):
-        ref[...] = values
+        ref[:here] = values
 
 
 def whole_pair_kernel(row_dim, heads, early, late, *refs):
@@ -180,13 +181,13 @@
     row, col = lax.axis_index("row"), lax.axis_index("col")
     f32, bf16 = jnp.float32, jnp.bfloat16
 
-    here = early_left_ref.shape[0]
+    here = early_left_ref.shape[0] - SPARE_ROWS
     left, right, base, normed = edge_operands(
         piece_refs, late, rows, rel_ref[here:], pair_mask_ref[here:], gains_ref[0:1], in_gate_ref[...], in_weight_ref[...]
     )
-    late_left_ref[...] = left
-    late_base_ref[...] = base
-    late_normed_ref[...] = normed
+    late_left_ref[:here] = left
+    late_base_ref[:here] = base
+    late_normed_ref[:here] = normed
     lefts = (early_left_ref, late_left_ref)
 
     for at, token in enumerate(token_rows(chips_of(early + late), rows)):
@@ -237,14 +238,11 @@
     values = dot(column, qkv_ref[:, 2 * width :]).astype(bf16)
     own_gate = sigmoid(dot(own, att_gate_ref[...]))
 
-    bias = []
-    att_f = normed_att[column_pairs:].astype(f32)
-    for r in range(rows):
-        part = att_f[r * tokens : (r + 1) * tokens]
-        spread = jnp.concatenate(
-            [jnp.broadcast_to(part[k : k + 1], (cols, width)) for k in range(tokens)], axis=0
-        )
-        bias.append(round_bf16(dot_t(att_bias_ref[...], spread.astype(bf16))))
+    bias = dot_t(att_bias_ref[...], normed_att[column_pairs:]).astype(bf16)
+    shape = (rows * tokens, rows * column_pairs)
+    source = lax.broadcasted_iota(jnp.int32, shape, 0)
+    repeated = source == lax.broadcasted_iota(jnp.int32, shape, 1) // cols
+    bias = dot(bias, repeated.astype(f32).astype(bf16))
 
     head_of = lax.broadcasted_iota(jnp.int32, (own_pairs, width), 1) // head_dim
     queries = round_bf16(queries)
@@ -253,7 +251,11 @@
     ).astype(bf16)
     scores = dot_t(by_head, keys) * (1.0 / math.sqrt(head_dim))
     biases = jnp.concatenate(
-        [jnp.broadcast_to(bias[r][h : h + 1], (cols, column_pairs)) for h in range(heads) for r in range(rows)],
+        [
+            jnp.broadcast_to(bias[h : h + 1, r * column_pairs : (r + 1) * column_pairs], (cols, column_pairs))
+            for h in range(heads)
+            for r in range(rows)
+        ],
         axis=0,
     )
     key_bias = jnp.concatenate([key_bias_ref[...]] * (heads * rows), axis=0)
@@ -349,7 +351,7 @@
     last = [move(both, 3), move(both, 5)]
     weights = (tri_in_weight, tri_in_gate, tri_out_gate, tri_out_weight, att_qkv, att_gate, att_out)
     rel, pair_mask, gains, *_ = staged
-    half = jax.ShapeDtypeStruct((tokens * tokens // 2, width), jnp.float32)
+    half = jax.ShapeDtypeStruct((tokens * tokens // 2 + SPARE_ROWS, width), jnp.float32)
     halves = pl.pallas_call(
         functools.partial(early_kernel, early),
         out_shape=[half] * 4,
@@ -363,7 +365,7 @@
         out_shape=jax.ShapeDtypeStruct(pair_in.shape, pair_in.dtype),
         in_specs=[vmem] * (len(last) + 9 + len(weights)),
         out_specs=vmem,
-        scratch_shapes=[pltpu.VMEM(half.shape, half.dtype)] * 3 + [pltpu.VMEM(wide_out.shape, wide_out.dtype)],
+        scratch_shapes=[pltpu.VMEM(half.shape, half.dtype)] * 3 + [pltpu.VMEM((tokens * tokens + SPARE_ROWS, width), jnp.float32)],
         compiler_params=params,
     )(*last, *halves, *staged, *weights)
 

time: 14.2 us -> 14.2 us (level)
  no operation moved by 1% of the time
where the time goes in v18:
time: 14.2 us; the launch traced here: 14 us
  starting transfers between devices  9.42 us (66%)
  Pallas kernels  2.68 us (19%)
  waiting for transfers between devices  1.03 us (7%)
  local copies, waits for them, and re-layouts  0.77 us (5%)
    ppermute x6, starting transfers between devices, move(): lax.ppermute(values, ('row', 'col'), [(device, device ^ step) for device...  9.42 us
    pallas_call x1, Pallas kernels, whole_pair_on_device(): pl.pallas_call(functools.partial(whole_pair_kernel, row_dim, heads, early...  2.09 us
    ppermute x6, waiting for transfers between devices, move(): lax.ppermute(values, ('row', 'col'), [(device, device ^ step) for device...  1.03 us
    unnamed x30, local copies, waits for them, and re-layouts  0.76 us
    pallas_call x1, Pallas kernels, whole_pair_on_device(): pl.pallas_call(functools.partial(early_kernel, early), out_shape=[half] *...  0.35 us
  transfers between devices with their start and end apart: 6, of which 3 were waited for; matrix products, arithmetic and copies ran while one was open for 0% of the time, Pallas kernels for 4%

profile of v18, /device:TPU:0, one launch (start us, length us, event | category | flops | bytes accessed | tf_op | source)
XLA Modules:
  0.0 14.0 jit_solution(2048423543159417306)
XLA Ops:
  0.0 0.0 copy-start.7
  0.0 0.5 %collective-permute-start = (bf16[2,8,128]{2,1,0:T(8,128)(2,1)}, bf16[2,8,128]{2,1,0:T(8,128)(2,1)S(1)}, u32[]{:S(2)}, u32[]{:S(2)}) collective-permute-start(bf16[2,8,128]{2,1,0:T(8,128)(2,1)} %pair_ref.1), channel_id=1, source_target_pairs={{0,1},{1,0},{2,3},{3,2},{4,5},{5,4},{6,7},{7,6},{8,9},{9,8},{10,11... | collective-permute-start | bytes 12296 | tf_op jit(solution)/shard_map/ppermute | solution.py:304
  0.5 0.0 copy-start.11
  0.5 0.0 copy-start.12
  0.5 0.0 copy-start.13
  0.5 0.0 copy-start.14
  0.5 0.0 copy-start.8
  0.5 0.0 copy-start.9
  0.5 0.0 copy-start.10
  0.5 0.2 %copy-done.7 = bf16[128,128]{1,0:T(8,128)(2,1)S(1)} copy-done((bf16[128,128]{1,0:T(8,128)(2,1)S(1)}, bf16[128,128]{1,0:T(8,128)(2,1)}, u32[]{:S(2)}) %copy-start.7) | copy-done | bytes 32792
  0.8 0.4 %copy-done.11 = s32[16]{0:T(128)S(1)} copy-done((s32[16]{0:T(128)S(1)}, s32[16]{0:T(128)}, u32[]{:S(2)}) %copy-start.11) | copy-done | bytes 88
  1.1 0.0 copy-done.12
  1.1 0.0 copy-done.13
  1.1 0.0 copy-done.14
  1.2 0.0 copy-done.8
  1.2 0.0 copy-done.9
  1.2 0.0 copy-done.10
  1.2 0.0 copy-start
  1.2 0.0 copy-start.1
  1.2 0.0 copy-start.2
  1.2 0.0 copy-start.4
  1.2 0.0 copy-start.5
  1.3 0.0 copy-start.6
  1.3 0.2 %shard_map.146 = (bf16[2,2,8,128]{3,2,1,0:T(8,128)(2,1)S(1)}, f32[256,128]{1,0:T(8,128)S(1)}, f32[256,128]{1,0:T(8,128)S(1)}, f32[3,128]{1,0:T(4,128)S(1)}, bf16...) custom-call(bf16[2,8,128]{2,1,0:T(8,128)(2,1)S(1)} %copy-done.8, s32[1,16]{1,0:T(1,128)S(1)} %bitcast.9, ...), custom_call_target="tpu_custom_call" | custom-call | flops 1000000000 | bytes 1048576 | tf_op jit(solution)/shard_map/pallas_call | solution.py:320
  1.5 0.0 copy-start.3
  1.5 0.0 collective-permute-done
  1.5 3.8 %collective-permute-start.1 = (bf16[2,2,8,128]{3,2,1,0:T(8,128)(2,1)S(1)}, bf16[2,2,8,128]{3,2,1,0:T(8,128)(2,1)S(1)}, u32[]{:S(2)}, u32[]{:S(2)}) collective-permute-start(bf16[2,2,8,128]{3,2,1,0:T(8,128)(2,1)S(1)} %bitcast_dynamic-update-slice_fusion.refs_0_), channel_id=1, source_target_pairs={{0,9},{1,8},{2,11},{3,10},{4,13},{5,12},{6,15},{7,14},{8,1},{9,0},... | collective-permute-start | bytes 24584 | tf_op jit(solution)/shard_map/ppermute | solution.py:304
  5.3 2.1 %collective-permute-start.4 = (bf16[2,2,8,128]{3,2,1,0:T(8,128)(2,1)S(1)}, bf16[2,2,8,128]{3,2,1,0:T(8,128)(2,1)S(1)}, u32[]{:S(2)}, u32[]{:S(2)}) collective-permute-start(bf16[2,2,8,128]{3,2,1,0:T(8,128)(2,1)S(1)} %bitcast_dynamic-update-slice_fusion.refs_0_), channel_id=1, source_target_pairs={{0,15},{1,14},{2,13},{3,12},{4,11},{5,10},{6,9},{7,8},{8,7},{9,6},... | collective-permute-start | bytes 24584 | tf_op jit(solution)/shard_map/ppermute | solution.py:304
  7.4 0.2 %collective-permute-start.5 = (bf16[2,2,8,128]{3,2,1,0:T(8,128)(2,1)S(1)}, bf16[2,2,8,128]{3,2,1,0:T(8,128)(2,1)S(1)}, u32[]{:S(2)}, u32[]{:S(2)}) collective-permute-start(bf16[2,2,8,128]{3,2,1,0:T(8,128)(2,1)S(1)} %bitcast_dynamic-update-slice_fusion.refs_0_), channel_id=1, source_target_pairs={{0,7},{1,6},{2,5},{3,4},{4,3},{5,2},{6,1},{7,0},{8,15},{9,14},{10,... | collective-permute-start | bytes 24584 | tf_op jit(solution)/shard_map/ppermute | solution.py:304
  7.7 0.0 collective-permute-done.1.refs_1_
  7.7 0.5 %collective-permute-start.2 = (bf16[4,2,8,128]{3,2,1,0:T(8,128)(2,1)S(1)}, bf16[4,2,8,128]{3,2,1,0:T(8,128)(2,1)S(1)}, u32[]{:S(2)}, u32[]{:S(2)}) collective-permute-start(bf16[4,2,8,128]{3,2,1,0:T(8,128)(2,1)S(1)} %pad_maximum_fusion), channel_id=1, source_target_pairs={{0,3},{1,2},{2,1},{3,0},{4,7},{5,6},{6,5},{7,4},{8,11},{9,10},{10,... | collective-permute-start | bytes 49160 | tf_op jit(solution)/shard_map/ppermute | solution.py:304
  8.2 2.3 %collective-permute-start.3 = (bf16[4,2,8,128]{3,2,1,0:T(8,128)(2,1)S(1)}, bf16[4,2,8,128]{3,2,1,0:T(8,128)(2,1)S(1)}, u32[]{:S(2)}, u32[]{:S(2)}) collective-permute-start(bf16[4,2,8,128]{3,2,1,0:T(8,128)(2,1)S(1)} %pad_maximum_fusion), channel_id=1, source_target_pairs={{0,5},{1,4},{2,7},{3,6},{4,1},{5,0},{6,3},{7,2},{8,13},{9,12},{10,... | collective-permute-start | bytes 49160 | tf_op jit(solution)/shard_map/ppermute | solution.py:304
  10.5 0.6 %collective-permute-done.4.refs_2_ = bf16[2,2,8,128]{3,2,1,0:T(8,128)(2,1)S(1)} collective-permute-done((bf16[2,2,8,128]{3,2,1,0:T(8,128)(2,1)S(1)}, bf16[2,2,8,128]{3,2,1,0:T(8,128)(2,1)S(1)}, u32[]{:S(2)}, u32[]{:S(2)}) %collective-permute-start.4) | collective-permute-done | bytes 8224 | tf_op jit(solution)/shard_map/ppermute | solution.py:304
  11.1 0.3 %collective-permute-done.5.refs_3_ = bf16[2,2,8,128]{3,2,1,0:T(8,128)(2,1)S(1)} collective-permute-done((bf16[2,2,8,128]{3,2,1,0:T(8,128)(2,1)S(1)}, bf16[2,2,8,128]{3,2,1,0:T(8,128)(2,1)S(1)}, u32[]{:S(2)}, u32[]{:S(2)}) %collective-permute-start.5) | collective-permute-done | bytes 8224 | tf_op jit(solution)/shard_map/ppermute | solution.py:304
  11.4 0.0 copy-done
  11.4 0.0 copy-done.1
  11.4 0.0 copy-done.2
  11.4 0.0 copy-done.4
  11.4 0.0 copy-done.5
  11.4 0.0 copy-done.6
  11.4 0.0 copy-done.3
  11.4 0.3 %shard_map.147 = (f32[144,128]{1,0:T(8,128)S(1)}, f32[144,128]{1,0:T(8,128)S(1)}, f32[144,128]{1,0:T(8,128)S(1)}, f32[144,128]{1,0:T(8,128)S(1)}) custom-call(bf16[2,2,8,128]{3,2,1,0:T(8,128)(2,1)S(1)} %bitcast_dynamic-update-slice_fusion.refs_0_, bf16[2,2,8,128]{3,2,1,0:T(8,128)(2,1)S(1)} %collective-permute-done.1.refs_1_, ...), custom_call_target="tpu_custom_call" | custom-call | flops 1000000000 | bytes 1048576 | tf_op jit(solution)/shard_map/pallas_call | solution.py:355
  11.8 0.0 collective-permute-done.2.refs_0_
  11.8 0.1 %collective-permute-done.3.refs_1_ = bf16[4,2,8,128]{3,2,1,0:T(8,128)(2,1)S(1)} collective-permute-done((bf16[4,2,8,128]{3,2,1,0:T(8,128)(2,1)S(1)}, bf16[4,2,8,128]{3,2,1,0:T(8,128)(2,1)S(1)}, u32[]{:S(2)}, u32[]{:S(2)}) %collective-permute-start.3) | collective-permute-done | bytes 16416 | tf_op jit(solution)/shard_map/ppermute | solution.py:304
  12.0 2.1 %shard_map.148 = bf16[2,8,128]{2,1,0:T(8,128)(2,1)} custom-call(bf16[4,2,8,128]{3,2,1,0:T(8,128)(2,1)S(1)} %collective-permute-done.2.refs_0_, bf16[4,2,8,128]{3,2,1,0:T(8,128)(2,1)S(1)} %collective-permute-done.3.refs_1_, f32[144,128]{1,0:T(8,128)S(1)} %get-tuple-element.31.refs_2_, f32[144,128]{1,0:T(8,128)S(1)} %get-tuple-element.32.refs_3_, ...), custom_call_target="tpu_custom_call" | custom-call | tf_op jit(solution)/shard_map/pallas_call | solution.py:363
  (3 shorter events, 0.0 us)
Async XLA Ops:
  0.0 0.8 %copy-start.7 = (bf16[128,128]{1,0:T(8,128)(2,1)S(1)}, bf16[128,128]{1,0:T(8,128)(2,1)}, u32[]{:S(2)}) copy-start(bf16[128,128]{1,0:T(8,128)(2,1)} %table_ref.1) | copy-start | bytes 98308
  0.0 1.5 %collective-permute-start = (bf16[2,8,128]{2,1,0:T(8,128)(2,1)}, bf16[2,8,128]{2,1,0:T(8,128)(2,1)S(1)}, u32[]{:S(2)}, u32[]{:S(2)}) collective-permute-start(bf16[2,8,128]{2,1,0:T(8,128)(2,1)} %pair_ref.1), channel_id=1, source_target_pairs={{0,1},{1,0},{2,3},{3,2},{4,5},{5,4},{6,7},{7,6},{8,9},{9,8},{10,11... | collective-permute-start | bytes 12296 | tf_op jit(solution)/shard_map/ppermute | solution.py:304
  0.5 0.7 %copy-start.11 = (s32[16]{0:T(128)S(1)}, s32[16]{0:T(128)}, u32[]{:S(2)}) copy-start(s32[16]{0:T(128)} %param.19) | copy-start | bytes 196
  0.5 0.7 %copy-start.12 = (f32[128]{0:T(128)S(1)}, f32[128]{0:T(128)}, u32[]{:S(2)}) copy-start(f32[128]{0:T(128)} %param.21) | copy-start | bytes 1540
  0.5 0.7 %copy-start.13 = (f32[128]{0:T(128)S(1)}, f32[128]{0:T(128)}, u32[]{:S(2)}) copy-start(f32[128]{0:T(128)} %param.25) | copy-start | bytes 1540
  0.5 0.7 %copy-start.14 = (f32[128]{0:T(128)S(1)}, f32[128]{0:T(128)}, u32[]{:S(2)}) copy-start(f32[128]{0:T(128)} %param.27) | copy-start | bytes 1540
  0.5 0.7 %copy-start.8 = (bf16[2,8,128]{2,1,0:T(8,128)(2,1)S(1)}, bf16[2,8,128]{2,1,0:T(8,128)(2,1)}, u32[]{:S(2)}) copy-start(bf16[2,8,128]{2,1,0:T(8,128)(2,1)} %pair_ref.1) | copy-start | bytes 12292
  0.5 0.7 %copy-start.9 = (bf16[128,4]{0,1:T(4,128)(2,1)S(1)}, bf16[128,4]{0,1:T(4,128)(2,1)}, u32[]{:S(2)}) copy-start(bf16[128,4]{0,1:T(4,128)(2,1)} %param.30) | copy-start | bytes 3076
  0.5 0.7 %copy-start.10 = (s32[16]{0:T(128)S(1)}, s32[16]{0:T(128)}, u32[]{:S(2)}) copy-start(s32[16]{0:T(128)} %param.18) | copy-start | bytes 196
  1.2 10.2 %copy-start = (bf16[128,384]{1,0:T(8,128)(2,1)S(1)}, bf16[128,384]{1,0:T(8,128)(2,1)}, u32[]{:S(2)}) copy-start(bf16[128,384]{1,0:T(8,128)(2,1)} %refs_15_.1) | copy-start | bytes 294916
  1.2 10.2 %copy-start.1 = (bf16[128,256]{1,0:T(8,128)(2,1)S(1)}, bf16[128,256]{1,0:T(8,128)(2,1)}, u32[]{:S(2)}) copy-start(bf16[128,256]{1,0:T(8,128)(2,1)} %refs_11_.3) | copy-start | bytes 196612
  1.2 10.2 %copy-start.2 = (bf16[128,256]{1,0:T(8,128)(2,1)S(1)}, bf16[128,256]{1,0:T(8,128)(2,1)}, u32[]{:S(2)}) copy-start(bf16[128,256]{1,0:T(8,128)(2,1)} %refs_12_.3) | copy-start | bytes 196612
  1.2 10.2 %copy-start.4 = (bf16[128,128]{1,0:T(8,128)(2,1)S(1)}, bf16[128,128]{1,0:T(8,128)(2,1)}, u32[]{:S(2)}) copy-start(bf16[128,128]{1,0:T(8,128)(2,1)} %refs_14_.1) | copy-start | bytes 98308
  1.2 10.2 %copy-start.5 = (bf16[128,128]{1,0:T(8,128)(2,1)S(1)}, bf16[128,128]{1,0:T(8,128)(2,1)}, u32[]{:S(2)}) copy-start(bf16[128,128]{1,0:T(8,128)(2,1)} %refs_16_.1) | copy-start | bytes 98308
  1.3 10.2 %copy-start.6 = (bf16[128,128]{1,0:T(8,128)(2,1)S(1)}, bf16[128,128]{1,0:T(8,128)(2,1)}, u32[]{:S(2)}) copy-start(bf16[128,128]{1,0:T(8,128)(2,1)} %refs_17_.1) | copy-start | bytes 98308
  1.5 9.9 %copy-start.3 = (bf16[128,128]{1,0:T(8,128)(2,1)S(1)}, bf16[128,128]{1,0:T(8,128)(2,1)}, u32[]{:S(2)}) copy-start(bf16[128,128]{1,0:T(8,128)(2,1)} %refs_13_.3) | copy-start | bytes 98308
  1.5 6.1 %collective-permute-start.1 = (bf16[2,2,8,128]{3,2,1,0:T(8,128)(2,1)S(1)}, bf16[2,2,8,128]{3,2,1,0:T(8,128)(2,1)S(1)}, u32[]{:S(2)}, u32[]{:S(2)}) collective-permute-start(bf16[2,2,8,128]{3,2,1,0:T(8,128)(2,1)S(1)} %bitcast_dynamic-update-slice_fusion.refs_0_), channel_id=1, source_target_pairs={{0,9},{1,8},{2,11},{3,10},{4,13},{5,12},{6,15},{7,14},{8,1},{9,0},... | collective-permute-start | bytes 24584 | tf_op jit(solution)/shard_map/ppermute | solution.py:304
  5.3 5.8 %collective-permute-start.4 = (bf16[2,2,8,128]{3,2,1,0:T(8,128)(2,1)S(1)}, bf16[2,2,8,128]{3,2,1,0:T(8,128)(2,1)S(1)}, u32[]{:S(2)}, u32[]{:S(2)}) collective-permute-start(bf16[2,2,8,128]{3,2,1,0:T(8,128)(2,1)S(1)} %bitcast_dynamic-update-slice_fusion.refs_0_), channel_id=1, source_target_pairs={{0,15},{1,14},{2,13},{3,12},{4,11},{5,10},{6,9},{7,8},{8,7},{9,6},... | collective-permute-start | bytes 24584 | tf_op jit(solution)/shard_map/ppermute | solution.py:304
  7.4 4.0 %collective-permute-start.5 = (bf16[2,2,8,128]{3,2,1,0:T(8,128)(2,1)S(1)}, bf16[2,2,8,128]{3,2,1,0:T(8,128)(2,1)S(1)}, u32[]{:S(2)}, u32[]{:S(2)}) collective-permute-start(bf16[2,2,8,128]{3,2,1,0:T(8,128)(2,1)S(1)} %bitcast_dynamic-update-slice_fusion.refs_0_), channel_id=1, source_target_pairs={{0,7},{1,6},{2,5},{3,4},{4,3},{5,2},{6,1},{7,0},{8,15},{9,14},{10,... | collective-permute-start | bytes 24584 | tf_op jit(solution)/shard_map/ppermute | solution.py:304
  7.7 4.1 %collective-permute-start.2 = (bf16[4,2,8,128]{3,2,1,0:T(8,128)(2,1)S(1)}, bf16[4,2,8,128]{3,2,1,0:T(8,128)(2,1)S(1)}, u32[]{:S(2)}, u32[]{:S(2)}) collective-permute-start(bf16[4,2,8,128]{3,2,1,0:T(8,128)(2,1)S(1)} %pad_maximum_fusion), channel_id=1, source_target_pairs={{0,3},{1,2},{2,1},{3,0},{4,7},{5,6},{6,5},{7,4},{8,11},{9,10},{10,... | collective-permute-start | bytes 49160 | tf_op jit(solution)/shard_map/ppermute | solution.py:304
  8.2 3.8 %collective-permute-start.3 = (bf16[4,2,8,128]{3,2,1,0:T(8,128)(2,1)S(1)}, bf16[4,2,8,128]{3,2,1,0:T(8,128)(2,1)S(1)}, u32[]{:S(2)}, u32[]{:S(2)}) collective-permute-start(bf16[4,2,8,128]{3,2,1,0:T(8,128)(2,1)S(1)} %pad_maximum_fusion), channel_id=1, source_target_pairs={{0,5},{1,4},{2,7},{3,6},{4,1},{5,0},{6,3},{7,2},{8,13},{9,12},{10,... | collective-permute-start | bytes 49160 | tf_op jit(solution)/shard_map/ppermute | solution.py:304

commit v19 on v18

--- a/solution.py
+++ b/solution.py
@@ -174,6 +174,7 @@
     late_base_ref,
     late_normed_ref,
     right_ref,
+    products_ref,
 ):
     rows, cols, width = piece_refs[0].shape[1:]
     tokens = row_dim * rows
@@ -199,20 +200,28 @@
             right_ref[place, :] = right[first - here : first - here + tokens]
 
     right_at = [right_ref[pl.ds(col * cols * tokens + m, cols, stride=tokens), :] for m in range(tokens)]
-    products = []
-    for i in range(tokens):
-        ref, first = lefts[i * tokens // here], i * tokens % here
-        total = ref[first : first + 1] * right_at[0]
-        for m in range(1, tokens):
-            total = total + ref[first + m : first + m + 1] * right_at[m]
-        products.append(total)
+    together = 4
+    for at, ref in enumerate(lefts):
+
+        def some_tokens(step, carry, at=at, ref=ref):
+            for i in range(together):
+                i = step * together + i
+                first = pl.multiple_of(i * tokens, tokens)
+                total = ref[pl.ds(first, 1), :] * right_at[0]
+                for m in range(1, tokens):
+                    total = total + ref[pl.ds(first + m, 1), :] * right_at[m]
+                place = pl.multiple_of((at * here // tokens + i) * cols, cols)
+                products_ref[pl.ds(place, cols), :] = total
+            return carry
+
+        lax.fori_loop(0, here // tokens // together, some_tokens, 0)
     extra = [None] * rows
     for m in range(tokens):
         left_at = jnp.concatenate([ref[pl.ds(m, here // tokens, stride=tokens), :] for ref in lefts], axis=0)
         for r in range(rows):
             term = left_at * early_right_ref[r * tokens + m : r * tokens + m + 1]
             extra[r] = term if m == 0 else extra[r] + term
-    products = round_bf16(jnp.concatenate(products + extra, axis=0))
+    products = round_bf16(jnp.concatenate([products_ref[...]] + extra, axis=0))
 
     own_token = row * rows
     own_column = ((own_token // cols) ^ col) * cols + own_token % cols
@@ -365,7 +374,7 @@
         out_shape=jax.ShapeDtypeStruct(pair_in.shape, pair_in.dtype),
         in_specs=[vmem] * (len(last) + 9 + len(weights)),
         out_specs=vmem,
-        scratch_shapes=[pltpu.VMEM(half.shape, half.dtype)] * 3 + [pltpu.VMEM((tokens * tokens + SPARE_ROWS, width), jnp.float32)],
+        scratch_shapes=[pltpu.VMEM(half.shape, half.dtype)] * 3 + [pltpu.VMEM((count, width), jnp.float32) for count in (tokens * tokens + SPARE_ROWS, tokens * cols)],
         compiler_params=params,
     )(*last, *halves, *staged, *weights)
 

time: 14.2 us -> 14.3 us (level)
  no operation moved by 1% of the time
where the time goes in v19:
time: 14.3 us; the launch traced here: 14.1 us
  starting transfers between devices  9.42 us (66%)
  Pallas kernels  2.74 us (19%)
  waiting for transfers between devices  1.03 us (7%)
  local copies, waits for them, and re-layouts  0.77 us (5%)
    ppermute x6, starting transfers between devices, move(): lax.ppermute(values, ('row', 'col'), [(device, device ^ step) for device...  9.42 us
    pallas_call x1, Pallas kernels, whole_pair_on_device(): pl.pallas_call(functools.partial(whole_pair_kernel, row_dim, heads, early...  2.15 us
    ppermute x6, waiting for transfers between devices, move(): lax.ppermute(values, ('row', 'col'), [(device, device ^ step) for device...  1.03 us
    unnamed x30, local copies, waits for them, and re-layouts  0.76 us
    pallas_call x1, Pallas kernels, whole_pair_on_device(): pl.pallas_call(functools.partial(early_kernel, early), out_shape=[half] *...  0.35 us
  transfers between devices with their start and end apart: 6, of which 3 were waited for; matrix products, arithmetic and copies ran while one was open for 0% of the time, Pallas kernels for 4%

profile of v19, /device:TPU:0, one launch (start us, length us, event | category | flops | bytes accessed | tf_op | source)
XLA Modules:
  0.0 14.1 jit_solution(3062384698192863948)
XLA Ops:
  0.0 0.0 copy-start.7
  0.0 0.5 %collective-permute-start = (bf16[2,8,128]{2,1,0:T(8,128)(2,1)}, bf16[2,8,128]{2,1,0:T(8,128)(2,1)S(1)}, u32[]{:S(2)}, u32[]{:S(2)}) collective-permute-start(bf16[2,8,128]{2,1,0:T(8,128)(2,1)} %pair_ref.1), channel_id=1, source_target_pairs={{0,1},{1,0},{2,3},{3,2},{4,5},{5,4},{6,7},{7,6},{8,9},{9,8},{10,11... | collective-permute-start | bytes 12296 | tf_op jit(solution)/shard_map/ppermute | solution.py:313
  0.5 0.0 copy-start.11
  0.5 0.0 copy-start.12
  0.5 0.0 copy-start.13
  0.5 0.0 copy-start.14
  0.5 0.0 copy-start.8
  0.5 0.0 copy-start.9
  0.5 0.0 copy-start.10
  0.5 0.2 %copy-done.7 = bf16[128,128]{1,0:T(8,128)(2,1)S(1)} copy-done((bf16[128,128]{1,0:T(8,128)(2,1)S(1)}, bf16[128,128]{1,0:T(8,128)(2,1)}, u32[]{:S(2)}) %copy-start.7) | copy-done | bytes 32792
  0.8 0.4 %copy-done.11 = s32[16]{0:T(128)S(1)} copy-done((s32[16]{0:T(128)S(1)}, s32[16]{0:T(128)}, u32[]{:S(2)}) %copy-start.11) | copy-done | bytes 88
  1.1 0.0 copy-done.12
  1.1 0.0 copy-done.13
  1.1 0.0 copy-done.14
  1.2 0.0 copy-done.8
  1.2 0.0 copy-done.9
  1.2 0.0 copy-done.10
  1.2 0.0 copy-start
  1.2 0.0 copy-start.1
  1.2 0.0 copy-start.2
  1.2 0.0 copy-start.4
  1.2 0.0 copy-start.5
  1.3 0.0 copy-start.6
  1.3 0.2 %shard_map.146 = (bf16[2,2,8,128]{3,2,1,0:T(8,128)(2,1)S(1)}, f32[256,128]{1,0:T(8,128)S(1)}, f32[256,128]{1,0:T(8,128)S(1)}, f32[3,128]{1,0:T(4,128)S(1)}, bf16...) custom-call(bf16[2,8,128]{2,1,0:T(8,128)(2,1)S(1)} %copy-done.8, s32[1,16]{1,0:T(1,128)S(1)} %bitcast.9, ...), custom_call_target="tpu_custom_call" | custom-call | flops 1000000000 | bytes 1048576 | tf_op jit(solution)/shard_map/pallas_call | solution.py:329
  1.5 0.0 copy-start.3
  1.5 0.0 collective-permute-done
  1.5 3.8 %collective-permute-start.1 = (bf16[2,2,8,128]{3,2,1,0:T(8,128)(2,1)S(1)}, bf16[2,2,8,128]{3,2,1,0:T(8,128)(2,1)S(1)}, u32[]{:S(2)}, u32[]{:S(2)}) collective-permute-start(bf16[2,2,8,128]{3,2,1,0:T(8,128)(2,1)S(1)} %bitcast_dynamic-update-slice_fusion.refs_0_), channel_id=1, source_target_pairs={{0,9},{1,8},{2,11},{3,10},{4,13},{5,12},{6,15},{7,14},{8,1},{9,0},... | collective-permute-start | bytes 24584 | tf_op jit(solution)/shard_map/ppermute | solution.py:313
  5.3 2.1 %collective-permute-start.4 = (bf16[2,2,8,128]{3,2,1,0:T(8,128)(2,1)S(1)}, bf16[2,2,8,128]{3,2,1,0:T(8,128)(2,1)S(1)}, u32[]{:S(2)}, u32[]{:S(2)}) collective-permute-start(bf16[2,2,8,128]{3,2,1,0:T(8,128)(2,1)S(1)} %bitcast_dynamic-update-slice_fusion.refs_0_), channel_id=1, source_target_pairs={{0,15},{1,14},{2,13},{3,12},{4,11},{5,10},{6,9},{7,8},{8,7},{9,6},... | collective-permute-start | bytes 24584 | tf_op jit(solution)/shard_map/ppermute | solution.py:313
  7.4 0.2 %collective-permute-start.5 = (bf16[2,2,8,128]{3,2,1,0:T(8,128)(2,1)S(1)}, bf16[2,2,8,128]{3,2,1,0:T(8,128)(2,1)S(1)}, u32[]{:S(2)}, u32[]{:S(2)}) collective-permute-start(bf16[2,2,8,128]{3,2,1,0:T(8,128)(2,1)S(1)} %bitcast_dynamic-update-slice_fusion.refs_0_), channel_id=1, source_target_pairs={{0,7},{1,6},{2,5},{3,4},{4,3},{5,2},{6,1},{7,0},{8,15},{9,14},{10,... | collective-permute-start | bytes 24584 | tf_op jit(solution)/shard_map/ppermute | solution.py:313
  7.7 0.0 collective-permute-done.1.refs_1_
  7.7 0.5 %collective-permute-start.2 = (bf16[4,2,8,128]{3,2,1,0:T(8,128)(2,1)S(1)}, bf16[4,2,8,128]{3,2,1,0:T(8,128)(2,1)S(1)}, u32[]{:S(2)}, u32[]{:S(2)}) collective-permute-start(bf16[4,2,8,128]{3,2,1,0:T(8,128)(2,1)S(1)} %pad_maximum_fusion), channel_id=1, source_target_pairs={{0,3},{1,2},{2,1},{3,0},{4,7},{5,6},{6,5},{7,4},{8,11},{9,10},{10,... | collective-permute-start | bytes 49160 | tf_op jit(solution)/shard_map/ppermute | solution.py:313
  8.2 2.3 %collective-permute-start.3 = (bf16[4,2,8,128]{3,2,1,0:T(8,128)(2,1)S(1)}, bf16[4,2,8,128]{3,2,1,0:T(8,128)(2,1)S(1)}, u32[]{:S(2)}, u32[]{:S(2)}) collective-permute-start(bf16[4,2,8,128]{3,2,1,0:T(8,128)(2,1)S(1)} %pad_maximum_fusion), channel_id=1, source_target_pairs={{0,5},{1,4},{2,7},{3,6},{4,1},{5,0},{6,3},{7,2},{8,13},{9,12},{10,... | collective-permute-start | bytes 49160 | tf_op jit(solution)/shard_map/ppermute | solution.py:313
  10.5 0.6 %collective-permute-done.4.refs_2_ = bf16[2,2,8,128]{3,2,1,0:T(8,128)(2,1)S(1)} collective-permute-done((bf16[2,2,8,128]{3,2,1,0:T(8,128)(2,1)S(1)}, bf16[2,2,8,128]{3,2,1,0:T(8,128)(2,1)S(1)}, u32[]{:S(2)}, u32[]{:S(2)}) %collective-permute-start.4) | collective-permute-done | bytes 8224 | tf_op jit(solution)/shard_map/ppermute | solution.py:313
  11.1 0.3 %collective-permute-done.5.refs_3_ = bf16[2,2,8,128]{3,2,1,0:T(8,128)(2,1)S(1)} collective-permute-done((bf16[2,2,8,128]{3,2,1,0:T(8,128)(2,1)S(1)}, bf16[2,2,8,128]{3,2,1,0:T(8,128)(2,1)S(1)}, u32[]{:S(2)}, u32[]{:S(2)}) %collective-permute-start.5) | collective-permute-done | bytes 8224 | tf_op jit(solution)/shard_map/ppermute | solution.py:313
  11.4 0.0 copy-done
  11.4 0.0 copy-done.1
  11.4 0.0 copy-done.2
  11.4 0.0 copy-done.4
  11.4 0.0 copy-done.5
  11.4 0.0 copy-done.6
  11.4 0.0 copy-done.3
  11.4 0.3 %shard_map.147 = (f32[144,128]{1,0:T(8,128)S(1)}, f32[144,128]{1,0:T(8,128)S(1)}, f32[144,128]{1,0:T(8,128)S(1)}, f32[144,128]{1,0:T(8,128)S(1)}) custom-call(bf16[2,2,8,128]{3,2,1,0:T(8,128)(2,1)S(1)} %bitcast_dynamic-update-slice_fusion.refs_0_, bf16[2,2,8,128]{3,2,1,0:T(8,128)(2,1)S(1)} %collective-permute-done.1.refs_1_, ...), custom_call_target="tpu_custom_call" | custom-call | flops 1000000000 | bytes 1048576 | tf_op jit(solution)/shard_map/pallas_call | solution.py:364
  11.8 0.0 collective-permute-done.2.refs_0_
  11.8 0.1 %collective-permute-done.3.refs_1_ = bf16[4,2,8,128]{3,2,1,0:T(8,128)(2,1)S(1)} collective-permute-done((bf16[4,2,8,128]{3,2,1,0:T(8,128)(2,1)S(1)}, bf16[4,2,8,128]{3,2,1,0:T(8,128)(2,1)S(1)}, u32[]{:S(2)}, u32[]{:S(2)}) %collective-permute-start.3) | collective-permute-done | bytes 16416 | tf_op jit(solution)/shard_map/ppermute | solution.py:313
  12.0 2.1 %shard_map.148 = bf16[2,8,128]{2,1,0:T(8,128)(2,1)} custom-call(bf16[4,2,8,128]{3,2,1,0:T(8,128)(2,1)S(1)} %collective-permute-done.2.refs_0_, bf16[4,2,8,128]{3,2,1,0:T(8,128)(2,1)S(1)} %collective-permute-done.3.refs_1_, f32[144,128]{1,0:T(8,128)S(1)} %get-tuple-element.31.refs_2_, f32[144,128]{1,0:T(8,128)S(1)} %get-tuple-element.32.refs_3_, ...), custom_call_target="tpu_custom_call" | custom-call | tf_op jit(solution)/shard_map/pallas_call | solution.py:372
  (3 shorter events, 0.0 us)
Async XLA Ops:
  0.0 0.8 %copy-start.7 = (bf16[128,128]{1,0:T(8,128)(2,1)S(1)}, bf16[128,128]{1,0:T(8,128)(2,1)}, u32[]{:S(2)}) copy-start(bf16[128,128]{1,0:T(8,128)(2,1)} %table_ref.1) | copy-start | bytes 98308
  0.0 1.5 %collective-permute-start = (bf16[2,8,128]{2,1,0:T(8,128)(2,1)}, bf16[2,8,128]{2,1,0:T(8,128)(2,1)S(1)}, u32[]{:S(2)}, u32[]{:S(2)}) collective-permute-start(bf16[2,8,128]{2,1,0:T(8,128)(2,1)} %pair_ref.1), channel_id=1, source_target_pairs={{0,1},{1,0},{2,3},{3,2},{4,5},{5,4},{6,7},{7,6},{8,9},{9,8},{10,11... | collective-permute-start | bytes 12296 | tf_op jit(solution)/shard_map/ppermute | solution.py:313
  0.5 0.7 %copy-start.11 = (s32[16]{0:T(128)S(1)}, s32[16]{0:T(128)}, u32[]{:S(2)}) copy-start(s32[16]{0:T(128)} %param.19) | copy-start | bytes 196
  0.5 0.7 %copy-start.12 = (f32[128]{0:T(128)S(1)}, f32[128]{0:T(128)}, u32[]{:S(2)}) copy-start(f32[128]{0:T(128)} %param.21) | copy-start | bytes 1540
  0.5 0.7 %copy-start.13 = (f32[128]{0:T(128)S(1)}, f32[128]{0:T(128)}, u32[]{:S(2)}) copy-start(f32[128]{0:T(128)} %param.25) | copy-start | bytes 1540
  0.5 0.7 %copy-start.14 = (f32[128]{0:T(128)S(1)}, f32[128]{0:T(128)}, u32[]{:S(2)}) copy-start(f32[128]{0:T(128)} %param.27) | copy-start | bytes 1540
  0.5 0.7 %copy-start.8 = (bf16[2,8,128]{2,1,0:T(8,128)(2,1)S(1)}, bf16[2,8,128]{2,1,0:T(8,128)(2,1)}, u32[]{:S(2)}) copy-start(bf16[2,8,128]{2,1,0:T(8,128)(2,1)} %pair_ref.1) | copy-start | bytes 12292
  0.5 0.7 %copy-start.9 = (bf16[128,4]{0,1:T(4,128)(2,1)S(1)}, bf16[128,4]{0,1:T(4,128)(2,1)}, u32[]{:S(2)}) copy-start(bf16[128,4]{0,1:T(4,128)(2,1)} %param.30) | copy-start | bytes 3076
  0.5 0.7 %copy-start.10 = (s32[16]{0:T(128)S(1)}, s32[16]{0:T(128)}, u32[]{:S(2)}) copy-start(s32[16]{0:T(128)} %param.18) | copy-start | bytes 196
  1.2 10.2 %copy-start = (bf16[128,384]{1,0:T(8,128)(2,1)S(1)}, bf16[128,384]{1,0:T(8,128)(2,1)}, u32[]{:S(2)}) copy-start(bf16[128,384]{1,0:T(8,128)(2,1)} %refs_15_.1) | copy-start | bytes 294916
  1.2 10.2 %copy-start.1 = (bf16[128,256]{1,0:T(8,128)(2,1)S(1)}, bf16[128,256]{1,0:T(8,128)(2,1)}, u32[]{:S(2)}) copy-start(bf16[128,256]{1,0:T(8,128)(2,1)} %refs_11_.3) | copy-start | bytes 196612
  1.2 10.2 %copy-start.2 = (bf16[128,256]{1,0:T(8,128)(2,1)S(1)}, bf16[128,256]{1,0:T(8,128)(2,1)}, u32[]{:S(2)}) copy-start(bf16[128,256]{1,0:T(8,128)(2,1)} %refs_12_.3) | copy-start | bytes 196612
  1.2 10.2 %copy-start.4 = (bf16[128,128]{1,0:T(8,128)(2,1)S(1)}, bf16[128,128]{1,0:T(8,128)(2,1)}, u32[]{:S(2)}) copy-start(bf16[128,128]{1,0:T(8,128)(2,1)} %refs_14_.1) | copy-start | bytes 98308
  1.2 10.2 %copy-start.5 = (bf16[128,128]{1,0:T(8,128)(2,1)S(1)}, bf16[128,128]{1,0:T(8,128)(2,1)}, u32[]{:S(2)}) copy-start(bf16[128,128]{1,0:T(8,128)(2,1)} %refs_16_.1) | copy-start | bytes 98308
  1.3 10.2 %copy-start.6 = (bf16[128,128]{1,0:T(8,128)(2,1)S(1)}, bf16[128,128]{1,0:T(8,128)(2,1)}, u32[]{:S(2)}) copy-start(bf16[128,128]{1,0:T(8,128)(2,1)} %refs_17_.1) | copy-start | bytes 98308
  1.5 9.9 %copy-start.3 = (bf16[128,128]{1,0:T(8,128)(2,1)S(1)}, bf16[128,128]{1,0:T(8,128)(2,1)}, u32[]{:S(2)}) copy-start(bf16[128,128]{1,0:T(8,128)(2,1)} %refs_13_.3) | copy-start | bytes 98308
  1.5 6.1 %collective-permute-start.1 = (bf16[2,2,8,128]{3,2,1,0:T(8,128)(2,1)S(1)}, bf16[2,2,8,128]{3,2,1,0:T(8,128)(2,1)S(1)}, u32[]{:S(2)}, u32[]{:S(2)}) collective-permute-start(bf16[2,2,8,128]{3,2,1,0:T(8,128)(2,1)S(1)} %bitcast_dynamic-update-slice_fusion.refs_0_), channel_id=1, source_target_pairs={{0,9},{1,8},{2,11},{3,10},{4,13},{5,12},{6,15},{7,14},{8,1},{9,0},... | collective-permute-start | bytes 24584 | tf_op jit(solution)/shard_map/ppermute | solution.py:313
  5.3 5.8 %collective-permute-start.4 = (bf16[2,2,8,128]{3,2,1,0:T(8,128)(2,1)S(1)}, bf16[2,2,8,128]{3,2,1,0:T(8,128)(2,1)S(1)}, u32[]{:S(2)}, u32[]{:S(2)}) collective-permute-start(bf16[2,2,8,128]{3,2,1,0:T(8,128)(2,1)S(1)} %bitcast_dynamic-update-slice_fusion.refs_0_), channel_id=1, source_target_pairs={{0,15},{1,14},{2,13},{3,12},{4,11},{5,10},{6,9},{7,8},{8,7},{9,6},... | collective-permute-start | bytes 24584 | tf_op jit(solution)/shard_map/ppermute | solution.py:313
  7.4 4.0 %collective-permute-start.5 = (bf16[2,2,8,128]{3,2,1,0:T(8,128)(2,1)S(1)}, bf16[2,2,8,128]{3,2,1,0:T(8,128)(2,1)S(1)}, u32[]{:S(2)}, u32[]{:S(2)}) collective-permute-start(bf16[2,2,8,128]{3,2,1,0:T(8,128)(2,1)S(1)} %bitcast_dynamic-update-slice_fusion.refs_0_), channel_id=1, source_target_pairs={{0,7},{1,6},{2,5},{3,4},{4,3},{5,2},{6,1},{7,0},{8,15},{9,14},{10,... | collective-permute-start | bytes 24584 | tf_op jit(solution)/shard_map/ppermute | solution.py:313
  7.7 4.1 %collective-permute-start.2 = (bf16[4,2,8,128]{3,2,1,0:T(8,128)(2,1)S(1)}, bf16[4,2,8,128]{3,2,1,0:T(8,128)(2,1)S(1)}, u32[]{:S(2)}, u32[]{:S(2)}) collective-permute-start(bf16[4,2,8,128]{3,2,1,0:T(8,128)(2,1)S(1)} %pad_maximum_fusion), channel_id=1, source_target_pairs={{0,3},{1,2},{2,1},{3,0},{4,7},{5,6},{6,5},{7,4},{8,11},{9,10},{10,... | collective-permute-start | bytes 49160 | tf_op jit(solution)/shard_map/ppermute | solution.py:313
  8.2 3.8 %collective-permute-start.3 = (bf16[4,2,8,128]{3,2,1,0:T(8,128)(2,1)S(1)}, bf16[4,2,8,128]{3,2,1,0:T(8,128)(2,1)S(1)}, u32[]{:S(2)}, u32[]{:S(2)}) collective-permute-start(bf16[4,2,8,128]{3,2,1,0:T(8,128)(2,1)S(1)} %pad_maximum_fusion), channel_id=1, source_target_pairs={{0,5},{1,4},{2,7},{3,6},{4,1},{5,0},{6,3},{7,2},{8,13},{9,12},{10,... | collective-permute-start | bytes 49160 | tf_op jit(solution)/shard_map/ppermute | solution.py:313

commit v20 on v18

--- a/solution.py
+++ b/solution.py
@@ -212,33 +212,44 @@
         for r in range(rows):
             term = left_at * early_right_ref[r * tokens + m : r * tokens + m + 1]
             extra[r] = term if m == 0 else extra[r] + term
-    products = round_bf16(jnp.concatenate(products + extra, axis=0))
 
     own_token = row * rows
     own_column = ((own_token // cols) ^ col) * cols + own_token % cols
 
-    def chosen(early_ref, late_ref):
+    def own_columns(early_ref, late_ref):
         pair = (early_ref, late_ref)
-        own = [pair[i * tokens // here][i * tokens % here : i * tokens % here + cols] for i in range(tokens)]
-        for r in range(rows):
-            own += [ref[pl.ds(own_column + r, here // tokens, stride=tokens), :] for ref in pair]
-        return jnp.concatenate(own, axis=0)
-
-    normed_out = layer_norm(products, gains_ref[1:2]).astype(bf16)
-    out_gate = sigmoid(dot(chosen(early_normed_ref, late_normed_ref).astype(bf16), out_gate_ref[...]))
-    updated = chosen(early_base_ref, late_base_ref) + out_gate * dot(normed_out, out_weight_ref[...])
-    normed_att = layer_norm(updated, gains_ref[2:3]).astype(bf16)
+        return jnp.concatenate(
+            [pair[i * tokens // here][i * tokens % here : i * tokens % here + cols] for i in range(tokens)], axis=0
+        )
+
+    def own_tokens(early_ref, late_ref):
+        return jnp.concatenate(
+            [
+                ref[pl.ds(own_column + r, here // tokens, stride=tokens), :]
+                for r in range(rows)
+                for ref in (early_ref, late_ref)
+            ],
+            axis=0,
+        )
+
+    def attention_input(products, chosen):
+        normed_out = layer_norm(round_bf16(jnp.concatenate(products, axis=0)), gains_ref[1:2]).astype(bf16)
+        out_gate = sigmoid(dot(chosen(early_normed_ref, late_normed_ref).astype(bf16), out_gate_ref[...]))
+        updated = chosen(early_base_ref, late_base_ref) + out_gate * dot(normed_out, out_weight_ref[...])
+        return updated, layer_norm(updated, gains_ref[2:3]).astype(bf16)
+
+    updated, column = attention_input(products, own_columns)
+    _, of_tokens = attention_input(extra, own_tokens)
     own_pairs = rows * cols
     column_pairs = tokens * cols
 
-    own = normed_att[:own_pairs]
-    column = normed_att[:column_pairs]
+    own = column[:own_pairs]
     queries = dot(own, qkv_ref[:, :width])
     keys = dot(column, qkv_ref[:, width : 2 * width]).astype(bf16)
     values = dot(column, qkv_ref[:, 2 * width :]).astype(bf16)
     own_gate = sigmoid(dot(own, att_gate_ref[...]))
 
-    bias = dot_t(att_bias_ref[...], normed_att[column_pairs:]).astype(bf16)
+    bias = dot_t(att_bias_ref[...], of_tokens).astype(bf16)
     shape = (rows * tokens, rows * column_pairs)
     source = lax.broadcasted_iota(jnp.int32, shape, 0)
     repeated = source == lax.broadcasted_iota(jnp.int32, shape, 1) // cols

time: 14.2 us -> 14.2 us (level)
  no operation moved by 1% of the time
where the time goes in v20:
time: 14.2 us; the launch traced here: 14.1 us
  starting transfers between devices  9.42 us (66%)
  Pallas kernels  2.68 us (19%)
  waiting for transfers between devices  1.03 us (7%)
  local copies, waits for them, and re-layouts  0.77 us (5%)
    ppermute x6, starting transfers between devices, move(): lax.ppermute(values, ('row', 'col'), [(device, device ^ step) for device...  9.42 us
    pallas_call x1, Pallas kernels, whole_pair_on_device(): pl.pallas_call(functools.partial(whole_pair_kernel, row_dim, heads, early...  2.09 us
    ppermute x6, waiting for transfers between devices, move(): lax.ppermute(values, ('row', 'col'), [(device, device ^ step) for device...  1.03 us
    unnamed x30, local copies, waits for them, and re-layouts  0.76 us
    pallas_call x1, Pallas kernels, whole_pair_on_device(): pl.pallas_call(functools.partial(early_kernel, early), out_shape=[half] *...  0.35 us
  transfers between devices with their start and end apart: 6, of which 3 were waited for; matrix products, arithmetic and copies ran while one was open for 0% of the time, Pallas kernels for 4%

profile of v20, /device:TPU:0, one launch (start us, length us, event | category | flops | bytes accessed | tf_op | source)
XLA Modules:
  0.0 14.1 jit_solution(838685256142176106)
XLA Ops:
  0.0 0.0 copy-start.7
  0.0 0.5 %collective-permute-start = (bf16[2,8,128]{2,1,0:T(8,128)(2,1)}, bf16[2,8,128]{2,1,0:T(8,128)(2,1)S(1)}, u32[]{:S(2)}, u32[]{:S(2)}) collective-permute-start(bf16[2,8,128]{2,1,0:T(8,128)(2,1)} %pair_ref.1), channel_id=1, source_target_pairs={{0,1},{1,0},{2,3},{3,2},{4,5},{5,4},{6,7},{7,6},{8,9},{9,8},{10,11... | collective-permute-start | bytes 12296 | tf_op jit(solution)/shard_map/ppermute | solution.py:315
  0.5 0.0 copy-start.11
  0.5 0.0 copy-start.12
  0.5 0.0 copy-start.13
  0.5 0.0 copy-start.14
  0.5 0.0 copy-start.8
  0.5 0.0 copy-start.9
  0.5 0.0 copy-start.10
  0.5 0.2 %copy-done.7 = bf16[128,128]{1,0:T(8,128)(2,1)S(1)} copy-done((bf16[128,128]{1,0:T(8,128)(2,1)S(1)}, bf16[128,128]{1,0:T(8,128)(2,1)}, u32[]{:S(2)}) %copy-start.7) | copy-done | bytes 32792
  0.8 0.4 %copy-done.11 = s32[16]{0:T(128)S(1)} copy-done((s32[16]{0:T(128)S(1)}, s32[16]{0:T(128)}, u32[]{:S(2)}) %copy-start.11) | copy-done | bytes 88
  1.1 0.0 copy-done.12
  1.1 0.0 copy-done.13
  1.1 0.0 copy-done.14
  1.2 0.0 copy-done.8
  1.2 0.0 copy-done.9
  1.2 0.0 copy-done.10
  1.2 0.0 copy-start
  1.2 0.0 copy-start.1
  1.2 0.0 copy-start.2
  1.2 0.0 copy-start.4
  1.2 0.0 copy-start.5
  1.3 0.0 copy-start.6
  1.3 0.2 %shard_map.146 = (bf16[2,2,8,128]{3,2,1,0:T(8,128)(2,1)S(1)}, f32[256,128]{1,0:T(8,128)S(1)}, f32[256,128]{1,0:T(8,128)S(1)}, f32[3,128]{1,0:T(4,128)S(1)}, bf16...) custom-call(bf16[2,8,128]{2,1,0:T(8,128)(2,1)S(1)} %copy-done.8, s32[1,16]{1,0:T(1,128)S(1)} %bitcast.9, ...), custom_call_target="tpu_custom_call" | custom-call | flops 1000000000 | bytes 1048576 | tf_op jit(solution)/shard_map/pallas_call | solution.py:331
  1.5 0.0 copy-start.3
  1.5 0.0 collective-permute-done
  1.5 3.8 %collective-permute-start.1 = (bf16[2,2,8,128]{3,2,1,0:T(8,128)(2,1)S(1)}, bf16[2,2,8,128]{3,2,1,0:T(8,128)(2,1)S(1)}, u32[]{:S(2)}, u32[]{:S(2)}) collective-permute-start(bf16[2,2,8,128]{3,2,1,0:T(8,128)(2,1)S(1)} %bitcast_dynamic-update-slice_fusion.refs_0_), channel_id=1, source_target_pairs={{0,9},{1,8},{2,11},{3,10},{4,13},{5,12},{6,15},{7,14},{8,1},{9,0},... | collective-permute-start | bytes 24584 | tf_op jit(solution)/shard_map/ppermute | solution.py:315
  5.3 2.1 %collective-permute-start.4 = (bf16[2,2,8,128]{3,2,1,0:T(8,128)(2,1)S(1)}, bf16[2,2,8,128]{3,2,1,0:T(8,128)(2,1)S(1)}, u32[]{:S(2)}, u32[]{:S(2)}) collective-permute-start(bf16[2,2,8,128]{3,2,1,0:T(8,128)(2,1)S(1)} %bitcast_dynamic-update-slice_fusion.refs_0_), channel_id=1, source_target_pairs={{0,15},{1,14},{2,13},{3,12},{4,11},{5,10},{6,9},{7,8},{8,7},{9,6},... | collective-permute-start | bytes 24584 | tf_op jit(solution)/shard_map/ppermute | solution.py:315
  7.4 0.2 %collective-permute-start.5 = (bf16[2,2,8,128]{3,2,1,0:T(8,128)(2,1)S(1)}, bf16[2,2,8,128]{3,2,1,0:T(8,128)(2,1)S(1)}, u32[]{:S(2)}, u32[]{:S(2)}) collective-permute-start(bf16[2,2,8,128]{3,2,1,0:T(8,128)(2,1)S(1)} %bitcast_dynamic-update-slice_fusion.refs_0_), channel_id=1, source_target_pairs={{0,7},{1,6},{2,5},{3,4},{4,3},{5,2},{6,1},{7,0},{8,15},{9,14},{10,... | collective-permute-start | bytes 24584 | tf_op jit(solution)/shard_map/ppermute | solution.py:315
  7.7 0.0 collective-permute-done.1.refs_1_
  7.7 0.5 %collective-permute-start.2 = (bf16[4,2,8,128]{3,2,1,0:T(8,128)(2,1)S(1)}, bf16[4,2,8,128]{3,2,1,0:T(8,128)(2,1)S(1)}, u32[]{:S(2)}, u32[]{:S(2)}) collective-permute-start(bf16[4,2,8,128]{3,2,1,0:T(8,128)(2,1)S(1)} %pad_maximum_fusion), channel_id=1, source_target_pairs={{0,3},{1,2},{2,1},{3,0},{4,7},{5,6},{6,5},{7,4},{8,11},{9,10},{10,... | collective-permute-start | bytes 49160 | tf_op jit(solution)/shard_map/ppermute | solution.py:315
  8.2 2.3 %collective-permute-start.3 = (bf16[4,2,8,128]{3,2,1,0:T(8,128)(2,1)S(1)}, bf16[4,2,8,128]{3,2,1,0:T(8,128)(2,1)S(1)}, u32[]{:S(2)}, u32[]{:S(2)}) collective-permute-start(bf16[4,2,8,128]{3,2,1,0:T(8,128)(2,1)S(1)} %pad_maximum_fusion), channel_id=1, source_target_pairs={{0,5},{1,4},{2,7},{3,6},{4,1},{5,0},{6,3},{7,2},{8,13},{9,12},{10,... | collective-permute-start | bytes 49160 | tf_op jit(solution)/shard_map/ppermute | solution.py:315
  10.5 0.6 %collective-permute-done.4.refs_2_ = bf16[2,2,8,128]{3,2,1,0:T(8,128)(2,1)S(1)} collective-permute-done((bf16[2,2,8,128]{3,2,1,0:T(8,128)(2,1)S(1)}, bf16[2,2,8,128]{3,2,1,0:T(8,128)(2,1)S(1)}, u32[]{:S(2)}, u32[]{:S(2)}) %collective-permute-start.4) | collective-permute-done | bytes 8224 | tf_op jit(solution)/shard_map/ppermute | solution.py:315
  11.1 0.3 %collective-permute-done.5.refs_3_ = bf16[2,2,8,128]{3,2,1,0:T(8,128)(2,1)S(1)} collective-permute-done((bf16[2,2,8,128]{3,2,1,0:T(8,128)(2,1)S(1)}, bf16[2,2,8,128]{3,2,1,0:T(8,128)(2,1)S(1)}, u32[]{:S(2)}, u32[]{:S(2)}) %collective-permute-start.5) | collective-permute-done | bytes 8224 | tf_op jit(solution)/shard_map/ppermute | solution.py:315
  11.4 0.0 copy-done
  11.4 0.0 copy-done.1
  11.4 0.0 copy-done.2
  11.4 0.0 copy-done.4
  11.4 0.0 copy-done.5
  11.4 0.0 copy-done.6
  11.4 0.0 copy-done.3
  11.4 0.3 %shard_map.147 = (f32[144,128]{1,0:T(8,128)S(1)}, f32[144,128]{1,0:T(8,128)S(1)}, f32[144,128]{1,0:T(8,128)S(1)}, f32[144,128]{1,0:T(8,128)S(1)}) custom-call(bf16[2,2,8,128]{3,2,1,0:T(8,128)(2,1)S(1)} %bitcast_dynamic-update-slice_fusion.refs_0_, bf16[2,2,8,128]{3,2,1,0:T(8,128)(2,1)S(1)} %collective-permute-done.1.refs_1_, ...), custom_call_target="tpu_custom_call" | custom-call | flops 1000000000 | bytes 1048576 | tf_op jit(solution)/shard_map/pallas_call | solution.py:366
  11.8 0.0 collective-permute-done.2.refs_0_
  11.8 0.1 %collective-permute-done.3.refs_1_ = bf16[4,2,8,128]{3,2,1,0:T(8,128)(2,1)S(1)} collective-permute-done((bf16[4,2,8,128]{3,2,1,0:T(8,128)(2,1)S(1)}, bf16[4,2,8,128]{3,2,1,0:T(8,128)(2,1)S(1)}, u32[]{:S(2)}, u32[]{:S(2)}) %collective-permute-start.3) | collective-permute-done | bytes 16416 | tf_op jit(solution)/shard_map/ppermute | solution.py:315
  12.0 2.1 %shard_map.148 = bf16[2,8,128]{2,1,0:T(8,128)(2,1)} custom-call(bf16[4,2,8,128]{3,2,1,0:T(8,128)(2,1)S(1)} %collective-permute-done.2.refs_0_, bf16[4,2,8,128]{3,2,1,0:T(8,128)(2,1)S(1)} %collective-permute-done.3.refs_1_, f32[144,128]{1,0:T(8,128)S(1)} %get-tuple-element.31.refs_2_, f32[144,128]{1,0:T(8,128)S(1)} %get-tuple-element.32.refs_3_, ...), custom_call_target="tpu_custom_call" | custom-call | tf_op jit(solution)/shard_map/pallas_call | solution.py:374
  (3 shorter events, 0.0 us)
Async XLA Ops:
  0.0 0.8 %copy-start.7 = (bf16[128,128]{1,0:T(8,128)(2,1)S(1)}, bf16[128,128]{1,0:T(8,128)(2,1)}, u32[]{:S(2)}) copy-start(bf16[128,128]{1,0:T(8,128)(2,1)} %table_ref.1) | copy-start | bytes 98308
  0.0 1.5 %collective-permute-start = (bf16[2,8,128]{2,1,0:T(8,128)(2,1)}, bf16[2,8,128]{2,1,0:T(8,128)(2,1)S(1)}, u32[]{:S(2)}, u32[]{:S(2)}) collective-permute-start(bf16[2,8,128]{2,1,0:T(8,128)(2,1)} %pair_ref.1), channel_id=1, source_target_pairs={{0,1},{1,0},{2,3},{3,2},{4,5},{5,4},{6,7},{7,6},{8,9},{9,8},{10,11... | collective-permute-start | bytes 12296 | tf_op jit(solution)/shard_map/ppermute | solution.py:315
  0.5 0.7 %copy-start.11 = (s32[16]{0:T(128)S(1)}, s32[16]{0:T(128)}, u32[]{:S(2)}) copy-start(s32[16]{0:T(128)} %param.19) | copy-start | bytes 196
  0.5 0.7 %copy-start.12 = (f32[128]{0:T(128)S(1)}, f32[128]{0:T(128)}, u32[]{:S(2)}) copy-start(f32[128]{0:T(128)} %param.21) | copy-start | bytes 1540
  0.5 0.7 %copy-start.13 = (f32[128]{0:T(128)S(1)}, f32[128]{0:T(128)}, u32[]{:S(2)}) copy-start(f32[128]{0:T(128)} %param.25) | copy-start | bytes 1540
  0.5 0.7 %copy-start.14 = (f32[128]{0:T(128)S(1)}, f32[128]{0:T(128)}, u32[]{:S(2)}) copy-start(f32[128]{0:T(128)} %param.27) | copy-start | bytes 1540
  0.5 0.7 %copy-start.8 = (bf16[2,8,128]{2,1,0:T(8,128)(2,1)S(1)}, bf16[2,8,128]{2,1,0:T(8,128)(2,1)}, u32[]{:S(2)}) copy-start(bf16[2,8,128]{2,1,0:T(8,128)(2,1)} %pair_ref.1) | copy-start | bytes 12292
  0.5 0.7 %copy-start.9 = (bf16[128,4]{0,1:T(4,128)(2,1)S(1)}, bf16[128,4]{0,1:T(4,128)(2,1)}, u32[]{:S(2)}) copy-start(bf16[128,4]{0,1:T(4,128)(2,1)} %param.30) | copy-start | bytes 3076
  0.5 0.7 %copy-start.10 = (s32[16]{0:T(128)S(1)}, s32[16]{0:T(128)}, u32[]{:S(2)}) copy-start(s32[16]{0:T(128)} %param.18) | copy-start | bytes 196
  1.2 10.2 %copy-start = (bf16[128,384]{1,0:T(8,128)(2,1)S(1)}, bf16[128,384]{1,0:T(8,128)(2,1)}, u32[]{:S(2)}) copy-start(bf16[128,384]{1,0:T(8,128)(2,1)} %refs_15_.1) | copy-start | bytes 294916
  1.2 10.2 %copy-start.1 = (bf16[128,256]{1,0:T(8,128)(2,1)S(1)}, bf16[128,256]{1,0:T(8,128)(2,1)}, u32[]{:S(2)}) copy-start(bf16[128,256]{1,0:T(8,128)(2,1)} %refs_11_.3) | copy-start | bytes 196612
  1.2 10.2 %copy-start.2 = (bf16[128,256]{1,0:T(8,128)(2,1)S(1)}, bf16[128,256]{1,0:T(8,128)(2,1)}, u32[]{:S(2)}) copy-start(bf16[128,256]{1,0:T(8,128)(2,1)} %refs_12_.3) | copy-start | bytes 196612
  1.2 10.2 %copy-start.4 = (bf16[128,128]{1,0:T(8,128)(2,1)S(1)}, bf16[128,128]{1,0:T(8,128)(2,1)}, u32[]{:S(2)}) copy-start(bf16[128,128]{1,0:T(8,128)(2,1)} %refs_14_.1) | copy-start | bytes 98308
  1.2 10.2 %copy-start.5 = (bf16[128,128]{1,0:T(8,128)(2,1)S(1)}, bf16[128,128]{1,0:T(8,128)(2,1)}, u32[]{:S(2)}) copy-start(bf16[128,128]{1,0:T(8,128)(2,1)} %refs_16_.1) | copy-start | bytes 98308
  1.3 10.2 %copy-start.6 = (bf16[128,128]{1,0:T(8,128)(2,1)S(1)}, bf16[128,128]{1,0:T(8,128)(2,1)}, u32[]{:S(2)}) copy-start(bf16[128,128]{1,0:T(8,128)(2,1)} %refs_17_.1) | copy-start | bytes 98308
  1.5 9.9 %copy-start.3 = (bf16[128,128]{1,0:T(8,128)(2,1)S(1)}, bf16[128,128]{1,0:T(8,128)(2,1)}, u32[]{:S(2)}) copy-start(bf16[128,128]{1,0:T(8,128)(2,1)} %refs_13_.3) | copy-start | bytes 98308
  1.5 6.1 %collective-permute-start.1 = (bf16[2,2,8,128]{3,2,1,0:T(8,128)(2,1)S(1)}, bf16[2,2,8,128]{3,2,1,0:T(8,128)(2,1)S(1)}, u32[]{:S(2)}, u32[]{:S(2)}) collective-permute-start(bf16[2,2,8,128]{3,2,1,0:T(8,128)(2,1)S(1)} %bitcast_dynamic-update-slice_fusion.refs_0_), channel_id=1, source_target_pairs={{0,9},{1,8},{2,11},{3,10},{4,13},{5,12},{6,15},{7,14},{8,1},{9,0},... | collective-permute-start | bytes 24584 | tf_op jit(solution)/shard_map/ppermute | solution.py:315
  5.3 5.8 %collective-permute-start.4 = (bf16[2,2,8,128]{3,2,1,0:T(8,128)(2,1)S(1)}, bf16[2,2,8,128]{3,2,1,0:T(8,128)(2,1)S(1)}, u32[]{:S(2)}, u32[]{:S(2)}) collective-permute-start(bf16[2,2,8,128]{3,2,1,0:T(8,128)(2,1)S(1)} %bitcast_dynamic-update-slice_fusion.refs_0_), channel_id=1, source_target_pairs={{0,15},{1,14},{2,13},{3,12},{4,11},{5,10},{6,9},{7,8},{8,7},{9,6},... | collective-permute-start | bytes 24584 | tf_op jit(solution)/shard_map/ppermute | solution.py:315
  7.4 4.0 %collective-permute-start.5 = (bf16[2,2,8,128]{3,2,1,0:T(8,128)(2,1)S(1)}, bf16[2,2,8,128]{3,2,1,0:T(8,128)(2,1)S(1)}, u32[]{:S(2)}, u32[]{:S(2)}) collective-permute-start(bf16[2,2,8,128]{3,2,1,0:T(8,128)(2,1)S(1)} %bitcast_dynamic-update-slice_fusion.refs_0_), channel_id=1, source_target_pairs={{0,7},{1,6},{2,5},{3,4},{4,3},{5,2},{6,1},{7,0},{8,15},{9,14},{10,... | collective-permute-start | bytes 24584 | tf_op jit(solution)/shard_map/ppermute | solution.py:315
  7.7 4.1 %collective-permute-start.2 = (bf16[4,2,8,128]{3,2,1,0:T(8,128)(2,1)S(1)}, bf16[4,2,8,128]{3,2,1,0:T(8,128)(2,1)S(1)}, u32[]{:S(2)}, u32[]{:S(2)}) collective-permute-start(bf16[4,2,8,128]{3,2,1,0:T(8,128)(2,1)S(1)} %pad_maximum_fusion), channel_id=1, source_target_pairs={{0,3},{1,2},{2,1},{3,0},{4,7},{5,6},{6,5},{7,4},{8,11},{9,10},{10,... | collective-permute-start | bytes 49160 | tf_op jit(solution)/shard_map/ppermute | solution.py:315
  8.2 3.8 %collective-permute-start.3 = (bf16[4,2,8,128]{3,2,1,0:T(8,128)(2,1)S(1)}, bf16[4,2,8,128]{3,2,1,0:T(8,128)(2,1)S(1)}, u32[]{:S(2)}, u32[]{:S(2)}) collective-permute-start(bf16[4,2,8,128]{3,2,1,0:T(8,128)(2,1)S(1)} %pad_maximum_fusion), channel_id=1, source_target_pairs={{0,5},{1,4},{2,7},{3,6},{4,1},{5,0},{6,3},{7,2},{8,13},{9,12},{10,... | collective-permute-start | bytes 49160 | tf_op jit(solution)/shard_map/ppermute | solution.py:315

commit v21 on v20

--- a/solution.py
+++ b/solution.py
@@ -107,18 +107,22 @@
     key_bias_ref[...] = (key_mask - 1.0) * 1000000000.0 + other_columns_ref[...]
 
 
-def edge_operands(pieces, orders, rows, rel, pair_mask, gain, in_gate, in_weight):
+def edge_operands(pieces, orders, rows, rel, pair_mask, gain, in_gate, in_weight, for_right=lambda values: values):
     width = rel.shape[1]
     blocks = {
         place: piece[at].astype(jnp.float32) for piece, order in zip(pieces, orders) for at, place in enumerate(order)
     }
     tiles = [blocks[2 * chip + half][r] for chip in chips_of(orders) for r in range(rows) for half in range(2)]
     base = jnp.concatenate(tiles, axis=0) + rel
-    normed = layer_norm(base, gain).astype(jnp.bfloat16)
-    projected = sigmoid(dot(normed, in_gate)) * dot(normed, in_weight)
-    left = round_bf16(projected[:, :width] * pair_mask)
-    right = round_bf16(projected[:, width:] * pair_mask)
-    return left, right, base, normed.astype(jnp.float32)
+    normed_f = layer_norm(base, gain).astype(jnp.bfloat16).astype(jnp.float32)
+
+    def operand(values, mask, columns):
+        values = values.astype(jnp.bfloat16)
+        return round_bf16(sigmoid(dot(values, in_gate[:, columns])) * dot(values, in_weight[:, columns]) * mask)
+
+    left = operand(normed_f, pair_mask, slice(0, width))
+    right = operand(for_right(normed_f), for_right(pair_mask), slice(width, 2 * width))
+    return left, right, base, normed_f
 
 
 def chips_of(orders):
@@ -182,21 +186,40 @@
     f32, bf16 = jnp.float32, jnp.bfloat16
 
     here = early_left_ref.shape[0] - SPARE_ROWS
+    late_chips = chips_of(late)
+    near = [chip for chip in late_chips if chip < row_dim // 2]
+    far = [chip for chip in late_chips if chip >= row_dim // 2]
+    near_is_own = row // (row_dim // 2) == col
+
+    def for_right(values):
+        count = rows * tokens
+        rows_of = {chip: values[at * count : (at + 1) * count] for at, chip in enumerate(late_chips)}
+        return jnp.concatenate([jnp.where(near_is_own, rows_of[n], rows_of[f]) for n, f in zip(near, far)], axis=0)
+
     left, right, base, normed = edge_operands(
-        piece_refs, late, rows, rel_ref[here:], pair_mask_ref[here:], gains_ref[0:1], in_gate_ref[...], in_weight_ref[...]
+        piece_refs,
+        late,
+        rows,
+        rel_ref[here:],
+        pair_mask_ref[here:],
+        gains_ref[0:1],
+        in_gate_ref[...],
+        in_weight_ref[...],
+        for_right,
     )
     late_left_ref[:here] = left
     late_base_ref[:here] = base
     late_normed_ref[:here] = normed
     lefts = (early_left_ref, late_left_ref)
 
-    for at, token in enumerate(token_rows(chips_of(early + late), rows)):
-        place = pl.ds(pl.multiple_of(token * tokens, tokens), tokens)
-        first = at * tokens
-        if first < here:
-            right_ref[place, :] = early_right_ref[first : first + tokens]
-        else:
-            right_ref[place, :] = right[first - here : first - here + tokens]
+    own_half = [jnp.where(near_is_own, n, f) for n, f in zip(near, far)]
+    for tokens_of, values in (
+        (token_rows(chips_of(early), rows), early_right_ref),
+        (token_rows(own_half, rows), right),
+    ):
+        for at, token in enumerate(tokens_of):
+            place = pl.ds(pl.multiple_of(token * tokens, tokens), tokens)
+            right_ref[place, :] = values[at * tokens : (at + 1) * tokens]
 
     right_at = [right_ref[pl.ds(col * cols * tokens + m, cols, stride=tokens), :] for m in range(tokens)]
     products = []

time: 14.2 us -> 14.2 us (level)
  no operation moved by 1% of the time
where the time goes in v21:
time: 14.2 us; the launch traced here: 14 us
  starting transfers between devices  9.42 us (66%)
  Pallas kernels  2.67 us (19%)
  waiting for transfers between devices  1.03 us (7%)
  local copies, waits for them, and re-layouts  0.77 us (5%)
    ppermute x6, starting transfers between devices, move(): lax.ppermute(values, ('row', 'col'), [(device, device ^ step) for device...  9.42 us
    pallas_call x1, Pallas kernels, whole_pair_on_device(): pl.pallas_call(functools.partial(whole_pair_kernel, row_dim, heads, early...  2.08 us
    ppermute x6, waiting for transfers between devices, move(): lax.ppermute(values, ('row', 'col'), [(device, device ^ step) for device...  1.03 us
    unnamed x30, local copies, waits for them, and re-layouts  0.76 us
    pallas_call x1, Pallas kernels, whole_pair_on_device(): pl.pallas_call(functools.partial(early_kernel, early), out_shape=[half] *...  0.35 us
  transfers between devices with their start and end apart: 6, of which 3 were waited for; matrix products, arithmetic and copies ran while one was open for 0% of the time, Pallas kernels for 4%

profile of v21, /device:TPU:0, one launch (start us, length us, event | category | flops | bytes accessed | tf_op | source)
XLA Modules:
  0.0 14.0 jit_solution(13356491772593854381)
XLA Ops:
  0.0 0.0 copy-start.7
  0.0 0.5 %collective-permute-start = (bf16[2,8,128]{2,1,0:T(8,128)(2,1)}, bf16[2,8,128]{2,1,0:T(8,128)(2,1)S(1)}, u32[]{:S(2)}, u32[]{:S(2)}) collective-permute-start(bf16[2,8,128]{2,1,0:T(8,128)(2,1)} %pair_ref.1), channel_id=1, source_target_pairs={{0,1},{1,0},{2,3},{3,2},{4,5},{5,4},{6,7},{7,6},{8,9},{9,8},{10,11... | collective-permute-start | bytes 12296 | tf_op jit(solution)/shard_map/ppermute | solution.py:338
  0.5 0.0 copy-start.11
  0.5 0.0 copy-start.12
  0.5 0.0 copy-start.13
  0.5 0.0 copy-start.14
  0.5 0.0 copy-start.8
  0.5 0.0 copy-start.9
  0.5 0.0 copy-start.10
  0.5 0.2 %copy-done.7 = bf16[128,128]{1,0:T(8,128)(2,1)S(1)} copy-done((bf16[128,128]{1,0:T(8,128)(2,1)S(1)}, bf16[128,128]{1,0:T(8,128)(2,1)}, u32[]{:S(2)}) %copy-start.7) | copy-done | bytes 32792
  0.8 0.4 %copy-done.11 = s32[16]{0:T(128)S(1)} copy-done((s32[16]{0:T(128)S(1)}, s32[16]{0:T(128)}, u32[]{:S(2)}) %copy-start.11) | copy-done | bytes 88
  1.1 0.0 copy-done.12
  1.1 0.0 copy-done.13
  1.1 0.0 copy-done.14
  1.2 0.0 copy-done.8
  1.2 0.0 copy-done.9
  1.2 0.0 copy-done.10
  1.2 0.0 copy-start
  1.2 0.0 copy-start.1
  1.2 0.0 copy-start.2
  1.2 0.0 copy-start.4
  1.2 0.0 copy-start.5
  1.3 0.0 copy-start.6
  1.3 0.2 %shard_map.146 = (bf16[2,2,8,128]{3,2,1,0:T(8,128)(2,1)S(1)}, f32[256,128]{1,0:T(8,128)S(1)}, f32[256,128]{1,0:T(8,128)S(1)}, f32[3,128]{1,0:T(4,128)S(1)}, bf16...) custom-call(bf16[2,8,128]{2,1,0:T(8,128)(2,1)S(1)} %copy-done.8, s32[1,16]{1,0:T(1,128)S(1)} %bitcast.9, ...), custom_call_target="tpu_custom_call" | custom-call | flops 1000000000 | bytes 1048576 | tf_op jit(solution)/shard_map/pallas_call | solution.py:354
  1.5 0.0 copy-start.3
  1.5 0.0 collective-permute-done
  1.5 3.8 %collective-permute-start.1 = (bf16[2,2,8,128]{3,2,1,0:T(8,128)(2,1)S(1)}, bf16[2,2,8,128]{3,2,1,0:T(8,128)(2,1)S(1)}, u32[]{:S(2)}, u32[]{:S(2)}) collective-permute-start(bf16[2,2,8,128]{3,2,1,0:T(8,128)(2,1)S(1)} %bitcast_dynamic-update-slice_fusion.refs_0_), channel_id=1, source_target_pairs={{0,9},{1,8},{2,11},{3,10},{4,13},{5,12},{6,15},{7,14},{8,1},{9,0},... | collective-permute-start | bytes 24584 | tf_op jit(solution)/shard_map/ppermute | solution.py:338
  5.3 2.1 %collective-permute-start.4 = (bf16[2,2,8,128]{3,2,1,0:T(8,128)(2,1)S(1)}, bf16[2,2,8,128]{3,2,1,0:T(8,128)(2,1)S(1)}, u32[]{:S(2)}, u32[]{:S(2)}) collective-permute-start(bf16[2,2,8,128]{3,2,1,0:T(8,128)(2,1)S(1)} %bitcast_dynamic-update-slice_fusion.refs_0_), channel_id=1, source_target_pairs={{0,15},{1,14},{2,13},{3,12},{4,11},{5,10},{6,9},{7,8},{8,7},{9,6},... | collective-permute-start | bytes 24584 | tf_op jit(solution)/shard_map/ppermute | solution.py:338
  7.4 0.2 %collective-permute-start.5 = (bf16[2,2,8,128]{3,2,1,0:T(8,128)(2,1)S(1)}, bf16[2,2,8,128]{3,2,1,0:T(8,128)(2,1)S(1)}, u32[]{:S(2)}, u32[]{:S(2)}) collective-permute-start(bf16[2,2,8,128]{3,2,1,0:T(8,128)(2,1)S(1)} %bitcast_dynamic-update-slice_fusion.refs_0_), channel_id=1, source_target_pairs={{0,7},{1,6},{2,5},{3,4},{4,3},{5,2},{6,1},{7,0},{8,15},{9,14},{10,... | collective-permute-start | bytes 24584 | tf_op jit(solution)/shard_map/ppermute | solution.py:338
  7.7 0.0 collective-permute-done.1.refs_1_
  7.7 0.5 %collective-permute-start.2 = (bf16[4,2,8,128]{3,2,1,0:T(8,128)(2,1)S(1)}, bf16[4,2,8,128]{3,2,1,0:T(8,128)(2,1)S(1)}, u32[]{:S(2)}, u32[]{:S(2)}) collective-permute-start(bf16[4,2,8,128]{3,2,1,0:T(8,128)(2,1)S(1)} %pad_maximum_fusion), channel_id=1, source_target_pairs={{0,3},{1,2},{2,1},{3,0},{4,7},{5,6},{6,5},{7,4},{8,11},{9,10},{10,... | collective-permute-start | bytes 49160 | tf_op jit(solution)/shard_map/ppermute | solution.py:338
  8.2 2.3 %collective-permute-start.3 = (bf16[4,2,8,128]{3,2,1,0:T(8,128)(2,1)S(1)}, bf16[4,2,8,128]{3,2,1,0:T(8,128)(2,1)S(1)}, u32[]{:S(2)}, u32[]{:S(2)}) collective-permute-start(bf16[4,2,8,128]{3,2,1,0:T(8,128)(2,1)S(1)} %pad_maximum_fusion), channel_id=1, source_target_pairs={{0,5},{1,4},{2,7},{3,6},{4,1},{5,0},{6,3},{7,2},{8,13},{9,12},{10,... | collective-permute-start | bytes 49160 | tf_op jit(solution)/shard_map/ppermute | solution.py:338
  10.5 0.6 %collective-permute-done.4.refs_2_ = bf16[2,2,8,128]{3,2,1,0:T(8,128)(2,1)S(1)} collective-permute-done((bf16[2,2,8,128]{3,2,1,0:T(8,128)(2,1)S(1)}, bf16[2,2,8,128]{3,2,1,0:T(8,128)(2,1)S(1)}, u32[]{:S(2)}, u32[]{:S(2)}) %collective-permute-start.4) | collective-permute-done | bytes 8224 | tf_op jit(solution)/shard_map/ppermute | solution.py:338
  11.1 0.3 %collective-permute-done.5.refs_3_ = bf16[2,2,8,128]{3,2,1,0:T(8,128)(2,1)S(1)} collective-permute-done((bf16[2,2,8,128]{3,2,1,0:T(8,128)(2,1)S(1)}, bf16[2,2,8,128]{3,2,1,0:T(8,128)(2,1)S(1)}, u32[]{:S(2)}, u32[]{:S(2)}) %collective-permute-start.5) | collective-permute-done | bytes 8224 | tf_op jit(solution)/shard_map/ppermute | solution.py:338
  11.4 0.0 copy-done
  11.4 0.0 copy-done.1
  11.4 0.0 copy-done.2
  11.4 0.0 copy-done.4
  11.4 0.0 copy-done.5
  11.4 0.0 copy-done.6
  11.4 0.0 copy-done.3
  11.4 0.3 %shard_map.147 = (f32[144,128]{1,0:T(8,128)S(1)}, f32[144,128]{1,0:T(8,128)S(1)}, f32[144,128]{1,0:T(8,128)S(1)}, f32[144,128]{1,0:T(8,128)S(1)}) custom-call(bf16[2,2,8,128]{3,2,1,0:T(8,128)(2,1)S(1)} %bitcast_dynamic-update-slice_fusion.refs_0_, bf16[2,2,8,128]{3,2,1,0:T(8,128)(2,1)S(1)} %collective-permute-done.1.refs_1_, ...), custom_call_target="tpu_custom_call" | custom-call | flops 1000000000 | bytes 1048576 | tf_op jit(solution)/shard_map/pallas_call | solution.py:389
  11.8 0.0 collective-permute-done.2.refs_0_
  11.8 0.1 %collective-permute-done.3.refs_1_ = bf16[4,2,8,128]{3,2,1,0:T(8,128)(2,1)S(1)} collective-permute-done((bf16[4,2,8,128]{3,2,1,0:T(8,128)(2,1)S(1)}, bf16[4,2,8,128]{3,2,1,0:T(8,128)(2,1)S(1)}, u32[]{:S(2)}, u32[]{:S(2)}) %collective-permute-start.3) | collective-permute-done | bytes 16416 | tf_op jit(solution)/shard_map/ppermute | solution.py:338
  12.0 2.1 %shard_map.148 = bf16[2,8,128]{2,1,0:T(8,128)(2,1)} custom-call(bf16[4,2,8,128]{3,2,1,0:T(8,128)(2,1)S(1)} %collective-permute-done.2.refs_0_, bf16[4,2,8,128]{3,2,1,0:T(8,128)(2,1)S(1)} %collective-permute-done.3.refs_1_, f32[144,128]{1,0:T(8,128)S(1)} %get-tuple-element.31.refs_2_, f32[144,128]{1,0:T(8,128)S(1)} %get-tuple-element.32.refs_3_, ...), custom_call_target="tpu_custom_call" | custom-call | tf_op jit(solution)/shard_map/pallas_call | solution.py:397
  (3 shorter events, 0.0 us)
Async XLA Ops:
  0.0 0.8 %copy-start.7 = (bf16[128,128]{1,0:T(8,128)(2,1)S(1)}, bf16[128,128]{1,0:T(8,128)(2,1)}, u32[]{:S(2)}) copy-start(bf16[128,128]{1,0:T(8,128)(2,1)} %table_ref.1) | copy-start | bytes 98308
  0.0 1.5 %collective-permute-start = (bf16[2,8,128]{2,1,0:T(8,128)(2,1)}, bf16[2,8,128]{2,1,0:T(8,128)(2,1)S(1)}, u32[]{:S(2)}, u32[]{:S(2)}) collective-permute-start(bf16[2,8,128]{2,1,0:T(8,128)(2,1)} %pair_ref.1), channel_id=1, source_target_pairs={{0,1},{1,0},{2,3},{3,2},{4,5},{5,4},{6,7},{7,6},{8,9},{9,8},{10,11... | collective-permute-start | bytes 12296 | tf_op jit(solution)/shard_map/ppermute | solution.py:338
  0.5 0.7 %copy-start.11 = (s32[16]{0:T(128)S(1)}, s32[16]{0:T(128)}, u32[]{:S(2)}) copy-start(s32[16]{0:T(128)} %param.19) | copy-start | bytes 196
  0.5 0.7 %copy-start.12 = (f32[128]{0:T(128)S(1)}, f32[128]{0:T(128)}, u32[]{:S(2)}) copy-start(f32[128]{0:T(128)} %param.21) | copy-start | bytes 1540
  0.5 0.7 %copy-start.13 = (f32[128]{0:T(128)S(1)}, f32[128]{0:T(128)}, u32[]{:S(2)}) copy-start(f32[128]{0:T(128)} %param.25) | copy-start | bytes 1540
  0.5 0.7 %copy-start.14 = (f32[128]{0:T(128)S(1)}, f32[128]{0:T(128)}, u32[]{:S(2)}) copy-start(f32[128]{0:T(128)} %param.27) | copy-start | bytes 1540
  0.5 0.7 %copy-start.8 = (bf16[2,8,128]{2,1,0:T(8,128)(2,1)S(1)}, bf16[2,8,128]{2,1,0:T(8,128)(2,1)}, u32[]{:S(2)}) copy-start(bf16[2,8,128]{2,1,0:T(8,128)(2,1)} %pair_ref.1) | copy-start | bytes 12292
  0.5 0.7 %copy-start.9 = (bf16[128,4]{0,1:T(4,128)(2,1)S(1)}, bf16[128,4]{0,1:T(4,128)(2,1)}, u32[]{:S(2)}) copy-start(bf16[128,4]{0,1:T(4,128)(2,1)} %param.30) | copy-start | bytes 3076
  0.5 0.7 %copy-start.10 = (s32[16]{0:T(128)S(1)}, s32[16]{0:T(128)}, u32[]{:S(2)}) copy-start(s32[16]{0:T(128)} %param.18) | copy-start | bytes 196
  1.2 10.2 %copy-start = (bf16[128,384]{1,0:T(8,128)(2,1)S(1)}, bf16[128,384]{1,0:T(8,128)(2,1)}, u32[]{:S(2)}) copy-start(bf16[128,384]{1,0:T(8,128)(2,1)} %refs_15_.1) | copy-start | bytes 294916
  1.2 10.2 %copy-start.1 = (bf16[128,256]{1,0:T(8,128)(2,1)S(1)}, bf16[128,256]{1,0:T(8,128)(2,1)}, u32[]{:S(2)}) copy-start(bf16[128,256]{1,0:T(8,128)(2,1)} %refs_11_.3) | copy-start | bytes 196612
  1.2 10.2 %copy-start.2 = (bf16[128,256]{1,0:T(8,128)(2,1)S(1)}, bf16[128,256]{1,0:T(8,128)(2,1)}, u32[]{:S(2)}) copy-start(bf16[128,256]{1,0:T(8,128)(2,1)} %refs_12_.3) | copy-start | bytes 196612
  1.2 10.2 %copy-start.4 = (bf16[128,128]{1,0:T(8,128)(2,1)S(1)}, bf16[128,128]{1,0:T(8,128)(2,1)}, u32[]{:S(2)}) copy-start(bf16[128,128]{1,0:T(8,128)(2,1)} %refs_14_.1) | copy-start | bytes 98308
  1.2 10.2 %copy-start.5 = (bf16[128,128]{1,0:T(8,128)(2,1)S(1)}, bf16[128,128]{1,0:T(8,128)(2,1)}, u32[]{:S(2)}) copy-start(bf16[128,128]{1,0:T(8,128)(2,1)} %refs_16_.1) | copy-start | bytes 98308
  1.3 10.2 %copy-start.6 = (bf16[128,128]{1,0:T(8,128)(2,1)S(1)}, bf16[128,128]{1,0:T(8,128)(2,1)}, u32[]{:S(2)}) copy-start(bf16[128,128]{1,0:T(8,128)(2,1)} %refs_17_.1) | copy-start | bytes 98308
  1.5 9.9 %copy-start.3 = (bf16[128,128]{1,0:T(8,128)(2,1)S(1)}, bf16[128,128]{1,0:T(8,128)(2,1)}, u32[]{:S(2)}) copy-start(bf16[128,128]{1,0:T(8,128)(2,1)} %refs_13_.3) | copy-start | bytes 98308
  1.5 6.1 %collective-permute-start.1 = (bf16[2,2,8,128]{3,2,1,0:T(8,128)(2,1)S(1)}, bf16[2,2,8,128]{3,2,1,0:T(8,128)(2,1)S(1)}, u32[]{:S(2)}, u32[]{:S(2)}) collective-permute-start(bf16[2,2,8,128]{3,2,1,0:T(8,128)(2,1)S(1)} %bitcast_dynamic-update-slice_fusion.refs_0_), channel_id=1, source_target_pairs={{0,9},{1,8},{2,11},{3,10},{4,13},{5,12},{6,15},{7,14},{8,1},{9,0},... | collective-permute-start | bytes 24584 | tf_op jit(solution)/shard_map/ppermute | solution.py:338
  5.3 5.8 %collective-permute-start.4 = (bf16[2,2,8,128]{3,2,1,0:T(8,128)(2,1)S(1)}, bf16[2,2,8,128]{3,2,1,0:T(8,128)(2,1)S(1)}, u32[]{:S(2)}, u32[]{:S(2)}) collective-permute-start(bf16[2,2,8,128]{3,2,1,0:T(8,128)(2,1)S(1)} %bitcast_dynamic-update-slice_fusion.refs_0_), channel_id=1, source_target_pairs={{0,15},{1,14},{2,13},{3,12},{4,11},{5,10},{6,9},{7,8},{8,7},{9,6},... | collective-permute-start | bytes 24584 | tf_op jit(solution)/shard_map/ppermute | solution.py:338
  7.4 4.0 %collective-permute-start.5 = (bf16[2,2,8,128]{3,2,1,0:T(8,128)(2,1)S(1)}, bf16[2,2,8,128]{3,2,1,0:T(8,128)(2,1)S(1)}, u32[]{:S(2)}, u32[]{:S(2)}) collective-permute-start(bf16[2,2,8,128]{3,2,1,0:T(8,128)(2,1)S(1)} %bitcast_dynamic-update-slice_fusion.refs_0_), channel_id=1, source_target_pairs={{0,7},{1,6},{2,5},{3,4},{4,3},{5,2},{6,1},{7,0},{8,15},{9,14},{10,... | collective-permute-start | bytes 24584 | tf_op jit(solution)/shard_map/ppermute | solution.py:338
  7.7 4.1 %collective-permute-start.2 = (bf16[4,2,8,128]{3,2,1,0:T(8,128)(2,1)S(1)}, bf16[4,2,8,128]{3,2,1,0:T(8,128)(2,1)S(1)}, u32[]{:S(2)}, u32[]{:S(2)}) collective-permute-start(bf16[4,2,8,128]{3,2,1,0:T(8,128)(2,1)S(1)} %pad_maximum_fusion), channel_id=1, source_target_pairs={{0,3},{1,2},{2,1},{3,0},{4,7},{5,6},{6,5},{7,4},{8,11},{9,10},{10,... | collective-permute-start | bytes 49160 | tf_op jit(solution)/shard_map/ppermute | solution.py:338
  8.2 3.8 %collective-permute-start.3 = (bf16[4,2,8,128]{3,2,1,0:T(8,128)(2,1)S(1)}, bf16[4,2,8,128]{3,2,1,0:T(8,128)(2,1)S(1)}, u32[]{:S(2)}, u32[]{:S(2)}) collective-permute-start(bf16[4,2,8,128]{3,2,1,0:T(8,128)(2,1)S(1)} %pad_maximum_fusion), channel_id=1, source_target_pairs={{0,5},{1,4},{2,7},{3,6},{4,1},{5,0},{6,3},{7,2},{8,13},{9,12},{10,... | collective-permute-start | bytes 49160 | tf_op jit(solution)/shard_map/ppermute | solution.py:338

commit v22 on v21

--- a/solution.py
+++ b/solution.py
@@ -107,7 +107,9 @@
     key_bias_ref[...] = (key_mask - 1.0) * 1000000000.0 + other_columns_ref[...]
 
 
-def edge_operands(pieces, orders, rows, rel, pair_mask, gain, in_gate, in_weight, for_right=lambda values: values):
+def edge_operands(
+    pieces, orders, rows, rel, pair_mask, gain, in_gate, in_weight, out_gate, for_right=lambda values: values
+):
     width = rel.shape[1]
     blocks = {
         place: piece[at].astype(jnp.float32) for piece, order in zip(pieces, orders) for at, place in enumerate(order)
@@ -122,7 +124,7 @@
 
     left = operand(normed_f, pair_mask, slice(0, width))
     right = operand(for_right(normed_f), for_right(pair_mask), slice(width, 2 * width))
-    return left, right, base, normed_f
+    return left, right, base, sigmoid(dot(normed_f.astype(jnp.bfloat16), out_gate))
 
 
 def chips_of(orders):
@@ -131,7 +133,7 @@
 
 def early_kernel(orders, *refs):
     piece_refs = refs[: len(orders)]
-    rel_ref, pair_mask_ref, gains_ref, in_weight_ref, in_gate_ref = refs[len(orders) : len(orders) + 5]
+    rel_ref, pair_mask_ref, gains_ref, in_weight_ref, in_gate_ref, out_gate_ref = refs[len(orders) : len(orders) + 6]
     here = refs[-1].shape[0] - SPARE_ROWS
     found = edge_operands(
         piece_refs,
@@ -142,6 +144,7 @@
         gains_ref[0:1],
         in_gate_ref[...],
         in_weight_ref[...],
+        out_gate_ref[...],
     )
     for ref, values in zip(refs[-4:], found):
         ref[:here] = values
@@ -160,7 +163,7 @@
     early_left_ref,
     early_right_ref,
     early_base_ref,
-    early_normed_ref,
+    early_gate_ref,
     rel_ref,
     pair_mask_ref,
     gains_ref,
@@ -176,7 +179,7 @@
     out_ref,
     late_left_ref,
     late_base_ref,
-    late_normed_ref,
+    late_gate_ref,
     right_ref,
 ):
     rows, cols, width = piece_refs[0].shape[1:]
@@ -196,7 +199,7 @@
         rows_of = {chip: values[at * count : (at + 1) * count] for at, chip in enumerate(late_chips)}
         return jnp.concatenate([jnp.where(near_is_own, rows_of[n], rows_of[f]) for n, f in zip(near, far)], axis=0)
 
-    left, right, base, normed = edge_operands(
+    left, right, base, gate = edge_operands(
         piece_refs,
         late,
         rows,
@@ -205,11 +208,12 @@
         gains_ref[0:1],
         in_gate_ref[...],
         in_weight_ref[...],
+        out_gate_ref[...],
         for_right,
     )
     late_left_ref[:here] = left
     late_base_ref[:here] = base
-    late_normed_ref[:here] = normed
+    late_gate_ref[:here] = gate
     lefts = (early_left_ref, late_left_ref)
 
     own_half = [jnp.where(near_is_own, n, f) for n, f in zip(near, far)]
@@ -257,8 +261,8 @@
 
     def attention_input(products, chosen):
         normed_out = layer_norm(round_bf16(jnp.concatenate(products, axis=0)), gains_ref[1:2]).astype(bf16)
-        out_gate = sigmoid(dot(chosen(early_normed_ref, late_normed_ref).astype(bf16), out_gate_ref[...]))
-        updated = chosen(early_base_ref, late_base_ref) + out_gate * dot(normed_out, out_weight_ref[...])
+        update = chosen(early_gate_ref, late_gate_ref) * dot(normed_out, out_weight_ref[...])
+        updated = chosen(early_base_ref, late_base_ref) + update
         return updated, layer_norm(updated, gains_ref[2:3]).astype(bf16)
 
     updated, column = attention_input(products, own_columns)

time: 14.2 us -> 14.2 us (level)
  no operation moved by 1% of the time
where the time goes in v22:
time: 14.2 us; the launch traced here: 14 us
  starting transfers between devices  9.42 us (66%)
  Pallas kernels  2.69 us (19%)
  waiting for transfers between devices  1.02 us (7%)
  local copies, waits for them, and re-layouts  0.77 us (5%)
    ppermute x6, starting transfers between devices, move(): lax.ppermute(values, ('row', 'col'), [(device, device ^ step) for device...  9.42 us
    pallas_call x1, Pallas kernels, whole_pair_on_device(): pl.pallas_call(functools.partial(whole_pair_kernel, row_dim, heads, early...  2.08 us
    ppermute x6, waiting for transfers between devices, move(): lax.ppermute(values, ('row', 'col'), [(device, device ^ step) for device...  1.02 us
    unnamed x30, local copies, waits for them, and re-layouts  0.76 us
    pallas_call x1, Pallas kernels, whole_pair_on_device(): pl.pallas_call(functools.partial(early_kernel, early), out_shape=[half] *...  0.36 us
  transfers between devices with their start and end apart: 6, of which 3 were waited for; matrix products, arithmetic and copies ran while one was open for 0% of the time, Pallas kernels for 4%

profile of v22, /device:TPU:0, one launch (start us, length us, event | category | flops | bytes accessed | tf_op | source)
XLA Modules:
  0.0 14.0 jit_solution(3784419631278176605)
XLA Ops:
  0.0 0.0 copy-start.7
  0.0 0.5 %collective-permute-start = (bf16[2,8,128]{2,1,0:T(8,128)(2,1)}, bf16[2,8,128]{2,1,0:T(8,128)(2,1)S(1)}, u32[]{:S(2)}, u32[]{:S(2)}) collective-permute-start(bf16[2,8,128]{2,1,0:T(8,128)(2,1)} %pair_ref.1), channel_id=1, source_target_pairs={{0,1},{1,0},{2,3},{3,2},{4,5},{5,4},{6,7},{7,6},{8,9},{9,8},{10,11... | collective-permute-start | bytes 12296 | tf_op jit(solution)/shard_map/ppermute | solution.py:342
  0.5 0.0 copy-start.11
  0.5 0.0 copy-start.12
  0.5 0.0 copy-start.13
  0.5 0.0 copy-start.14
  0.5 0.0 copy-start.8
  0.5 0.0 copy-start.9
  0.5 0.0 copy-start.10
  0.5 0.2 %copy-done.7 = bf16[128,128]{1,0:T(8,128)(2,1)S(1)} copy-done((bf16[128,128]{1,0:T(8,128)(2,1)S(1)}, bf16[128,128]{1,0:T(8,128)(2,1)}, u32[]{:S(2)}) %copy-start.7) | copy-done | bytes 32792
  0.8 0.4 %copy-done.11 = s32[16]{0:T(128)S(1)} copy-done((s32[16]{0:T(128)S(1)}, s32[16]{0:T(128)}, u32[]{:S(2)}) %copy-start.11) | copy-done | bytes 88
  1.1 0.0 copy-done.12
  1.1 0.0 copy-done.13
  1.1 0.0 copy-done.14
  1.2 0.0 copy-done.8
  1.2 0.0 copy-done.9
  1.2 0.0 copy-done.10
  1.2 0.0 copy-start
  1.2 0.0 copy-start.1
  1.2 0.0 copy-start.2
  1.2 0.0 copy-start.4
  1.2 0.0 copy-start.5
  1.3 0.0 copy-start.6
  1.3 0.2 %shard_map.146 = (bf16[2,2,8,128]{3,2,1,0:T(8,128)(2,1)S(1)}, f32[256,128]{1,0:T(8,128)S(1)}, f32[256,128]{1,0:T(8,128)S(1)}, f32[3,128]{1,0:T(4,128)S(1)}, bf16...) custom-call(bf16[2,8,128]{2,1,0:T(8,128)(2,1)S(1)} %copy-done.8, s32[1,16]{1,0:T(1,128)S(1)} %bitcast.9, ...), custom_call_target="tpu_custom_call" | custom-call | flops 1000000000 | bytes 1048576 | tf_op jit(solution)/shard_map/pallas_call | solution.py:358
  1.5 0.0 copy-start.3
  1.5 0.0 collective-permute-done
  1.5 3.8 %collective-permute-start.1 = (bf16[2,2,8,128]{3,2,1,0:T(8,128)(2,1)S(1)}, bf16[2,2,8,128]{3,2,1,0:T(8,128)(2,1)S(1)}, u32[]{:S(2)}, u32[]{:S(2)}) collective-permute-start(bf16[2,2,8,128]{3,2,1,0:T(8,128)(2,1)S(1)} %bitcast_dynamic-update-slice_fusion.refs_0_), channel_id=1, source_target_pairs={{0,9},{1,8},{2,11},{3,10},{4,13},{5,12},{6,15},{7,14},{8,1},{9,0},... | collective-permute-start | bytes 24584 | tf_op jit(solution)/shard_map/ppermute | solution.py:342
  5.3 2.1 %collective-permute-start.4 = (bf16[2,2,8,128]{3,2,1,0:T(8,128)(2,1)S(1)}, bf16[2,2,8,128]{3,2,1,0:T(8,128)(2,1)S(1)}, u32[]{:S(2)}, u32[]{:S(2)}) collective-permute-start(bf16[2,2,8,128]{3,2,1,0:T(8,128)(2,1)S(1)} %bitcast_dynamic-update-slice_fusion.refs_0_), channel_id=1, source_target_pairs={{0,15},{1,14},{2,13},{3,12},{4,11},{5,10},{6,9},{7,8},{8,7},{9,6},... | collective-permute-start | bytes 24584 | tf_op jit(solution)/shard_map/ppermute | solution.py:342
  7.4 0.2 %collective-permute-start.5 = (bf16[2,2,8,128]{3,2,1,0:T(8,128)(2,1)S(1)}, bf16[2,2,8,128]{3,2,1,0:T(8,128)(2,1)S(1)}, u32[]{:S(2)}, u32[]{:S(2)}) collective-permute-start(bf16[2,2,8,128]{3,2,1,0:T(8,128)(2,1)S(1)} %bitcast_dynamic-update-slice_fusion.refs_0_), channel_id=1, source_target_pairs={{0,7},{1,6},{2,5},{3,4},{4,3},{5,2},{6,1},{7,0},{8,15},{9,14},{10,... | collective-permute-start | bytes 24584 | tf_op jit(solution)/shard_map/ppermute | solution.py:342
  7.7 0.0 collective-permute-done.1.refs_1_
  7.7 0.5 %collective-permute-start.2 = (bf16[4,2,8,128]{3,2,1,0:T(8,128)(2,1)S(1)}, bf16[4,2,8,128]{3,2,1,0:T(8,128)(2,1)S(1)}, u32[]{:S(2)}, u32[]{:S(2)}) collective-permute-start(bf16[4,2,8,128]{3,2,1,0:T(8,128)(2,1)S(1)} %pad_maximum_fusion), channel_id=1, source_target_pairs={{0,3},{1,2},{2,1},{3,0},{4,7},{5,6},{6,5},{7,4},{8,11},{9,10},{10,... | collective-permute-start | bytes 49160 | tf_op jit(solution)/shard_map/ppermute | solution.py:342
  8.2 2.3 %collective-permute-start.3 = (bf16[4,2,8,128]{3,2,1,0:T(8,128)(2,1)S(1)}, bf16[4,2,8,128]{3,2,1,0:T(8,128)(2,1)S(1)}, u32[]{:S(2)}, u32[]{:S(2)}) collective-permute-start(bf16[4,2,8,128]{3,2,1,0:T(8,128)(2,1)S(1)} %pad_maximum_fusion), channel_id=1, source_target_pairs={{0,5},{1,4},{2,7},{3,6},{4,1},{5,0},{6,3},{7,2},{8,13},{9,12},{10,... | collective-permute-start | bytes 49160 | tf_op jit(solution)/shard_map/ppermute | solution.py:342
  10.5 0.6 %collective-permute-done.4.refs_2_ = bf16[2,2,8,128]{3,2,1,0:T(8,128)(2,1)S(1)} collective-permute-done((bf16[2,2,8,128]{3,2,1,0:T(8,128)(2,1)S(1)}, bf16[2,2,8,128]{3,2,1,0:T(8,128)(2,1)S(1)}, u32[]{:S(2)}, u32[]{:S(2)}) %collective-permute-start.4) | collective-permute-done | bytes 8224 | tf_op jit(solution)/shard_map/ppermute | solution.py:342
  11.1 0.3 %collective-permute-done.5.refs_3_ = bf16[2,2,8,128]{3,2,1,0:T(8,128)(2,1)S(1)} collective-permute-done((bf16[2,2,8,128]{3,2,1,0:T(8,128)(2,1)S(1)}, bf16[2,2,8,128]{3,2,1,0:T(8,128)(2,1)S(1)}, u32[]{:S(2)}, u32[]{:S(2)}) %collective-permute-start.5) | collective-permute-done | bytes 8224 | tf_op jit(solution)/shard_map/ppermute | solution.py:342
  11.4 0.0 copy-done
  11.4 0.0 copy-done.1
  11.4 0.0 copy-done.2
  11.4 0.0 copy-done.4
  11.4 0.0 copy-done.5
  11.4 0.0 copy-done.6
  11.4 0.0 copy-done.3
  11.4 0.4 %shard_map.147 = (f32[144,128]{1,0:T(8,128)S(1)}, f32[144,128]{1,0:T(8,128)S(1)}, f32[144,128]{1,0:T(8,128)S(1)}, f32[144,128]{1,0:T(8,128)S(1)}) custom-call(bf16[2,2,8,128]{3,2,1,0:T(8,128)(2,1)S(1)} %bitcast_dynamic-update-slice_fusion.refs_0_, bf16[2,2,8,128]{3,2,1,0:T(8,128)(2,1)S(1)} %collective-permute-done.1.refs_1_, ...), custom_call_target="tpu_custom_call" | custom-call | flops 1000000000 | bytes 1048576 | tf_op jit(solution)/shard_map/pallas_call | solution.py:393
  11.8 0.0 collective-permute-done.2.refs_0_
  11.8 0.1 collective-permute-done.3.refs_1_
  12.0 2.1 %shard_map.148 = bf16[2,8,128]{2,1,0:T(8,128)(2,1)} custom-call(bf16[4,2,8,128]{3,2,1,0:T(8,128)(2,1)S(1)} %collective-permute-done.2.refs_0_, bf16[4,2,8,128]{3,2,1,0:T(8,128)(2,1)S(1)} %collective-permute-done.3.refs_1_, f32[144,128]{1,0:T(8,128)S(1)} %get-tuple-element.31.refs_2_, f32[144,128]{1,0:T(8,128)S(1)} %get-tuple-element.32.refs_3_, ...), custom_call_target="tpu_custom_call" | custom-call | tf_op jit(solution)/shard_map/pallas_call | solution.py:401
  (3 shorter events, 0.0 us)
Async XLA Ops:
  0.0 0.8 %copy-start.7 = (bf16[128,128]{1,0:T(8,128)(2,1)S(1)}, bf16[128,128]{1,0:T(8,128)(2,1)}, u32[]{:S(2)}) copy-start(bf16[128,128]{1,0:T(8,128)(2,1)} %table_ref.1) | copy-start | bytes 98308
  0.0 1.5 %collective-permute-start = (bf16[2,8,128]{2,1,0:T(8,128)(2,1)}, bf16[2,8,128]{2,1,0:T(8,128)(2,1)S(1)}, u32[]{:S(2)}, u32[]{:S(2)}) collective-permute-start(bf16[2,8,128]{2,1,0:T(8,128)(2,1)} %pair_ref.1), channel_id=1, source_target_pairs={{0,1},{1,0},{2,3},{3,2},{4,5},{5,4},{6,7},{7,6},{8,9},{9,8},{10,11... | collective-permute-start | bytes 12296 | tf_op jit(solution)/shard_map/ppermute | solution.py:342
  0.5 0.7 %copy-start.11 = (s32[16]{0:T(128)S(1)}, s32[16]{0:T(128)}, u32[]{:S(2)}) copy-start(s32[16]{0:T(128)} %param.19) | copy-start | bytes 196
  0.5 0.7 %copy-start.12 = (f32[128]{0:T(128)S(1)}, f32[128]{0:T(128)}, u32[]{:S(2)}) copy-start(f32[128]{0:T(128)} %param.21) | copy-start | bytes 1540
  0.5 0.7 %copy-start.13 = (f32[128]{0:T(128)S(1)}, f32[128]{0:T(128)}, u32[]{:S(2)}) copy-start(f32[128]{0:T(128)} %param.25) | copy-start | bytes 1540
  0.5 0.7 %copy-start.14 = (f32[128]{0:T(128)S(1)}, f32[128]{0:T(128)}, u32[]{:S(2)}) copy-start(f32[128]{0:T(128)} %param.27) | copy-start | bytes 1540
  0.5 0.7 %copy-start.8 = (bf16[2,8,128]{2,1,0:T(8,128)(2,1)S(1)}, bf16[2,8,128]{2,1,0:T(8,128)(2,1)}, u32[]{:S(2)}) copy-start(bf16[2,8,128]{2,1,0:T(8,128)(2,1)} %pair_ref.1) | copy-start | bytes 12292
  0.5 0.7 %copy-start.9 = (bf16[128,4]{0,1:T(4,128)(2,1)S(1)}, bf16[128,4]{0,1:T(4,128)(2,1)}, u32[]{:S(2)}) copy-start(bf16[128,4]{0,1:T(4,128)(2,1)} %param.30) | copy-start | bytes 3076
  0.5 0.7 %copy-start.10 = (s32[16]{0:T(128)S(1)}, s32[16]{0:T(128)}, u32[]{:S(2)}) copy-start(s32[16]{0:T(128)} %param.18) | copy-start | bytes 196
  1.2 10.2 %copy-start = (bf16[128,384]{1,0:T(8,128)(2,1)S(1)}, bf16[128,384]{1,0:T(8,128)(2,1)}, u32[]{:S(2)}) copy-start(bf16[128,384]{1,0:T(8,128)(2,1)} %refs_15_.1) | copy-start | bytes 294916
  1.2 10.2 %copy-start.1 = (bf16[128,256]{1,0:T(8,128)(2,1)S(1)}, bf16[128,256]{1,0:T(8,128)(2,1)}, u32[]{:S(2)}) copy-start(bf16[128,256]{1,0:T(8,128)(2,1)} %refs_11_.3) | copy-start | bytes 196612
  1.2 10.2 %copy-start.2 = (bf16[128,256]{1,0:T(8,128)(2,1)S(1)}, bf16[128,256]{1,0:T(8,128)(2,1)}, u32[]{:S(2)}) copy-start(bf16[128,256]{1,0:T(8,128)(2,1)} %refs_12_.3) | copy-start | bytes 196612
  1.2 10.2 %copy-start.4 = (bf16[128,128]{1,0:T(8,128)(2,1)S(1)}, bf16[128,128]{1,0:T(8,128)(2,1)}, u32[]{:S(2)}) copy-start(bf16[128,128]{1,0:T(8,128)(2,1)} %refs_14_.1) | copy-start | bytes 98308
  1.2 10.2 %copy-start.5 = (bf16[128,128]{1,0:T(8,128)(2,1)S(1)}, bf16[128,128]{1,0:T(8,128)(2,1)}, u32[]{:S(2)}) copy-start(bf16[128,128]{1,0:T(8,128)(2,1)} %refs_16_.1) | copy-start | bytes 98308
  1.3 10.2 %copy-start.6 = (bf16[128,128]{1,0:T(8,128)(2,1)S(1)}, bf16[128,128]{1,0:T(8,128)(2,1)}, u32[]{:S(2)}) copy-start(bf16[128,128]{1,0:T(8,128)(2,1)} %refs_17_.1) | copy-start | bytes 98308
  1.5 9.9 %copy-start.3 = (bf16[128,128]{1,0:T(8,128)(2,1)S(1)}, bf16[128,128]{1,0:T(8,128)(2,1)}, u32[]{:S(2)}) copy-start(bf16[128,128]{1,0:T(8,128)(2,1)} %refs_13_.3) | copy-start | bytes 98308
  1.5 6.1 %collective-permute-start.1 = (bf16[2,2,8,128]{3,2,1,0:T(8,128)(2,1)S(1)}, bf16[2,2,8,128]{3,2,1,0:T(8,128)(2,1)S(1)}, u32[]{:S(2)}, u32[]{:S(2)}) collective-permute-start(bf16[2,2,8,128]{3,2,1,0:T(8,128)(2,1)S(1)} %bitcast_dynamic-update-slice_fusion.refs_0_), channel_id=1, source_target_pairs={{0,9},{1,8},{2,11},{3,10},{4,13},{5,12},{6,15},{7,14},{8,1},{9,0},... | collective-permute-start | bytes 24584 | tf_op jit(solution)/shard_map/ppermute | solution.py:342
  5.3 5.8 %collective-permute-start.4 = (bf16[2,2,8,128]{3,2,1,0:T(8,128)(2,1)S(1)}, bf16[2,2,8,128]{3,2,1,0:T(8,128)(2,1)S(1)}, u32[]{:S(2)}, u32[]{:S(2)}) collective-permute-start(bf16[2,2,8,128]{3,2,1,0:T(8,128)(2,1)S(1)} %bitcast_dynamic-update-slice_fusion.refs_0_), channel_id=1, source_target_pairs={{0,15},{1,14},{2,13},{3,12},{4,11},{5,10},{6,9},{7,8},{8,7},{9,6},... | collective-permute-start | bytes 24584 | tf_op jit(solution)/shard_map/ppermute | solution.py:342
  7.4 4.0 %collective-permute-start.5 = (bf16[2,2,8,128]{3,2,1,0:T(8,128)(2,1)S(1)}, bf16[2,2,8,128]{3,2,1,0:T(8,128)(2,1)S(1)}, u32[]{:S(2)}, u32[]{:S(2)}) collective-permute-start(bf16[2,2,8,128]{3,2,1,0:T(8,128)(2,1)S(1)} %bitcast_dynamic-update-slice_fusion.refs_0_), channel_id=1, source_target_pairs={{0,7},{1,6},{2,5},{3,4},{4,3},{5,2},{6,1},{7,0},{8,15},{9,14},{10,... | collective-permute-start | bytes 24584 | tf_op jit(solution)/shard_map/ppermute | solution.py:342
  7.7 4.2 %collective-permute-start.2 = (bf16[4,2,8,128]{3,2,1,0:T(8,128)(2,1)S(1)}, bf16[4,2,8,128]{3,2,1,0:T(8,128)(2,1)S(1)}, u32[]{:S(2)}, u32[]{:S(2)}) collective-permute-start(bf16[4,2,8,128]{3,2,1,0:T(8,128)(2,1)S(1)} %pad_maximum_fusion), channel_id=1, source_target_pairs={{0,3},{1,2},{2,1},{3,0},{4,7},{5,6},{6,5},{7,4},{8,11},{9,10},{10,... | collective-permute-start | bytes 49160 | tf_op jit(solution)/shard_map/ppermute | solution.py:342
  8.2 3.8 %collective-permute-start.3 = (bf16[4,2,8,128]{3,2,1,0:T(8,128)(2,1)S(1)}, bf16[4,2,8,128]{3,2,1,0:T(8,128)(2,1)S(1)}, u32[]{:S(2)}, u32[]{:S(2)}) collective-permute-start(bf16[4,2,8,128]{3,2,1,0:T(8,128)(2,1)S(1)} %pad_maximum_fusion), channel_id=1, source_target_pairs={{0,5},{1,4},{2,7},{3,6},{4,1},{5,0},{6,3},{7,2},{8,13},{9,12},{10,... | collective-permute-start | bytes 49160 | tf_op jit(solution)/shard_map/ppermute | solution.py:342

commit v23 on v21

--- a/solution.py
+++ b/solution.py
@@ -34,6 +34,11 @@
     return lax.dot_general(
         left, right, (((1,), (1,)), ((), ())), preferred_element_type=jnp.float32
     )
+
+
+def two_dots(left, first, second):
+    both = dot(left, jnp.concatenate([first, second], axis=1))
+    return both[:, : first.shape[1]], both[:, first.shape[1] :]
 
 
 def round_bf16(values):
@@ -118,7 +123,8 @@
 
     def operand(values, mask, columns):
         values = values.astype(jnp.bfloat16)
-        return round_bf16(sigmoid(dot(values, in_gate[:, columns])) * dot(values, in_weight[:, columns]) * mask)
+        gate, value = two_dots(values, in_gate[:, columns], in_weight[:, columns])
+        return round_bf16(sigmoid(gate) * value * mask)
 
     left = operand(normed_f, pair_mask, slice(0, width))
     right = operand(for_right(normed_f), for_right(pair_mask), slice(width, 2 * width))
@@ -267,10 +273,10 @@
     column_pairs = tokens * cols
 
     own = column[:own_pairs]
-    queries = dot(own, qkv_ref[:, :width])
-    keys = dot(column, qkv_ref[:, width : 2 * width]).astype(bf16)
-    values = dot(column, qkv_ref[:, 2 * width :]).astype(bf16)
-    own_gate = sigmoid(dot(own, att_gate_ref[...]))
+    queries, own_gate = two_dots(own, qkv_ref[:, :width], att_gate_ref[...])
+    own_gate = sigmoid(own_gate)
+    both = dot(column, qkv_ref[:, width:]).astype(bf16)
+    keys, values = both[:, :width], both[:, width:]
 
     bias = dot_t(att_bias_ref[...], of_tokens).astype(bf16)
     shape = (rows * tokens, rows * column_pairs)

time: 14.2 us -> 14.3 us (level)
  no operation moved by 1% of the time
where the time goes in v23:
time: 14.3 us; the launch traced here: 14.1 us
  starting transfers between devices  9.42 us (66%)
  Pallas kernels  2.71 us (19%)
  waiting for transfers between devices  1.03 us (7%)
  local copies, waits for them, and re-layouts  0.77 us (5%)
    ppermute x6, starting transfers between devices, move(): lax.ppermute(values, ('row', 'col'), [(device, device ^ step) for device...  9.42 us
    pallas_call x1, Pallas kernels, whole_pair_on_device(): pl.pallas_call(functools.partial(whole_pair_kernel, row_dim, heads, early...  2.12 us
    ppermute x6, waiting for transfers between devices, move(): lax.ppermute(values, ('row', 'col'), [(device, device ^ step) for device...  1.03 us
    unnamed x30, local copies, waits for them, and re-layouts  0.76 us
    pallas_call x1, Pallas kernels, whole_pair_on_device(): pl.pallas_call(functools.partial(early_kernel, early), out_shape=[half] *...  0.35 us
  transfers between devices with their start and end apart: 6, of which 3 were waited for; matrix products, arithmetic and copies ran while one was open for 0% of the time, Pallas kernels for 4%

profile of v23, /device:TPU:0, one launch (start us, length us, event | category | flops | bytes accessed | tf_op | source)
XLA Modules:
  0.0 14.1 jit_solution(2128495533284082834)
XLA Ops:
  0.0 0.0 copy-start.7
  0.0 0.5 %collective-permute-start = (bf16[2,8,128]{2,1,0:T(8,128)(2,1)}, bf16[2,8,128]{2,1,0:T(8,128)(2,1)S(1)}, u32[]{:S(2)}, u32[]{:S(2)}) collective-permute-start(bf16[2,8,128]{2,1,0:T(8,128)(2,1)} %pair_ref.1), channel_id=1, source_target_pairs={{0,1},{1,0},{2,3},{3,2},{4,5},{5,4},{6,7},{7,6},{8,9},{9,8},{10,11... | collective-permute-start | bytes 12296 | tf_op jit(solution)/shard_map/ppermute | solution.py:344
  0.5 0.0 copy-start.11
  0.5 0.0 copy-start.12
  0.5 0.0 copy-start.13
  0.5 0.0 copy-start.14
  0.5 0.0 copy-start.8
  0.5 0.0 copy-start.9
  0.5 0.0 copy-start.10
  0.5 0.2 %copy-done.7 = bf16[128,128]{1,0:T(8,128)(2,1)S(1)} copy-done((bf16[128,128]{1,0:T(8,128)(2,1)S(1)}, bf16[128,128]{1,0:T(8,128)(2,1)}, u32[]{:S(2)}) %copy-start.7) | copy-done | bytes 32792
  0.8 0.4 %copy-done.11 = s32[16]{0:T(128)S(1)} copy-done((s32[16]{0:T(128)S(1)}, s32[16]{0:T(128)}, u32[]{:S(2)}) %copy-start.11) | copy-done | bytes 88
  1.1 0.0 copy-done.12
  1.1 0.0 copy-done.13
  1.1 0.0 copy-done.14
  1.2 0.0 copy-done.8
  1.2 0.0 copy-done.9
  1.2 0.0 copy-done.10
  1.2 0.0 copy-start
  1.2 0.0 copy-start.1
  1.2 0.0 copy-start.2
  1.2 0.0 copy-start.4
  1.2 0.0 copy-start.5
  1.3 0.0 copy-start.6
  1.3 0.2 %shard_map.146 = (bf16[2,2,8,128]{3,2,1,0:T(8,128)(2,1)S(1)}, f32[256,128]{1,0:T(8,128)S(1)}, f32[256,128]{1,0:T(8,128)S(1)}, f32[3,128]{1,0:T(4,128)S(1)}, bf16...) custom-call(bf16[2,8,128]{2,1,0:T(8,128)(2,1)S(1)} %copy-done.8, s32[1,16]{1,0:T(1,128)S(1)} %bitcast.9, ...), custom_call_target="tpu_custom_call" | custom-call | flops 1000000000 | bytes 1048576 | tf_op jit(solution)/shard_map/pallas_call | solution.py:360
  1.5 0.0 copy-start.3
  1.5 0.0 collective-permute-done
  1.5 3.8 %collective-permute-start.1 = (bf16[2,2,8,128]{3,2,1,0:T(8,128)(2,1)S(1)}, bf16[2,2,8,128]{3,2,1,0:T(8,128)(2,1)S(1)}, u32[]{:S(2)}, u32[]{:S(2)}) collective-permute-start(bf16[2,2,8,128]{3,2,1,0:T(8,128)(2,1)S(1)} %bitcast_dynamic-update-slice_fusion.refs_0_), channel_id=1, source_target_pairs={{0,9},{1,8},{2,11},{3,10},{4,13},{5,12},{6,15},{7,14},{8,1},{9,0},... | collective-permute-start | bytes 24584 | tf_op jit(solution)/shard_map/ppermute | solution.py:344
  5.3 2.1 %collective-permute-start.4 = (bf16[2,2,8,128]{3,2,1,0:T(8,128)(2,1)S(1)}, bf16[2,2,8,128]{3,2,1,0:T(8,128)(2,1)S(1)}, u32[]{:S(2)}, u32[]{:S(2)}) collective-permute-start(bf16[2,2,8,128]{3,2,1,0:T(8,128)(2,1)S(1)} %bitcast_dynamic-update-slice_fusion.refs_0_), channel_id=1, source_target_pairs={{0,15},{1,14},{2,13},{3,12},{4,11},{5,10},{6,9},{7,8},{8,7},{9,6},... | collective-permute-start | bytes 24584 | tf_op jit(solution)/shard_map/ppermute | solution.py:344
  7.4 0.2 %collective-permute-start.5 = (bf16[2,2,8,128]{3,2,1,0:T(8,128)(2,1)S(1)}, bf16[2,2,8,128]{3,2,1,0:T(8,128)(2,1)S(1)}, u32[]{:S(2)}, u32[]{:S(2)}) collective-permute-start(bf16[2,2,8,128]{3,2,1,0:T(8,128)(2,1)S(1)} %bitcast_dynamic-update-slice_fusion.refs_0_), channel_id=1, source_target_pairs={{0,7},{1,6},{2,5},{3,4},{4,3},{5,2},{6,1},{7,0},{8,15},{9,14},{10,... | collective-permute-start | bytes 24584 | tf_op jit(solution)/shard_map/ppermute | solution.py:344
  7.7 0.0 collective-permute-done.1.refs_1_
  7.7 0.5 %collective-permute-start.2 = (bf16[4,2,8,128]{3,2,1,0:T(8,128)(2,1)S(1)}, bf16[4,2,8,128]{3,2,1,0:T(8,128)(2,1)S(1)}, u32[]{:S(2)}, u32[]{:S(2)}) collective-permute-start(bf16[4,2,8,128]{3,2,1,0:T(8,128)(2,1)S(1)} %pad_maximum_fusion), channel_id=1, source_target_pairs={{0,3},{1,2},{2,1},{3,0},{4,7},{5,6},{6,5},{7,4},{8,11},{9,10},{10,... | collective-permute-start | bytes 49160 | tf_op jit(solution)/shard_map/ppermute | solution.py:344
  8.2 2.3 %collective-permute-start.3 = (bf16[4,2,8,128]{3,2,1,0:T(8,128)(2,1)S(1)}, bf16[4,2,8,128]{3,2,1,0:T(8,128)(2,1)S(1)}, u32[]{:S(2)}, u32[]{:S(2)}) collective-permute-start(bf16[4,2,8,128]{3,2,1,0:T(8,128)(2,1)S(1)} %pad_maximum_fusion), channel_id=1, source_target_pairs={{0,5},{1,4},{2,7},{3,6},{4,1},{5,0},{6,3},{7,2},{8,13},{9,12},{10,... | collective-permute-start | bytes 49160 | tf_op jit(solution)/shard_map/ppermute | solution.py:344
  10.5 0.6 %collective-permute-done.4.refs_2_ = bf16[2,2,8,128]{3,2,1,0:T(8,128)(2,1)S(1)} collective-permute-done((bf16[2,2,8,128]{3,2,1,0:T(8,128)(2,1)S(1)}, bf16[2,2,8,128]{3,2,1,0:T(8,128)(2,1)S(1)}, u32[]{:S(2)}, u32[]{:S(2)}) %collective-permute-start.4) | collective-permute-done | bytes 8224 | tf_op jit(solution)/shard_map/ppermute | solution.py:344
  11.1 0.3 %collective-permute-done.5.refs_3_ = bf16[2,2,8,128]{3,2,1,0:T(8,128)(2,1)S(1)} collective-permute-done((bf16[2,2,8,128]{3,2,1,0:T(8,128)(2,1)S(1)}, bf16[2,2,8,128]{3,2,1,0:T(8,128)(2,1)S(1)}, u32[]{:S(2)}, u32[]{:S(2)}) %collective-permute-start.5) | collective-permute-done | bytes 8224 | tf_op jit(solution)/shard_map/ppermute | solution.py:344
  11.4 0.0 copy-done
  11.4 0.0 copy-done.1
  11.4 0.0 copy-done.2
  11.4 0.0 copy-done.4
  11.4 0.0 copy-done.5
  11.4 0.0 copy-done.6
  11.4 0.0 copy-done.3
  11.4 0.3 %shard_map.147 = (f32[144,128]{1,0:T(8,128)S(1)}, f32[144,128]{1,0:T(8,128)S(1)}, f32[144,128]{1,0:T(8,128)S(1)}, f32[144,128]{1,0:T(8,128)S(1)}) custom-call(bf16[2,2,8,128]{3,2,1,0:T(8,128)(2,1)S(1)} %bitcast_dynamic-update-slice_fusion.refs_0_, bf16[2,2,8,128]{3,2,1,0:T(8,128)(2,1)S(1)} %collective-permute-done.1.refs_1_, ...), custom_call_target="tpu_custom_call" | custom-call | flops 1000000000 | bytes 1048576 | tf_op jit(solution)/shard_map/pallas_call | solution.py:395
  11.8 0.0 collective-permute-done.2.refs_0_
  11.8 0.1 %collective-permute-done.3.refs_1_ = bf16[4,2,8,128]{3,2,1,0:T(8,128)(2,1)S(1)} collective-permute-done((bf16[4,2,8,128]{3,2,1,0:T(8,128)(2,1)S(1)}, bf16[4,2,8,128]{3,2,1,0:T(8,128)(2,1)S(1)}, u32[]{:S(2)}, u32[]{:S(2)}) %collective-permute-start.3) | collective-permute-done | bytes 16416 | tf_op jit(solution)/shard_map/ppermute | solution.py:344
  12.0 2.1 %shard_map.148 = bf16[2,8,128]{2,1,0:T(8,128)(2,1)} custom-call(bf16[4,2,8,128]{3,2,1,0:T(8,128)(2,1)S(1)} %collective-permute-done.2.refs_0_, bf16[4,2,8,128]{3,2,1,0:T(8,128)(2,1)S(1)} %collective-permute-done.3.refs_1_, f32[144,128]{1,0:T(8,128)S(1)} %get-tuple-element.31.refs_2_, f32[144,128]{1,0:T(8,128)S(1)} %get-tuple-element.32.refs_3_, ...), custom_call_target="tpu_custom_call" | custom-call | tf_op jit(solution)/shard_map/pallas_call | solution.py:403
  (3 shorter events, 0.0 us)
Async XLA Ops:
  0.0 0.8 %copy-start.7 = (bf16[128,128]{1,0:T(8,128)(2,1)S(1)}, bf16[128,128]{1,0:T(8,128)(2,1)}, u32[]{:S(2)}) copy-start(bf16[128,128]{1,0:T(8,128)(2,1)} %table_ref.1) | copy-start | bytes 98308
  0.0 1.5 %collective-permute-start = (bf16[2,8,128]{2,1,0:T(8,128)(2,1)}, bf16[2,8,128]{2,1,0:T(8,128)(2,1)S(1)}, u32[]{:S(2)}, u32[]{:S(2)}) collective-permute-start(bf16[2,8,128]{2,1,0:T(8,128)(2,1)} %pair_ref.1), channel_id=1, source_target_pairs={{0,1},{1,0},{2,3},{3,2},{4,5},{5,4},{6,7},{7,6},{8,9},{9,8},{10,11... | collective-permute-start | bytes 12296 | tf_op jit(solution)/shard_map/ppermute | solution.py:344
  0.5 0.7 %copy-start.11 = (s32[16]{0:T(128)S(1)}, s32[16]{0:T(128)}, u32[]{:S(2)}) copy-start(s32[16]{0:T(128)} %param.19) | copy-start | bytes 196
  0.5 0.7 %copy-start.12 = (f32[128]{0:T(128)S(1)}, f32[128]{0:T(128)}, u32[]{:S(2)}) copy-start(f32[128]{0:T(128)} %param.21) | copy-start | bytes 1540
  0.5 0.7 %copy-start.13 = (f32[128]{0:T(128)S(1)}, f32[128]{0:T(128)}, u32[]{:S(2)}) copy-start(f32[128]{0:T(128)} %param.25) | copy-start | bytes 1540
  0.5 0.7 %copy-start.14 = (f32[128]{0:T(128)S(1)}, f32[128]{0:T(128)}, u32[]{:S(2)}) copy-start(f32[128]{0:T(128)} %param.27) | copy-start | bytes 1540
  0.5 0.7 %copy-start.8 = (bf16[2,8,128]{2,1,0:T(8,128)(2,1)S(1)}, bf16[2,8,128]{2,1,0:T(8,128)(2,1)}, u32[]{:S(2)}) copy-start(bf16[2,8,128]{2,1,0:T(8,128)(2,1)} %pair_ref.1) | copy-start | bytes 12292
  0.5 0.7 %copy-start.9 = (bf16[128,4]{0,1:T(4,128)(2,1)S(1)}, bf16[128,4]{0,1:T(4,128)(2,1)}, u32[]{:S(2)}) copy-start(bf16[128,4]{0,1:T(4,128)(2,1)} %param.30) | copy-start | bytes 3076
  0.5 0.7 %copy-start.10 = (s32[16]{0:T(128)S(1)}, s32[16]{0:T(128)}, u32[]{:S(2)}) copy-start(s32[16]{0:T(128)} %param.18) | copy-start | bytes 196
  1.2 10.2 %copy-start = (bf16[128,384]{1,0:T(8,128)(2,1)S(1)}, bf16[128,384]{1,0:T(8,128)(2,1)}, u32[]{:S(2)}) copy-start(bf16[128,384]{1,0:T(8,128)(2,1)} %refs_15_.1) | copy-start | bytes 294916
  1.2 10.2 %copy-start.1 = (bf16[128,256]{1,0:T(8,128)(2,1)S(1)}, bf16[128,256]{1,0:T(8,128)(2,1)}, u32[]{:S(2)}) copy-start(bf16[128,256]{1,0:T(8,128)(2,1)} %refs_11_.3) | copy-start | bytes 196612
  1.2 10.2 %copy-start.2 = (bf16[128,256]{1,0:T(8,128)(2,1)S(1)}, bf16[128,256]{1,0:T(8,128)(2,1)}, u32[]{:S(2)}) copy-start(bf16[128,256]{1,0:T(8,128)(2,1)} %refs_12_.3) | copy-start | bytes 196612
  1.2 10.2 %copy-start.4 = (bf16[128,128]{1,0:T(8,128)(2,1)S(1)}, bf16[128,128]{1,0:T(8,128)(2,1)}, u32[]{:S(2)}) copy-start(bf16[128,128]{1,0:T(8,128)(2,1)} %refs_14_.1) | copy-start | bytes 98308
  1.2 10.2 %copy-start.5 = (bf16[128,128]{1,0:T(8,128)(2,1)S(1)}, bf16[128,128]{1,0:T(8,128)(2,1)}, u32[]{:S(2)}) copy-start(bf16[128,128]{1,0:T(8,128)(2,1)} %refs_16_.1) | copy-start | bytes 98308
  1.3 10.2 %copy-start.6 = (bf16[128,128]{1,0:T(8,128)(2,1)S(1)}, bf16[128,128]{1,0:T(8,128)(2,1)}, u32[]{:S(2)}) copy-start(bf16[128,128]{1,0:T(8,128)(2,1)} %refs_17_.1) | copy-start | bytes 98308
  1.5 9.9 %copy-start.3 = (bf16[128,128]{1,0:T(8,128)(2,1)S(1)}, bf16[128,128]{1,0:T(8,128)(2,1)}, u32[]{:S(2)}) copy-start(bf16[128,128]{1,0:T(8,128)(2,1)} %refs_13_.3) | copy-start | bytes 98308
  1.5 6.1 %collective-permute-start.1 = (bf16[2,2,8,128]{3,2,1,0:T(8,128)(2,1)S(1)}, bf16[2,2,8,128]{3,2,1,0:T(8,128)(2,1)S(1)}, u32[]{:S(2)}, u32[]{:S(2)}) collective-permute-start(bf16[2,2,8,128]{3,2,1,0:T(8,128)(2,1)S(1)} %bitcast_dynamic-update-slice_fusion.refs_0_), channel_id=1, source_target_pairs={{0,9},{1,8},{2,11},{3,10},{4,13},{5,12},{6,15},{7,14},{8,1},{9,0},... | collective-permute-start | bytes 24584 | tf_op jit(solution)/shard_map/ppermute | solution.py:344
  5.3 5.8 %collective-permute-start.4 = (bf16[2,2,8,128]{3,2,1,0:T(8,128)(2,1)S(1)}, bf16[2,2,8,128]{3,2,1,0:T(8,128)(2,1)S(1)}, u32[]{:S(2)}, u32[]{:S(2)}) collective-permute-start(bf16[2,2,8,128]{3,2,1,0:T(8,128)(2,1)S(1)} %bitcast_dynamic-update-slice_fusion.refs_0_), channel_id=1, source_target_pairs={{0,15},{1,14},{2,13},{3,12},{4,11},{5,10},{6,9},{7,8},{8,7},{9,6},... | collective-permute-start | bytes 24584 | tf_op jit(solution)/shard_map/ppermute | solution.py:344
  7.4 4.0 %collective-permute-start.5 = (bf16[2,2,8,128]{3,2,1,0:T(8,128)(2,1)S(1)}, bf16[2,2,8,128]{3,2,1,0:T(8,128)(2,1)S(1)}, u32[]{:S(2)}, u32[]{:S(2)}) collective-permute-start(bf16[2,2,8,128]{3,2,1,0:T(8,128)(2,1)S(1)} %bitcast_dynamic-update-slice_fusion.refs_0_), channel_id=1, source_target_pairs={{0,7},{1,6},{2,5},{3,4},{4,3},{5,2},{6,1},{7,0},{8,15},{9,14},{10,... | collective-permute-start | bytes 24584 | tf_op jit(solution)/shard_map/ppermute | solution.py:344
  7.7 4.1 %collective-permute-start.2 = (bf16[4,2,8,128]{3,2,1,0:T(8,128)(2,1)S(1)}, bf16[4,2,8,128]{3,2,1,0:T(8,128)(2,1)S(1)}, u32[]{:S(2)}, u32[]{:S(2)}) collective-permute-start(bf16[4,2,8,128]{3,2,1,0:T(8,128)(2,1)S(1)} %pad_maximum_fusion), channel_id=1, source_target_pairs={{0,3},{1,2},{2,1},{3,0},{4,7},{5,6},{6,5},{7,4},{8,11},{9,10},{10,... | collective-permute-start | bytes 49160 | tf_op jit(solution)/shard_map/ppermute | solution.py:344
  8.2 3.8 %collective-permute-start.3 = (bf16[4,2,8,128]{3,2,1,0:T(8,128)(2,1)S(1)}, bf16[4,2,8,128]{3,2,1,0:T(8,128)(2,1)S(1)}, u32[]{:S(2)}, u32[]{:S(2)}) collective-permute-start(bf16[4,2,8,128]{3,2,1,0:T(8,128)(2,1)S(1)} %pad_maximum_fusion), channel_id=1, source_target_pairs={{0,5},{1,4},{2,7},{3,6},{4,1},{5,0},{6,3},{7,2},{8,13},{9,12},{10,... | collective-permute-start | bytes 49160 | tf_op jit(solution)/shard_map/ppermute | solution.py:344

commit v24 on v21

--- a/solution.py
+++ b/solution.py
@@ -296,12 +296,10 @@
     scores = scores + biases + key_bias
     expo = jnp.exp(scores - jnp.max(scores, axis=-1, keepdims=True))
     shares = 1.0 / jnp.sum(expo, axis=-1, keepdims=True)
-    mixed = dot(expo.astype(bf16), values) * shares
-    attended = jnp.zeros((own_pairs, width), f32)
-    for h in range(heads):
-        attended = jnp.where(head_of == h, mixed[h * own_pairs : (h + 1) * own_pairs], attended)
-
-    gated = (own_gate * attended).astype(bf16)
+    gates = jnp.concatenate([jnp.where(head_of == h, own_gate, 0.0) for h in range(heads)], axis=0)
+    mixed = dot(expo.astype(bf16), values) * (gates * shares)
+
+    gated = sum(mixed[h * own_pairs : (h + 1) * own_pairs] for h in range(heads)).astype(bf16)
     result = updated[:own_pairs] + dot(gated, att_out_ref[...])
     out_ref[...] = result.reshape(rows, cols, width).astype(bf16)
 

time: 14.2 us -> 14.2 us (level)
  no operation moved by 1% of the time
where the time goes in v24:
time: 14.2 us; the launch traced here: 14 us
  starting transfers between devices  9.42 us (66%)
  Pallas kernels  2.67 us (19%)
  waiting for transfers between devices  1.03 us (7%)
  local copies, waits for them, and re-layouts  0.77 us (5%)
    ppermute x6, starting transfers between devices, move(): lax.ppermute(values, ('row', 'col'), [(device, device ^ step) for device...  9.42 us
    pallas_call x1, Pallas kernels, whole_pair_on_device(): pl.pallas_call(functools.partial(whole_pair_kernel, row_dim, heads, early...  2.08 us
    ppermute x6, waiting for transfers between devices, move(): lax.ppermute(values, ('row', 'col'), [(device, device ^ step) for device...  1.03 us
    unnamed x30, local copies, waits for them, and re-layouts  0.76 us
    pallas_call x1, Pallas kernels, whole_pair_on_device(): pl.pallas_call(functools.partial(early_kernel, early), out_shape=[half] *...  0.35 us
  transfers between devices with their start and end apart: 6, of which 3 were waited for; matrix products, arithmetic and copies ran while one was open for 0% of the time, Pallas kernels for 4%

profile of v24, /device:TPU:0, one launch (start us, length us, event | category | flops | bytes accessed | tf_op | source)
XLA Modules:
  0.0 14.0 jit_solution(426236263825117632)
XLA Ops:
  0.0 0.0 copy-start.7
  0.0 0.5 %collective-permute-start = (bf16[2,8,128]{2,1,0:T(8,128)(2,1)}, bf16[2,8,128]{2,1,0:T(8,128)(2,1)S(1)}, u32[]{:S(2)}, u32[]{:S(2)}) collective-permute-start(bf16[2,8,128]{2,1,0:T(8,128)(2,1)} %pair_ref.1), channel_id=1, source_target_pairs={{0,1},{1,0},{2,3},{3,2},{4,5},{5,4},{6,7},{7,6},{8,9},{9,8},{10,11... | collective-permute-start | bytes 12296 | tf_op jit(solution)/shard_map/ppermute | solution.py:336
  0.5 0.0 copy-start.11
  0.5 0.0 copy-start.12
  0.5 0.0 copy-start.13
  0.5 0.0 copy-start.14
  0.5 0.0 copy-start.8
  0.5 0.0 copy-start.9
  0.5 0.0 copy-start.10
  0.5 0.2 %copy-done.7 = bf16[128,128]{1,0:T(8,128)(2,1)S(1)} copy-done((bf16[128,128]{1,0:T(8,128)(2,1)S(1)}, bf16[128,128]{1,0:T(8,128)(2,1)}, u32[]{:S(2)}) %copy-start.7) | copy-done | bytes 32792
  0.8 0.4 %copy-done.11 = s32[16]{0:T(128)S(1)} copy-done((s32[16]{0:T(128)S(1)}, s32[16]{0:T(128)}, u32[]{:S(2)}) %copy-start.11) | copy-done | bytes 88
  1.1 0.0 copy-done.12
  1.1 0.0 copy-done.13
  1.1 0.0 copy-done.14
  1.2 0.0 copy-done.8
  1.2 0.0 copy-done.9
  1.2 0.0 copy-done.10
  1.2 0.0 copy-start
  1.2 0.0 copy-start.1
  1.2 0.0 copy-start.2
  1.2 0.0 copy-start.4
  1.2 0.0 copy-start.5
  1.3 0.0 copy-start.6
  1.3 0.2 %shard_map.146 = (bf16[2,2,8,128]{3,2,1,0:T(8,128)(2,1)S(1)}, f32[256,128]{1,0:T(8,128)S(1)}, f32[256,128]{1,0:T(8,128)S(1)}, f32[3,128]{1,0:T(4,128)S(1)}, bf16...) custom-call(bf16[2,8,128]{2,1,0:T(8,128)(2,1)S(1)} %copy-done.8, s32[1,16]{1,0:T(1,128)S(1)} %bitcast.9, ...), custom_call_target="tpu_custom_call" | custom-call | flops 1000000000 | bytes 1048576 | tf_op jit(solution)/shard_map/pallas_call | solution.py:352
  1.5 0.0 copy-start.3
  1.5 0.0 collective-permute-done
  1.5 3.8 %collective-permute-start.1 = (bf16[2,2,8,128]{3,2,1,0:T(8,128)(2,1)S(1)}, bf16[2,2,8,128]{3,2,1,0:T(8,128)(2,1)S(1)}, u32[]{:S(2)}, u32[]{:S(2)}) collective-permute-start(bf16[2,2,8,128]{3,2,1,0:T(8,128)(2,1)S(1)} %bitcast_dynamic-update-slice_fusion.refs_0_), channel_id=1, source_target_pairs={{0,9},{1,8},{2,11},{3,10},{4,13},{5,12},{6,15},{7,14},{8,1},{9,0},... | collective-permute-start | bytes 24584 | tf_op jit(solution)/shard_map/ppermute | solution.py:336
  5.3 2.1 %collective-permute-start.4 = (bf16[2,2,8,128]{3,2,1,0:T(8,128)(2,1)S(1)}, bf16[2,2,8,128]{3,2,1,0:T(8,128)(2,1)S(1)}, u32[]{:S(2)}, u32[]{:S(2)}) collective-permute-start(bf16[2,2,8,128]{3,2,1,0:T(8,128)(2,1)S(1)} %bitcast_dynamic-update-slice_fusion.refs_0_), channel_id=1, source_target_pairs={{0,15},{1,14},{2,13},{3,12},{4,11},{5,10},{6,9},{7,8},{8,7},{9,6},... | collective-permute-start | bytes 24584 | tf_op jit(solution)/shard_map/ppermute | solution.py:336
  7.4 0.2 %collective-permute-start.5 = (bf16[2,2,8,128]{3,2,1,0:T(8,128)(2,1)S(1)}, bf16[2,2,8,128]{3,2,1,0:T(8,128)(2,1)S(1)}, u32[]{:S(2)}, u32[]{:S(2)}) collective-permute-start(bf16[2,2,8,128]{3,2,1,0:T(8,128)(2,1)S(1)} %bitcast_dynamic-update-slice_fusion.refs_0_), channel_id=1, source_target_pairs={{0,7},{1,6},{2,5},{3,4},{4,3},{5,2},{6,1},{7,0},{8,15},{9,14},{10,... | collective-permute-start | bytes 24584 | tf_op jit(solution)/shard_map/ppermute | solution.py:336
  7.7 0.0 collective-permute-done.1.refs_1_
  7.7 0.5 %collective-permute-start.2 = (bf16[4,2,8,128]{3,2,1,0:T(8,128)(2,1)S(1)}, bf16[4,2,8,128]{3,2,1,0:T(8,128)(2,1)S(1)}, u32[]{:S(2)}, u32[]{:S(2)}) collective-permute-start(bf16[4,2,8,128]{3,2,1,0:T(8,128)(2,1)S(1)} %pad_maximum_fusion), channel_id=1, source_target_pairs={{0,3},{1,2},{2,1},{3,0},{4,7},{5,6},{6,5},{7,4},{8,11},{9,10},{10,... | collective-permute-start | bytes 49160 | tf_op jit(solution)/shard_map/ppermute | solution.py:336
  8.2 2.3 %collective-permute-start.3 = (bf16[4,2,8,128]{3,2,1,0:T(8,128)(2,1)S(1)}, bf16[4,2,8,128]{3,2,1,0:T(8,128)(2,1)S(1)}, u32[]{:S(2)}, u32[]{:S(2)}) collective-permute-start(bf16[4,2,8,128]{3,2,1,0:T(8,128)(2,1)S(1)} %pad_maximum_fusion), channel_id=1, source_target_pairs={{0,5},{1,4},{2,7},{3,6},{4,1},{5,0},{6,3},{7,2},{8,13},{9,12},{10,... | collective-permute-start | bytes 49160 | tf_op jit(solution)/shard_map/ppermute | solution.py:336
  10.5 0.6 %collective-permute-done.4.refs_2_ = bf16[2,2,8,128]{3,2,1,0:T(8,128)(2,1)S(1)} collective-permute-done((bf16[2,2,8,128]{3,2,1,0:T(8,128)(2,1)S(1)}, bf16[2,2,8,128]{3,2,1,0:T(8,128)(2,1)S(1)}, u32[]{:S(2)}, u32[]{:S(2)}) %collective-permute-start.4) | collective-permute-done | bytes 8224 | tf_op jit(solution)/shard_map/ppermute | solution.py:336
  11.1 0.3 %collective-permute-done.5.refs_3_ = bf16[2,2,8,128]{3,2,1,0:T(8,128)(2,1)S(1)} collective-permute-done((bf16[2,2,8,128]{3,2,1,0:T(8,128)(2,1)S(1)}, bf16[2,2,8,128]{3,2,1,0:T(8,128)(2,1)S(1)}, u32[]{:S(2)}, u32[]{:S(2)}) %collective-permute-start.5) | collective-permute-done | bytes 8224 | tf_op jit(solution)/shard_map/ppermute | solution.py:336
  11.4 0.0 copy-done
  11.4 0.0 copy-done.1
  11.4 0.0 copy-done.2
  11.4 0.0 copy-done.4
  11.4 0.0 copy-done.5
  11.4 0.0 copy-done.6
  11.4 0.0 copy-done.3
  11.4 0.3 %shard_map.147 = (f32[144,128]{1,0:T(8,128)S(1)}, f32[144,128]{1,0:T(8,128)S(1)}, f32[144,128]{1,0:T(8,128)S(1)}, f32[144,128]{1,0:T(8,128)S(1)}) custom-call(bf16[2,2,8,128]{3,2,1,0:T(8,128)(2,1)S(1)} %bitcast_dynamic-update-slice_fusion.refs_0_, bf16[2,2,8,128]{3,2,1,0:T(8,128)(2,1)S(1)} %collective-permute-done.1.refs_1_, ...), custom_call_target="tpu_custom_call" | custom-call | flops 1000000000 | bytes 1048576 | tf_op jit(solution)/shard_map/pallas_call | solution.py:387
  11.8 0.0 collective-permute-done.2.refs_0_
  11.8 0.1 %collective-permute-done.3.refs_1_ = bf16[4,2,8,128]{3,2,1,0:T(8,128)(2,1)S(1)} collective-permute-done((bf16[4,2,8,128]{3,2,1,0:T(8,128)(2,1)S(1)}, bf16[4,2,8,128]{3,2,1,0:T(8,128)(2,1)S(1)}, u32[]{:S(2)}, u32[]{:S(2)}) %collective-permute-start.3) | collective-permute-done | bytes 16416 | tf_op jit(solution)/shard_map/ppermute | solution.py:336
  12.0 2.1 %shard_map.148 = bf16[2,8,128]{2,1,0:T(8,128)(2,1)} custom-call(bf16[4,2,8,128]{3,2,1,0:T(8,128)(2,1)S(1)} %collective-permute-done.2.refs_0_, bf16[4,2,8,128]{3,2,1,0:T(8,128)(2,1)S(1)} %collective-permute-done.3.refs_1_, f32[144,128]{1,0:T(8,128)S(1)} %get-tuple-element.31.refs_2_, f32[144,128]{1,0:T(8,128)S(1)} %get-tuple-element.32.refs_3_, ...), custom_call_target="tpu_custom_call" | custom-call | tf_op jit(solution)/shard_map/pallas_call | solution.py:395
  (3 shorter events, 0.0 us)
Async XLA Ops:
  0.0 0.8 %copy-start.7 = (bf16[128,128]{1,0:T(8,128)(2,1)S(1)}, bf16[128,128]{1,0:T(8,128)(2,1)}, u32[]{:S(2)}) copy-start(bf16[128,128]{1,0:T(8,128)(2,1)} %table_ref.1) | copy-start | bytes 98308
  0.0 1.5 %collective-permute-start = (bf16[2,8,128]{2,1,0:T(8,128)(2,1)}, bf16[2,8,128]{2,1,0:T(8,128)(2,1)S(1)}, u32[]{:S(2)}, u32[]{:S(2)}) collective-permute-start(bf16[2,8,128]{2,1,0:T(8,128)(2,1)} %pair_ref.1), channel_id=1, source_target_pairs={{0,1},{1,0},{2,3},{3,2},{4,5},{5,4},{6,7},{7,6},{8,9},{9,8},{10,11... | collective-permute-start | bytes 12296 | tf_op jit(solution)/shard_map/ppermute | solution.py:336
  0.5 0.7 %copy-start.11 = (s32[16]{0:T(128)S(1)}, s32[16]{0:T(128)}, u32[]{:S(2)}) copy-start(s32[16]{0:T(128)} %param.19) | copy-start | bytes 196
  0.5 0.7 %copy-start.12 = (f32[128]{0:T(128)S(1)}, f32[128]{0:T(128)}, u32[]{:S(2)}) copy-start(f32[128]{0:T(128)} %param.21) | copy-start | bytes 1540
  0.5 0.7 %copy-start.13 = (f32[128]{0:T(128)S(1)}, f32[128]{0:T(128)}, u32[]{:S(2)}) copy-start(f32[128]{0:T(128)} %param.25) | copy-start | bytes 1540
  0.5 0.7 %copy-start.14 = (f32[128]{0:T(128)S(1)}, f32[128]{0:T(128)}, u32[]{:S(2)}) copy-start(f32[128]{0:T(128)} %param.27) | copy-start | bytes 1540
  0.5 0.7 %copy-start.8 = (bf16[2,8,128]{2,1,0:T(8,128)(2,1)S(1)}, bf16[2,8,128]{2,1,0:T(8,128)(2,1)}, u32[]{:S(2)}) copy-start(bf16[2,8,128]{2,1,0:T(8,128)(2,1)} %pair_ref.1) | copy-start | bytes 12292
  0.5 0.7 %copy-start.9 = (bf16[128,4]{0,1:T(4,128)(2,1)S(1)}, bf16[128,4]{0,1:T(4,128)(2,1)}, u32[]{:S(2)}) copy-start(bf16[128,4]{0,1:T(4,128)(2,1)} %param.30) | copy-start | bytes 3076
  0.5 0.7 %copy-start.10 = (s32[16]{0:T(128)S(1)}, s32[16]{0:T(128)}, u32[]{:S(2)}) copy-start(s32[16]{0:T(128)} %param.18) | copy-start | bytes 196
  1.2 10.2 %copy-start = (bf16[128,384]{1,0:T(8,128)(2,1)S(1)}, bf16[128,384]{1,0:T(8,128)(2,1)}, u32[]{:S(2)}) copy-start(bf16[128,384]{1,0:T(8,128)(2,1)} %refs_15_.1) | copy-start | bytes 294916
  1.2 10.2 %copy-start.1 = (bf16[128,256]{1,0:T(8,128)(2,1)S(1)}, bf16[128,256]{1,0:T(8,128)(2,1)}, u32[]{:S(2)}) copy-start(bf16[128,256]{1,0:T(8,128)(2,1)} %refs_11_.3) | copy-start | bytes 196612
  1.2 10.2 %copy-start.2 = (bf16[128,256]{1,0:T(8,128)(2,1)S(1)}, bf16[128,256]{1,0:T(8,128)(2,1)}, u32[]{:S(2)}) copy-start(bf16[128,256]{1,0:T(8,128)(2,1)} %refs_12_.3) | copy-start | bytes 196612
  1.2 10.2 %copy-start.4 = (bf16[128,128]{1,0:T(8,128)(2,1)S(1)}, bf16[128,128]{1,0:T(8,128)(2,1)}, u32[]{:S(2)}) copy-start(bf16[128,128]{1,0:T(8,128)(2,1)} %refs_14_.1) | copy-start | bytes 98308
  1.2 10.2 %copy-start.5 = (bf16[128,128]{1,0:T(8,128)(2,1)S(1)}, bf16[128,128]{1,0:T(8,128)(2,1)}, u32[]{:S(2)}) copy-start(bf16[128,128]{1,0:T(8,128)(2,1)} %refs_16_.1) | copy-start | bytes 98308
  1.3 10.2 %copy-start.6 = (bf16[128,128]{1,0:T(8,128)(2,1)S(1)}, bf16[128,128]{1,0:T(8,128)(2,1)}, u32[]{:S(2)}) copy-start(bf16[128,128]{1,0:T(8,128)(2,1)} %refs_17_.1) | copy-start | bytes 98308
  1.5 9.9 %copy-start.3 = (bf16[128,128]{1,0:T(8,128)(2,1)S(1)}, bf16[128,128]{1,0:T(8,128)(2,1)}, u32[]{:S(2)}) copy-start(bf16[128,128]{1,0:T(8,128)(2,1)} %refs_13_.3) | copy-start | bytes 98308
  1.5 6.1 %collective-permute-start.1 = (bf16[2,2,8,128]{3,2,1,0:T(8,128)(2,1)S(1)}, bf16[2,2,8,128]{3,2,1,0:T(8,128)(2,1)S(1)}, u32[]{:S(2)}, u32[]{:S(2)}) collective-permute-start(bf16[2,2,8,128]{3,2,1,0:T(8,128)(2,1)S(1)} %bitcast_dynamic-update-slice_fusion.refs_0_), channel_id=1, source_target_pairs={{0,9},{1,8},{2,11},{3,10},{4,13},{5,12},{6,15},{7,14},{8,1},{9,0},... | collective-permute-start | bytes 24584 | tf_op jit(solution)/shard_map/ppermute | solution.py:336
  5.3 5.8 %collective-permute-start.4 = (bf16[2,2,8,128]{3,2,1,0:T(8,128)(2,1)S(1)}, bf16[2,2,8,128]{3,2,1,0:T(8,128)(2,1)S(1)}, u32[]{:S(2)}, u32[]{:S(2)}) collective-permute-start(bf16[2,2,8,128]{3,2,1,0:T(8,128)(2,1)S(1)} %bitcast_dynamic-update-slice_fusion.refs_0_), channel_id=1, source_target_pairs={{0,15},{1,14},{2,13},{3,12},{4,11},{5,10},{6,9},{7,8},{8,7},{9,6},... | collective-permute-start | bytes 24584 | tf_op jit(solution)/shard_map/ppermute | solution.py:336
  7.4 4.0 %collective-permute-start.5 = (bf16[2,2,8,128]{3,2,1,0:T(8,128)(2,1)S(1)}, bf16[2,2,8,128]{3,2,1,0:T(8,128)(2,1)S(1)}, u32[]{:S(2)}, u32[]{:S(2)}) collective-permute-start(bf16[2,2,8,128]{3,2,1,0:T(8,128)(2,1)S(1)} %bitcast_dynamic-update-slice_fusion.refs_0_), channel_id=1, source_target_pairs={{0,7},{1,6},{2,5},{3,4},{4,3},{5,2},{6,1},{7,0},{8,15},{9,14},{10,... | collective-permute-start | bytes 24584 | tf_op jit(solution)/shard_map/ppermute | solution.py:336
  7.7 4.1 %collective-permute-start.2 = (bf16[4,2,8,128]{3,2,1,0:T(8,128)(2,1)S(1)}, bf16[4,2,8,128]{3,2,1,0:T(8,128)(2,1)S(1)}, u32[]{:S(2)}, u32[]{:S(2)}) collective-permute-start(bf16[4,2,8,128]{3,2,1,0:T(8,128)(2,1)S(1)} %pad_maximum_fusion), channel_id=1, source_target_pairs={{0,3},{1,2},{2,1},{3,0},{4,7},{5,6},{6,5},{7,4},{8,11},{9,10},{10,... | collective-permute-start | bytes 49160 | tf_op jit(solution)/shard_map/ppermute | solution.py:336
  8.2 3.8 %collective-permute-start.3 = (bf16[4,2,8,128]{3,2,1,0:T(8,128)(2,1)S(1)}, bf16[4,2,8,128]{3,2,1,0:T(8,128)(2,1)S(1)}, u32[]{:S(2)}, u32[]{:S(2)}) collective-permute-start(bf16[4,2,8,128]{3,2,1,0:T(8,128)(2,1)S(1)} %pad_maximum_fusion), channel_id=1, source_target_pairs={{0,5},{1,4},{2,7},{3,6},{4,1},{5,0},{6,3},{7,2},{8,13},{9,12},{10,... | collective-permute-start | bytes 49160 | tf_op jit(solution)/shard_map/ppermute | solution.py:336

commit v25 on v24

--- a/solution.py
+++ b/solution.py
@@ -100,7 +100,7 @@
         for half in halves:
             bucket = jnp.clip(pos - pos_rows_ref[half, :], -centre, centre - 1.0) + centre
             first = len(hot) * cols
-            pair_mask_ref[first : first + cols, :] = mask_rows_ref[half, :] * mask
+            pair_mask_ref[first : first + cols, :] = mask_rows_ref[half, :] * (0.5 * mask)
             hot.append((bucket == lane).astype(f32))
         key_mask = jnp.where(key_of == at, mask, key_mask)
     rel_ref[...] = dot(jnp.concatenate(hot, axis=0).astype(jnp.bfloat16), table_ref[...])
@@ -118,7 +118,8 @@
 
     def operand(values, mask, columns):
         values = values.astype(jnp.bfloat16)
-        return round_bf16(sigmoid(dot(values, in_gate[:, columns])) * dot(values, in_weight[:, columns]) * mask)
+        gate = jnp.tanh(0.5 * dot(values, in_gate[:, columns])) + 1.0
+        return round_bf16(gate * (dot(values, in_weight[:, columns]) * mask))
 
     left = operand(normed_f, pair_mask, slice(0, width))
     right = operand(for_right(normed_f), for_right(pair_mask), slice(width, 2 * width))

time: 14.2 us -> 14.2 us (level)
  no operation moved by 1% of the time
where the time goes in v25:
time: 14.2 us; the launch traced here: 14 us
  starting transfers between devices  9.42 us (66%)
  Pallas kernels  2.66 us (19%)
  waiting for transfers between devices  1.04 us (7%)
  local copies, waits for them, and re-layouts  0.77 us (5%)
    ppermute x6, starting transfers between devices, move(): lax.ppermute(values, ('row', 'col'), [(device, device ^ step) for device...  9.42 us
    pallas_call x1, Pallas kernels, whole_pair_on_device(): pl.pallas_call(functools.partial(whole_pair_kernel, row_dim, heads, early...  2.08 us
    ppermute x6, waiting for transfers between devices, move(): lax.ppermute(values, ('row', 'col'), [(device, device ^ step) for device...  1.04 us
    unnamed x30, local copies, waits for them, and re-layouts  0.76 us
    pallas_call x1, Pallas kernels, whole_pair_on_device(): pl.pallas_call(functools.partial(early_kernel, early), out_shape=[half] *...  0.34 us
  transfers between devices with their start and end apart: 6, of which 3 were waited for; matrix products, arithmetic and copies ran while one was open for 0% of the time, Pallas kernels for 4%

profile of v25, /device:TPU:0, one launch (start us, length us, event | category | flops | bytes accessed | tf_op | source)
XLA Modules:
  0.0 14.0 jit_solution(13330929540767972856)
XLA Ops:
  0.0 0.0 copy-start.7
  0.0 0.5 %collective-permute-start = (bf16[2,8,128]{2,1,0:T(8,128)(2,1)}, bf16[2,8,128]{2,1,0:T(8,128)(2,1)S(1)}, u32[]{:S(2)}, u32[]{:S(2)}) collective-permute-start(bf16[2,8,128]{2,1,0:T(8,128)(2,1)} %pair_ref.1), channel_id=1, source_target_pairs={{0,1},{1,0},{2,3},{3,2},{4,5},{5,4},{6,7},{7,6},{8,9},{9,8},{10,11... | collective-permute-start | bytes 12296 | tf_op jit(solution)/shard_map/ppermute | solution.py:337
  0.5 0.0 copy-start.11
  0.5 0.0 copy-start.12
  0.5 0.0 copy-start.13
  0.5 0.0 copy-start.14
  0.5 0.0 copy-start.8
  0.5 0.0 copy-start.9
  0.5 0.0 copy-start.10
  0.5 0.2 %copy-done.7 = bf16[128,128]{1,0:T(8,128)(2,1)S(1)} copy-done((bf16[128,128]{1,0:T(8,128)(2,1)S(1)}, bf16[128,128]{1,0:T(8,128)(2,1)}, u32[]{:S(2)}) %copy-start.7) | copy-done | bytes 32792
  0.8 0.4 %copy-done.11 = s32[16]{0:T(128)S(1)} copy-done((s32[16]{0:T(128)S(1)}, s32[16]{0:T(128)}, u32[]{:S(2)}) %copy-start.11) | copy-done | bytes 88
  1.1 0.0 copy-done.12
  1.1 0.0 copy-done.13
  1.1 0.0 copy-done.14
  1.2 0.0 copy-done.8
  1.2 0.0 copy-done.9
  1.2 0.0 copy-done.10
  1.2 0.0 copy-start
  1.2 0.0 copy-start.1
  1.2 0.0 copy-start.2
  1.2 0.0 copy-start.4
  1.2 0.0 copy-start.5
  1.3 0.0 copy-start.6
  1.3 0.2 %shard_map.146 = (bf16[2,2,8,128]{3,2,1,0:T(8,128)(2,1)S(1)}, f32[256,128]{1,0:T(8,128)S(1)}, f32[256,128]{1,0:T(8,128)S(1)}, f32[3,128]{1,0:T(4,128)S(1)}, bf16...) custom-call(bf16[2,8,128]{2,1,0:T(8,128)(2,1)S(1)} %copy-done.8, s32[1,16]{1,0:T(1,128)S(1)} %bitcast.9, ...), custom_call_target="tpu_custom_call" | custom-call | flops 1000000000 | bytes 1048576 | tf_op jit(solution)/shard_map/pallas_call | solution.py:353
  1.5 0.0 copy-start.3
  1.5 0.0 collective-permute-done
  1.5 3.8 %collective-permute-start.1 = (bf16[2,2,8,128]{3,2,1,0:T(8,128)(2,1)S(1)}, bf16[2,2,8,128]{3,2,1,0:T(8,128)(2,1)S(1)}, u32[]{:S(2)}, u32[]{:S(2)}) collective-permute-start(bf16[2,2,8,128]{3,2,1,0:T(8,128)(2,1)S(1)} %bitcast_dynamic-update-slice_fusion.refs_0_), channel_id=1, source_target_pairs={{0,9},{1,8},{2,11},{3,10},{4,13},{5,12},{6,15},{7,14},{8,1},{9,0},... | collective-permute-start | bytes 24584 | tf_op jit(solution)/shard_map/ppermute | solution.py:337
  5.3 2.1 %collective-permute-start.4 = (bf16[2,2,8,128]{3,2,1,0:T(8,128)(2,1)S(1)}, bf16[2,2,8,128]{3,2,1,0:T(8,128)(2,1)S(1)}, u32[]{:S(2)}, u32[]{:S(2)}) collective-permute-start(bf16[2,2,8,128]{3,2,1,0:T(8,128)(2,1)S(1)} %bitcast_dynamic-update-slice_fusion.refs_0_), channel_id=1, source_target_pairs={{0,15},{1,14},{2,13},{3,12},{4,11},{5,10},{6,9},{7,8},{8,7},{9,6},... | collective-permute-start | bytes 24584 | tf_op jit(solution)/shard_map/ppermute | solution.py:337
  7.4 0.2 %collective-permute-start.5 = (bf16[2,2,8,128]{3,2,1,0:T(8,128)(2,1)S(1)}, bf16[2,2,8,128]{3,2,1,0:T(8,128)(2,1)S(1)}, u32[]{:S(2)}, u32[]{:S(2)}) collective-permute-start(bf16[2,2,8,128]{3,2,1,0:T(8,128)(2,1)S(1)} %bitcast_dynamic-update-slice_fusion.refs_0_), channel_id=1, source_target_pairs={{0,7},{1,6},{2,5},{3,4},{4,3},{5,2},{6,1},{7,0},{8,15},{9,14},{10,... | collective-permute-start | bytes 24584 | tf_op jit(solution)/shard_map/ppermute | solution.py:337
  7.7 0.0 collective-permute-done.1.refs_1_
  7.7 0.5 %collective-permute-start.2 = (bf16[4,2,8,128]{3,2,1,0:T(8,128)(2,1)S(1)}, bf16[4,2,8,128]{3,2,1,0:T(8,128)(2,1)S(1)}, u32[]{:S(2)}, u32[]{:S(2)}) collective-permute-start(bf16[4,2,8,128]{3,2,1,0:T(8,128)(2,1)S(1)} %pad_maximum_fusion), channel_id=1, source_target_pairs={{0,3},{1,2},{2,1},{3,0},{4,7},{5,6},{6,5},{7,4},{8,11},{9,10},{10,... | collective-permute-start | bytes 49160 | tf_op jit(solution)/shard_map/ppermute | solution.py:337
  8.2 2.3 %collective-permute-start.3 = (bf16[4,2,8,128]{3,2,1,0:T(8,128)(2,1)S(1)}, bf16[4,2,8,128]{3,2,1,0:T(8,128)(2,1)S(1)}, u32[]{:S(2)}, u32[]{:S(2)}) collective-permute-start(bf16[4,2,8,128]{3,2,1,0:T(8,128)(2,1)S(1)} %pad_maximum_fusion), channel_id=1, source_target_pairs={{0,5},{1,4},{2,7},{3,6},{4,1},{5,0},{6,3},{7,2},{8,13},{9,12},{10,... | collective-permute-start | bytes 49160 | tf_op jit(solution)/shard_map/ppermute | solution.py:337
  10.5 0.6 %collective-permute-done.4.refs_2_ = bf16[2,2,8,128]{3,2,1,0:T(8,128)(2,1)S(1)} collective-permute-done((bf16[2,2,8,128]{3,2,1,0:T(8,128)(2,1)S(1)}, bf16[2,2,8,128]{3,2,1,0:T(8,128)(2,1)S(1)}, u32[]{:S(2)}, u32[]{:S(2)}) %collective-permute-start.4) | collective-permute-done | bytes 8224 | tf_op jit(solution)/shard_map/ppermute | solution.py:337
  11.1 0.3 %collective-permute-done.5.refs_3_ = bf16[2,2,8,128]{3,2,1,0:T(8,128)(2,1)S(1)} collective-permute-done((bf16[2,2,8,128]{3,2,1,0:T(8,128)(2,1)S(1)}, bf16[2,2,8,128]{3,2,1,0:T(8,128)(2,1)S(1)}, u32[]{:S(2)}, u32[]{:S(2)}) %collective-permute-start.5) | collective-permute-done | bytes 8224 | tf_op jit(solution)/shard_map/ppermute | solution.py:337
  11.4 0.0 copy-done
  11.4 0.0 copy-done.1
  11.4 0.0 copy-done.2
  11.4 0.0 copy-done.4
  11.4 0.0 copy-done.5
  11.4 0.0 copy-done.6
  11.4 0.0 copy-done.3
  11.4 0.3 %shard_map.147 = (f32[144,128]{1,0:T(8,128)S(1)}, f32[144,128]{1,0:T(8,128)S(1)}, f32[144,128]{1,0:T(8,128)S(1)}, f32[144,128]{1,0:T(8,128)S(1)}) custom-call(bf16[2,2,8,128]{3,2,1,0:T(8,128)(2,1)S(1)} %bitcast_dynamic-update-slice_fusion.refs_0_, bf16[2,2,8,128]{3,2,1,0:T(8,128)(2,1)S(1)} %collective-permute-done.1.refs_1_, ...), custom_call_target="tpu_custom_call" | custom-call | flops 1000000000 | bytes 1048576 | tf_op jit(solution)/shard_map/pallas_call | solution.py:388
  11.8 0.0 collective-permute-done.2.refs_0_
  11.8 0.1 %collective-permute-done.3.refs_1_ = bf16[4,2,8,128]{3,2,1,0:T(8,128)(2,1)S(1)} collective-permute-done((bf16[4,2,8,128]{3,2,1,0:T(8,128)(2,1)S(1)}, bf16[4,2,8,128]{3,2,1,0:T(8,128)(2,1)S(1)}, u32[]{:S(2)}, u32[]{:S(2)}) %collective-permute-start.3) | collective-permute-done | bytes 16416 | tf_op jit(solution)/shard_map/ppermute | solution.py:337
  12.0 2.1 %shard_map.148 = bf16[2,8,128]{2,1,0:T(8,128)(2,1)} custom-call(bf16[4,2,8,128]{3,2,1,0:T(8,128)(2,1)S(1)} %collective-permute-done.2.refs_0_, bf16[4,2,8,128]{3,2,1,0:T(8,128)(2,1)S(1)} %collective-permute-done.3.refs_1_, f32[144,128]{1,0:T(8,128)S(1)} %get-tuple-element.31.refs_2_, f32[144,128]{1,0:T(8,128)S(1)} %get-tuple-element.32.refs_3_, ...), custom_call_target="tpu_custom_call" | custom-call | tf_op jit(solution)/shard_map/pallas_call | solution.py:396
  (3 shorter events, 0.0 us)
Async XLA Ops:
  0.0 0.8 %copy-start.7 = (bf16[128,128]{1,0:T(8,128)(2,1)S(1)}, bf16[128,128]{1,0:T(8,128)(2,1)}, u32[]{:S(2)}) copy-start(bf16[128,128]{1,0:T(8,128)(2,1)} %table_ref.1) | copy-start | bytes 98308
  0.0 1.5 %collective-permute-start = (bf16[2,8,128]{2,1,0:T(8,128)(2,1)}, bf16[2,8,128]{2,1,0:T(8,128)(2,1)S(1)}, u32[]{:S(2)}, u32[]{:S(2)}) collective-permute-start(bf16[2,8,128]{2,1,0:T(8,128)(2,1)} %pair_ref.1), channel_id=1, source_target_pairs={{0,1},{1,0},{2,3},{3,2},{4,5},{5,4},{6,7},{7,6},{8,9},{9,8},{10,11... | collective-permute-start | bytes 12296 | tf_op jit(solution)/shard_map/ppermute | solution.py:337
  0.5 0.7 %copy-start.11 = (s32[16]{0:T(128)S(1)}, s32[16]{0:T(128)}, u32[]{:S(2)}) copy-start(s32[16]{0:T(128)} %param.19) | copy-start | bytes 196
  0.5 0.7 %copy-start.12 = (f32[128]{0:T(128)S(1)}, f32[128]{0:T(128)}, u32[]{:S(2)}) copy-start(f32[128]{0:T(128)} %param.21) | copy-start | bytes 1540
  0.5 0.7 %copy-start.13 = (f32[128]{0:T(128)S(1)}, f32[128]{0:T(128)}, u32[]{:S(2)}) copy-start(f32[128]{0:T(128)} %param.25) | copy-start | bytes 1540
  0.5 0.7 %copy-start.14 = (f32[128]{0:T(128)S(1)}, f32[128]{0:T(128)}, u32[]{:S(2)}) copy-start(f32[128]{0:T(128)} %param.27) | copy-start | bytes 1540
  0.5 0.7 %copy-start.8 = (bf16[2,8,128]{2,1,0:T(8,128)(2,1)S(1)}, bf16[2,8,128]{2,1,0:T(8,128)(2,1)}, u32[]{:S(2)}) copy-start(bf16[2,8,128]{2,1,0:T(8,128)(2,1)} %pair_ref.1) | copy-start | bytes 12292
  0.5 0.7 %copy-start.9 = (bf16[128,4]{0,1:T(4,128)(2,1)S(1)}, bf16[128,4]{0,1:T(4,128)(2,1)}, u32[]{:S(2)}) copy-start(bf16[128,4]{0,1:T(4,128)(2,1)} %param.30) | copy-start | bytes 3076
  0.5 0.7 %copy-start.10 = (s32[16]{0:T(128)S(1)}, s32[16]{0:T(128)}, u32[]{:S(2)}) copy-start(s32[16]{0:T(128)} %param.18) | copy-start | bytes 196
  1.2 10.2 %copy-start = (bf16[128,384]{1,0:T(8,128)(2,1)S(1)}, bf16[128,384]{1,0:T(8,128)(2,1)}, u32[]{:S(2)}) copy-start(bf16[128,384]{1,0:T(8,128)(2,1)} %refs_15_.1) | copy-start | bytes 294916
  1.2 10.2 %copy-start.1 = (bf16[128,256]{1,0:T(8,128)(2,1)S(1)}, bf16[128,256]{1,0:T(8,128)(2,1)}, u32[]{:S(2)}) copy-start(bf16[128,256]{1,0:T(8,128)(2,1)} %refs_11_.3) | copy-start | bytes 196612
  1.2 10.2 %copy-start.2 = (bf16[128,256]{1,0:T(8,128)(2,1)S(1)}, bf16[128,256]{1,0:T(8,128)(2,1)}, u32[]{:S(2)}) copy-start(bf16[128,256]{1,0:T(8,128)(2,1)} %refs_12_.3) | copy-start | bytes 196612
  1.2 10.2 %copy-start.4 = (bf16[128,128]{1,0:T(8,128)(2,1)S(1)}, bf16[128,128]{1,0:T(8,128)(2,1)}, u32[]{:S(2)}) copy-start(bf16[128,128]{1,0:T(8,128)(2,1)} %refs_14_.1) | copy-start | bytes 98308
  1.2 10.2 %copy-start.5 = (bf16[128,128]{1,0:T(8,128)(2,1)S(1)}, bf16[128,128]{1,0:T(8,128)(2,1)}, u32[]{:S(2)}) copy-start(bf16[128,128]{1,0:T(8,128)(2,1)} %refs_16_.1) | copy-start | bytes 98308
  1.3 10.2 %copy-start.6 = (bf16[128,128]{1,0:T(8,128)(2,1)S(1)}, bf16[128,128]{1,0:T(8,128)(2,1)}, u32[]{:S(2)}) copy-start(bf16[128,128]{1,0:T(8,128)(2,1)} %refs_17_.1) | copy-start | bytes 98308
  1.5 9.9 %copy-start.3 = (bf16[128,128]{1,0:T(8,128)(2,1)S(1)}, bf16[128,128]{1,0:T(8,128)(2,1)}, u32[]{:S(2)}) copy-start(bf16[128,128]{1,0:T(8,128)(2,1)} %refs_13_.3) | copy-start | bytes 98308
  1.5 6.1 %collective-permute-start.1 = (bf16[2,2,8,128]{3,2,1,0:T(8,128)(2,1)S(1)}, bf16[2,2,8,128]{3,2,1,0:T(8,128)(2,1)S(1)}, u32[]{:S(2)}, u32[]{:S(2)}) collective-permute-start(bf16[2,2,8,128]{3,2,1,0:T(8,128)(2,1)S(1)} %bitcast_dynamic-update-slice_fusion.refs_0_), channel_id=1, source_target_pairs={{0,9},{1,8},{2,11},{3,10},{4,13},{5,12},{6,15},{7,14},{8,1},{9,0},... | collective-permute-start | bytes 24584 | tf_op jit(solution)/shard_map/ppermute | solution.py:337
  5.3 5.8 %collective-permute-start.4 = (bf16[2,2,8,128]{3,2,1,0:T(8,128)(2,1)S(1)}, bf16[2,2,8,128]{3,2,1,0:T(8,128)(2,1)S(1)}, u32[]{:S(2)}, u32[]{:S(2)}) collective-permute-start(bf16[2,2,8,128]{3,2,1,0:T(8,128)(2,1)S(1)} %bitcast_dynamic-update-slice_fusion.refs_0_), channel_id=1, source_target_pairs={{0,15},{1,14},{2,13},{3,12},{4,11},{5,10},{6,9},{7,8},{8,7},{9,6},... | collective-permute-start | bytes 24584 | tf_op jit(solution)/shard_map/ppermute | solution.py:337
  7.4 4.0 %collective-permute-start.5 = (bf16[2,2,8,128]{3,2,1,0:T(8,128)(2,1)S(1)}, bf16[2,2,8,128]{3,2,1,0:T(8,128)(2,1)S(1)}, u32[]{:S(2)}, u32[]{:S(2)}) collective-permute-start(bf16[2,2,8,128]{3,2,1,0:T(8,128)(2,1)S(1)} %bitcast_dynamic-update-slice_fusion.refs_0_), channel_id=1, source_target_pairs={{0,7},{1,6},{2,5},{3,4},{4,3},{5,2},{6,1},{7,0},{8,15},{9,14},{10,... | collective-permute-start | bytes 24584 | tf_op jit(solution)/shard_map/ppermute | solution.py:337
  7.7 4.1 %collective-permute-start.2 = (bf16[4,2,8,128]{3,2,1,0:T(8,128)(2,1)S(1)}, bf16[4,2,8,128]{3,2,1,0:T(8,128)(2,1)S(1)}, u32[]{:S(2)}, u32[]{:S(2)}) collective-permute-start(bf16[4,2,8,128]{3,2,1,0:T(8,128)(2,1)S(1)} %pad_maximum_fusion), channel_id=1, source_target_pairs={{0,3},{1,2},{2,1},{3,0},{4,7},{5,6},{6,5},{7,4},{8,11},{9,10},{10,... | collective-permute-start | bytes 49160 | tf_op jit(solution)/shard_map/ppermute | solution.py:337
  8.2 3.8 %collective-permute-start.3 = (bf16[4,2,8,128]{3,2,1,0:T(8,128)(2,1)S(1)}, bf16[4,2,8,128]{3,2,1,0:T(8,128)(2,1)S(1)}, u32[]{:S(2)}, u32[]{:S(2)}) collective-permute-start(bf16[4,2,8,128]{3,2,1,0:T(8,128)(2,1)S(1)} %pad_maximum_fusion), channel_id=1, source_target_pairs={{0,5},{1,4},{2,7},{3,6},{4,1},{5,0},{6,3},{7,2},{8,13},{9,12},{10,... | collective-permute-start | bytes 49160 | tf_op jit(solution)/shard_map/ppermute | solution.py:337
